TPU v7x, 256 devices: a whole 4x4x8 slice. The times are simulated.
256 devices in a mesh: group: 8 (over y_lo, x), blk: 32 (over z, y_hi, core).
Axes of the slice: x: 4, y: 4 (y_hi: 2, y_lo: 2; y = y_hi * 2 + y_lo), z: 8, core: 2. Of those that a mesh axis runs over, the one named last changes fastest.
Arguments:
- candidates: bfloat16 [32768, 8, 4096], P('blk', 'group'), may hold values from -6 to 6
- queries: bfloat16 [1024, 8, 4096], P('blk', 'group'), may hold values from -6 to 6
- out_factor: float32 [8, 64, 64], P('group'), may hold values from -0.75 to 0.75
- in_factor: float32 [8, 64, 64], P('group'), may hold values from -0.75 to 0.75
- panel_order: int32 [32], replicated, may hold values from 0 to 31, each once
Outputs:
- scores: float32 [32768, 1024], P('blk', 'group')
Inputs may be any that keep to these rules, and one draw needn't show every extreme that they name: `panel_order`: a permutation of the panel numbers.
All inputs are finite; a program needn't handle non-finite values.
Results may differ from a plain program's by a relative error of at most 0.0029.
Values may be sent and summed in bfloat16 or wider, within the bound.
No kernel may reach another device: no remote copies, remote signals or barrier semaphores. Data moves between devices by JAX's collectives and lax.ppermute only.
A program may use at most 64 MiB of HBM per device.

v0:
```python
import jax
import jax.numpy as jnp
from jax import lax
from jax.sharding import PartitionSpec as P


def passed_along(block, axis, distance):
    devices = range(lax.axis_size(axis))
    route = [((i - distance) % len(devices), i) for i in devices]
    return lax.ppermute(block, axis, route)


def score_block(flat, panel, factor):
    part = lax.dot_general(
        flat, panel, (((1,), (1,)), ((), ())), preferred_element_type=jnp.float32
    )
    return part * factor


def slot_of(panel_order, source):
    places = jnp.arange(panel_order.shape[0], dtype=jnp.int32)
    return jnp.sum(jnp.where(panel_order == source, places, 0))


def place(buffer, part, panel_order, source, width):
    column = slot_of(panel_order, source) * width
    return lax.dynamic_update_slice(buffer, part, (jnp.int32(0), column))


def body(candidates, queries, out_factor, in_factor, panel_order):
    cand_rows, layer_count, features = candidates.shape
    width = queries.shape[0]
    out_units = out_factor.shape[1]
    in_units = in_factor.shape[1]
    cycle = lax.axis_size("blk")
    groups = lax.axis_size("group")
    factor = 1.0 / (features * layer_count * groups) ** 0.5
    grads = queries.astype(jnp.float32).reshape(width, layer_count, out_units, in_units)
    left = jnp.einsum("lab,qlbc->qlac", out_factor, grads, precision=lax.Precision.HIGHEST)
    precond = jnp.einsum("qlac,lcd->qlad", left, in_factor, precision=lax.Precision.HIGHEST)
    panel = precond.reshape(width, layer_count * features).astype(jnp.bfloat16)
    flat = candidates.reshape(cand_rows, layer_count * features)
    index = lax.axis_index("blk")
    total_cols = width * cycle
    buffer = jnp.zeros((cand_rows, total_cols), jnp.float32)
    second = passed_along(panel, "blk", 1)
    both = score_block(flat, jnp.concatenate([panel, second], axis=0), factor)
    buffer = place(buffer, both[:, :width], panel_order, index, width)
    buffer = place(buffer, both[:, width:], panel_order, (index - 1) % cycle, width)

    def turn(step, carry):
        first_panel, second_panel, buffer = carry
        first_panel, second_panel = passed_along((first_panel, second_panel), "blk", 2)
        both = score_block(flat, jnp.concatenate([first_panel, second_panel], axis=0), factor)
        buffer = place(buffer, both[:, :width], panel_order, (index - 2 * step) % cycle, width)
        buffer = place(buffer, both[:, width:], panel_order, (index - 2 * step - 1) % cycle, width)
        return (first_panel, second_panel, buffer)

    first_panel, second_panel, buffer = lax.fori_loop(1, cycle // 2, turn, (panel, second, buffer))
    return lax.psum_scatter(buffer, "group", scatter_dimension=1, tiled=True)


def solution(mesh):
    in_specs = (
        P("blk", "group", None),
        P("blk", "group", None),
        P("group", None, None),
        P("group", None, None),
        P(),
    )
    out_specs = P("blk", "group")
    return jax.shard_map(body, mesh=mesh, in_specs=in_specs, out_specs=out_specs, check_vma=False)
```

profile of v0, /device:TPU:1, one launch (start us, length us, event | category | flops | bytes accessed | tf_op | source)
XLA Modules:
  0.0 417.3 jit_solution(10889871405641037593)
XLA Ops:
  11.7 4.4 %collective-permute-start.2 = (bf16[32,4096]{1,0:T(8,128)(2,1)S(1)}, bf16[32,4096]{1,0:T(8,128)(2,1)S(1)}, u32[]{:S(2)}, u32[]{:S(2)}) collective-permute-start(bf16[32,4096]{1,0:T(8,128)(2,1)S(1)} %convert_element_type.20), channel_id=1, source_target_pairs={{31,0},{0,1},{1,2},{2,3},{3,4},{4,5},{5,6},{6,7},{7,8},{8,9},{9,10... | collective-permute-start | bytes 786440 | tf_op jit(solution)/shard_map/ppermute | solution.py:10
  19.4 6.0 %fusion.8 = f32[1024,64]{0,1:T(8,128)S(1)} fusion(bf16[32,4096]{1,0:T(8,128)(2,1)S(1)} %collective-permute-done.2, bf16[32,4096]{1,0:T(8,128)(2,1)S(1)} %convert_element_type.20, bf16[1024,1,4096]{2,0,1:T(8,128)(2,1)} %param.7), kind=kOutput, calls=%fused_computation.16 | convolution fusion | flops 537985024 | bytes 9175040 | tf_op jit(solution)/shard_map/dot_general | solution.py:14
  28.0 301.3 %while.19 = (s32[]{:T(128)}, bf16[32,4096]{1,0:T(8,128)(2,1)S(1)}, bf16[32,4096]{1,0:T(8,128)(2,1)S(1)}, f32[1024,1024]{0,1:T(8,128)}, bf16[1024,4096]{1,0:T(8,1...) while((s32[]{:T(128)}, bf16[32,4096]{1,0:T(8,128)(2,1)S(1)}, ...), condition=%wide.region_5.6_spmd, body=%wide.region_2.5_spmd.sunk | while | flops 537985216 | bytes 12845767 | solution.py:59
  29.4 2.9 collective-permute-start
  36.8 2.8 collective-permute-done
  39.6 6.0 %fusion.28 = f32[1024,64]{0,1:T(8,128)S(1)} fusion(bf16[1024,4096]{1,0:T(8,128)(2,1)} %get-tuple-element.281, bf16[32,4096]{1,0:T(8,128)(2,1)S(1)} %collective-permute-done.1, bf16[32,4096]{1,0:T(8,128)(2,1)S(1)} %collective-permute-done), kind=kOutput, calls=%fused_computation.1.clone.1 | convolution fusion | flops 537985024 | bytes 9175040 | tf_op jit(solution)/shard_map/while/body/eval_jaxpr/dot_general | solution.py:14
  48.9 4.6 %collective-permute-start = (bf16[32,4096]{1,0:T(8,128)(2,1)S(1)}, bf16[32,4096]{1,0:T(8,128)(2,1)S(1)}, u32[]{:S(2)}, u32[]{:S(2)}) collective-permute-start(bf16[32,4096]{1,0:T(8,128)(2,1)S(1)} %get-tuple-element.264), channel_id=1, source_target_pairs={{30,0},{31,1},{0,2},{1,3},{2,4},{3,5},{4,6},{5,7},{6,8},{7,9},{8,1... | collective-permute-start | bytes 786440 | tf_op jit(solution)/shard_map/while/body/eval_jaxpr/ppermute | solution.py:10
  56.0 3.0 collective-permute-done
  58.9 6.0 %fusion.28 = f32[1024,64]{0,1:T(8,128)S(1)} fusion(bf16[1024,4096]{1,0:T(8,128)(2,1)} %get-tuple-element.281, bf16[32,4096]{1,0:T(8,128)(2,1)S(1)} %collective-permute-done.1, bf16[32,4096]{1,0:T(8,128)(2,1)S(1)} %collective-permute-done), kind=kOutput, calls=%fused_computation.1.clone.1 | convolution fusion | flops 537985024 | bytes 9175040 | tf_op jit(solution)/shard_map/while/body/eval_jaxpr/dot_general | solution.py:14
  66.3 3.8 collective-permute-start.1
  70.1 3.8 collective-permute-start
  77.9 2.8 collective-permute-done
  80.7 6.0 %fusion.28 = f32[1024,64]{0,1:T(8,128)S(1)} fusion(bf16[1024,4096]{1,0:T(8,128)(2,1)} %get-tuple-element.281, bf16[32,4096]{1,0:T(8,128)(2,1)S(1)} %collective-permute-done.1, bf16[32,4096]{1,0:T(8,128)(2,1)S(1)} %collective-permute-done), kind=kOutput, calls=%fused_computation.1.clone.1 | convolution fusion | flops 537985024 | bytes 9175040 | tf_op jit(solution)/shard_map/while/body/eval_jaxpr/dot_general | solution.py:14
  97.4 2.8 collective-permute-done
  100.2 6.0 %fusion.28 = f32[1024,64]{0,1:T(8,128)S(1)} fusion(bf16[1024,4096]{1,0:T(8,128)(2,1)} %get-tuple-element.281, bf16[32,4096]{1,0:T(8,128)(2,1)S(1)} %collective-permute-done.1, bf16[32,4096]{1,0:T(8,128)(2,1)S(1)} %collective-permute-done), kind=kOutput, calls=%fused_computation.1.clone.1 | convolution fusion | flops 537985024 | bytes 9175040 | tf_op jit(solution)/shard_map/while/body/eval_jaxpr/dot_general | solution.py:14
  108.9 2.8 collective-permute-start
  116.5 2.8 collective-permute-done
  119.3 6.0 %fusion.28 = f32[1024,64]{0,1:T(8,128)S(1)} fusion(bf16[1024,4096]{1,0:T(8,128)(2,1)} %get-tuple-element.281, bf16[32,4096]{1,0:T(8,128)(2,1)S(1)} %collective-permute-done.1, bf16[32,4096]{1,0:T(8,128)(2,1)S(1)} %collective-permute-done), kind=kOutput, calls=%fused_computation.1.clone.1 | convolution fusion | flops 537985024 | bytes 9175040 | tf_op jit(solution)/shard_map/while/body/eval_jaxpr/dot_general | solution.py:14
  126.8 2.8 collective-permute-start
  131.7 4.0 collective-permute-done.1
  135.7 2.8 collective-permute-done
  138.5 6.0 %fusion.28 = f32[1024,64]{0,1:T(8,128)S(1)} fusion(bf16[1024,4096]{1,0:T(8,128)(2,1)} %get-tuple-element.281, bf16[32,4096]{1,0:T(8,128)(2,1)S(1)} %collective-permute-done.1, bf16[32,4096]{1,0:T(8,128)(2,1)S(1)} %collective-permute-done), kind=kOutput, calls=%fused_computation.1.clone.1 | convolution fusion | flops 537985024 | bytes 9175040 | tf_op jit(solution)/shard_map/while/body/eval_jaxpr/dot_general | solution.py:14
  149.6 5.2 %collective-permute-done.1 = bf16[32,4096]{1,0:T(8,128)(2,1)S(1)} collective-permute-done((bf16[32,4096]{1,0:T(8,128)(2,1)S(1)}, bf16[32,4096]{1,0:T(8,128)(2,1)S(1)}, u32[]{:S(2)}, u32[]{:S(2)}) %collective-permute-start.1) | collective-permute-done | bytes 262176 | tf_op jit(solution)/shard_map/while/body/eval_jaxpr/ppermute | solution.py:10
  154.8 2.8 collective-permute-done
  157.6 6.0 %fusion.28 = f32[1024,64]{0,1:T(8,128)S(1)} fusion(bf16[1024,4096]{1,0:T(8,128)(2,1)} %get-tuple-element.281, bf16[32,4096]{1,0:T(8,128)(2,1)S(1)} %collective-permute-done.1, bf16[32,4096]{1,0:T(8,128)(2,1)S(1)} %collective-permute-done), kind=kOutput, calls=%fused_computation.1.clone.1 | convolution fusion | flops 537985024 | bytes 9175040 | tf_op jit(solution)/shard_map/while/body/eval_jaxpr/dot_general | solution.py:14
  167.6 6.4 %collective-permute-done.1 = bf16[32,4096]{1,0:T(8,128)(2,1)S(1)} collective-permute-done((bf16[32,4096]{1,0:T(8,128)(2,1)S(1)}, bf16[32,4096]{1,0:T(8,128)(2,1)S(1)}, u32[]{:S(2)}, u32[]{:S(2)}) %collective-permute-start.1) | collective-permute-done | bytes 262176 | tf_op jit(solution)/shard_map/while/body/eval_jaxpr/ppermute | solution.py:10
  174.0 2.8 collective-permute-done
  176.8 6.0 %fusion.28 = f32[1024,64]{0,1:T(8,128)S(1)} fusion(bf16[1024,4096]{1,0:T(8,128)(2,1)} %get-tuple-element.281, bf16[32,4096]{1,0:T(8,128)(2,1)S(1)} %collective-permute-done.1, bf16[32,4096]{1,0:T(8,128)(2,1)S(1)} %collective-permute-done), kind=kOutput, calls=%fused_computation.1.clone.1 | convolution fusion | flops 537985024 | bytes 9175040 | tf_op jit(solution)/shard_map/while/body/eval_jaxpr/dot_general | solution.py:14
  186.4 6.7 %collective-permute-done.1 = bf16[32,4096]{1,0:T(8,128)(2,1)S(1)} collective-permute-done((bf16[32,4096]{1,0:T(8,128)(2,1)S(1)}, bf16[32,4096]{1,0:T(8,128)(2,1)S(1)}, u32[]{:S(2)}, u32[]{:S(2)}) %collective-permute-start.1) | collective-permute-done | bytes 262176 | tf_op jit(solution)/shard_map/while/body/eval_jaxpr/ppermute | solution.py:10
  193.1 2.8 collective-permute-done
  195.9 6.0 %fusion.28 = f32[1024,64]{0,1:T(8,128)S(1)} fusion(bf16[1024,4096]{1,0:T(8,128)(2,1)} %get-tuple-element.281, bf16[32,4096]{1,0:T(8,128)(2,1)S(1)} %collective-permute-done.1, bf16[32,4096]{1,0:T(8,128)(2,1)S(1)} %collective-permute-done), kind=kOutput, calls=%fused_computation.1.clone.1 | convolution fusion | flops 537985024 | bytes 9175040 | tf_op jit(solution)/shard_map/while/body/eval_jaxpr/dot_general | solution.py:14
  205.6 6.7 %collective-permute-done.1 = bf16[32,4096]{1,0:T(8,128)(2,1)S(1)} collective-permute-done((bf16[32,4096]{1,0:T(8,128)(2,1)S(1)}, bf16[32,4096]{1,0:T(8,128)(2,1)S(1)}, u32[]{:S(2)}, u32[]{:S(2)}) %collective-permute-start.1) | collective-permute-done | bytes 262176 | tf_op jit(solution)/shard_map/while/body/eval_jaxpr/ppermute | solution.py:10
  212.2 2.8 collective-permute-done
  215.0 6.0 %fusion.28 = f32[1024,64]{0,1:T(8,128)S(1)} fusion(bf16[1024,4096]{1,0:T(8,128)(2,1)} %get-tuple-element.281, bf16[32,4096]{1,0:T(8,128)(2,1)S(1)} %collective-permute-done.1, bf16[32,4096]{1,0:T(8,128)(2,1)S(1)} %collective-permute-done), kind=kOutput, calls=%fused_computation.1.clone.1 | convolution fusion | flops 537985024 | bytes 9175040 | tf_op jit(solution)/shard_map/while/body/eval_jaxpr/dot_general | solution.py:14
  224.7 6.7 %collective-permute-done.1 = bf16[32,4096]{1,0:T(8,128)(2,1)S(1)} collective-permute-done((bf16[32,4096]{1,0:T(8,128)(2,1)S(1)}, bf16[32,4096]{1,0:T(8,128)(2,1)S(1)}, u32[]{:S(2)}, u32[]{:S(2)}) %collective-permute-start.1) | collective-permute-done | bytes 262176 | tf_op jit(solution)/shard_map/while/body/eval_jaxpr/ppermute | solution.py:10
  234.2 6.0 %fusion.28 = f32[1024,64]{0,1:T(8,128)S(1)} fusion(bf16[1024,4096]{1,0:T(8,128)(2,1)} %get-tuple-element.281, bf16[32,4096]{1,0:T(8,128)(2,1)S(1)} %collective-permute-done.1, bf16[32,4096]{1,0:T(8,128)(2,1)S(1)} %collective-permute-done), kind=kOutput, calls=%fused_computation.1.clone.1 | convolution fusion | flops 537985024 | bytes 9175040 | tf_op jit(solution)/shard_map/while/body/eval_jaxpr/dot_general | solution.py:14
  243.9 7.8 %collective-permute-done.1 = bf16[32,4096]{1,0:T(8,128)(2,1)S(1)} collective-permute-done((bf16[32,4096]{1,0:T(8,128)(2,1)S(1)}, bf16[32,4096]{1,0:T(8,128)(2,1)S(1)}, u32[]{:S(2)}, u32[]{:S(2)}) %collective-permute-start.1) | collective-permute-done | bytes 262176 | tf_op jit(solution)/shard_map/while/body/eval_jaxpr/ppermute | solution.py:10
  254.5 6.0 %fusion.28 = f32[1024,64]{0,1:T(8,128)S(1)} fusion(bf16[1024,4096]{1,0:T(8,128)(2,1)} %get-tuple-element.281, bf16[32,4096]{1,0:T(8,128)(2,1)S(1)} %collective-permute-done.1, bf16[32,4096]{1,0:T(8,128)(2,1)S(1)} %collective-permute-done), kind=kOutput, calls=%fused_computation.1.clone.1 | convolution fusion | flops 537985024 | bytes 9175040 | tf_op jit(solution)/shard_map/while/body/eval_jaxpr/dot_general | solution.py:14
  264.2 8.9 %collective-permute-done.1 = bf16[32,4096]{1,0:T(8,128)(2,1)S(1)} collective-permute-done((bf16[32,4096]{1,0:T(8,128)(2,1)S(1)}, bf16[32,4096]{1,0:T(8,128)(2,1)S(1)}, u32[]{:S(2)}, u32[]{:S(2)}) %collective-permute-start.1) | collective-permute-done | bytes 262176 | tf_op jit(solution)/shard_map/while/body/eval_jaxpr/ppermute | solution.py:10
  275.9 6.0 %fusion.28 = f32[1024,64]{0,1:T(8,128)S(1)} fusion(bf16[1024,4096]{1,0:T(8,128)(2,1)} %get-tuple-element.281, bf16[32,4096]{1,0:T(8,128)(2,1)S(1)} %collective-permute-done.1, bf16[32,4096]{1,0:T(8,128)(2,1)S(1)} %collective-permute-done), kind=kOutput, calls=%fused_computation.1.clone.1 | convolution fusion | flops 537985024 | bytes 9175040 | tf_op jit(solution)/shard_map/while/body/eval_jaxpr/dot_general | solution.py:14
  285.5 9.8 %collective-permute-done.1 = bf16[32,4096]{1,0:T(8,128)(2,1)S(1)} collective-permute-done((bf16[32,4096]{1,0:T(8,128)(2,1)S(1)}, bf16[32,4096]{1,0:T(8,128)(2,1)S(1)}, u32[]{:S(2)}, u32[]{:S(2)}) %collective-permute-start.1) | collective-permute-done | bytes 262176 | tf_op jit(solution)/shard_map/while/body/eval_jaxpr/ppermute | solution.py:10
  295.4 3.0 collective-permute-done
  298.3 6.0 %fusion.28 = f32[1024,64]{0,1:T(8,128)S(1)} fusion(bf16[1024,4096]{1,0:T(8,128)(2,1)} %get-tuple-element.281, bf16[32,4096]{1,0:T(8,128)(2,1)S(1)} %collective-permute-done.1, bf16[32,4096]{1,0:T(8,128)(2,1)S(1)} %collective-permute-done), kind=kOutput, calls=%fused_computation.1.clone.1 | convolution fusion | flops 537985024 | bytes 9175040 | tf_op jit(solution)/shard_map/while/body/eval_jaxpr/dot_general | solution.py:14
  308.0 9.8 %collective-permute-done.1 = bf16[32,4096]{1,0:T(8,128)(2,1)S(1)} collective-permute-done((bf16[32,4096]{1,0:T(8,128)(2,1)S(1)}, bf16[32,4096]{1,0:T(8,128)(2,1)S(1)}, u32[]{:S(2)}, u32[]{:S(2)}) %collective-permute-start.1) | collective-permute-done | bytes 262176 | tf_op jit(solution)/shard_map/while/body/eval_jaxpr/ppermute | solution.py:10
  317.8 4.1 collective-permute-done
  321.8 6.0 %fusion.28 = f32[1024,64]{0,1:T(8,128)S(1)} fusion(bf16[1024,4096]{1,0:T(8,128)(2,1)} %get-tuple-element.281, bf16[32,4096]{1,0:T(8,128)(2,1)S(1)} %collective-permute-done.1, bf16[32,4096]{1,0:T(8,128)(2,1)S(1)} %collective-permute-done), kind=kOutput, calls=%fused_computation.1.clone.1 | convolution fusion | flops 537985024 | bytes 9175040 | tf_op jit(solution)/shard_map/while/body/eval_jaxpr/dot_general | solution.py:14
  329.3 5.4 %copy.8 = f32[1024,1024]{1,0:T(8,128)} copy(f32[1024,1024]{0,1:T(8,128)} %get-tuple-element.183) | data formatting | bytes 8388608 | tf_op jit(solution)/shard_map/while | solution.py:59
  334.6 75.8 %reduce-scatter.2.cloned.1.call-done = f32[1024,128]{1,0:T(8,128)} async-done(((f32[1024,1024]{1,0:T(8,128)}), f32[1024,128]{1,0:T(8,128)}) %reduce-scatter.2.cloned.1.call-update) | async-done | bytes 524304 | tf_op jit(solution)/shard_map/reduce_scatter | solution.py:60
  (124 shorter events, 72.0 us)
Async XLA Ops:
  6.5 1.5 copy-start
  6.5 9.6 %copy-start.2 = (s32[32]{0:T(128)S(1)}, s32[32]{0:T(128)}, u32[]{:S(2)}) copy-start(s32[32]{0:T(128)} %param.11) | copy-start | bytes 388
  6.5 403.9 %reduce-scatter.2.cloned.1.call-start = ((), (), s32[]{:S(2)}) async-start(), calls=%async_computation.1 | async-start | bytes 4718592 | tf_op jit(solution)/shard_map/reduce_scatter | solution.py:60
  11.7 7.7 %collective-permute-start.2 = (bf16[32,4096]{1,0:T(8,128)(2,1)S(1)}, bf16[32,4096]{1,0:T(8,128)(2,1)S(1)}, u32[]{:S(2)}, u32[]{:S(2)}) collective-permute-start(bf16[32,4096]{1,0:T(8,128)(2,1)S(1)} %convert_element_type.20), channel_id=1, source_target_pairs={{31,0},{0,1},{1,2},{2,3},{3,4},{4,5},{5,6},{6,7},{7,8},{8,9},{9,10... | collective-permute-start | bytes 786440 | tf_op jit(solution)/shard_map/ppermute | solution.py:10
  26.0 1.9 copy-start.1
  28.0 8.8 %collective-permute-start.1 = (bf16[32,4096]{1,0:T(8,128)(2,1)S(1)}, bf16[32,4096]{1,0:T(8,128)(2,1)S(1)}, u32[]{:S(2)}, u32[]{:S(2)}) collective-permute-start(bf16[32,4096]{1,0:T(8,128)(2,1)S(1)} %get-tuple-element.265), channel_id=1, source_target_pairs={{30,0},{31,1},{0,2},{1,3},{2,4},{3,5},{4,6},{5,7},{6,8},{7,9},{8,1... | collective-permute-start | bytes 786440 | tf_op jit(solution)/shard_map/while/body/eval_jaxpr/ppermute | solution.py:10
  29.4 10.2 %collective-permute-start = (bf16[32,4096]{1,0:T(8,128)(2,1)S(1)}, bf16[32,4096]{1,0:T(8,128)(2,1)S(1)}, u32[]{:S(2)}, u32[]{:S(2)}) collective-permute-start(bf16[32,4096]{1,0:T(8,128)(2,1)S(1)} %get-tuple-element.264), channel_id=1, source_target_pairs={{30,0},{31,1},{0,2},{1,3},{2,4},{3,5},{4,6},{5,7},{6,8},{7,9},{8,1... | collective-permute-start | bytes 786440 | tf_op jit(solution)/shard_map/while/body/eval_jaxpr/ppermute | solution.py:10
  47.0 8.9 %collective-permute-start.1 = (bf16[32,4096]{1,0:T(8,128)(2,1)S(1)}, bf16[32,4096]{1,0:T(8,128)(2,1)S(1)}, u32[]{:S(2)}, u32[]{:S(2)}) collective-permute-start(bf16[32,4096]{1,0:T(8,128)(2,1)S(1)} %get-tuple-element.265), channel_id=1, source_target_pairs={{30,0},{31,1},{0,2},{1,3},{2,4},{3,5},{4,6},{5,7},{6,8},{7,9},{8,1... | collective-permute-start | bytes 786440 | tf_op jit(solution)/shard_map/while/body/eval_jaxpr/ppermute | solution.py:10
  48.9 10.0 %collective-permute-start = (bf16[32,4096]{1,0:T(8,128)(2,1)S(1)}, bf16[32,4096]{1,0:T(8,128)(2,1)S(1)}, u32[]{:S(2)}, u32[]{:S(2)}) collective-permute-start(bf16[32,4096]{1,0:T(8,128)(2,1)S(1)} %get-tuple-element.264), channel_id=1, source_target_pairs={{30,0},{31,1},{0,2},{1,3},{2,4},{3,5},{4,6},{5,7},{6,8},{7,9},{8,1... | collective-permute-start | bytes 786440 | tf_op jit(solution)/shard_map/while/body/eval_jaxpr/ppermute | solution.py:10
  66.3 11.6 %collective-permute-start.1 = (bf16[32,4096]{1,0:T(8,128)(2,1)S(1)}, bf16[32,4096]{1,0:T(8,128)(2,1)S(1)}, u32[]{:S(2)}, u32[]{:S(2)}) collective-permute-start(bf16[32,4096]{1,0:T(8,128)(2,1)S(1)} %get-tuple-element.265), channel_id=1, source_target_pairs={{30,0},{31,1},{0,2},{1,3},{2,4},{3,5},{4,6},{5,7},{6,8},{7,9},{8,1... | collective-permute-start | bytes 786440 | tf_op jit(solution)/shard_map/while/body/eval_jaxpr/ppermute | solution.py:10
  70.1 10.6 %collective-permute-start = (bf16[32,4096]{1,0:T(8,128)(2,1)S(1)}, bf16[32,4096]{1,0:T(8,128)(2,1)S(1)}, u32[]{:S(2)}, u32[]{:S(2)}) collective-permute-start(bf16[32,4096]{1,0:T(8,128)(2,1)S(1)} %get-tuple-element.264), channel_id=1, source_target_pairs={{30,0},{31,1},{0,2},{1,3},{2,4},{3,5},{4,6},{5,7},{6,8},{7,9},{8,1... | collective-permute-start | bytes 786440 | tf_op jit(solution)/shard_map/while/body/eval_jaxpr/ppermute | solution.py:10
  88.2 9.2 %collective-permute-start.1 = (bf16[32,4096]{1,0:T(8,128)(2,1)S(1)}, bf16[32,4096]{1,0:T(8,128)(2,1)S(1)}, u32[]{:S(2)}, u32[]{:S(2)}) collective-permute-start(bf16[32,4096]{1,0:T(8,128)(2,1)S(1)} %get-tuple-element.265), channel_id=1, source_target_pairs={{30,0},{31,1},{0,2},{1,3},{2,4},{3,5},{4,6},{5,7},{6,8},{7,9},{8,1... | collective-permute-start | bytes 786440 | tf_op jit(solution)/shard_map/while/body/eval_jaxpr/ppermute | solution.py:10
  90.5 9.7 %collective-permute-start = (bf16[32,4096]{1,0:T(8,128)(2,1)S(1)}, bf16[32,4096]{1,0:T(8,128)(2,1)S(1)}, u32[]{:S(2)}, u32[]{:S(2)}) collective-permute-start(bf16[32,4096]{1,0:T(8,128)(2,1)S(1)} %get-tuple-element.264), channel_id=1, source_target_pairs={{30,0},{31,1},{0,2},{1,3},{2,4},{3,5},{4,6},{5,7},{6,8},{7,9},{8,1... | collective-permute-start | bytes 786440 | tf_op jit(solution)/shard_map/while/body/eval_jaxpr/ppermute | solution.py:10
  107.6 8.9 %collective-permute-start.1 = (bf16[32,4096]{1,0:T(8,128)(2,1)S(1)}, bf16[32,4096]{1,0:T(8,128)(2,1)S(1)}, u32[]{:S(2)}, u32[]{:S(2)}) collective-permute-start(bf16[32,4096]{1,0:T(8,128)(2,1)S(1)} %get-tuple-element.265), channel_id=1, source_target_pairs={{30,0},{31,1},{0,2},{1,3},{2,4},{3,5},{4,6},{5,7},{6,8},{7,9},{8,1... | collective-permute-start | bytes 786440 | tf_op jit(solution)/shard_map/while/body/eval_jaxpr/ppermute | solution.py:10
  108.9 10.4 %collective-permute-start = (bf16[32,4096]{1,0:T(8,128)(2,1)S(1)}, bf16[32,4096]{1,0:T(8,128)(2,1)S(1)}, u32[]{:S(2)}, u32[]{:S(2)}) collective-permute-start(bf16[32,4096]{1,0:T(8,128)(2,1)S(1)} %get-tuple-element.264), channel_id=1, source_target_pairs={{30,0},{31,1},{0,2},{1,3},{2,4},{3,5},{4,6},{5,7},{6,8},{7,9},{8,1... | collective-permute-start | bytes 786440 | tf_op jit(solution)/shard_map/while/body/eval_jaxpr/ppermute | solution.py:10
  126.7 8.9 %collective-permute-start.1 = (bf16[32,4096]{1,0:T(8,128)(2,1)S(1)}, bf16[32,4096]{1,0:T(8,128)(2,1)S(1)}, u32[]{:S(2)}, u32[]{:S(2)}) collective-permute-start(bf16[32,4096]{1,0:T(8,128)(2,1)S(1)} %get-tuple-element.265), channel_id=1, source_target_pairs={{30,0},{31,1},{0,2},{1,3},{2,4},{3,5},{4,6},{5,7},{6,8},{7,9},{8,1... | collective-permute-start | bytes 786440 | tf_op jit(solution)/shard_map/while/body/eval_jaxpr/ppermute | solution.py:10
  126.8 11.6 %collective-permute-start = (bf16[32,4096]{1,0:T(8,128)(2,1)S(1)}, bf16[32,4096]{1,0:T(8,128)(2,1)S(1)}, u32[]{:S(2)}, u32[]{:S(2)}) collective-permute-start(bf16[32,4096]{1,0:T(8,128)(2,1)S(1)} %get-tuple-element.264), channel_id=1, source_target_pairs={{30,0},{31,1},{0,2},{1,3},{2,4},{3,5},{4,6},{5,7},{6,8},{7,9},{8,1... | collective-permute-start | bytes 786440 | tf_op jit(solution)/shard_map/while/body/eval_jaxpr/ppermute | solution.py:10
  145.9 8.9 %collective-permute-start.1 = (bf16[32,4096]{1,0:T(8,128)(2,1)S(1)}, bf16[32,4096]{1,0:T(8,128)(2,1)S(1)}, u32[]{:S(2)}, u32[]{:S(2)}) collective-permute-start(bf16[32,4096]{1,0:T(8,128)(2,1)S(1)} %get-tuple-element.265), channel_id=1, source_target_pairs={{30,0},{31,1},{0,2},{1,3},{2,4},{3,5},{4,6},{5,7},{6,8},{7,9},{8,1... | collective-permute-start | bytes 786440 | tf_op jit(solution)/shard_map/while/body/eval_jaxpr/ppermute | solution.py:10
  146.0 11.6 %collective-permute-start = (bf16[32,4096]{1,0:T(8,128)(2,1)S(1)}, bf16[32,4096]{1,0:T(8,128)(2,1)S(1)}, u32[]{:S(2)}, u32[]{:S(2)}) collective-permute-start(bf16[32,4096]{1,0:T(8,128)(2,1)S(1)} %get-tuple-element.264), channel_id=1, source_target_pairs={{30,0},{31,1},{0,2},{1,3},{2,4},{3,5},{4,6},{5,7},{6,8},{7,9},{8,1... | collective-permute-start | bytes 786440 | tf_op jit(solution)/shard_map/while/body/eval_jaxpr/ppermute | solution.py:10
  165.0 8.9 %collective-permute-start.1 = (bf16[32,4096]{1,0:T(8,128)(2,1)S(1)}, bf16[32,4096]{1,0:T(8,128)(2,1)S(1)}, u32[]{:S(2)}, u32[]{:S(2)}) collective-permute-start(bf16[32,4096]{1,0:T(8,128)(2,1)S(1)} %get-tuple-element.265), channel_id=1, source_target_pairs={{30,0},{31,1},{0,2},{1,3},{2,4},{3,5},{4,6},{5,7},{6,8},{7,9},{8,1... | collective-permute-start | bytes 786440 | tf_op jit(solution)/shard_map/while/body/eval_jaxpr/ppermute | solution.py:10
  165.1 11.6 %collective-permute-start = (bf16[32,4096]{1,0:T(8,128)(2,1)S(1)}, bf16[32,4096]{1,0:T(8,128)(2,1)S(1)}, u32[]{:S(2)}, u32[]{:S(2)}) collective-permute-start(bf16[32,4096]{1,0:T(8,128)(2,1)S(1)} %get-tuple-element.264), channel_id=1, source_target_pairs={{30,0},{31,1},{0,2},{1,3},{2,4},{3,5},{4,6},{5,7},{6,8},{7,9},{8,1... | collective-permute-start | bytes 786440 | tf_op jit(solution)/shard_map/while/body/eval_jaxpr/ppermute | solution.py:10
  184.2 8.9 %collective-permute-start.1 = (bf16[32,4096]{1,0:T(8,128)(2,1)S(1)}, bf16[32,4096]{1,0:T(8,128)(2,1)S(1)}, u32[]{:S(2)}, u32[]{:S(2)}) collective-permute-start(bf16[32,4096]{1,0:T(8,128)(2,1)S(1)} %get-tuple-element.265), channel_id=1, source_target_pairs={{30,0},{31,1},{0,2},{1,3},{2,4},{3,5},{4,6},{5,7},{6,8},{7,9},{8,1... | collective-permute-start | bytes 786440 | tf_op jit(solution)/shard_map/while/body/eval_jaxpr/ppermute | solution.py:10
  184.3 11.6 %collective-permute-start = (bf16[32,4096]{1,0:T(8,128)(2,1)S(1)}, bf16[32,4096]{1,0:T(8,128)(2,1)S(1)}, u32[]{:S(2)}, u32[]{:S(2)}) collective-permute-start(bf16[32,4096]{1,0:T(8,128)(2,1)S(1)} %get-tuple-element.264), channel_id=1, source_target_pairs={{30,0},{31,1},{0,2},{1,3},{2,4},{3,5},{4,6},{5,7},{6,8},{7,9},{8,1... | collective-permute-start | bytes 786440 | tf_op jit(solution)/shard_map/while/body/eval_jaxpr/ppermute | solution.py:10
  203.3 8.9 %collective-permute-start.1 = (bf16[32,4096]{1,0:T(8,128)(2,1)S(1)}, bf16[32,4096]{1,0:T(8,128)(2,1)S(1)}, u32[]{:S(2)}, u32[]{:S(2)}) collective-permute-start(bf16[32,4096]{1,0:T(8,128)(2,1)S(1)} %get-tuple-element.265), channel_id=1, source_target_pairs={{30,0},{31,1},{0,2},{1,3},{2,4},{3,5},{4,6},{5,7},{6,8},{7,9},{8,1... | collective-permute-start | bytes 786440 | tf_op jit(solution)/shard_map/while/body/eval_jaxpr/ppermute | solution.py:10
  203.4 11.6 %collective-permute-start = (bf16[32,4096]{1,0:T(8,128)(2,1)S(1)}, bf16[32,4096]{1,0:T(8,128)(2,1)S(1)}, u32[]{:S(2)}, u32[]{:S(2)}) collective-permute-start(bf16[32,4096]{1,0:T(8,128)(2,1)S(1)} %get-tuple-element.264), channel_id=1, source_target_pairs={{30,0},{31,1},{0,2},{1,3},{2,4},{3,5},{4,6},{5,7},{6,8},{7,9},{8,1... | collective-permute-start | bytes 786440 | tf_op jit(solution)/shard_map/while/body/eval_jaxpr/ppermute | solution.py:10
  222.4 9.0 %collective-permute-start.1 = (bf16[32,4096]{1,0:T(8,128)(2,1)S(1)}, bf16[32,4096]{1,0:T(8,128)(2,1)S(1)}, u32[]{:S(2)}, u32[]{:S(2)}) collective-permute-start(bf16[32,4096]{1,0:T(8,128)(2,1)S(1)} %get-tuple-element.265), channel_id=1, source_target_pairs={{30,0},{31,1},{0,2},{1,3},{2,4},{3,5},{4,6},{5,7},{6,8},{7,9},{8,1... | collective-permute-start | bytes 786440 | tf_op jit(solution)/shard_map/while/body/eval_jaxpr/ppermute | solution.py:10
  222.5 11.7 %collective-permute-start = (bf16[32,4096]{1,0:T(8,128)(2,1)S(1)}, bf16[32,4096]{1,0:T(8,128)(2,1)S(1)}, u32[]{:S(2)}, u32[]{:S(2)}) collective-permute-start(bf16[32,4096]{1,0:T(8,128)(2,1)S(1)} %get-tuple-element.264), channel_id=1, source_target_pairs={{30,0},{31,1},{0,2},{1,3},{2,4},{3,5},{4,6},{5,7},{6,8},{7,9},{8,1... | collective-permute-start | bytes 786440 | tf_op jit(solution)/shard_map/while/body/eval_jaxpr/ppermute | solution.py:10
  241.6 10.1 %collective-permute-start.1 = (bf16[32,4096]{1,0:T(8,128)(2,1)S(1)}, bf16[32,4096]{1,0:T(8,128)(2,1)S(1)}, u32[]{:S(2)}, u32[]{:S(2)}) collective-permute-start(bf16[32,4096]{1,0:T(8,128)(2,1)S(1)} %get-tuple-element.265), channel_id=1, source_target_pairs={{30,0},{31,1},{0,2},{1,3},{2,4},{3,5},{4,6},{5,7},{6,8},{7,9},{8,1... | collective-permute-start | bytes 786440 | tf_op jit(solution)/shard_map/while/body/eval_jaxpr/ppermute | solution.py:10
  241.7 12.8 %collective-permute-start = (bf16[32,4096]{1,0:T(8,128)(2,1)S(1)}, bf16[32,4096]{1,0:T(8,128)(2,1)S(1)}, u32[]{:S(2)}, u32[]{:S(2)}) collective-permute-start(bf16[32,4096]{1,0:T(8,128)(2,1)S(1)} %get-tuple-element.264), channel_id=1, source_target_pairs={{30,0},{31,1},{0,2},{1,3},{2,4},{3,5},{4,6},{5,7},{6,8},{7,9},{8,1... | collective-permute-start | bytes 786440 | tf_op jit(solution)/shard_map/while/body/eval_jaxpr/ppermute | solution.py:10
  261.9 11.2 %collective-permute-start.1 = (bf16[32,4096]{1,0:T(8,128)(2,1)S(1)}, bf16[32,4096]{1,0:T(8,128)(2,1)S(1)}, u32[]{:S(2)}, u32[]{:S(2)}) collective-permute-start(bf16[32,4096]{1,0:T(8,128)(2,1)S(1)} %get-tuple-element.265), channel_id=1, source_target_pairs={{30,0},{31,1},{0,2},{1,3},{2,4},{3,5},{4,6},{5,7},{6,8},{7,9},{8,1... | collective-permute-start | bytes 786440 | tf_op jit(solution)/shard_map/while/body/eval_jaxpr/ppermute | solution.py:10
  262.0 13.9 %collective-permute-start = (bf16[32,4096]{1,0:T(8,128)(2,1)S(1)}, bf16[32,4096]{1,0:T(8,128)(2,1)S(1)}, u32[]{:S(2)}, u32[]{:S(2)}) collective-permute-start(bf16[32,4096]{1,0:T(8,128)(2,1)S(1)} %get-tuple-element.264), channel_id=1, source_target_pairs={{30,0},{31,1},{0,2},{1,3},{2,4},{3,5},{4,6},{5,7},{6,8},{7,9},{8,1... | collective-permute-start | bytes 786440 | tf_op jit(solution)/shard_map/while/body/eval_jaxpr/ppermute | solution.py:10
  283.3 12.1 %collective-permute-start.1 = (bf16[32,4096]{1,0:T(8,128)(2,1)S(1)}, bf16[32,4096]{1,0:T(8,128)(2,1)S(1)}, u32[]{:S(2)}, u32[]{:S(2)}) collective-permute-start(bf16[32,4096]{1,0:T(8,128)(2,1)S(1)} %get-tuple-element.265), channel_id=1, source_target_pairs={{30,0},{31,1},{0,2},{1,3},{2,4},{3,5},{4,6},{5,7},{6,8},{7,9},{8,1... | collective-permute-start | bytes 786440 | tf_op jit(solution)/shard_map/while/body/eval_jaxpr/ppermute | solution.py:10
  283.4 14.9 %collective-permute-start = (bf16[32,4096]{1,0:T(8,128)(2,1)S(1)}, bf16[32,4096]{1,0:T(8,128)(2,1)S(1)}, u32[]{:S(2)}, u32[]{:S(2)}) collective-permute-start(bf16[32,4096]{1,0:T(8,128)(2,1)S(1)} %get-tuple-element.264), channel_id=1, source_target_pairs={{30,0},{31,1},{0,2},{1,3},{2,4},{3,5},{4,6},{5,7},{6,8},{7,9},{8,1... | collective-permute-start | bytes 786440 | tf_op jit(solution)/shard_map/while/body/eval_jaxpr/ppermute | solution.py:10
  305.7 12.0 %collective-permute-start.1 = (bf16[32,4096]{1,0:T(8,128)(2,1)S(1)}, bf16[32,4096]{1,0:T(8,128)(2,1)S(1)}, u32[]{:S(2)}, u32[]{:S(2)}) collective-permute-start(bf16[32,4096]{1,0:T(8,128)(2,1)S(1)} %get-tuple-element.265), channel_id=1, source_target_pairs={{30,0},{31,1},{0,2},{1,3},{2,4},{3,5},{4,6},{5,7},{6,8},{7,9},{8,1... | collective-permute-start | bytes 786440 | tf_op jit(solution)/shard_map/while/body/eval_jaxpr/ppermute | solution.py:10
  305.8 16.0 %collective-permute-start = (bf16[32,4096]{1,0:T(8,128)(2,1)S(1)}, bf16[32,4096]{1,0:T(8,128)(2,1)S(1)}, u32[]{:S(2)}, u32[]{:S(2)}) collective-permute-start(bf16[32,4096]{1,0:T(8,128)(2,1)S(1)} %get-tuple-element.264), channel_id=1, source_target_pairs={{30,0},{31,1},{0,2},{1,3},{2,4},{3,5},{4,6},{5,7},{6,8},{7,9},{8,1... | collective-permute-start | bytes 786440 | tf_op jit(solution)/shard_map/while/body/eval_jaxpr/ppermute | solution.py:10
Sparse Core Ops, SparseCore 0:
  334.8 75.6 reduce-scatter.1
where the time goes:
time: 418 us; the launch traced here: 417 us
  waiting for transfers between devices  203 us (49%)
  matrix products  99.8 us (24%)
  starting transfers between devices  38.2 us (9%)
  local copies, waits for them, and re-layouts  30.1 us (7%)
  loops' own time  20.5 us (5%)
  between operations  14.7 us (4%)
  other arithmetic  11.4 us (3%)
    ppermute x31, waiting for transfers between devices, passed_along(): return lax.ppermute(block, axis, route)  127 us
    dot_general x16, matrix products, score_block(): lax.dot_general(flat, panel, (((1,), (1,)), ((), ())), preferred_element_...  96.6 us
    reduce_scatter x1, waiting for transfers between devices, body(): return lax.psum_scatter(buffer, 'group', scatter_dimension=1, tiled=True)  75.8 us
    ppermute x31, starting transfers between devices, passed_along(): return lax.ppermute(block, axis, route)  38.2 us
    another operation x1, loops' own time, body(): lax.fori_loop(1, cycle // 2, turn, (panel, second, buffer))  20.5 us
    dynamic_update_slice x32, local copies, waits for them, and re-layouts, place(): return lax.dynamic_update_slice(buffer, part, (jnp.int32(0), column))  19.8 us
    reduce_sum x16, other arithmetic, slot_of(): return jnp.sum(jnp.where(panel_order == source, places, 0))  11.4 us
  transfers between devices with their start and end apart: 32, of which 32 were waited for; matrix products, arithmetic and copies ran while one was open for 3% of the time, Pallas kernels for 0%

commit v1 on v0

v1 whole, which is shorter than its diff:
```python
import functools

import jax
import jax.numpy as jnp
from jax import lax
from jax.experimental import pallas as pl
from jax.experimental.pallas import tpu as pltpu
from jax.sharding import PartitionSpec as P

NZ = 8
PANEL = 32
CBLK = 256


def _move(x, dz=0, flip_y=False, flip_core=False):
    route = []
    for i in range(NZ * 4):
        z, rest = divmod(i, 4)
        route.append((i, ((z + dz) % NZ) * 4 + (rest ^ (2 * flip_y) ^ (1 * flip_core))))
    return lax.ppermute(x, "blk", route)


def _score_kernel(scale, count, *refs):
    c_ref, o_ref = refs[count], refs[count + 1]
    panels = jnp.concatenate([r[...] for r in refs[:count]], axis=0)
    part = lax.dot_general(
        panels, c_ref[...], (((1,), (1,)), ((), ())), preferred_element_type=jnp.float32
    )
    o_ref[...] = (part * scale).astype(o_ref.dtype)


def _score(pieces, flat, scale):
    rows, feats = flat.shape
    n = sum(p.shape[0] for p in pieces)
    return pl.pallas_call(
        functools.partial(_score_kernel, scale, len(pieces)),
        grid=(rows // CBLK,),
        in_specs=[pl.BlockSpec(p.shape, lambda i: (0, 0)) for p in pieces]
        + [pl.BlockSpec((CBLK, feats), lambda i: (i, 0))],
        out_specs=pl.BlockSpec((n, CBLK), lambda i: (0, i)),
        out_shape=jax.ShapeDtypeStruct((n, rows), jnp.bfloat16),
        compiler_params=pltpu.CompilerParams(vmem_limit_bytes=24 << 20),
        cost_estimate=pl.CostEstimate(
            flops=2 * n * rows * feats, bytes_accessed=2 * (rows * feats + n * feats + n * rows), transcendentals=0
        ),
        name="score",
    )(*pieces, flat)


def _place_kernel(counts, where_ref, *refs):
    out = refs[-1]
    slot = 0
    for ref, count in zip(refs[:-1], counts):
        for i in range(count):
            out[where_ref[slot]] = ref[i * PANEL : (i + 1) * PANEL, :]
            slot += 1


def _place(parts, where):
    counts = [p.shape[0] // PANEL for p in parts]
    rows = parts[0].shape[1]
    return pl.pallas_call(
        functools.partial(_place_kernel, counts),
        in_specs=[pl.BlockSpec(memory_space=pltpu.SMEM)]
        + [pl.BlockSpec(memory_space=pltpu.VMEM) for _ in parts],
        out_specs=pl.BlockSpec(memory_space=pltpu.VMEM),
        out_shape=jax.ShapeDtypeStruct((sum(counts), PANEL, rows), jnp.bfloat16),
        compiler_params=pltpu.CompilerParams(vmem_limit_bytes=16 << 20),
        name="place",
    )(where, *parts)


def _total_kernel(in_ref, o_ref):
    total = in_ref[0].astype(jnp.float32)
    for g in range(1, in_ref.shape[0]):
        total += in_ref[g].astype(jnp.float32)
    o_ref[...] = total.T


def _total(parts):
    groups, width, rows = parts.shape
    return pl.pallas_call(
        _total_kernel,
        grid=(rows // CBLK,),
        in_specs=[pl.BlockSpec((groups, width, CBLK), lambda i: (0, 0, i))],
        out_specs=pl.BlockSpec((CBLK, width), lambda i: (i, 0)),
        out_shape=jax.ShapeDtypeStruct((rows, width), jnp.float32),
        compiler_params=pltpu.CompilerParams(vmem_limit_bytes=16 << 20),
        name="total",
    )(parts)


def body(candidates, queries, out_factor, in_factor, panel_order):
    cand_rows, layer_count, features = candidates.shape
    width = queries.shape[0]
    out_units = out_factor.shape[1]
    in_units = in_factor.shape[1]
    groups = lax.axis_size("group")
    scale = 1.0 / (features * layer_count * groups) ** 0.5
    grads = queries.astype(jnp.float32).reshape(width, layer_count, out_units, in_units)
    left = jnp.einsum("lab,qlbc->qlac", out_factor, grads, precision=lax.Precision.HIGHEST)
    precond = jnp.einsum("qlac,lcd->qlad", left, in_factor, precision=lax.Precision.HIGHEST)
    panel = precond.reshape(width, layer_count * features).astype(jnp.bfloat16)
    flat = candidates.reshape(cand_rows, layer_count * features)

    slots = []

    own = jnp.concatenate([panel, _move(panel, flip_y=True)], axis=0)
    steps = []

    def meet(arrivals):
        pieces = [a for a, _ in arrivals]
        pieces += [_move(a, flip_core=True) for a, _ in arrivals]
        for dc in (0, 1):
            for _, where in arrivals:
                slots.extend((dz, dy, dc) for dz, dy in where)
        steps.append(_score(pieces, flat, scale))

    meet([(own, [(0, 0), (0, 1)])])
    fw = bw = own
    for s in range(1, NZ // 2):
        fw, bw = _move(fw, dz=1), _move(bw, dz=-1)
        meet([(fw, [(-s, 0), (-s, 1)]), (bw, [(s, 0), (s, 1)])])
    s = NZ // 2
    last_fw, last_bw = _move(fw[:PANEL], dz=1), _move(bw[PANEL:], dz=-1)
    meet([(last_fw, [(-s, 0)]), (last_bw, [(s, 1)])])

    me = lax.axis_index("blk")
    z, rest = me // 4, me % 4
    dz = jnp.array([t[0] for t in slots], jnp.int32)
    flip = jnp.array([t[1] * 2 + t[2] for t in slots], jnp.int32)
    source = ((z + dz) % NZ) * 4 + (rest ^ flip)
    places = jnp.arange(panel_order.shape[0], dtype=jnp.int32)
    where = jnp.sum(jnp.where(panel_order[None, :] == source[:, None], places[None, :], 0), axis=1).astype(jnp.int32)
    buffer = _place(steps, where).reshape(groups, -1, cand_rows)
    parts = lax.all_to_all(buffer, "group", split_axis=0, concat_axis=0, tiled=True)
    return _total(parts)


def solution(mesh):
    in_specs = (
        P("blk", "group", None),
        P("blk", "group", None),
        P("group", None, None),
        P("group", None, None),
        P(),
    )
    out_specs = P("blk", "group")
    return jax.shard_map(body, mesh=mesh, in_specs=in_specs, out_specs=out_specs, check_vma=False)
```

time: 418 us -> 120 us (0.29)
  waiting for transfers between devices: 203 us -> 30.3 us
  matrix products: 99.8 us -> 2.47 us
  blocking collectives: 0 us -> 31.1 us
  local copies, waits for them, and re-layouts: 30.1 us -> 5.42 us
  Pallas kernels: 0 us -> 21.1 us
  loops' own time: 20.5 us -> 0 us
  between operations: 14.7 us -> 0.24 us
  other arithmetic: 11.4 us -> 0.19 us
  starting transfers between devices: 38.2 us -> 28.6 us
    dot_general x16 -> x0, matrix products: 96.6 us -> none  [score_block(): lax.dot_general(flat, panel, (((1,), (1,)), ((), ())), preferred_element_...]
    ppermute x31 -> x18, waiting for transfers between devices: 127 us -> 30.3 us  [_move(): return lax.ppermute(x, 'blk', route)]
    reduce_scatter x1 -> x0, waiting for transfers between devices: 75.8 us -> none  [body(): return lax.psum_scatter(buffer, 'group', scatter_dimension=1, tiled=True)]
    all_to_all x0 -> x1, blocking collectives: none -> 31.1 us  [body(): lax.all_to_all(buffer, 'group', split_axis=0, concat_axis=0, tiled=True)]
    pallas_call x0 -> x7, Pallas kernels: none -> 21.1 us  [the longest x5 18.5 us: _score(): pl.pallas_call(functools.partial(_score_kernel, scale, len(pieces)), grid...]
    another operation x1 -> x0, loops' own time: 20.5 us -> none  [body(): lax.fori_loop(1, cycle // 2, turn, (panel, second, buffer))]
    dynamic_update_slice x32 -> x0, local copies, waits for them, and re-layouts: 19.8 us -> none  [place(): return lax.dynamic_update_slice(buffer, part, (jnp.int32(0), column))]
    reduce_sum x16 -> x1, other arithmetic: 11.4 us -> 0.18 us  [body(): jnp.sum(jnp.where(panel_order[None, :] == source[:, None], places[None, :...]
  transfers between devices with their start and end apart: 32 -> 18, of which waited for: 32 -> 4; matrix products, arithmetic and copies ran while one was open for 3% -> 0% of each run, Pallas kernels for 0% -> 13%
where the time goes in v1:
time: 120 us; the launch traced here: 119 us
  blocking collectives  31.1 us (26%)
  waiting for transfers between devices  30.3 us (25%)
  starting transfers between devices  28.6 us (24%)
  Pallas kernels  21.1 us (18%)
  local copies, waits for them, and re-layouts  5.42 us (5%)
  matrix products  2.47 us (2%)
    all_to_all x1, blocking collectives, body(): lax.all_to_all(buffer, 'group', split_axis=0, concat_axis=0, tiled=True)  31.1 us
    ppermute x18, waiting for transfers between devices, _move(): return lax.ppermute(x, 'blk', route)  30.3 us
    ppermute x18, starting transfers between devices, _move(): return lax.ppermute(x, 'blk', route)  28.6 us
    pallas_call x5, Pallas kernels, _score(): pl.pallas_call(functools.partial(_score_kernel, scale, len(pieces)), grid...  18.5 us
    unnamed x15, local copies, waits for them, and re-layouts  3.43 us
  transfers between devices with their start and end apart: 18, of which 4 were waited for; matrix products, arithmetic and copies ran while one was open for 0% of the time, Pallas kernels for 13%

profile of v1, /device:TPU:1, one launch (start us, length us, event | category | flops | bytes accessed | tf_op | source)
XLA Modules:
  0.0 119.4 jit_solution(15320868869787758015)
XLA Ops:
  0.0 1.5 %reshape.27 = bf16[32,64,64]{2,1,0:T(8,128)(2,1)S(1)} reshape(bf16[32,1,4096]{2,0,1:T(8,128)(2,1)} %param.8) | data formatting | bytes 524288 | tf_op jit(solution)/shard_map/reshape
  1.5 0.7 convolution_bitcast_fusion
  2.2 0.0 copy-start.4
  2.2 0.0 copy-start.5
  2.2 0.0 copy-start.6
  2.2 1.8 %fusion = bf16[32,1,64,64]{3,2,0,1:T(8,128)(2,1)S(1)} fusion(f32[32,64,64]{1,2,0:T(8,128)S(1)} %convolution_bitcast_fusion, f32[1,64,64]{2,1,0:T(8,128)S(1)} %copy-done.3), kind=kOutput, calls=%fused_computation.2 | convolution fusion | flops 100794368 | bytes 802816 | tf_op jit(solution)/shard_map/qlac,lcd->qlad/dot_general | solution.py:102
  4.0 0.5 convert_element_type.20
  4.5 3.8 %collective-permute-start = (bf16[32,4096]{1,0:T(8,128)(2,1)S(1)}, bf16[32,4096]{1,0:T(8,128)(2,1)S(1)}, u32[]{:S(2)}, u32[]{:S(2)}) collective-permute-start(bf16[32,4096]{1,0:T(8,128)(2,1)S(1)} %convert_element_type.20), channel_id=1, source_target_pairs={{0,2},{1,3},{2,0},{3,1},{4,6},{5,7},{6,4},{7,5},{8,10},{9,11},{10,... | collective-permute-start | bytes 786440 | tf_op jit(solution)/shard_map/ppermute | solution.py:20
  8.3 5.0 %collective-permute-done = bf16[32,4096]{1,0:T(8,128)(2,1)S(1)} collective-permute-done((bf16[32,4096]{1,0:T(8,128)(2,1)S(1)}, bf16[32,4096]{1,0:T(8,128)(2,1)S(1)}, u32[]{:S(2)}, u32[]{:S(2)}) %collective-permute-start) | collective-permute-done | bytes 262176 | tf_op jit(solution)/shard_map/ppermute | solution.py:20
  13.3 2.5 %collective-permute-start.2 = (bf16[64,4096]{1,0:T(8,128)(2,1)S(1)}, bf16[64,4096]{1,0:T(8,128)(2,1)S(1)}, u32[]{:S(2)}, u32[]{:S(2)}) collective-permute-start(bf16[64,4096]{1,0:T(8,128)(2,1)S(1)} %constant_dynamic-update-slice_fusion.refs_0_), channel_id=1, source_target_pairs={{0,4},{1,5},{2,6},{3,7},{4,8},{5,9},{6,10},{7,11},{8,12},{9,13},{1... | collective-permute-start | bytes 1572872 | tf_op jit(solution)/shard_map/ppermute | solution.py:20
  15.8 4.0 %collective-permute-start.3 = (bf16[64,4096]{1,0:T(8,128)(2,1)S(1)}, bf16[64,4096]{1,0:T(8,128)(2,1)S(1)}, u32[]{:S(2)}, u32[]{:S(2)}) collective-permute-start(bf16[64,4096]{1,0:T(8,128)(2,1)S(1)} %constant_dynamic-update-slice_fusion.refs_0_), channel_id=1, source_target_pairs={{0,28},{1,29},{2,30},{3,31},{4,0},{5,1},{6,2},{7,3},{8,4},{9,5},{1... | collective-permute-start | bytes 1572872 | tf_op jit(solution)/shard_map/ppermute | solution.py:20
  19.8 10.6 %collective-permute-done.2.refs_0_ = bf16[64,4096]{1,0:T(8,128)(2,1)S(1)} collective-permute-done((bf16[64,4096]{1,0:T(8,128)(2,1)S(1)}, bf16[64,4096]{1,0:T(8,128)(2,1)S(1)}, u32[]{:S(2)}, u32[]{:S(2)}) %collective-permute-start.2) | collective-permute-done | bytes 524320 | tf_op jit(solution)/shard_map/ppermute | solution.py:20
  30.4 0.0 collective-permute-start.6
  30.4 0.0 collective-permute-done.3.refs_1_
  30.4 2.7 %collective-permute-start.7 = (bf16[64,4096]{1,0:T(8,128)(2,1)S(1)}, bf16[64,4096]{1,0:T(8,128)(2,1)}, u32[]{:S(2)}, u32[]{:S(2)}) collective-permute-start(bf16[64,4096]{1,0:T(8,128)(2,1)S(1)} %collective-permute-done.3.refs_1_), channel_id=1, source_target_pairs={{0,28},{1,29},{2,30},{3,31},{4,0},{5,1},{6,2},{7,3},{8,4},{9,5},{1... | collective-permute-start | bytes 1572872 | tf_op jit(solution)/shard_map/ppermute | solution.py:20
  33.1 9.9 %collective-permute-done.6.refs_0_ = bf16[64,4096]{1,0:T(8,128)(2,1)} collective-permute-done((bf16[64,4096]{1,0:T(8,128)(2,1)S(1)}, bf16[64,4096]{1,0:T(8,128)(2,1)}, u32[]{:S(2)}, u32[]{:S(2)}) %collective-permute-start.6) | collective-permute-done | bytes 524320 | tf_op jit(solution)/shard_map/ppermute | solution.py:20
  43.0 0.0 collective-permute-start.10
  43.0 0.0 collective-permute-done.7.refs_1_
  43.0 2.7 %collective-permute-start.11 = (bf16[64,4096]{1,0:T(8,128)(2,1)}, bf16[64,4096]{1,0:T(8,128)(2,1)S(1)}, u32[]{:S(2)}, u32[]{:S(2)}) collective-permute-start(bf16[64,4096]{1,0:T(8,128)(2,1)} %collective-permute-done.7.refs_1_), channel_id=1, source_target_pairs={{0,28},{1,29},{2,30},{3,31},{4,0},{5,1},{6,2},{7,3},{8,4},{9,5},{1... | collective-permute-start | bytes 1572872 | tf_op jit(solution)/shard_map/ppermute | solution.py:20
  45.7 3.7 %collective-permute-start.1 = (bf16[64,4096]{1,0:T(8,128)(2,1)S(1)}, bf16[64,4096]{1,0:T(8,128)(2,1)S(1)}, u32[]{:S(2)}, u32[]{:S(2)}) collective-permute-start(bf16[64,4096]{1,0:T(8,128)(2,1)S(1)} %constant_dynamic-update-slice_fusion.refs_0_), channel_id=1, source_target_pairs={{0,1},{1,0},{2,3},{3,2},{4,5},{5,4},{6,7},{7,6},{8,9},{9,8},{10,11... | collective-permute-start | bytes 1572872 | tf_op jit(solution)/shard_map/ppermute | solution.py:20
  49.3 0.0 collective-permute-start.4
  49.3 0.5 collective-permute-start.5
  49.8 4.9 %collective-permute-done.10.refs_0_ = bf16[64,4096]{1,0:T(8,128)(2,1)S(1)} collective-permute-done((bf16[64,4096]{1,0:T(8,128)(2,1)}, bf16[64,4096]{1,0:T(8,128)(2,1)S(1)}, u32[]{:S(2)}, u32[]{:S(2)}) %collective-permute-start.10) | collective-permute-done | bytes 524320 | tf_op jit(solution)/shard_map/ppermute | solution.py:20
  54.7 4.0 %collective-permute-start.8 = (bf16[64,4096]{1,0:T(8,128)(2,1)}, bf16[64,4096]{1,0:T(8,128)(2,1)}, u32[]{:S(2)}, u32[]{:S(2)}) collective-permute-start(bf16[64,4096]{1,0:T(8,128)(2,1)} %collective-permute-done.6.refs_0_), channel_id=1, source_target_pairs={{0,1},{1,0},{2,3},{3,2},{4,5},{5,4},{6,7},{7,6},{8,9},{9,8},{10,11... | collective-permute-start | bytes 1572872 | tf_op jit(solution)/shard_map/ppermute | solution.py:20
  58.8 0.0 collective-permute-done.11.refs_1_
  58.8 0.1 collective-permute-start.9
  58.9 0.1 collective-permute-start.14
  59.0 0.0 collective-permute-done.4.refs_2_
  59.0 2.8 %collective-permute-start.15 = (bf16[32,4096]{1,0:T(8,128)(2,1)S(1)}, bf16[32,4096]{1,0:T(8,128)(2,1)S(1)}, u32[]{:S(2)}, u32[]{:S(2)}) collective-permute-start(bf16[32,4096]{1,0:T(8,128)(2,1)S(1)} %slice.9), channel_id=1, source_target_pairs={{0,28},{1,29},{2,30},{3,31},{4,0},{5,1},{6,2},{7,3},{8,4},{9,5},{1... | collective-permute-start | bytes 786440 | tf_op jit(solution)/shard_map/ppermute | solution.py:20
  61.8 0.2 select_reduce_fusion.where_ref
  62.0 0.0 collective-permute-done.5.refs_3_
  62.0 1.0 collective-permute-start.12
  63.0 0.0 collective-permute-done.8.refs_2_
  63.0 0.1 collective-permute-start.13
  63.1 3.4 %copy-done.1 = bf16[1024,1,4096]{2,0,1:T(8,128)(2,1)S(1)} copy-done((bf16[1024,1,4096]{2,0,1:T(8,128)(2,1)S(1)}, bf16[1024,1,4096]{2,0,1:T(8,128)(2,1)}, u32[]{:S(2)}) %copy-start.1) | copy-done | bytes 8388632
  66.5 3.3 %score.5.refs_0_ = bf16[128,1024]{1,0:T(8,128)(2,1)S(1)} custom-call(bf16[64,4096]{1,0:T(8,128)(2,1)S(1)} %constant_dynamic-update-slice_fusion.refs_0_, bf16[64,4096]{1,0:T(8,128)(2,1)S(1)} %collective-permute-done.1.refs_1_, bf16[1024,4096]{1,0:T(8,128)(2,1)S(1)} %bitcast.30), custom_call_target="tpu_custom_call" | custom-call | flops 1073741824 | bytes 9699328 | tf_op jit(solution)/shard_map/score/pallas_call | solution.py:35
  69.9 0.0 collective-permute-done.14.refs_0_
  69.9 0.5 collective-permute-start.16
  70.4 0.1 collective-permute-start.17
  70.5 4.3 %score.6.refs_1_ = bf16[256,1024]{1,0:T(8,128)(2,1)S(1)} custom-call(bf16[64,4096]{1,0:T(8,128)(2,1)S(1)} %collective-permute-done.2.refs_0_, bf16[64,4096]{1,0:T(8,128)(2,1)S(1)} %collective-permute-done.3.refs_1_, bf16[64,4096]{1,0:T(8,128)(2,1)} %collective-permute-done.4.refs_2_, bf16[64,4096]{1,0:T(8,128)(2,1)} %collective-permute-done.5.refs_3_, ...), custom_call_target="tpu_custom_call" | custom-call | flops 2147483648 | bytes 11010048 | tf_op jit(solution)/shard_map/score/pallas_call | solution.py:35
  74.8 4.4 %score.7.refs_2_ = bf16[256,1024]{1,0:T(8,128)(2,1)S(1)} custom-call(bf16[64,4096]{1,0:T(8,128)(2,1)} %collective-permute-done.6.refs_0_, bf16[64,4096]{1,0:T(8,128)(2,1)} %collective-permute-done.7.refs_1_, bf16[64,4096]{1,0:T(8,128)(2,1)} %collective-permute-done.8.refs_2_, bf16[64,4096]{1,0:T(8,128)(2,1)S(1)} %collective-permute-done.9.refs_3_, ...), custom_call_target="tpu_custom_call" | custom-call | flops 2147483648 | bytes 11010048 | tf_op jit(solution)/shard_map/score/pallas_call | solution.py:35
  79.2 0.0 collective-permute-done.16.refs_2_
  79.2 3.4 %score.9.refs_4_ = bf16[128,1024]{1,0:T(8,128)(2,1)S(1)} custom-call(bf16[32,4096]{1,0:T(8,128)(2,1)S(1)} %collective-permute-done.14.refs_0_, bf16[32,4096]{1,0:T(8,128)(2,1)S(1)} %collective-permute-done.15.refs_1_, bf16[32,4096]{1,0:T(8,128)(2,1)S(1)} %collective-permute-done.16.refs_2_, bf16[32,4096]{1,0:T(8,128)(2,1)S(1)} %collective-permute-done.17.refs_3_, ...), custom_call_target="tpu_custom_call" | custom-call | flops 1073741824 | bytes 9699328 | tf_op jit(solution)/shard_map/score/pallas_call | solution.py:35
  82.6 0.0 collective-permute-done.13.refs_3_
  82.6 3.1 %score.8.refs_3_ = bf16[256,1024]{1,0:T(8,128)(2,1)S(1)} custom-call(bf16[64,4096]{1,0:T(8,128)(2,1)S(1)} %collective-permute-done.10.refs_0_, bf16[64,4096]{1,0:T(8,128)(2,1)S(1)} %collective-permute-done.11.refs_1_, bf16[64,4096]{1,0:T(8,128)(2,1)S(1)} %collective-permute-done.12.refs_2_, bf16[64,4096]{1,0:T(8,128)(2,1)S(1)} %collective-permute-done.13.refs_3_, ...), custom_call_target="tpu_custom_call" | custom-call | flops 2147483648 | bytes 11010048 | tf_op jit(solution)/shard_map/score/pallas_call | solution.py:35
  85.7 0.7 place.1
  86.4 31.1 %all_to_all.5.in_ref = bf16[8,128,1024]{2,1,0:T(8,128)(2,1)S(1)} all-to-all(bf16[8,128,1024]{2,1,0:T(8,128)(2,1)S(1)} %bitcast.35), channel_id=1, replica_groups=mesh['group'=8,'blk'=32] {'group'}, dimensions={0} | all-to-all | bytes 4194304 | tf_op jit(solution)/shard_map/all_to_all | solution.py:136
  117.5 1.9 %total.1 = f32[1024,128]{1,0:T(8,128)} custom-call(bf16[8,128,1024]{2,1,0:T(8,128)(2,1)S(1)} %all_to_all.5.in_ref), custom_call_target="tpu_custom_call" | custom-call | tf_op jit(solution)/shard_map/total/pallas_call | solution.py:82
  (20 shorter events, 0.1 us)
Async XLA Ops:
  0.0 1.5 %copy-start = (f32[1,64,64]{2,1,0:T(8,128)S(1)}, f32[1,64,64]{2,1,0:T(8,128)}, u32[]{:S(2)}) copy-start(f32[1,64,64]{2,1,0:T(8,128)} %param.9) | copy-start | bytes 49156
  0.0 2.2 %copy-start.3 = (f32[1,64,64]{2,1,0:T(8,128)S(1)}, f32[1,64,64]{2,1,0:T(8,128)}, u32[]{:S(2)}) copy-start(f32[1,64,64]{2,1,0:T(8,128)} %param.10) | copy-start | bytes 49156
  2.2 59.6 %copy-start.4 = (s32[32]{0:T(128)S(1)}, s32[32]{0:T(128)}, u32[]{:S(2)}) copy-start(s32[32]{0:T(128)} %constant.50.clone) | copy-start | bytes 388
  2.2 59.6 %copy-start.5 = (s32[32]{0:T(128)S(1)}, s32[32]{0:T(128)}, u32[]{:S(2)}) copy-start(s32[32]{0:T(128)} %constant.51.clone) | copy-start | bytes 388
  2.2 59.6 %copy-start.6 = (s32[32]{0:T(128)S(1)}, s32[32]{0:T(128)}, u32[]{:S(2)}) copy-start(s32[32]{0:T(128)} %param.11) | copy-start | bytes 388
  4.5 8.8 %collective-permute-start = (bf16[32,4096]{1,0:T(8,128)(2,1)S(1)}, bf16[32,4096]{1,0:T(8,128)(2,1)S(1)}, u32[]{:S(2)}, u32[]{:S(2)}) collective-permute-start(bf16[32,4096]{1,0:T(8,128)(2,1)S(1)} %convert_element_type.20), channel_id=1, source_target_pairs={{0,2},{1,3},{2,0},{3,1},{4,6},{5,7},{6,4},{7,5},{8,10},{9,11},{10,... | collective-permute-start | bytes 786440 | tf_op jit(solution)/shard_map/ppermute | solution.py:20
  13.3 17.1 %collective-permute-start.2 = (bf16[64,4096]{1,0:T(8,128)(2,1)S(1)}, bf16[64,4096]{1,0:T(8,128)(2,1)S(1)}, u32[]{:S(2)}, u32[]{:S(2)}) collective-permute-start(bf16[64,4096]{1,0:T(8,128)(2,1)S(1)} %constant_dynamic-update-slice_fusion.refs_0_), channel_id=1, source_target_pairs={{0,4},{1,5},{2,6},{3,7},{4,8},{5,9},{6,10},{7,11},{8,12},{9,13},{1... | collective-permute-start | bytes 1572872 | tf_op jit(solution)/shard_map/ppermute | solution.py:20
  15.8 14.6 %collective-permute-start.3 = (bf16[64,4096]{1,0:T(8,128)(2,1)S(1)}, bf16[64,4096]{1,0:T(8,128)(2,1)S(1)}, u32[]{:S(2)}, u32[]{:S(2)}) collective-permute-start(bf16[64,4096]{1,0:T(8,128)(2,1)S(1)} %constant_dynamic-update-slice_fusion.refs_0_), channel_id=1, source_target_pairs={{0,28},{1,29},{2,30},{3,31},{4,0},{5,1},{6,2},{7,3},{8,4},{9,5},{1... | collective-permute-start | bytes 1572872 | tf_op jit(solution)/shard_map/ppermute | solution.py:20
  30.4 12.5 %collective-permute-start.6 = (bf16[64,4096]{1,0:T(8,128)(2,1)S(1)}, bf16[64,4096]{1,0:T(8,128)(2,1)}, u32[]{:S(2)}, u32[]{:S(2)}) collective-permute-start(bf16[64,4096]{1,0:T(8,128)(2,1)S(1)} %collective-permute-done.2.refs_0_), channel_id=1, source_target_pairs={{0,4},{1,5},{2,6},{3,7},{4,8},{5,9},{6,10},{7,11},{8,12},{9,13},{1... | collective-permute-start | bytes 1572872 | tf_op jit(solution)/shard_map/ppermute | solution.py:20
  30.4 12.5 %collective-permute-start.7 = (bf16[64,4096]{1,0:T(8,128)(2,1)S(1)}, bf16[64,4096]{1,0:T(8,128)(2,1)}, u32[]{:S(2)}, u32[]{:S(2)}) collective-permute-start(bf16[64,4096]{1,0:T(8,128)(2,1)S(1)} %collective-permute-done.3.refs_1_), channel_id=1, source_target_pairs={{0,28},{1,29},{2,30},{3,31},{4,0},{5,1},{6,2},{7,3},{8,4},{9,5},{1... | collective-permute-start | bytes 1572872 | tf_op jit(solution)/shard_map/ppermute | solution.py:20
  43.0 11.7 %collective-permute-start.10 = (bf16[64,4096]{1,0:T(8,128)(2,1)}, bf16[64,4096]{1,0:T(8,128)(2,1)S(1)}, u32[]{:S(2)}, u32[]{:S(2)}) collective-permute-start(bf16[64,4096]{1,0:T(8,128)(2,1)} %collective-permute-done.6.refs_0_), channel_id=1, source_target_pairs={{0,4},{1,5},{2,6},{3,7},{4,8},{5,9},{6,10},{7,11},{8,12},{9,13},{1... | collective-permute-start | bytes 1572872 | tf_op jit(solution)/shard_map/ppermute | solution.py:20
  43.0 15.8 %collective-permute-start.11 = (bf16[64,4096]{1,0:T(8,128)(2,1)}, bf16[64,4096]{1,0:T(8,128)(2,1)S(1)}, u32[]{:S(2)}, u32[]{:S(2)}) collective-permute-start(bf16[64,4096]{1,0:T(8,128)(2,1)} %collective-permute-done.7.refs_1_), channel_id=1, source_target_pairs={{0,28},{1,29},{2,30},{3,31},{4,0},{5,1},{6,2},{7,3},{8,4},{9,5},{1... | collective-permute-start | bytes 1572872 | tf_op jit(solution)/shard_map/ppermute | solution.py:20
  45.7 13.2 %collective-permute-start.1 = (bf16[64,4096]{1,0:T(8,128)(2,1)S(1)}, bf16[64,4096]{1,0:T(8,128)(2,1)S(1)}, u32[]{:S(2)}, u32[]{:S(2)}) collective-permute-start(bf16[64,4096]{1,0:T(8,128)(2,1)S(1)} %constant_dynamic-update-slice_fusion.refs_0_), channel_id=1, source_target_pairs={{0,1},{1,0},{2,3},{3,2},{4,5},{5,4},{6,7},{7,6},{8,9},{9,8},{10,11... | collective-permute-start | bytes 1572872 | tf_op jit(solution)/shard_map/ppermute | solution.py:20
  49.3 9.7 %collective-permute-start.4 = (bf16[64,4096]{1,0:T(8,128)(2,1)S(1)}, bf16[64,4096]{1,0:T(8,128)(2,1)}, u32[]{:S(2)}, u32[]{:S(2)}) collective-permute-start(bf16[64,4096]{1,0:T(8,128)(2,1)S(1)} %collective-permute-done.2.refs_0_), channel_id=1, source_target_pairs={{0,1},{1,0},{2,3},{3,2},{4,5},{5,4},{6,7},{7,6},{8,9},{9,8},{10,11... | collective-permute-start | bytes 1572872 | tf_op jit(solution)/shard_map/ppermute | solution.py:20
  49.3 12.7 %collective-permute-start.5 = (bf16[64,4096]{1,0:T(8,128)(2,1)S(1)}, bf16[64,4096]{1,0:T(8,128)(2,1)}, u32[]{:S(2)}, u32[]{:S(2)}) collective-permute-start(bf16[64,4096]{1,0:T(8,128)(2,1)S(1)} %collective-permute-done.3.refs_1_), channel_id=1, source_target_pairs={{0,1},{1,0},{2,3},{3,2},{4,5},{5,4},{6,7},{7,6},{8,9},{9,8},{10,11... | collective-permute-start | bytes 1572872 | tf_op jit(solution)/shard_map/ppermute | solution.py:20
  54.7 8.3 %collective-permute-start.8 = (bf16[64,4096]{1,0:T(8,128)(2,1)}, bf16[64,4096]{1,0:T(8,128)(2,1)}, u32[]{:S(2)}, u32[]{:S(2)}) collective-permute-start(bf16[64,4096]{1,0:T(8,128)(2,1)} %collective-permute-done.6.refs_0_), channel_id=1, source_target_pairs={{0,1},{1,0},{2,3},{3,2},{4,5},{5,4},{6,7},{7,6},{8,9},{9,8},{10,11... | collective-permute-start | bytes 1572872 | tf_op jit(solution)/shard_map/ppermute | solution.py:20
  58.8 16.0 %collective-permute-start.9 = (bf16[64,4096]{1,0:T(8,128)(2,1)}, bf16[64,4096]{1,0:T(8,128)(2,1)S(1)}, u32[]{:S(2)}, u32[]{:S(2)}) collective-permute-start(bf16[64,4096]{1,0:T(8,128)(2,1)} %collective-permute-done.7.refs_1_), channel_id=1, source_target_pairs={{0,1},{1,0},{2,3},{3,2},{4,5},{5,4},{6,7},{7,6},{8,9},{9,8},{10,11... | collective-permute-start | bytes 1572872 | tf_op jit(solution)/shard_map/ppermute | solution.py:20
  58.9 11.0 %collective-permute-start.14 = (bf16[32,4096]{1,0:T(8,128)(2,1)S(1)}, bf16[32,4096]{1,0:T(8,128)(2,1)S(1)}, u32[]{:S(2)}, u32[]{:S(2)}) collective-permute-start(bf16[32,4096]{1,0:T(8,128)(2,1)S(1)} %slice.8), channel_id=1, source_target_pairs={{0,4},{1,5},{2,6},{3,7},{4,8},{5,9},{6,10},{7,11},{8,12},{9,13},{1... | collective-permute-start | bytes 786440 | tf_op jit(solution)/shard_map/ppermute | solution.py:20
  59.0 11.4 %collective-permute-start.15 = (bf16[32,4096]{1,0:T(8,128)(2,1)S(1)}, bf16[32,4096]{1,0:T(8,128)(2,1)S(1)}, u32[]{:S(2)}, u32[]{:S(2)}) collective-permute-start(bf16[32,4096]{1,0:T(8,128)(2,1)S(1)} %slice.9), channel_id=1, source_target_pairs={{0,28},{1,29},{2,30},{3,31},{4,0},{5,1},{6,2},{7,3},{8,4},{9,5},{1... | collective-permute-start | bytes 786440 | tf_op jit(solution)/shard_map/ppermute | solution.py:20
  62.0 20.6 %collective-permute-start.12 = (bf16[64,4096]{1,0:T(8,128)(2,1)S(1)}, bf16[64,4096]{1,0:T(8,128)(2,1)S(1)}, u32[]{:S(2)}, u32[]{:S(2)}) collective-permute-start(bf16[64,4096]{1,0:T(8,128)(2,1)S(1)} %collective-permute-done.10.refs_0_), channel_id=1, source_target_pairs={{0,1},{1,0},{2,3},{3,2},{4,5},{5,4},{6,7},{7,6},{8,9},{9,8},{10,11... | collective-permute-start | bytes 1572872 | tf_op jit(solution)/shard_map/ppermute | solution.py:20
  63.0 19.6 %collective-permute-start.13 = (bf16[64,4096]{1,0:T(8,128)(2,1)S(1)}, bf16[64,4096]{1,0:T(8,128)(2,1)S(1)}, u32[]{:S(2)}, u32[]{:S(2)}) collective-permute-start(bf16[64,4096]{1,0:T(8,128)(2,1)S(1)} %collective-permute-done.11.refs_1_), channel_id=1, source_target_pairs={{0,1},{1,0},{2,3},{3,2},{4,5},{5,4},{6,7},{7,6},{8,9},{9,8},{10,11... | collective-permute-start | bytes 1572872 | tf_op jit(solution)/shard_map/ppermute | solution.py:20
  63.1 3.4 %copy-start.1 = (bf16[1024,1,4096]{2,0,1:T(8,128)(2,1)S(1)}, bf16[1024,1,4096]{2,0,1:T(8,128)(2,1)}, u32[]{:S(2)}) copy-start(bf16[1024,1,4096]{2,0,1:T(8,128)(2,1)} %param.7) | copy-start | bytes 25165828
  66.5 4.0 %copy-start.2 = (bf16[1024,1,4096]{2,0,1:T(8,128)(2,1)S(1)}, bf16[1024,1,4096]{2,0,1:T(8,128)(2,1)}, u32[]{:S(2)}) copy-start(bf16[1024,1,4096]{2,0,1:T(8,128)(2,1)} %param.7) | copy-start | bytes 25165828
  69.9 9.3 %collective-permute-start.16 = (bf16[32,4096]{1,0:T(8,128)(2,1)S(1)}, bf16[32,4096]{1,0:T(8,128)(2,1)S(1)}, u32[]{:S(2)}, u32[]{:S(2)}) collective-permute-start(bf16[32,4096]{1,0:T(8,128)(2,1)S(1)} %collective-permute-done.14.refs_0_), channel_id=1, source_target_pairs={{0,1},{1,0},{2,3},{3,2},{4,5},{5,4},{6,7},{7,6},{8,9},{9,8},{10,11... | collective-permute-start | bytes 786440 | tf_op jit(solution)/shard_map/ppermute | solution.py:20
  70.4 8.9 %collective-permute-start.17 = (bf16[32,4096]{1,0:T(8,128)(2,1)S(1)}, bf16[32,4096]{1,0:T(8,128)(2,1)S(1)}, u32[]{:S(2)}, u32[]{:S(2)}) collective-permute-start(bf16[32,4096]{1,0:T(8,128)(2,1)S(1)} %collective-permute-done.15.refs_1_), channel_id=1, source_target_pairs={{0,1},{1,0},{2,3},{3,2},{4,5},{5,4},{6,7},{7,6},{8,9},{9,8},{10,11... | collective-permute-start | bytes 786440 | tf_op jit(solution)/shard_map/ppermute | solution.py:20

commit v2 on v1

--- a/solution.py
+++ b/solution.py
@@ -10,14 +10,23 @@
 NZ = 8
 PANEL = 32
 CBLK = 256
+SBLK = 512
 
 
-def _move(x, dz=0, flip_y=False, flip_core=False):
-    route = []
-    for i in range(NZ * 4):
-        z, rest = divmod(i, 4)
-        route.append((i, ((z + dz) % NZ) * 4 + (rest ^ (2 * flip_y) ^ (1 * flip_core))))
-    return lax.ppermute(x, "blk", route)
+def _route(x, target):
+    return lax.ppermute(x, "blk", [(i, target(*divmod(i, 4))) for i in range(NZ * 4)])
+
+
+def _along(x):
+    return _route(x, lambda z, rest: ((z + (1 if rest % 2 == 0 else -1)) % NZ) * 4 + rest)
+
+
+def _swap_core(x):
+    return _route(x, lambda z, rest: z * 4 + (rest ^ 1))
+
+
+def _swap_y(x):
+    return _route(x, lambda z, rest: z * 4 + (rest ^ 2))
 
 
 def _score_kernel(scale, count, *refs):
@@ -34,10 +43,10 @@
     n = sum(p.shape[0] for p in pieces)
     return pl.pallas_call(
         functools.partial(_score_kernel, scale, len(pieces)),
-        grid=(rows // CBLK,),
+        grid=(rows // SBLK,),
         in_specs=[pl.BlockSpec(p.shape, lambda i: (0, 0)) for p in pieces]
-        + [pl.BlockSpec((CBLK, feats), lambda i: (i, 0))],
-        out_specs=pl.BlockSpec((n, CBLK), lambda i: (0, i)),
+        + [pl.BlockSpec((SBLK, feats), lambda i: (i, 0))],
+        out_specs=pl.BlockSpec((n, SBLK), lambda i: (0, i)),
         out_shape=jax.ShapeDtypeStruct((n, rows), jnp.bfloat16),
         compiler_params=pltpu.CompilerParams(vmem_limit_bytes=24 << 20),
         cost_estimate=pl.CostEstimate(
@@ -65,7 +74,7 @@
         + [pl.BlockSpec(memory_space=pltpu.VMEM) for _ in parts],
         out_specs=pl.BlockSpec(memory_space=pltpu.VMEM),
         out_shape=jax.ShapeDtypeStruct((sum(counts), PANEL, rows), jnp.bfloat16),
-        compiler_params=pltpu.CompilerParams(vmem_limit_bytes=16 << 20),
+        compiler_params=pltpu.CompilerParams(vmem_limit_bytes=12 << 20),
         name="place",
     )(where, *parts)
 
@@ -85,7 +94,7 @@
         in_specs=[pl.BlockSpec((groups, width, CBLK), lambda i: (0, 0, i))],
         out_specs=pl.BlockSpec((CBLK, width), lambda i: (i, 0)),
         out_shape=jax.ShapeDtypeStruct((rows, width), jnp.float32),
-        compiler_params=pltpu.CompilerParams(vmem_limit_bytes=16 << 20),
+        compiler_params=pltpu.CompilerParams(vmem_limit_bytes=12 << 20),
         name="total",
     )(parts)
 
@@ -103,33 +112,44 @@
     panel = precond.reshape(width, layer_count * features).astype(jnp.bfloat16)
     flat = candidates.reshape(cand_rows, layer_count * features)
 
-    slots = []
-
-    own = jnp.concatenate([panel, _move(panel, flip_y=True)], axis=0)
-    steps = []
-
-    def meet(arrivals):
-        pieces = [a for a, _ in arrivals]
-        pieces += [_move(a, flip_core=True) for a, _ in arrivals]
-        for dc in (0, 1):
-            for _, where in arrivals:
-                slots.extend((dz, dy, dc) for dz, dy in where)
-        steps.append(_score(pieces, flat, scale))
-
-    meet([(own, [(0, 0), (0, 1)])])
-    fw = bw = own
-    for s in range(1, NZ // 2):
-        fw, bw = _move(fw, dz=1), _move(bw, dz=-1)
-        meet([(fw, [(-s, 0), (-s, 1)]), (bw, [(s, 0), (s, 1)])])
-    s = NZ // 2
-    last_fw, last_bw = _move(fw[:PANEL], dz=1), _move(bw[PANEL:], dz=-1)
-    meet([(last_fw, [(-s, 0)]), (last_bw, [(s, 1)])])
-
+    flat = pltpu.with_memory_space_constraint(flat, pltpu.HBM)
     me = lax.axis_index("blk")
     z, rest = me // 4, me % 4
-    dz = jnp.array([t[0] for t in slots], jnp.int32)
-    flip = jnp.array([t[1] * 2 + t[2] for t in slots], jnp.int32)
-    source = ((z + dz) % NZ) * 4 + (rest ^ flip)
+    core = me % 2
+    up = 1 - 2 * core
+
+    sources = []
+
+    def note(dz, dy):
+        sources.append(((z + dz) % NZ) * 4 + (rest ^ (2 * dy)))
+        sources.append(((z + dz) % NZ) * 4 + (rest ^ (2 * dy) ^ 1))
+
+    def note_far(dz, dy):
+        sources.append(((z + dz) % NZ) * 4 + (rest ^ (2 * dy) ^ 1))
+        sources.append(((z + dz) % NZ) * 4 + (rest ^ (2 * dy)))
+
+    across = _swap_y(panel)
+    near = jnp.concatenate([panel, _swap_core(panel)], axis=0)
+    far = jnp.concatenate([across, _swap_core(across)], axis=0)
+    note(0, 0)
+    note(0, 1)
+    steps = [_score([near, far], flat, scale)]
+    for s in range(1, NZ // 2):
+        near, far = _along(near), _along(far)
+        steps[-1], near = lax.optimization_barrier((steps[-1], near))
+        steps[-1], far = lax.optimization_barrier((steps[-1], far))
+        note(-s * up, 0)
+        note_far(s * up, 0)
+        note(-s * up, 1)
+        note_far(s * up, 1)
+        steps.append(_score([near, _swap_core(near), far, _swap_core(far)], flat, scale))
+    last = _along(jnp.where(core == 0, near, far))
+    steps[-1], last = lax.optimization_barrier((steps[-1], last))
+    note(NZ // 2, core)
+    note_far(NZ // 2, 1 - core)
+    steps.append(_score([last, _swap_core(last)], flat, scale))
+
+    source = jnp.stack(sources)
     places = jnp.arange(panel_order.shape[0], dtype=jnp.int32)
     where = jnp.sum(jnp.where(panel_order[None, :] == source[:, None], places[None, :], 0), axis=1).astype(jnp.int32)
     buffer = _place(steps, where).reshape(groups, -1, cand_rows)

time: 120 us -> 115 us (0.958)
  waiting for transfers between devices: 30.3 us -> 21.7 us
  Pallas kernels: 21.1 us -> 27.7 us
  local copies, waits for them, and re-layouts: 5.42 us -> 3.96 us
    ppermute x18 -> x17, waiting for transfers between devices: 30.3 us -> 21.7 us  [_route(): lax.ppermute(x, 'blk', [(i, target(*divmod(i, 4))) for i in range(NZ * 4)])]
    pallas_call x5, Pallas kernels: 18.5 us -> 25.1 us  [_score(): pl.pallas_call(functools.partial(_score_kernel, scale, len(pieces)), grid...]
    unnamed x15 -> x12, local copies, waits for them, and re-layouts: 3.43 us -> 1.88 us
    ppermute x18 -> x17, starting transfers between devices: 28.6 us -> 27.8 us  [_route(): lax.ppermute(x, 'blk', [(i, target(*divmod(i, 4))) for i in range(NZ * 4)])]
  transfers between devices with their start and end apart: 18 -> 17, of which waited for: 4 -> 11; matrix products, arithmetic and copies ran while one was open for 0% -> 0% of each run, Pallas kernels for 13% -> 17%
where the time goes in v2:
time: 115 us
  blocking collectives  31.1 us (27%)
  starting transfers between devices  27.8 us (24%)
  Pallas kernels  27.7 us (24%)
  waiting for transfers between devices  21.7 us (19%)
  local copies, waits for them, and re-layouts  3.96 us (3%)
  matrix products  2.47 us (2%)
    all_to_all x1, blocking collectives, body(): lax.all_to_all(buffer, 'group', split_axis=0, concat_axis=0, tiled=True)  31.1 us
    ppermute x17, starting transfers between devices, _route(): lax.ppermute(x, 'blk', [(i, target(*divmod(i, 4))) for i in range(NZ * 4)])  27.8 us
    pallas_call x5, Pallas kernels, _score(): pl.pallas_call(functools.partial(_score_kernel, scale, len(pieces)), grid...  25.1 us
    ppermute x17, waiting for transfers between devices, _route(): lax.ppermute(x, 'blk', [(i, target(*divmod(i, 4))) for i in range(NZ * 4)])  21.7 us
  transfers between devices with their start and end apart: 17, of which 11 were waited for; matrix products, arithmetic and copies ran while one was open for 0% of the time, Pallas kernels for 17%

profile of v2, /device:TPU:1, one launch (start us, length us, event | category | flops | bytes accessed | tf_op | source)
XLA Modules:
  0.0 115.1 jit_solution(266637502103685023)
XLA Ops:
  0.0 1.5 %reshape.27 = bf16[32,64,64]{2,1,0:T(8,128)(2,1)S(1)} reshape(bf16[32,1,4096]{2,0,1:T(8,128)(2,1)} %param.6) | data formatting | bytes 524288 | tf_op jit(solution)/shard_map/reshape
  1.5 0.7 convolution_bitcast_fusion
  2.2 1.8 %fusion = bf16[32,1,64,64]{3,2,0,1:T(8,128)(2,1)S(1)} fusion(f32[32,64,64]{1,2,0:T(8,128)S(1)} %convolution_bitcast_fusion, f32[1,64,64]{2,1,0:T(8,128)S(1)} %copy-done.3), kind=kOutput, calls=%fused_computation.2 | convolution fusion | flops 100794368 | bytes 802816 | tf_op jit(solution)/shard_map/qlac,lcd->qlad/dot_general | solution.py:111
  4.0 0.5 convert_element_type.20
  4.4 3.3 %collective-permute-start = (bf16[32,4096]{1,0:T(8,128)(2,1)S(1)}, bf16[32,4096]{1,0:T(8,128)(2,1)S(1)}, u32[]{:S(2)}, u32[]{:S(2)}) collective-permute-start(bf16[32,4096]{1,0:T(8,128)(2,1)S(1)} %convert_element_type.20), channel_id=1, source_target_pairs={{0,1},{1,0},{2,3},{3,2},{4,5},{5,4},{6,7},{7,6},{8,9},{9,8},{10,11... | collective-permute-start | bytes 786440 | tf_op jit(solution)/shard_map/ppermute | solution.py:17
  7.8 1.2 %collective-permute-start.1 = (bf16[32,4096]{1,0:T(8,128)(2,1)S(1)}, bf16[32,4096]{1,0:T(8,128)(2,1)S(1)}, u32[]{:S(2)}, u32[]{:S(2)}) collective-permute-start(bf16[32,4096]{1,0:T(8,128)(2,1)S(1)} %convert_element_type.20), channel_id=1, source_target_pairs={{0,2},{1,3},{2,0},{3,1},{4,6},{5,7},{6,4},{7,5},{8,10},{9,11},{10,... | collective-permute-start | bytes 786440 | tf_op jit(solution)/shard_map/ppermute | solution.py:17
  9.0 5.7 %collective-permute-start.3 = (bf16[64,4096]{1,0:T(8,128)(2,1)S(1)}, bf16[64,4096]{1,0:T(8,128)(2,1)S(1)}, u32[]{:S(2)}, u32[]{:S(2)}) collective-permute-start(bf16[64,4096]{1,0:T(8,128)(2,1)S(1)} %constant_dynamic-update-slice_fusion.refs_0_), channel_id=1, source_target_pairs={{0,4},{1,29},{2,6},{3,31},{4,8},{5,1},{6,10},{7,3},{8,12},{9,5},{1... | collective-permute-start | bytes 1572872 | tf_op jit(solution)/shard_map/ppermute | solution.py:17
  14.7 2.5 %collective-permute-done.1 = bf16[32,4096]{1,0:T(8,128)(2,1)S(1)} collective-permute-done((bf16[32,4096]{1,0:T(8,128)(2,1)S(1)}, bf16[32,4096]{1,0:T(8,128)(2,1)S(1)}, u32[]{:S(2)}, u32[]{:S(2)}) %collective-permute-start.1) | collective-permute-done | bytes 262176 | tf_op jit(solution)/shard_map/ppermute | solution.py:17
  17.1 0.9 collective-permute-start.2
  18.0 1.1 collective-permute-done.2
  19.2 3.9 %collective-permute-start.4 = (bf16[64,4096]{1,0:T(8,128)(2,1)S(1)}, bf16[64,4096]{1,0:T(8,128)(2,1)S(1)}, u32[]{:S(2)}, u32[]{:S(2)}) collective-permute-start(bf16[64,4096]{1,0:T(8,128)(2,1)S(1)} %constant_dynamic-update-slice_fusion.2.refs_1_), channel_id=1, source_target_pairs={{0,4},{1,29},{2,6},{3,31},{4,8},{5,1},{6,10},{7,3},{8,12},{9,5},{1... | collective-permute-start | bytes 1572872 | tf_op jit(solution)/shard_map/ppermute | solution.py:17
  23.1 5.3 %score.5.refs_0_ = bf16[128,1024]{1,0:T(8,128)(2,1)S(1)} custom-call(bf16[64,4096]{1,0:T(8,128)(2,1)S(1)} %constant_dynamic-update-slice_fusion.refs_0_, bf16[64,4096]{1,0:T(8,128)(2,1)S(1)} %constant_dynamic-update-slice_fusion.2.refs_1_, bf16[1024,4096]{1,0:T(8,128)(2,1)} %bitcast.63), custom_call_target="tpu_custom_call" | custom-call | flops 1073741824 | bytes 9699328 | tf_op jit(solution)/shard_map/score/pallas_call | solution.py:44
  28.4 0.1 collective-permute-start.5
  28.5 0.7 collective-permute-done.4.refs_2_
  29.2 1.7 %collective-permute-start.6 = (bf16[64,4096]{1,0:T(8,128)(2,1)S(1)}, bf16[64,4096]{1,0:T(8,128)(2,1)S(1)}, u32[]{:S(2)}, u32[]{:S(2)}) collective-permute-start(bf16[64,4096]{1,0:T(8,128)(2,1)S(1)} %collective-permute-done.4.refs_2_), channel_id=1, source_target_pairs={{0,1},{1,0},{2,3},{3,2},{4,5},{5,4},{6,7},{7,6},{8,9},{9,8},{10,11... | collective-permute-start | bytes 1572872 | tf_op jit(solution)/shard_map/ppermute | solution.py:17
  30.9 1.7 %collective-permute-start.7 = (bf16[64,4096]{1,0:T(8,128)(2,1)S(1)}, bf16[64,4096]{1,0:T(8,128)(2,1)S(1)}, u32[]{:S(2)}, u32[]{:S(2)}) collective-permute-start(bf16[64,4096]{1,0:T(8,128)(2,1)S(1)} %collective-permute-done.3.refs_0_), channel_id=1, source_target_pairs={{0,4},{1,29},{2,6},{3,31},{4,8},{5,1},{6,10},{7,3},{8,12},{9,5},{1... | collective-permute-start | bytes 1572872 | tf_op jit(solution)/shard_map/ppermute | solution.py:17
  32.7 0.7 collective-permute-start.8
  33.4 0.0 collective-permute-done.5.refs_1_
  33.4 0.0 collective-permute-done.6.refs_3_
  33.4 4.8 %score.6.refs_1_ = bf16[256,1024]{1,0:T(8,128)(2,1)S(1)} custom-call(bf16[64,4096]{1,0:T(8,128)(2,1)S(1)} %collective-permute-done.3.refs_0_, bf16[64,4096]{1,0:T(8,128)(2,1)S(1)} %collective-permute-done.5.refs_1_, bf16[64,4096]{1,0:T(8,128)(2,1)S(1)} %collective-permute-done.4.refs_2_, bf16[64,4096]{1,0:T(8,128)(2,1)S(1)} %collective-permute-done.6.refs_3_, ...), custom_call_target="tpu_custom_call" | custom-call | flops 2147483648 | bytes 11010048 | tf_op jit(solution)/shard_map/score/pallas_call | solution.py:44
  38.2 1.0 collective-permute-done.7.refs_0_
  39.3 5.6 %collective-permute-done.8.refs_2_ = bf16[64,4096]{1,0:T(8,128)(2,1)S(1)} collective-permute-done((bf16[64,4096]{1,0:T(8,128)(2,1)S(1)}, bf16[64,4096]{1,0:T(8,128)(2,1)S(1)}, u32[]{:S(2)}, u32[]{:S(2)}) %collective-permute-start.8) | collective-permute-done | bytes 524320 | tf_op jit(solution)/shard_map/ppermute | solution.py:17
  44.9 2.1 %collective-permute-start.9 = (bf16[64,4096]{1,0:T(8,128)(2,1)S(1)}, bf16[64,4096]{1,0:T(8,128)(2,1)S(1)}, u32[]{:S(2)}, u32[]{:S(2)}) collective-permute-start(bf16[64,4096]{1,0:T(8,128)(2,1)S(1)} %collective-permute-done.7.refs_0_), channel_id=1, source_target_pairs={{0,1},{1,0},{2,3},{3,2},{4,5},{5,4},{6,7},{7,6},{8,9},{9,8},{10,11... | collective-permute-start | bytes 1572872 | tf_op jit(solution)/shard_map/ppermute | solution.py:17
  46.9 0.0 collective-permute-start.10
  46.9 1.1 collective-permute-start.11
  48.0 0.2 collective-permute-start.12
  48.2 1.0 collective-permute-done.9.refs_1_
  49.2 0.8 copy-done.1
  50.0 1.0 copy-done.2
  51.0 4.9 %score.7.refs_2_ = bf16[256,1024]{1,0:T(8,128)(2,1)S(1)} custom-call(bf16[64,4096]{1,0:T(8,128)(2,1)S(1)} %collective-permute-done.7.refs_0_, bf16[64,4096]{1,0:T(8,128)(2,1)S(1)} %copy-done.2, bf16[64,4096]{1,0:T(8,128)(2,1)S(1)} %collective-permute-done.8.refs_2_, bf16[64,4096]{1,0:T(8,128)(2,1)} %collective-permute-done.10.refs_3_, ...), custom_call_target="tpu_custom_call" | custom-call | flops 2147483648 | bytes 11010048 | tf_op jit(solution)/shard_map/score/pallas_call | solution.py:44
  56.0 4.9 %collective-permute-done.12.refs_2_ = bf16[64,4096]{1,0:T(8,128)(2,1)S(1)} collective-permute-done((bf16[64,4096]{1,0:T(8,128)(2,1)S(1)}, bf16[64,4096]{1,0:T(8,128)(2,1)S(1)}, u32[]{:S(2)}, u32[]{:S(2)}) %collective-permute-start.12) | collective-permute-done | bytes 524320 | tf_op jit(solution)/shard_map/ppermute | solution.py:17
  60.9 2.6 %collective-permute-start.13 = (bf16[64,4096]{1,0:T(8,128)(2,1)S(1)}, bf16[64,4096]{1,0:T(8,128)(2,1)S(1)}, u32[]{:S(2)}, u32[]{:S(2)}) collective-permute-start(bf16[64,4096]{1,0:T(8,128)(2,1)S(1)} %collective-permute-done.11.refs_0_), channel_id=1, source_target_pairs={{0,1},{1,0},{2,3},{3,2},{4,5},{5,4},{6,7},{7,6},{8,9},{9,8},{10,11... | collective-permute-start | bytes 1572872 | tf_op jit(solution)/shard_map/ppermute | solution.py:17
  63.5 0.0 collective-permute-start.14
  63.5 0.1 broadcast_select_fusion
  63.5 0.0 copy-start.4
  63.5 0.1 collective-permute-start.15
  63.6 1.4 %collective-permute-done.13.refs_1_ = bf16[64,4096]{1,0:T(8,128)(2,1)S(1)} collective-permute-done((bf16[64,4096]{1,0:T(8,128)(2,1)S(1)}, bf16[64,4096]{1,0:T(8,128)(2,1)S(1)}, u32[]{:S(2)}, u32[]{:S(2)}) %collective-permute-start.13) | collective-permute-done | bytes 524320 | tf_op jit(solution)/shard_map/ppermute | solution.py:17
  65.0 0.7 collective-permute-done.14.refs_3_
  65.7 4.8 %score.8.refs_3_ = bf16[256,1024]{1,0:T(8,128)(2,1)S(1)} custom-call(bf16[64,4096]{1,0:T(8,128)(2,1)S(1)} %collective-permute-done.11.refs_0_, bf16[64,4096]{1,0:T(8,128)(2,1)S(1)} %collective-permute-done.13.refs_1_, bf16[64,4096]{1,0:T(8,128)(2,1)S(1)} %collective-permute-done.12.refs_2_, bf16[64,4096]{1,0:T(8,128)(2,1)S(1)} %collective-permute-done.14.refs_3_, ...), custom_call_target="tpu_custom_call" | custom-call | flops 2147483648 | bytes 11010048 | tf_op jit(solution)/shard_map/score/pallas_call | solution.py:44
  70.6 1.4 %collective-permute-done.15.refs_0_ = bf16[64,4096]{1,0:T(8,128)(2,1)S(1)} collective-permute-done((bf16[64,4096]{1,0:T(8,128)(2,1)S(1)}, bf16[64,4096]{1,0:T(8,128)(2,1)S(1)}, u32[]{:S(2)}, u32[]{:S(2)}) %collective-permute-start.15) | collective-permute-done | bytes 524320 | tf_op jit(solution)/shard_map/ppermute | solution.py:17
  71.9 2.6 %collective-permute-start.16 = (bf16[64,4096]{1,0:T(8,128)(2,1)S(1)}, bf16[64,4096]{1,0:T(8,128)(2,1)S(1)}, u32[]{:S(2)}, u32[]{:S(2)}) collective-permute-start(bf16[64,4096]{1,0:T(8,128)(2,1)S(1)} %collective-permute-done.15.refs_0_), channel_id=1, source_target_pairs={{0,1},{1,0},{2,3},{3,2},{4,5},{5,4},{6,7},{7,6},{8,9},{9,8},{10,11... | collective-permute-start | bytes 1572872 | tf_op jit(solution)/shard_map/ppermute | solution.py:17
  74.5 0.1 stack.131
  74.6 0.2 select_reduce_fusion.where_ref
  74.8 1.2 %collective-permute-done.16.refs_1_ = bf16[64,4096]{1,0:T(8,128)(2,1)S(1)} collective-permute-done((bf16[64,4096]{1,0:T(8,128)(2,1)S(1)}, bf16[64,4096]{1,0:T(8,128)(2,1)S(1)}, u32[]{:S(2)}, u32[]{:S(2)}) %collective-permute-start.16) | collective-permute-done | bytes 524320 | tf_op jit(solution)/shard_map/ppermute | solution.py:17
  76.1 5.3 %score.9.refs_4_ = bf16[128,1024]{1,0:T(8,128)(2,1)S(1)} custom-call(bf16[64,4096]{1,0:T(8,128)(2,1)S(1)} %collective-permute-done.15.refs_0_, bf16[64,4096]{1,0:T(8,128)(2,1)S(1)} %collective-permute-done.16.refs_1_, bf16[1024,4096]{1,0:T(8,128)(2,1)} %bitcast.67), custom_call_target="tpu_custom_call" | custom-call | flops 1073741824 | bytes 9699328 | tf_op jit(solution)/shard_map/score/pallas_call | solution.py:44
  81.3 0.7 place.1
  82.0 31.1 %all_to_all.5.in_ref = bf16[8,128,1024]{2,1,0:T(8,128)(2,1)S(1)} all-to-all(bf16[8,128,1024]{2,1,0:T(8,128)(2,1)S(1)} %bitcast.62), channel_id=1, replica_groups=mesh['group'=8,'blk'=32] {'group'}, dimensions={0} | all-to-all | bytes 4194304 | tf_op jit(solution)/shard_map/all_to_all | solution.py:156
  113.2 1.9 %total.1 = f32[1024,128]{1,0:T(8,128)} custom-call(bf16[8,128,1024]{2,1,0:T(8,128)(2,1)S(1)} %all_to_all.5.in_ref), custom_call_target="tpu_custom_call" | custom-call | tf_op jit(solution)/shard_map/total/pallas_call | solution.py:91
  (15 shorter events, 0.1 us)
Async XLA Ops:
  0.0 1.5 %copy-start = (f32[1,64,64]{2,1,0:T(8,128)S(1)}, f32[1,64,64]{2,1,0:T(8,128)}, u32[]{:S(2)}) copy-start(f32[1,64,64]{2,1,0:T(8,128)} %param.7) | copy-start | bytes 49156
  0.0 2.2 %copy-start.3 = (f32[1,64,64]{2,1,0:T(8,128)S(1)}, f32[1,64,64]{2,1,0:T(8,128)}, u32[]{:S(2)}) copy-start(f32[1,64,64]{2,1,0:T(8,128)} %param.8) | copy-start | bytes 49156
  4.4 4.5 %collective-permute-start = (bf16[32,4096]{1,0:T(8,128)(2,1)S(1)}, bf16[32,4096]{1,0:T(8,128)(2,1)S(1)}, u32[]{:S(2)}, u32[]{:S(2)}) collective-permute-start(bf16[32,4096]{1,0:T(8,128)(2,1)S(1)} %convert_element_type.20), channel_id=1, source_target_pairs={{0,1},{1,0},{2,3},{3,2},{4,5},{5,4},{6,7},{7,6},{8,9},{9,8},{10,11... | collective-permute-start | bytes 786440 | tf_op jit(solution)/shard_map/ppermute | solution.py:17
  7.8 9.4 %collective-permute-start.1 = (bf16[32,4096]{1,0:T(8,128)(2,1)S(1)}, bf16[32,4096]{1,0:T(8,128)(2,1)S(1)}, u32[]{:S(2)}, u32[]{:S(2)}) collective-permute-start(bf16[32,4096]{1,0:T(8,128)(2,1)S(1)} %convert_element_type.20), channel_id=1, source_target_pairs={{0,2},{1,3},{2,0},{3,1},{4,6},{5,7},{6,4},{7,5},{8,10},{9,11},{10,... | collective-permute-start | bytes 786440 | tf_op jit(solution)/shard_map/ppermute | solution.py:17
  9.0 19.4 %collective-permute-start.3 = (bf16[64,4096]{1,0:T(8,128)(2,1)S(1)}, bf16[64,4096]{1,0:T(8,128)(2,1)S(1)}, u32[]{:S(2)}, u32[]{:S(2)}) collective-permute-start(bf16[64,4096]{1,0:T(8,128)(2,1)S(1)} %constant_dynamic-update-slice_fusion.refs_0_), channel_id=1, source_target_pairs={{0,4},{1,29},{2,6},{3,31},{4,8},{5,1},{6,10},{7,3},{8,12},{9,5},{1... | collective-permute-start | bytes 1572872 | tf_op jit(solution)/shard_map/ppermute | solution.py:17
  17.1 2.0 %collective-permute-start.2 = (bf16[32,4096]{1,0:T(8,128)(2,1)S(1)}, bf16[32,4096]{1,0:T(8,128)(2,1)S(1)}, u32[]{:S(2)}, u32[]{:S(2)}) collective-permute-start(bf16[32,4096]{1,0:T(8,128)(2,1)S(1)} %collective-permute-done.1), channel_id=1, source_target_pairs={{0,1},{1,0},{2,3},{3,2},{4,5},{5,4},{6,7},{7,6},{8,9},{9,8},{10,11... | collective-permute-start | bytes 786440 | tf_op jit(solution)/shard_map/ppermute | solution.py:17
  19.2 10.0 %collective-permute-start.4 = (bf16[64,4096]{1,0:T(8,128)(2,1)S(1)}, bf16[64,4096]{1,0:T(8,128)(2,1)S(1)}, u32[]{:S(2)}, u32[]{:S(2)}) collective-permute-start(bf16[64,4096]{1,0:T(8,128)(2,1)S(1)} %constant_dynamic-update-slice_fusion.2.refs_1_), channel_id=1, source_target_pairs={{0,4},{1,29},{2,6},{3,31},{4,8},{5,1},{6,10},{7,3},{8,12},{9,5},{1... | collective-permute-start | bytes 1572872 | tf_op jit(solution)/shard_map/ppermute | solution.py:17
  28.4 5.0 %collective-permute-start.5 = (bf16[64,4096]{1,0:T(8,128)(2,1)S(1)}, bf16[64,4096]{1,0:T(8,128)(2,1)S(1)}, u32[]{:S(2)}, u32[]{:S(2)}) collective-permute-start(bf16[64,4096]{1,0:T(8,128)(2,1)S(1)} %collective-permute-done.3.refs_0_), channel_id=1, source_target_pairs={{0,1},{1,0},{2,3},{3,2},{4,5},{5,4},{6,7},{7,6},{8,9},{9,8},{10,11... | collective-permute-start | bytes 1572872 | tf_op jit(solution)/shard_map/ppermute | solution.py:17
  29.2 4.2 %collective-permute-start.6 = (bf16[64,4096]{1,0:T(8,128)(2,1)S(1)}, bf16[64,4096]{1,0:T(8,128)(2,1)S(1)}, u32[]{:S(2)}, u32[]{:S(2)}) collective-permute-start(bf16[64,4096]{1,0:T(8,128)(2,1)S(1)} %collective-permute-done.4.refs_2_), channel_id=1, source_target_pairs={{0,1},{1,0},{2,3},{3,2},{4,5},{5,4},{6,7},{7,6},{8,9},{9,8},{10,11... | collective-permute-start | bytes 1572872 | tf_op jit(solution)/shard_map/ppermute | solution.py:17
  30.9 8.3 %collective-permute-start.7 = (bf16[64,4096]{1,0:T(8,128)(2,1)S(1)}, bf16[64,4096]{1,0:T(8,128)(2,1)S(1)}, u32[]{:S(2)}, u32[]{:S(2)}) collective-permute-start(bf16[64,4096]{1,0:T(8,128)(2,1)S(1)} %collective-permute-done.3.refs_0_), channel_id=1, source_target_pairs={{0,4},{1,29},{2,6},{3,31},{4,8},{5,1},{6,10},{7,3},{8,12},{9,5},{1... | collective-permute-start | bytes 1572872 | tf_op jit(solution)/shard_map/ppermute | solution.py:17
  32.7 12.2 %collective-permute-start.8 = (bf16[64,4096]{1,0:T(8,128)(2,1)S(1)}, bf16[64,4096]{1,0:T(8,128)(2,1)S(1)}, u32[]{:S(2)}, u32[]{:S(2)}) collective-permute-start(bf16[64,4096]{1,0:T(8,128)(2,1)S(1)} %collective-permute-done.4.refs_2_), channel_id=1, source_target_pairs={{0,4},{1,29},{2,6},{3,31},{4,8},{5,1},{6,10},{7,3},{8,12},{9,5},{1... | collective-permute-start | bytes 1572872 | tf_op jit(solution)/shard_map/ppermute | solution.py:17
  44.9 4.3 %collective-permute-start.9 = (bf16[64,4096]{1,0:T(8,128)(2,1)S(1)}, bf16[64,4096]{1,0:T(8,128)(2,1)S(1)}, u32[]{:S(2)}, u32[]{:S(2)}) collective-permute-start(bf16[64,4096]{1,0:T(8,128)(2,1)S(1)} %collective-permute-done.7.refs_0_), channel_id=1, source_target_pairs={{0,1},{1,0},{2,3},{3,2},{4,5},{5,4},{6,7},{7,6},{8,9},{9,8},{10,11... | collective-permute-start | bytes 1572872 | tf_op jit(solution)/shard_map/ppermute | solution.py:17
  46.9 3.0 %collective-permute-start.10 = (bf16[64,4096]{1,0:T(8,128)(2,1)S(1)}, bf16[64,4096]{1,0:T(8,128)(2,1)}, u32[]{:S(2)}, u32[]{:S(2)}) collective-permute-start(bf16[64,4096]{1,0:T(8,128)(2,1)S(1)} %collective-permute-done.8.refs_2_), channel_id=1, source_target_pairs={{0,1},{1,0},{2,3},{3,2},{4,5},{5,4},{6,7},{7,6},{8,9},{9,8},{10,11... | collective-permute-start | bytes 1572872 | tf_op jit(solution)/shard_map/ppermute | solution.py:17
  46.9 9.0 %collective-permute-start.11 = (bf16[64,4096]{1,0:T(8,128)(2,1)S(1)}, bf16[64,4096]{1,0:T(8,128)(2,1)S(1)}, u32[]{:S(2)}, u32[]{:S(2)}) collective-permute-start(bf16[64,4096]{1,0:T(8,128)(2,1)S(1)} %collective-permute-done.7.refs_0_), channel_id=1, source_target_pairs={{0,4},{1,29},{2,6},{3,31},{4,8},{5,1},{6,10},{7,3},{8,12},{9,5},{1... | collective-permute-start | bytes 1572872 | tf_op jit(solution)/shard_map/ppermute | solution.py:17
  48.0 12.8 %collective-permute-start.12 = (bf16[64,4096]{1,0:T(8,128)(2,1)S(1)}, bf16[64,4096]{1,0:T(8,128)(2,1)S(1)}, u32[]{:S(2)}, u32[]{:S(2)}) collective-permute-start(bf16[64,4096]{1,0:T(8,128)(2,1)S(1)} %collective-permute-done.8.refs_2_), channel_id=1, source_target_pairs={{0,4},{1,29},{2,6},{3,31},{4,8},{5,1},{6,10},{7,3},{8,12},{9,5},{1... | collective-permute-start | bytes 1572872 | tf_op jit(solution)/shard_map/ppermute | solution.py:17
  49.2 0.8 copy-start.1
  50.0 1.0 copy-start.2
  60.9 4.1 %collective-permute-start.13 = (bf16[64,4096]{1,0:T(8,128)(2,1)S(1)}, bf16[64,4096]{1,0:T(8,128)(2,1)S(1)}, u32[]{:S(2)}, u32[]{:S(2)}) collective-permute-start(bf16[64,4096]{1,0:T(8,128)(2,1)S(1)} %collective-permute-done.11.refs_0_), channel_id=1, source_target_pairs={{0,1},{1,0},{2,3},{3,2},{4,5},{5,4},{6,7},{7,6},{8,9},{9,8},{10,11... | collective-permute-start | bytes 1572872 | tf_op jit(solution)/shard_map/ppermute | solution.py:17
  63.5 2.3 %collective-permute-start.14 = (bf16[64,4096]{1,0:T(8,128)(2,1)S(1)}, bf16[64,4096]{1,0:T(8,128)(2,1)S(1)}, u32[]{:S(2)}, u32[]{:S(2)}) collective-permute-start(bf16[64,4096]{1,0:T(8,128)(2,1)S(1)} %collective-permute-done.12.refs_2_), channel_id=1, source_target_pairs={{0,1},{1,0},{2,3},{3,2},{4,5},{5,4},{6,7},{7,6},{8,9},{9,8},{10,11... | collective-permute-start | bytes 1572872 | tf_op jit(solution)/shard_map/ppermute | solution.py:17
  63.5 11.1 %copy-start.4 = (s32[32]{0:T(128)S(1)}, s32[32]{0:T(128)}, u32[]{:S(2)}) copy-start(s32[32]{0:T(128)} %param.9) | copy-start | bytes 388
  63.5 8.4 %collective-permute-start.15 = (bf16[64,4096]{1,0:T(8,128)(2,1)S(1)}, bf16[64,4096]{1,0:T(8,128)(2,1)S(1)}, u32[]{:S(2)}, u32[]{:S(2)}) collective-permute-start(bf16[64,4096]{1,0:T(8,128)(2,1)S(1)} %broadcast_select_fusion), channel_id=1, source_target_pairs={{0,4},{1,29},{2,6},{3,31},{4,8},{5,1},{6,10},{7,3},{8,12},{9,5},{1... | collective-permute-start | bytes 1572872 | tf_op jit(solution)/shard_map/ppermute | solution.py:17
  71.9 4.1 %collective-permute-start.16 = (bf16[64,4096]{1,0:T(8,128)(2,1)S(1)}, bf16[64,4096]{1,0:T(8,128)(2,1)S(1)}, u32[]{:S(2)}, u32[]{:S(2)}) collective-permute-start(bf16[64,4096]{1,0:T(8,128)(2,1)S(1)} %collective-permute-done.15.refs_0_), channel_id=1, source_target_pairs={{0,1},{1,0},{2,3},{3,2},{4,5},{5,4},{6,7},{7,6},{8,9},{9,8},{10,11... | collective-permute-start | bytes 1572872 | tf_op jit(solution)/shard_map/ppermute | solution.py:17

commit v3 on v2

--- a/solution.py
+++ b/solution.py
@@ -10,7 +10,6 @@
 NZ = 8
 PANEL = 32
 CBLK = 256
-SBLK = 512
 
 
 def _route(x, target):
@@ -29,13 +28,35 @@
     return _route(x, lambda z, rest: z * 4 + (rest ^ 2))
 
 
+def _joined_kernel(*refs):
+    *parts, out = refs
+    at = 0
+    for r in parts:
+        out[at : at + PANEL, :] = r[:PANEL, :]
+        at += PANEL
+
+
+def _joined(*parts):
+    feats = parts[0].shape[1]
+    return pl.pallas_call(
+        _joined_kernel,
+        in_specs=[pl.BlockSpec(memory_space=pltpu.VMEM) for _ in parts],
+        out_specs=pl.BlockSpec(memory_space=pltpu.VMEM),
+        out_shape=jax.ShapeDtypeStruct((len(parts) * PANEL, feats), parts[0].dtype),
+        compiler_params=pltpu.CompilerParams(vmem_limit_bytes=4 << 20),
+        name="joined",
+    )(*parts)
+
+
 def _score_kernel(scale, count, *refs):
     c_ref, o_ref = refs[count], refs[count + 1]
     panels = jnp.concatenate([r[...] for r in refs[:count]], axis=0)
-    part = lax.dot_general(
-        panels, c_ref[...], (((1,), (1,)), ((), ())), preferred_element_type=jnp.float32
-    )
-    o_ref[...] = (part * scale).astype(o_ref.dtype)
+    for i in range(c_ref.shape[0] // CBLK):
+        block = slice(i * CBLK, (i + 1) * CBLK)
+        part = lax.dot_general(
+            panels, c_ref[block, :], (((1,), (1,)), ((), ())), preferred_element_type=jnp.float32
+        )
+        o_ref[:, block] = (part * scale).astype(o_ref.dtype)
 
 
 def _score(pieces, flat, scale):
@@ -43,12 +64,10 @@
     n = sum(p.shape[0] for p in pieces)
     return pl.pallas_call(
         functools.partial(_score_kernel, scale, len(pieces)),
-        grid=(rows // SBLK,),
-        in_specs=[pl.BlockSpec(p.shape, lambda i: (0, 0)) for p in pieces]
-        + [pl.BlockSpec((SBLK, feats), lambda i: (i, 0))],
-        out_specs=pl.BlockSpec((n, SBLK), lambda i: (0, i)),
+        in_specs=[pl.BlockSpec(memory_space=pltpu.VMEM) for _ in range(len(pieces) + 1)],
+        out_specs=pl.BlockSpec(memory_space=pltpu.VMEM),
         out_shape=jax.ShapeDtypeStruct((n, rows), jnp.bfloat16),
-        compiler_params=pltpu.CompilerParams(vmem_limit_bytes=24 << 20),
+        compiler_params=pltpu.CompilerParams(vmem_limit_bytes=16 << 20),
         cost_estimate=pl.CostEstimate(
             flops=2 * n * rows * feats, bytes_accessed=2 * (rows * feats + n * feats + n * rows), transcendentals=0
         ),
@@ -112,7 +131,7 @@
     panel = precond.reshape(width, layer_count * features).astype(jnp.bfloat16)
     flat = candidates.reshape(cand_rows, layer_count * features)
 
-    flat = pltpu.with_memory_space_constraint(flat, pltpu.HBM)
+    flat = pltpu.with_memory_space_constraint(flat, pltpu.VMEM)
     me = lax.axis_index("blk")
     z, rest = me // 4, me % 4
     core = me % 2
@@ -128,30 +147,39 @@
         sources.append(((z + dz) % NZ) * 4 + (rest ^ (2 * dy) ^ 1))
         sources.append(((z + dz) % NZ) * 4 + (rest ^ (2 * dy)))
 
-    across = _swap_y(panel)
-    near = jnp.concatenate([panel, _swap_core(panel)], axis=0)
-    far = jnp.concatenate([across, _swap_core(across)], axis=0)
     note(0, 0)
     note(0, 1)
-    steps = [_score([near, far], flat, scale)]
     for s in range(1, NZ // 2):
-        near, far = _along(near), _along(far)
-        steps[-1], near = lax.optimization_barrier((steps[-1], near))
-        steps[-1], far = lax.optimization_barrier((steps[-1], far))
         note(-s * up, 0)
         note_far(s * up, 0)
         note(-s * up, 1)
         note_far(s * up, 1)
-        steps.append(_score([near, _swap_core(near), far, _swap_core(far)], flat, scale))
-    last = _along(jnp.where(core == 0, near, far))
-    steps[-1], last = lax.optimization_barrier((steps[-1], last))
-    note(NZ // 2, core)
-    note_far(NZ // 2, 1 - core)
-    steps.append(_score([last, _swap_core(last)], flat, scale))
-
+    for dy in (0, 1):
+        sources.append(((z + NZ // 2) % NZ) * 4 + (rest ^ (2 * dy)))
+        sources.append(((z + NZ // 2) % NZ) * 4 + (rest ^ (2 * dy) ^ 1))
     source = jnp.stack(sources)
     places = jnp.arange(panel_order.shape[0], dtype=jnp.int32)
     where = jnp.sum(jnp.where(panel_order[None, :] == source[:, None], places[None, :], 0), axis=1).astype(jnp.int32)
+
+    steps = []
+
+    def after(step, x):
+        steps[step], x = lax.optimization_barrier((steps[step], x))
+        return x
+
+    across = _swap_y(panel)
+    near = _joined(panel, _swap_core(panel))
+    steps.append(_score([near], flat, scale))
+    steps[0], where, across = lax.optimization_barrier((steps[0], where, across))
+    far = _joined(across, _swap_core(across))
+    steps.append(_score([far], flat, scale))
+    for s in range(1, NZ // 2):
+        near, far = _along(near), _along(far)
+        far = after(s, far)
+        steps.append(_score([near, _swap_core(near), far, _swap_core(far)], flat, scale))
+    near, far = _along(_joined(near)), _along(_joined(far))
+    far = after(NZ // 2, far)
+    steps.append(_score([near, _swap_core(near), far, _swap_core(far)], flat, scale))
     buffer = _place(steps, where).reshape(groups, -1, cand_rows)
     parts = lax.all_to_all(buffer, "group", split_axis=0, concat_axis=0, tiled=True)
     return _total(parts)

time: 115 us -> 107 us (0.930)
  Pallas kernels: 27.7 us -> 18.2 us
  waiting for transfers between devices: 21.7 us -> 17.6 us
  starting transfers between devices: 27.8 us -> 30.6 us
  local copies, waits for them, and re-layouts: 3.96 us -> 5.43 us
    pallas_call x5 -> x10, Pallas kernels: 25.1 us -> 15.6 us  [the longest x6 15.5 us: _score(): pl.pallas_call(functools.partial(_score_kernel, scale, len(pieces)), in_s...]
    ppermute x17 -> x19, waiting for transfers between devices: 21.7 us -> 17.6 us  [_route(): lax.ppermute(x, 'blk', [(i, target(*divmod(i, 4))) for i in range(NZ * 4)])]
    ppermute x17 -> x19, starting transfers between devices: 27.8 us -> 30.6 us  [_route(): lax.ppermute(x, 'blk', [(i, target(*divmod(i, 4))) for i in range(NZ * 4)])]
    unnamed x12 -> x10, local copies, waits for them, and re-layouts: 1.88 us -> 3.39 us
  transfers between devices with their start and end apart: 17 -> 19, of which waited for: 11 -> 8; matrix products, arithmetic and copies ran while one was open for 0% -> 0% of each run, Pallas kernels for 17% -> 12%
where the time goes in v3:
time: 107 us
  blocking collectives  31.9 us (30%)
  starting transfers between devices  30.6 us (29%)
  Pallas kernels  18.2 us (17%)
  waiting for transfers between devices  17.6 us (16%)
  local copies, waits for them, and re-layouts  5.43 us (5%)
  matrix products  2.47 us (2%)
    all_to_all x1, blocking collectives, body(): lax.all_to_all(buffer, 'group', split_axis=0, concat_axis=0, tiled=True)  31.9 us
    ppermute x19, starting transfers between devices, _route(): lax.ppermute(x, 'blk', [(i, target(*divmod(i, 4))) for i in range(NZ * 4)])  30.6 us
    ppermute x19, waiting for transfers between devices, _route(): lax.ppermute(x, 'blk', [(i, target(*divmod(i, 4))) for i in range(NZ * 4)])  17.6 us
    pallas_call x6, Pallas kernels, _score(): pl.pallas_call(functools.partial(_score_kernel, scale, len(pieces)), in_s...  15.5 us
    unnamed x10, local copies, waits for them, and re-layouts  3.39 us
  transfers between devices with their start and end apart: 19, of which 8 were waited for; matrix products, arithmetic and copies ran while one was open for 0% of the time, Pallas kernels for 12%

profile of v3, /device:TPU:1, one launch (start us, length us, event | category | flops | bytes accessed | tf_op | source)
XLA Modules:
  0.0 106.6 jit_solution(7385356941518781926)
XLA Ops:
  0.0 1.5 %reshape.27 = bf16[32,64,64]{2,1,0:T(8,128)(2,1)S(1)} reshape(bf16[32,1,4096]{2,0,1:T(8,128)(2,1)} %param.6) | data formatting | bytes 524288 | tf_op jit(solution)/shard_map/reshape
  1.5 0.0 copy-start.4
  1.5 0.7 convolution_bitcast_fusion
  2.2 1.8 %fusion = bf16[32,1,64,64]{3,2,0,1:T(8,128)(2,1)S(1)} fusion(f32[32,64,64]{1,2,0:T(8,128)S(1)} %convolution_bitcast_fusion, f32[1,64,64]{2,1,0:T(8,128)S(1)} %copy-done.3), kind=kOutput, calls=%fused_computation.2 | convolution fusion | flops 100794368 | bytes 802816 | tf_op jit(solution)/shard_map/qlac,lcd->qlad/dot_general | solution.py:130
  4.0 0.5 convert_element_type.16.refs_0_
  4.5 3.3 %collective-permute-start = (bf16[32,4096]{1,0:T(8,128)(2,1)S(1)}, bf16[32,4096]{1,0:T(8,128)(2,1)S(1)}, u32[]{:S(2)}, u32[]{:S(2)}) collective-permute-start(bf16[32,4096]{1,0:T(8,128)(2,1)S(1)} %convert_element_type.16.refs_0_), channel_id=1, source_target_pairs={{0,1},{1,0},{2,3},{3,2},{4,5},{5,4},{6,7},{7,6},{8,9},{9,8},{10,11... | collective-permute-start | bytes 786440 | tf_op jit(solution)/shard_map/ppermute | solution.py:16
  7.8 1.2 %collective-permute-start.1 = (bf16[32,4096]{1,0:T(8,128)(2,1)S(1)}, bf16[32,4096]{1,0:T(8,128)(2,1)S(1)}, u32[]{:S(2)}, u32[]{:S(2)}) collective-permute-start(bf16[32,4096]{1,0:T(8,128)(2,1)S(1)} %convert_element_type.16.refs_0_), channel_id=1, source_target_pairs={{0,2},{1,3},{2,0},{3,1},{4,6},{5,7},{6,4},{7,5},{8,10},{9,11},{10,... | collective-permute-start | bytes 786440 | tf_op jit(solution)/shard_map/ppermute | solution.py:16
  9.0 0.1 stack.131
  9.1 0.2 select_reduce_fusion.where_ref
  9.3 0.0 collective-permute-done.refs_1_
  9.3 0.0 copy-start.1
  9.3 3.4 %copy-done.1 = bf16[1024,1,4096]{2,0,1:T(8,128)(2,1)S(1)} copy-done((bf16[1024,1,4096]{2,0,1:T(8,128)(2,1)S(1)}, bf16[1024,1,4096]{2,0,1:T(8,128)(2,1)}, u32[]{:S(2)}) %copy-start.1) | copy-done | bytes 8388632
  12.7 2.6 %score.6.refs_0_ = bf16[64,1024]{1,0:T(8,128)(2,1)S(1)} custom-call(bf16[64,4096]{1,0:T(8,128)(2,1)S(1)} %joined.4.refs_0_, bf16[1024,4096]{1,0:T(8,128)(2,1)S(1)} %bitcast.62), custom_call_target="tpu_custom_call" | custom-call | flops 536870912 | bytes 9043968 | tf_op jit(solution)/shard_map/score/pallas_call | solution.py:65
  15.4 1.8 %collective-permute-done.1.refs_0_ = bf16[32,4096]{1,0:T(8,128)(2,1)S(1)} collective-permute-done((bf16[32,4096]{1,0:T(8,128)(2,1)S(1)}, bf16[32,4096]{1,0:T(8,128)(2,1)S(1)}, u32[]{:S(2)}, u32[]{:S(2)}) %collective-permute-start.1) | collective-permute-done | bytes 262176 | tf_op jit(solution)/shard_map/ppermute | solution.py:16
  17.2 0.9 collective-permute-start.2
  18.0 3.8 %collective-permute-start.4 = (bf16[64,4096]{1,0:T(8,128)(2,1)S(1)}, bf16[64,4096]{1,0:T(8,128)(2,1)S(1)}, u32[]{:S(2)}, u32[]{:S(2)}) collective-permute-start(bf16[64,4096]{1,0:T(8,128)(2,1)S(1)} %joined.4.refs_0_), channel_id=1, source_target_pairs={{0,4},{1,29},{2,6},{3,31},{4,8},{5,1},{6,10},{7,3},{8,12},{9,5},{1... | collective-permute-start | bytes 1572872 | tf_op jit(solution)/shard_map/ppermute | solution.py:16
  21.9 1.2 %collective-permute-start.3 = (bf16[64,4096]{1,0:T(8,128)(2,1)S(1)}, bf16[64,4096]{1,0:T(8,128)(2,1)S(1)}, u32[]{:S(2)}, u32[]{:S(2)}) collective-permute-start(bf16[64,4096]{1,0:T(8,128)(2,1)S(1)} %joined.5.refs_0_), channel_id=1, source_target_pairs={{0,4},{1,29},{2,6},{3,31},{4,8},{5,1},{6,10},{7,3},{8,12},{9,5},{1... | collective-permute-start | bytes 1572872 | tf_op jit(solution)/shard_map/ppermute | solution.py:16
  23.1 2.6 %score.7.refs_1_ = bf16[64,1024]{1,0:T(8,128)(2,1)S(1)} custom-call(bf16[64,4096]{1,0:T(8,128)(2,1)S(1)} %joined.5.refs_0_, bf16[1024,4096]{1,0:T(8,128)(2,1)S(1)} %bitcast.63), custom_call_target="tpu_custom_call" | custom-call | flops 536870912 | bytes 9043968 | tf_op jit(solution)/shard_map/score/pallas_call | solution.py:65
  25.8 2.2 %collective-permute-done.4.refs_0_ = bf16[64,4096]{1,0:T(8,128)(2,1)S(1)} collective-permute-done((bf16[64,4096]{1,0:T(8,128)(2,1)S(1)}, bf16[64,4096]{1,0:T(8,128)(2,1)S(1)}, u32[]{:S(2)}, u32[]{:S(2)}) %collective-permute-start.4) | collective-permute-done | bytes 524320 | tf_op jit(solution)/shard_map/ppermute | solution.py:16
  28.0 1.3 %collective-permute-start.5 = (bf16[64,4096]{1,0:T(8,128)(2,1)S(1)}, bf16[64,4096]{1,0:T(8,128)(2,1)S(1)}, u32[]{:S(2)}, u32[]{:S(2)}) collective-permute-start(bf16[64,4096]{1,0:T(8,128)(2,1)S(1)} %collective-permute-done.4.refs_0_), channel_id=1, source_target_pairs={{0,1},{1,0},{2,3},{3,2},{4,5},{5,4},{6,7},{7,6},{8,9},{9,8},{10,11... | collective-permute-start | bytes 1572872 | tf_op jit(solution)/shard_map/ppermute | solution.py:16
  29.3 1.8 %collective-permute-start.8 = (bf16[64,4096]{1,0:T(8,128)(2,1)S(1)}, bf16[64,4096]{1,0:T(8,128)(2,1)S(1)}, u32[]{:S(2)}, u32[]{:S(2)}) collective-permute-start(bf16[64,4096]{1,0:T(8,128)(2,1)S(1)} %collective-permute-done.4.refs_0_), channel_id=1, source_target_pairs={{0,4},{1,29},{2,6},{3,31},{4,8},{5,1},{6,10},{7,3},{8,12},{9,5},{1... | collective-permute-start | bytes 1572872 | tf_op jit(solution)/shard_map/ppermute | solution.py:16
  31.1 2.5 %collective-permute-done.3.refs_2_ = bf16[64,4096]{1,0:T(8,128)(2,1)S(1)} collective-permute-done((bf16[64,4096]{1,0:T(8,128)(2,1)S(1)}, bf16[64,4096]{1,0:T(8,128)(2,1)S(1)}, u32[]{:S(2)}, u32[]{:S(2)}) %collective-permute-start.3) | collective-permute-done | bytes 524320 | tf_op jit(solution)/shard_map/ppermute | solution.py:16
  33.6 1.3 %collective-permute-start.6 = (bf16[64,4096]{1,0:T(8,128)(2,1)S(1)}, bf16[64,4096]{1,0:T(8,128)(2,1)S(1)}, u32[]{:S(2)}, u32[]{:S(2)}) collective-permute-start(bf16[64,4096]{1,0:T(8,128)(2,1)S(1)} %collective-permute-done.3.refs_2_), channel_id=1, source_target_pairs={{0,1},{1,0},{2,3},{3,2},{4,5},{5,4},{6,7},{7,6},{8,9},{9,8},{10,11... | collective-permute-start | bytes 1572872 | tf_op jit(solution)/shard_map/ppermute | solution.py:16
  34.9 1.8 %collective-permute-start.7 = (bf16[64,4096]{1,0:T(8,128)(2,1)S(1)}, bf16[64,4096]{1,0:T(8,128)(2,1)S(1)}, u32[]{:S(2)}, u32[]{:S(2)}) collective-permute-start(bf16[64,4096]{1,0:T(8,128)(2,1)S(1)} %collective-permute-done.3.refs_2_), channel_id=1, source_target_pairs={{0,4},{1,29},{2,6},{3,31},{4,8},{5,1},{6,10},{7,3},{8,12},{9,5},{1... | collective-permute-start | bytes 1572872 | tf_op jit(solution)/shard_map/ppermute | solution.py:16
  36.7 2.5 %collective-permute-done.8.refs_0_ = bf16[64,4096]{1,0:T(8,128)(2,1)S(1)} collective-permute-done((bf16[64,4096]{1,0:T(8,128)(2,1)S(1)}, bf16[64,4096]{1,0:T(8,128)(2,1)S(1)}, u32[]{:S(2)}, u32[]{:S(2)}) %collective-permute-start.8) | collective-permute-done | bytes 524320 | tf_op jit(solution)/shard_map/ppermute | solution.py:16
  39.2 1.3 %collective-permute-start.9 = (bf16[64,4096]{1,0:T(8,128)(2,1)S(1)}, bf16[64,4096]{1,0:T(8,128)(2,1)S(1)}, u32[]{:S(2)}, u32[]{:S(2)}) collective-permute-start(bf16[64,4096]{1,0:T(8,128)(2,1)S(1)} %collective-permute-done.8.refs_0_), channel_id=1, source_target_pairs={{0,1},{1,0},{2,3},{3,2},{4,5},{5,4},{6,7},{7,6},{8,9},{9,8},{10,11... | collective-permute-start | bytes 1572872 | tf_op jit(solution)/shard_map/ppermute | solution.py:16
  40.5 1.8 %collective-permute-start.12 = (bf16[64,4096]{1,0:T(8,128)(2,1)S(1)}, bf16[64,4096]{1,0:T(8,128)(2,1)S(1)}, u32[]{:S(2)}, u32[]{:S(2)}) collective-permute-start(bf16[64,4096]{1,0:T(8,128)(2,1)S(1)} %collective-permute-done.8.refs_0_), channel_id=1, source_target_pairs={{0,4},{1,29},{2,6},{3,31},{4,8},{5,1},{6,10},{7,3},{8,12},{9,5},{1... | collective-permute-start | bytes 1572872 | tf_op jit(solution)/shard_map/ppermute | solution.py:16
  42.4 2.5 %score.8.refs_2_ = bf16[256,1024]{1,0:T(8,128)(2,1)S(1)} custom-call(bf16[64,4096]{1,0:T(8,128)(2,1)S(1)} %collective-permute-done.4.refs_0_, bf16[64,4096]{1,0:T(8,128)(2,1)S(1)} %collective-permute-done.5.refs_1_, bf16[64,4096]{1,0:T(8,128)(2,1)S(1)} %collective-permute-done.3.refs_2_, bf16[64,4096]{1,0:T(8,128)(2,1)S(1)} %collective-permute-done.6.refs_3_, ...), custom_call_target="tpu_custom_call" | custom-call | flops 2147483648 | bytes 11010048 | tf_op jit(solution)/shard_map/score/pallas_call | solution.py:65
  44.8 0.0 collective-permute-done.7.refs_2_
  44.8 1.3 %collective-permute-start.10 = (bf16[64,4096]{1,0:T(8,128)(2,1)S(1)}, bf16[64,4096]{1,0:T(8,128)(2,1)S(1)}, u32[]{:S(2)}, u32[]{:S(2)}) collective-permute-start(bf16[64,4096]{1,0:T(8,128)(2,1)S(1)} %collective-permute-done.7.refs_2_), channel_id=1, source_target_pairs={{0,1},{1,0},{2,3},{3,2},{4,5},{5,4},{6,7},{7,6},{8,9},{9,8},{10,11... | collective-permute-start | bytes 1572872 | tf_op jit(solution)/shard_map/ppermute | solution.py:16
  46.2 1.8 %collective-permute-start.11 = (bf16[64,4096]{1,0:T(8,128)(2,1)S(1)}, bf16[64,4096]{1,0:T(8,128)(2,1)S(1)}, u32[]{:S(2)}, u32[]{:S(2)}) collective-permute-start(bf16[64,4096]{1,0:T(8,128)(2,1)S(1)} %collective-permute-done.7.refs_2_), channel_id=1, source_target_pairs={{0,4},{1,29},{2,6},{3,31},{4,8},{5,1},{6,10},{7,3},{8,12},{9,5},{1... | collective-permute-start | bytes 1572872 | tf_op jit(solution)/shard_map/ppermute | solution.py:16
  48.0 2.5 %collective-permute-done.12.refs_0_ = bf16[64,4096]{1,0:T(8,128)(2,1)S(1)} collective-permute-done((bf16[64,4096]{1,0:T(8,128)(2,1)S(1)}, bf16[64,4096]{1,0:T(8,128)(2,1)S(1)}, u32[]{:S(2)}, u32[]{:S(2)}) %collective-permute-start.12) | collective-permute-done | bytes 524320 | tf_op jit(solution)/shard_map/ppermute | solution.py:16
  50.5 1.3 %collective-permute-start.13 = (bf16[64,4096]{1,0:T(8,128)(2,1)S(1)}, bf16[64,4096]{1,0:T(8,128)(2,1)S(1)}, u32[]{:S(2)}, u32[]{:S(2)}) collective-permute-start(bf16[64,4096]{1,0:T(8,128)(2,1)S(1)} %collective-permute-done.12.refs_0_), channel_id=1, source_target_pairs={{0,1},{1,0},{2,3},{3,2},{4,5},{5,4},{6,7},{7,6},{8,9},{9,8},{10,11... | collective-permute-start | bytes 1572872 | tf_op jit(solution)/shard_map/ppermute | solution.py:16
  51.8 2.4 %score.9.refs_3_ = bf16[256,1024]{1,0:T(8,128)(2,1)S(1)} custom-call(bf16[64,4096]{1,0:T(8,128)(2,1)S(1)} %collective-permute-done.8.refs_0_, bf16[64,4096]{1,0:T(8,128)(2,1)S(1)} %collective-permute-done.9.refs_1_, bf16[64,4096]{1,0:T(8,128)(2,1)S(1)} %collective-permute-done.7.refs_2_, bf16[64,4096]{1,0:T(8,128)(2,1)S(1)} %collective-permute-done.10.refs_3_, ...), custom_call_target="tpu_custom_call" | custom-call | flops 2147483648 | bytes 11010048 | tf_op jit(solution)/shard_map/score/pallas_call | solution.py:65
  54.2 1.8 %collective-permute-done.11.refs_2_.refs_0_ = bf16[64,4096]{1,0:T(8,128)(2,1)S(1)} collective-permute-done((bf16[64,4096]{1,0:T(8,128)(2,1)S(1)}, bf16[64,4096]{1,0:T(8,128)(2,1)S(1)}, u32[]{:S(2)}, u32[]{:S(2)}) %collective-permute-start.11) | collective-permute-done | bytes 524320 | tf_op jit(solution)/shard_map/ppermute | solution.py:16
  56.1 1.3 %collective-permute-start.14 = (bf16[64,4096]{1,0:T(8,128)(2,1)S(1)}, bf16[64,4096]{1,0:T(8,128)(2,1)S(1)}, u32[]{:S(2)}, u32[]{:S(2)}) collective-permute-start(bf16[64,4096]{1,0:T(8,128)(2,1)S(1)} %collective-permute-done.11.refs_2_.refs_0_), channel_id=1, source_target_pairs={{0,1},{1,0},{2,3},{3,2},{4,5},{5,4},{6,7},{7,6},{8,9},{9,8},{10,11... | collective-permute-start | bytes 1572872 | tf_op jit(solution)/shard_map/ppermute | solution.py:16
  57.4 1.9 %collective-permute-start.16 = (bf16[32,4096]{1,0:T(8,128)(2,1)S(1)}, bf16[32,4096]{1,0:T(8,128)(2,1)S(1)}, u32[]{:S(2)}, u32[]{:S(2)}) collective-permute-start(bf16[32,4096]{1,0:T(8,128)(2,1)S(1)} %joined.7), channel_id=1, source_target_pairs={{0,4},{1,29},{2,6},{3,31},{4,8},{5,1},{6,10},{7,3},{8,12},{9,5},{1... | collective-permute-start | bytes 786440 | tf_op jit(solution)/shard_map/ppermute | solution.py:16
  59.3 0.7 collective-permute-start.15
  60.1 2.9 %collective-permute-done.16.refs_0_ = bf16[32,4096]{1,0:T(8,128)(2,1)S(1)} collective-permute-done((bf16[32,4096]{1,0:T(8,128)(2,1)S(1)}, bf16[32,4096]{1,0:T(8,128)(2,1)S(1)}, u32[]{:S(2)}, u32[]{:S(2)}) %collective-permute-start.16) | collective-permute-done | bytes 262176 | tf_op jit(solution)/shard_map/ppermute | solution.py:16
  63.0 2.1 %collective-permute-start.17 = (bf16[32,4096]{1,0:T(8,128)(2,1)S(1)}, bf16[32,4096]{1,0:T(8,128)(2,1)S(1)}, u32[]{:S(2)}, u32[]{:S(2)}) collective-permute-start(bf16[32,4096]{1,0:T(8,128)(2,1)S(1)} %collective-permute-done.16.refs_0_), channel_id=1, source_target_pairs={{0,1},{1,0},{2,3},{3,2},{4,5},{5,4},{6,7},{7,6},{8,9},{9,8},{10,11... | collective-permute-start | bytes 786440 | tf_op jit(solution)/shard_map/ppermute | solution.py:16
  65.1 2.4 %score.10.refs_4_ = bf16[256,1024]{1,0:T(8,128)(2,1)S(1)} custom-call(bf16[64,4096]{1,0:T(8,128)(2,1)S(1)} %collective-permute-done.12.refs_0_, bf16[64,4096]{1,0:T(8,128)(2,1)S(1)} %collective-permute-done.13.refs_1_, bf16[64,4096]{1,0:T(8,128)(2,1)S(1)} %collective-permute-done.11.refs_2_.refs_0_, bf16[64,4096]{1,0:T(8,128)(2,1)S(1)} %collective-permute-done.14.refs_3_, ...), custom_call_target="tpu_custom_call" | custom-call | flops 2147483648 | bytes 11010048 | tf_op jit(solution)/shard_map/score/pallas_call | solution.py:65
  67.5 0.0 collective-permute-done.15.refs_2_
  67.5 0.3 collective-permute-start.18
  67.9 1.3 %collective-permute-done.18.refs_3_ = bf16[32,4096]{1,0:T(8,128)(2,1)S(1)} collective-permute-done((bf16[32,4096]{1,0:T(8,128)(2,1)S(1)}, bf16[32,4096]{1,0:T(8,128)(2,1)S(1)}, u32[]{:S(2)}, u32[]{:S(2)}) %collective-permute-start.18) | collective-permute-done | bytes 262176 | tf_op jit(solution)/shard_map/ppermute | solution.py:16
  69.2 2.9 %score.11.refs_5_ = bf16[128,1024]{1,0:T(8,128)(2,1)S(1)} custom-call(bf16[32,4096]{1,0:T(8,128)(2,1)S(1)} %collective-permute-done.16.refs_0_, bf16[32,4096]{1,0:T(8,128)(2,1)S(1)} %collective-permute-done.17.refs_1_, bf16[32,4096]{1,0:T(8,128)(2,1)S(1)} %collective-permute-done.15.refs_2_, bf16[32,4096]{1,0:T(8,128)(2,1)S(1)} %collective-permute-done.18.refs_3_, ...), custom_call_target="tpu_custom_call" | custom-call | flops 1073741824 | bytes 9699328 | tf_op jit(solution)/shard_map/score/pallas_call | solution.py:65
  72.0 0.7 place.1
  72.7 31.9 %all_to_all.5.in_ref = bf16[8,128,1024]{2,1,0:T(8,128)(2,1)S(1)} all-to-all(bf16[8,128,1024]{2,1,0:T(8,128)(2,1)S(1)} %bitcast.68), channel_id=1, replica_groups=mesh['group'=8,'blk'=32] {'group'}, dimensions={0} | all-to-all | bytes 4194304 | tf_op jit(solution)/shard_map/all_to_all | solution.py:184
  104.6 1.9 %total.1 = f32[1024,128]{1,0:T(8,128)} custom-call(bf16[8,128,1024]{2,1,0:T(8,128)(2,1)S(1)} %all_to_all.5.in_ref), custom_call_target="tpu_custom_call" | custom-call | tf_op jit(solution)/shard_map/total/pallas_call | solution.py:110
  (19 shorter events, 0.1 us)
Async XLA Ops:
  0.0 1.5 %copy-start = (f32[1,64,64]{2,1,0:T(8,128)S(1)}, f32[1,64,64]{2,1,0:T(8,128)}, u32[]{:S(2)}) copy-start(f32[1,64,64]{2,1,0:T(8,128)} %param.7) | copy-start | bytes 49156
  0.0 2.2 %copy-start.3 = (f32[1,64,64]{2,1,0:T(8,128)S(1)}, f32[1,64,64]{2,1,0:T(8,128)}, u32[]{:S(2)}) copy-start(f32[1,64,64]{2,1,0:T(8,128)} %param.8) | copy-start | bytes 49156
  1.5 7.6 %copy-start.4 = (s32[32]{0:T(128)S(1)}, s32[32]{0:T(128)}, u32[]{:S(2)}) copy-start(s32[32]{0:T(128)} %param.9) | copy-start | bytes 388
  4.5 4.8 %collective-permute-start = (bf16[32,4096]{1,0:T(8,128)(2,1)S(1)}, bf16[32,4096]{1,0:T(8,128)(2,1)S(1)}, u32[]{:S(2)}, u32[]{:S(2)}) collective-permute-start(bf16[32,4096]{1,0:T(8,128)(2,1)S(1)} %convert_element_type.16.refs_0_), channel_id=1, source_target_pairs={{0,1},{1,0},{2,3},{3,2},{4,5},{5,4},{6,7},{7,6},{8,9},{9,8},{10,11... | collective-permute-start | bytes 786440 | tf_op jit(solution)/shard_map/ppermute | solution.py:16
  7.8 9.4 %collective-permute-start.1 = (bf16[32,4096]{1,0:T(8,128)(2,1)S(1)}, bf16[32,4096]{1,0:T(8,128)(2,1)S(1)}, u32[]{:S(2)}, u32[]{:S(2)}) collective-permute-start(bf16[32,4096]{1,0:T(8,128)(2,1)S(1)} %convert_element_type.16.refs_0_), channel_id=1, source_target_pairs={{0,2},{1,3},{2,0},{3,1},{4,6},{5,7},{6,4},{7,5},{8,10},{9,11},{10,... | collective-permute-start | bytes 786440 | tf_op jit(solution)/shard_map/ppermute | solution.py:16
  9.3 3.4 %copy-start.1 = (bf16[1024,1,4096]{2,0,1:T(8,128)(2,1)S(1)}, bf16[1024,1,4096]{2,0,1:T(8,128)(2,1)}, u32[]{:S(2)}) copy-start(bf16[1024,1,4096]{2,0,1:T(8,128)(2,1)} %param.5) | copy-start | bytes 25165828
  12.7 10.4 %copy-start.2 = (bf16[1024,1,4096]{2,0,1:T(8,128)(2,1)S(1)}, bf16[1024,1,4096]{2,0,1:T(8,128)(2,1)}, u32[]{:S(2)}) copy-start(bf16[1024,1,4096]{2,0,1:T(8,128)(2,1)} %param.5) | copy-start | bytes 25165828
  17.2 4.7 %collective-permute-start.2 = (bf16[32,4096]{1,0:T(8,128)(2,1)S(1)}, bf16[32,4096]{1,0:T(8,128)(2,1)S(1)}, u32[]{:S(2)}, u32[]{:S(2)}) collective-permute-start(bf16[32,4096]{1,0:T(8,128)(2,1)S(1)} %collective-permute-done.1.refs_0_), channel_id=1, source_target_pairs={{0,1},{1,0},{2,3},{3,2},{4,5},{5,4},{6,7},{7,6},{8,9},{9,8},{10,11... | collective-permute-start | bytes 786440 | tf_op jit(solution)/shard_map/ppermute | solution.py:16
  18.0 10.0 %collective-permute-start.4 = (bf16[64,4096]{1,0:T(8,128)(2,1)S(1)}, bf16[64,4096]{1,0:T(8,128)(2,1)S(1)}, u32[]{:S(2)}, u32[]{:S(2)}) collective-permute-start(bf16[64,4096]{1,0:T(8,128)(2,1)S(1)} %joined.4.refs_0_), channel_id=1, source_target_pairs={{0,4},{1,29},{2,6},{3,31},{4,8},{5,1},{6,10},{7,3},{8,12},{9,5},{1... | collective-permute-start | bytes 1572872 | tf_op jit(solution)/shard_map/ppermute | solution.py:16
  21.9 11.7 %collective-permute-start.3 = (bf16[64,4096]{1,0:T(8,128)(2,1)S(1)}, bf16[64,4096]{1,0:T(8,128)(2,1)S(1)}, u32[]{:S(2)}, u32[]{:S(2)}) collective-permute-start(bf16[64,4096]{1,0:T(8,128)(2,1)S(1)} %joined.5.refs_0_), channel_id=1, source_target_pairs={{0,4},{1,29},{2,6},{3,31},{4,8},{5,1},{6,10},{7,3},{8,12},{9,5},{1... | collective-permute-start | bytes 1572872 | tf_op jit(solution)/shard_map/ppermute | solution.py:16
  28.0 14.4 %collective-permute-start.5 = (bf16[64,4096]{1,0:T(8,128)(2,1)S(1)}, bf16[64,4096]{1,0:T(8,128)(2,1)S(1)}, u32[]{:S(2)}, u32[]{:S(2)}) collective-permute-start(bf16[64,4096]{1,0:T(8,128)(2,1)S(1)} %collective-permute-done.4.refs_0_), channel_id=1, source_target_pairs={{0,1},{1,0},{2,3},{3,2},{4,5},{5,4},{6,7},{7,6},{8,9},{9,8},{10,11... | collective-permute-start | bytes 1572872 | tf_op jit(solution)/shard_map/ppermute | solution.py:16
  29.3 9.9 %collective-permute-start.8 = (bf16[64,4096]{1,0:T(8,128)(2,1)S(1)}, bf16[64,4096]{1,0:T(8,128)(2,1)S(1)}, u32[]{:S(2)}, u32[]{:S(2)}) collective-permute-start(bf16[64,4096]{1,0:T(8,128)(2,1)S(1)} %collective-permute-done.4.refs_0_), channel_id=1, source_target_pairs={{0,4},{1,29},{2,6},{3,31},{4,8},{5,1},{6,10},{7,3},{8,12},{9,5},{1... | collective-permute-start | bytes 1572872 | tf_op jit(solution)/shard_map/ppermute | solution.py:16
  33.6 8.7 %collective-permute-start.6 = (bf16[64,4096]{1,0:T(8,128)(2,1)S(1)}, bf16[64,4096]{1,0:T(8,128)(2,1)S(1)}, u32[]{:S(2)}, u32[]{:S(2)}) collective-permute-start(bf16[64,4096]{1,0:T(8,128)(2,1)S(1)} %collective-permute-done.3.refs_2_), channel_id=1, source_target_pairs={{0,1},{1,0},{2,3},{3,2},{4,5},{5,4},{6,7},{7,6},{8,9},{9,8},{10,11... | collective-permute-start | bytes 1572872 | tf_op jit(solution)/shard_map/ppermute | solution.py:16
  34.9 9.9 %collective-permute-start.7 = (bf16[64,4096]{1,0:T(8,128)(2,1)S(1)}, bf16[64,4096]{1,0:T(8,128)(2,1)S(1)}, u32[]{:S(2)}, u32[]{:S(2)}) collective-permute-start(bf16[64,4096]{1,0:T(8,128)(2,1)S(1)} %collective-permute-done.3.refs_2_), channel_id=1, source_target_pairs={{0,4},{1,29},{2,6},{3,31},{4,8},{5,1},{6,10},{7,3},{8,12},{9,5},{1... | collective-permute-start | bytes 1572872 | tf_op jit(solution)/shard_map/ppermute | solution.py:16
  39.2 12.6 %collective-permute-start.9 = (bf16[64,4096]{1,0:T(8,128)(2,1)S(1)}, bf16[64,4096]{1,0:T(8,128)(2,1)S(1)}, u32[]{:S(2)}, u32[]{:S(2)}) collective-permute-start(bf16[64,4096]{1,0:T(8,128)(2,1)S(1)} %collective-permute-done.8.refs_0_), channel_id=1, source_target_pairs={{0,1},{1,0},{2,3},{3,2},{4,5},{5,4},{6,7},{7,6},{8,9},{9,8},{10,11... | collective-permute-start | bytes 1572872 | tf_op jit(solution)/shard_map/ppermute | solution.py:16
  40.5 9.9 %collective-permute-start.12 = (bf16[64,4096]{1,0:T(8,128)(2,1)S(1)}, bf16[64,4096]{1,0:T(8,128)(2,1)S(1)}, u32[]{:S(2)}, u32[]{:S(2)}) collective-permute-start(bf16[64,4096]{1,0:T(8,128)(2,1)S(1)} %collective-permute-done.8.refs_0_), channel_id=1, source_target_pairs={{0,4},{1,29},{2,6},{3,31},{4,8},{5,1},{6,10},{7,3},{8,12},{9,5},{1... | collective-permute-start | bytes 1572872 | tf_op jit(solution)/shard_map/ppermute | solution.py:16
  44.8 6.9 %collective-permute-start.10 = (bf16[64,4096]{1,0:T(8,128)(2,1)S(1)}, bf16[64,4096]{1,0:T(8,128)(2,1)S(1)}, u32[]{:S(2)}, u32[]{:S(2)}) collective-permute-start(bf16[64,4096]{1,0:T(8,128)(2,1)S(1)} %collective-permute-done.7.refs_2_), channel_id=1, source_target_pairs={{0,1},{1,0},{2,3},{3,2},{4,5},{5,4},{6,7},{7,6},{8,9},{9,8},{10,11... | collective-permute-start | bytes 1572872 | tf_op jit(solution)/shard_map/ppermute | solution.py:16
  46.2 9.9 %collective-permute-start.11 = (bf16[64,4096]{1,0:T(8,128)(2,1)S(1)}, bf16[64,4096]{1,0:T(8,128)(2,1)S(1)}, u32[]{:S(2)}, u32[]{:S(2)}) collective-permute-start(bf16[64,4096]{1,0:T(8,128)(2,1)S(1)} %collective-permute-done.7.refs_2_), channel_id=1, source_target_pairs={{0,4},{1,29},{2,6},{3,31},{4,8},{5,1},{6,10},{7,3},{8,12},{9,5},{1... | collective-permute-start | bytes 1572872 | tf_op jit(solution)/shard_map/ppermute | solution.py:16
  50.5 14.6 %collective-permute-start.13 = (bf16[64,4096]{1,0:T(8,128)(2,1)S(1)}, bf16[64,4096]{1,0:T(8,128)(2,1)S(1)}, u32[]{:S(2)}, u32[]{:S(2)}) collective-permute-start(bf16[64,4096]{1,0:T(8,128)(2,1)S(1)} %collective-permute-done.12.refs_0_), channel_id=1, source_target_pairs={{0,1},{1,0},{2,3},{3,2},{4,5},{5,4},{6,7},{7,6},{8,9},{9,8},{10,11... | collective-permute-start | bytes 1572872 | tf_op jit(solution)/shard_map/ppermute | solution.py:16
  56.1 9.0 %collective-permute-start.14 = (bf16[64,4096]{1,0:T(8,128)(2,1)S(1)}, bf16[64,4096]{1,0:T(8,128)(2,1)S(1)}, u32[]{:S(2)}, u32[]{:S(2)}) collective-permute-start(bf16[64,4096]{1,0:T(8,128)(2,1)S(1)} %collective-permute-done.11.refs_2_.refs_0_), channel_id=1, source_target_pairs={{0,1},{1,0},{2,3},{3,2},{4,5},{5,4},{6,7},{7,6},{8,9},{9,8},{10,11... | collective-permute-start | bytes 1572872 | tf_op jit(solution)/shard_map/ppermute | solution.py:16
  57.4 5.6 %collective-permute-start.16 = (bf16[32,4096]{1,0:T(8,128)(2,1)S(1)}, bf16[32,4096]{1,0:T(8,128)(2,1)S(1)}, u32[]{:S(2)}, u32[]{:S(2)}) collective-permute-start(bf16[32,4096]{1,0:T(8,128)(2,1)S(1)} %joined.7), channel_id=1, source_target_pairs={{0,4},{1,29},{2,6},{3,31},{4,8},{5,1},{6,10},{7,3},{8,12},{9,5},{1... | collective-permute-start | bytes 786440 | tf_op jit(solution)/shard_map/ppermute | solution.py:16
  59.3 8.2 %collective-permute-start.15 = (bf16[32,4096]{1,0:T(8,128)(2,1)S(1)}, bf16[32,4096]{1,0:T(8,128)(2,1)S(1)}, u32[]{:S(2)}, u32[]{:S(2)}) collective-permute-start(bf16[32,4096]{1,0:T(8,128)(2,1)S(1)} %joined.6), channel_id=1, source_target_pairs={{0,4},{1,29},{2,6},{3,31},{4,8},{5,1},{6,10},{7,3},{8,12},{9,5},{1... | collective-permute-start | bytes 786440 | tf_op jit(solution)/shard_map/ppermute | solution.py:16
  63.0 4.9 %collective-permute-start.17 = (bf16[32,4096]{1,0:T(8,128)(2,1)S(1)}, bf16[32,4096]{1,0:T(8,128)(2,1)S(1)}, u32[]{:S(2)}, u32[]{:S(2)}) collective-permute-start(bf16[32,4096]{1,0:T(8,128)(2,1)S(1)} %collective-permute-done.16.refs_0_), channel_id=1, source_target_pairs={{0,1},{1,0},{2,3},{3,2},{4,5},{5,4},{6,7},{7,6},{8,9},{9,8},{10,11... | collective-permute-start | bytes 786440 | tf_op jit(solution)/shard_map/ppermute | solution.py:16
  67.5 1.6 %collective-permute-start.18 = (bf16[32,4096]{1,0:T(8,128)(2,1)S(1)}, bf16[32,4096]{1,0:T(8,128)(2,1)S(1)}, u32[]{:S(2)}, u32[]{:S(2)}) collective-permute-start(bf16[32,4096]{1,0:T(8,128)(2,1)S(1)} %collective-permute-done.15.refs_2_), channel_id=1, source_target_pairs={{0,1},{1,0},{2,3},{3,2},{4,5},{5,4},{6,7},{7,6},{8,9},{9,8},{10,11... | collective-permute-start | bytes 786440 | tf_op jit(solution)/shard_map/ppermute | solution.py:16

commit v4 on v3

--- a/solution.py
+++ b/solution.py
@@ -9,6 +9,7 @@
 
 NZ = 8
 PANEL = 32
+LANES = 128
 CBLK = 256
 
 
@@ -20,12 +21,89 @@
     return _route(x, lambda z, rest: ((z + (1 if rest % 2 == 0 else -1)) % NZ) * 4 + rest)
 
 
+def _across(x):
+    return _route(x, lambda z, rest: ((z + (1 if rest % 2 == 0 else -1)) % NZ) * 4 + (rest ^ 2))
+
+
 def _swap_core(x):
     return _route(x, lambda z, rest: z * 4 + (rest ^ 1))
 
 
 def _swap_y(x):
     return _route(x, lambda z, rest: z * 4 + (rest ^ 2))
+
+
+def _precond_kernel(a_ref, b_ref, q_ref, o_ref, one_ref, two_ref, left_ref):
+    width = q_ref.shape[0]
+    tiles = q_ref.shape[1] // LANES
+    half = LANES // 2
+    zero = jnp.zeros((half, half), jnp.float32)
+    b = b_ref[...]
+    right = jnp.concatenate(
+        [
+            jnp.concatenate([b, zero, zero, b], axis=1),
+            jnp.concatenate([zero, b, b, zero], axis=1),
+        ],
+        axis=0,
+    )
+    rows = jnp.concatenate([q_ref[:, t * LANES : (t + 1) * LANES] for t in range(tiles)], axis=0)
+    done = None
+    for _ in range(3):
+        term = right.astype(jnp.bfloat16)
+        right = right - term.astype(jnp.float32)
+        part = jnp.dot(rows, term, preferred_element_type=jnp.float32)
+        done = part if done is None else done + part
+    one_ref[...] = done[:, :LANES]
+    two_ref[...] = done[:, LANES:]
+    row = lax.broadcasted_iota(jnp.int32, (half, half), 0)
+    col = lax.broadcasted_iota(jnp.int32, (half, half), 1)
+    unit = jnp.where(col < half // 2, 2 * col, 2 * (col - half // 2) + 1)
+    pick = jnp.where(row == unit, 1.0, 0.0).astype(jnp.float32)
+    left_ref[...] = jnp.dot(
+        a_ref[...], pick, precision=lax.Precision.HIGHEST, preferred_element_type=jnp.float32
+    )
+    even = left_ref[pl.ds(0, half // 2, stride=2), :]
+    odd = left_ref[pl.ds(1, half // 2, stride=2), :]
+    odd = jnp.concatenate([odd[:, half // 2 :], odd[:, : half // 2]], axis=1)
+    left = jnp.concatenate([even, odd], axis=0)
+    lanes = lax.broadcasted_iota(jnp.int32, (tiles, LANES), 1)
+    chunk = 8
+    for q0 in range(0, width, chunk):
+        columns = [
+            jnp.concatenate(
+                [one_ref[pl.ds(q, tiles, stride=width), :], two_ref[pl.ds(q, tiles, stride=width), :]], axis=0
+            )
+            for q in range(q0, q0 + chunk)
+        ]
+        both = jnp.dot(
+            left,
+            jnp.concatenate(columns, axis=1),
+            precision=lax.Precision.HIGHEST,
+            preferred_element_type=jnp.float32,
+        )
+        for i in range(chunk):
+            block = both[:, i * LANES : (i + 1) * LANES]
+            one_ref[pl.ds(q0 + i, tiles, stride=width), :] = jnp.where(lanes < half, block[:tiles], block[tiles:])
+    for t in range(tiles):
+        o_ref[:, t * LANES : (t + 1) * LANES] = one_ref[t * width : (t + 1) * width, :].astype(o_ref.dtype)
+
+
+def _precond(out_factor, in_factor, queries):
+    width, feats = queries.shape
+    rows = width * feats // LANES
+    return pl.pallas_call(
+        _precond_kernel,
+        in_specs=[pl.BlockSpec(memory_space=pltpu.VMEM) for _ in range(3)],
+        out_specs=pl.BlockSpec(memory_space=pltpu.VMEM),
+        out_shape=jax.ShapeDtypeStruct((width, feats), jnp.bfloat16),
+        scratch_shapes=[
+            pltpu.VMEM((rows, LANES), jnp.float32),
+            pltpu.VMEM((rows, LANES), jnp.float32),
+            pltpu.VMEM(out_factor.shape, jnp.float32),
+        ],
+        compiler_params=pltpu.CompilerParams(vmem_limit_bytes=12 << 20),
+        name="precond",
+    )(out_factor, in_factor, queries)
 
 
 def _joined_kernel(*refs):
@@ -121,14 +199,9 @@
 def body(candidates, queries, out_factor, in_factor, panel_order):
     cand_rows, layer_count, features = candidates.shape
     width = queries.shape[0]
-    out_units = out_factor.shape[1]
-    in_units = in_factor.shape[1]
     groups = lax.axis_size("group")
     scale = 1.0 / (features * layer_count * groups) ** 0.5
-    grads = queries.astype(jnp.float32).reshape(width, layer_count, out_units, in_units)
-    left = jnp.einsum("lab,qlbc->qlac", out_factor, grads, precision=lax.Precision.HIGHEST)
-    precond = jnp.einsum("qlac,lcd->qlad", left, in_factor, precision=lax.Precision.HIGHEST)
-    panel = precond.reshape(width, layer_count * features).astype(jnp.bfloat16)
+    panel = _precond(out_factor[0], in_factor[0], queries.reshape(width, layer_count * features))
     flat = candidates.reshape(cand_rows, layer_count * features)
 
     flat = pltpu.with_memory_space_constraint(flat, pltpu.VMEM)
@@ -148,12 +221,13 @@
         sources.append(((z + dz) % NZ) * 4 + (rest ^ (2 * dy)))
 
     note(0, 0)
-    note(0, 1)
     for s in range(1, NZ // 2):
         note(-s * up, 0)
         note_far(s * up, 0)
         note(-s * up, 1)
         note_far(s * up, 1)
+        if s == 2:
+            note(0, 1)
     for dy in (0, 1):
         sources.append(((z + NZ // 2) % NZ) * 4 + (rest ^ (2 * dy)))
         sources.append(((z + NZ // 2) % NZ) * 4 + (rest ^ (2 * dy) ^ 1))
@@ -163,23 +237,32 @@
 
     steps = []
 
-    def after(step, x):
-        steps[step], x = lax.optimization_barrier((steps[step], x))
-        return x
-
-    across = _swap_y(panel)
     near = _joined(panel, _swap_core(panel))
-    steps.append(_score([near], flat, scale))
-    steps[0], where, across = lax.optimization_barrier((steps[0], where, across))
-    far = _joined(across, _swap_core(across))
-    steps.append(_score([far], flat, scale))
-    for s in range(1, NZ // 2):
-        near, far = _along(near), _along(far)
-        far = after(s, far)
-        steps.append(_score([near, _swap_core(near), far, _swap_core(far)], flat, scale))
-    near, far = _along(_joined(near)), _along(_joined(far))
-    far = after(NZ // 2, far)
-    steps.append(_score([near, _swap_core(near), far, _swap_core(far)], flat, scale))
+    near, where = lax.optimization_barrier((near, where))
+    pieces = [near]
+    start = near
+    near, far = _along(start), _across(start)
+    more = []
+    for s in range(1, NZ // 2 + 1):
+        if s == NZ // 2 - 1:
+            cut = _joined(near)
+            near, cut, pieces[0] = lax.optimization_barrier((near, cut, pieces[0]))
+        else:
+            near, pieces[0] = lax.optimization_barrier((near, pieces[0]))
+        steps.append(_score(pieces, flat, scale))
+        if s == 1:
+            steps[0], far, start = lax.optimization_barrier((steps[0], far, start))
+            more = [_swap_y(start)]
+        else:
+            steps[-1], far = lax.optimization_barrier((steps[-1], far))
+        pieces = [near, _swap_core(near), far, _swap_core(far)]
+        if s == 2:
+            pieces += more
+        if s < NZ // 2 - 1:
+            near, far = _along(near), _along(far)
+        elif s == NZ // 2 - 1:
+            near, far = _along(cut), _along(_joined(far))
+    steps.append(_score(pieces, flat, scale))
     buffer = _place(steps, where).reshape(groups, -1, cand_rows)
     parts = lax.all_to_all(buffer, "group", split_axis=0, concat_axis=0, tiled=True)
     return _total(parts)

time: 107 us -> 105 us (0.981)
  matrix products: 2.47 us -> 0 us
  waiting for transfers between devices: 17.6 us -> 15.7 us
  starting transfers between devices: 30.6 us -> 32.1 us
    pallas_call x0 -> x1, Pallas kernels: none -> 2.67 us  [_precond(): pl.pallas_call(_precond_kernel, in_specs=[pl.BlockSpec(memory_space=pltpu...]
    dot_general x2 -> x0, matrix products: 2.47 us -> none  [the longest x1 1.8 us: body(): jnp.einsum('qlac,lcd->qlad', left, in_factor, precision=lax.Precision.HIG...]
    unnamed x10, local copies, waits for them, and re-layouts: 3.39 us -> 5.85 us
    pallas_call x6 -> x5, Pallas kernels: 15.5 us -> 13.3 us  [_score(): pl.pallas_call(functools.partial(_score_kernel, scale, len(pieces)), in_s...]
    ppermute x19 -> x18, waiting for transfers between devices: 17.6 us -> 15.7 us  [_route(): lax.ppermute(x, 'blk', [(i, target(*divmod(i, 4))) for i in range(NZ * 4)])]
    ppermute x19 -> x18, starting transfers between devices: 30.6 us -> 32.1 us  [_route(): lax.ppermute(x, 'blk', [(i, target(*divmod(i, 4))) for i in range(NZ * 4)])]
    reshape x1 -> x0, local copies, waits for them, and re-layouts: 1.48 us -> none
  transfers between devices with their start and end apart: 19 -> 18, of which waited for: 8 -> 7; matrix products, arithmetic and copies ran while one was open for 0% -> 1% of each run, Pallas kernels for 12% -> 10%
where the time goes in v4:
time: 105 us; the launch traced here: 104 us
  starting transfers between devices  32.1 us (31%)
  blocking collectives  31 us (30%)
  Pallas kernels  18.7 us (18%)
  waiting for transfers between devices  15.7 us (15%)
  local copies, waits for them, and re-layouts  5.96 us (6%)
    ppermute x18, starting transfers between devices, _route(): lax.ppermute(x, 'blk', [(i, target(*divmod(i, 4))) for i in range(NZ * 4)])  32.1 us
    all_to_all x1, blocking collectives, body(): lax.all_to_all(buffer, 'group', split_axis=0, concat_axis=0, tiled=True)  31 us
    ppermute x18, waiting for transfers between devices, _route(): lax.ppermute(x, 'blk', [(i, target(*divmod(i, 4))) for i in range(NZ * 4)])  15.7 us
    pallas_call x5, Pallas kernels, _score(): pl.pallas_call(functools.partial(_score_kernel, scale, len(pieces)), in_s...  13.3 us
    unnamed x10, local copies, waits for them, and re-layouts  5.85 us
    pallas_call x1, Pallas kernels, _precond(): pl.pallas_call(_precond_kernel, in_specs=[pl.BlockSpec(memory_space=pltpu...  2.67 us
  transfers between devices with their start and end apart: 18, of which 7 were waited for; matrix products, arithmetic and copies ran while one was open for 1% of the time, Pallas kernels for 10%

profile of v4, /device:TPU:1, one launch (start us, length us, event | category | flops | bytes accessed | tf_op | source)
XLA Modules:
  0.0 104.4 jit_solution(2865643451667433040)
XLA Ops:
  0.0 0.9 copy-done.2
  1.0 0.8 copy-done.3
  1.7 0.8 copy-done.4
  2.5 2.7 %precond.1.refs_0_ = bf16[32,4096]{1,0:T(8,128)(2,1)S(1)} custom-call(f32[64,64]{1,0:T(8,128)S(1)} %bitcast.44, f32[64,64]{1,0:T(8,128)S(1)} %bitcast.45, bf16[32,4096]{1,0:T(8,128)(2,1)S(1)} %bitcast.43), custom_call_target="tpu_custom_call" | custom-call | tf_op jit(solution)/shard_map/precond/pallas_call | solution.py:94
  5.1 3.3 %collective-permute-start = (bf16[32,4096]{1,0:T(8,128)(2,1)S(1)}, bf16[32,4096]{1,0:T(8,128)(2,1)S(1)}, u32[]{:S(2)}, u32[]{:S(2)}) collective-permute-start(bf16[32,4096]{1,0:T(8,128)(2,1)S(1)} %precond.1.refs_0_), channel_id=1, source_target_pairs={{0,1},{1,0},{2,3},{3,2},{4,5},{5,4},{6,7},{7,6},{8,9},{9,8},{10,11... | collective-permute-start | bytes 786440 | tf_op jit(solution)/shard_map/ppermute | solution.py:17
  8.5 0.1 stack.131
  8.6 0.8 select_reduce_fusion.where_ref
  9.4 0.2 collective-permute-done.refs_1_
  9.7 3.9 %collective-permute-start.1 = (bf16[64,4096]{1,0:T(8,128)(2,1)S(1)}, bf16[64,4096]{1,0:T(8,128)(2,1)S(1)}, u32[]{:S(2)}, u32[]{:S(2)}) collective-permute-start(bf16[64,4096]{1,0:T(8,128)(2,1)S(1)} %joined.3.refs_0_), channel_id=1, source_target_pairs={{0,4},{1,29},{2,6},{3,31},{4,8},{5,1},{6,10},{7,3},{8,12},{9,5},{1... | collective-permute-start | bytes 1572872 | tf_op jit(solution)/shard_map/ppermute | solution.py:17
  13.6 3.4 %collective-permute-start.2 = (bf16[64,4096]{1,0:T(8,128)(2,1)S(1)}, bf16[64,4096]{1,0:T(8,128)(2,1)S(1)}, u32[]{:S(2)}, u32[]{:S(2)}) collective-permute-start(bf16[64,4096]{1,0:T(8,128)(2,1)S(1)} %joined.3.refs_0_), channel_id=1, source_target_pairs={{0,6},{1,31},{2,4},{3,29},{4,10},{5,3},{6,8},{7,1},{8,14},{9,7},{1... | collective-permute-start | bytes 1572872 | tf_op jit(solution)/shard_map/ppermute | solution.py:17
  17.0 2.8 %collective-permute-done.1.refs_0_ = bf16[64,4096]{1,0:T(8,128)(2,1)S(1)} collective-permute-done((bf16[64,4096]{1,0:T(8,128)(2,1)S(1)}, bf16[64,4096]{1,0:T(8,128)(2,1)S(1)}, u32[]{:S(2)}, u32[]{:S(2)}) %collective-permute-start.1) | collective-permute-done | bytes 524320 | tf_op jit(solution)/shard_map/ppermute | solution.py:17
  19.7 3.1 %collective-permute-start.3 = (bf16[64,4096]{1,0:T(8,128)(2,1)S(1)}, bf16[64,4096]{1,0:T(8,128)(2,1)S(1)}, u32[]{:S(2)}, u32[]{:S(2)}) collective-permute-start(bf16[64,4096]{1,0:T(8,128)(2,1)S(1)} %collective-permute-done.1.refs_0_), channel_id=1, source_target_pairs={{0,4},{1,29},{2,6},{3,31},{4,8},{5,1},{6,10},{7,3},{8,12},{9,5},{1... | collective-permute-start | bytes 1572872 | tf_op jit(solution)/shard_map/ppermute | solution.py:17
  22.8 0.0 collective-permute-start.4
  22.8 3.4 %copy-done = bf16[1024,1,4096]{2,0,1:T(8,128)(2,1)S(1)} copy-done((bf16[1024,1,4096]{2,0,1:T(8,128)(2,1)S(1)}, bf16[1024,1,4096]{2,0,1:T(8,128)(2,1)}, u32[]{:S(2)}) %copy-start) | copy-done | bytes 8388632
  26.2 2.6 %score.5.refs_0_ = bf16[64,1024]{1,0:T(8,128)(2,1)S(1)} custom-call(bf16[64,4096]{1,0:T(8,128)(2,1)S(1)} %joined.3.refs_0_, bf16[1024,4096]{1,0:T(8,128)(2,1)S(1)} %bitcast.37), custom_call_target="tpu_custom_call" | custom-call | flops 536870912 | bytes 9043968 | tf_op jit(solution)/shard_map/score/pallas_call | solution.py:143
  28.9 1.9 %collective-permute-start.5 = (bf16[64,4096]{1,0:T(8,128)(2,1)S(1)}, bf16[64,4096]{1,0:T(8,128)(2,1)S(1)}, u32[]{:S(2)}, u32[]{:S(2)}) collective-permute-start(bf16[64,4096]{1,0:T(8,128)(2,1)S(1)} %collective-permute-done.2.refs_2_), channel_id=1, source_target_pairs={{0,1},{1,0},{2,3},{3,2},{4,5},{5,4},{6,7},{7,6},{8,9},{9,8},{10,11... | collective-permute-start | bytes 1572872 | tf_op jit(solution)/shard_map/ppermute | solution.py:17
  30.8 6.2 %collective-permute-start.6 = (bf16[64,4096]{1,0:T(8,128)(2,1)S(1)}, bf16[64,4096]{1,0:T(8,128)(2,1)S(1)}, u32[]{:S(2)}, u32[]{:S(2)}) collective-permute-start(bf16[64,4096]{1,0:T(8,128)(2,1)S(1)} %collective-permute-done.2.refs_2_), channel_id=1, source_target_pairs={{0,4},{1,29},{2,6},{3,31},{4,8},{5,1},{6,10},{7,3},{8,12},{9,5},{1... | collective-permute-start | bytes 1572872 | tf_op jit(solution)/shard_map/ppermute | solution.py:17
  37.0 0.1 collective-permute-start.10
  37.1 0.0 collective-permute-done.3.refs_0_
  37.1 0.0 collective-permute-start.7
  37.1 0.0 collective-permute-done.4.refs_1_
  37.1 0.3 collective-permute-start.8
  37.4 0.0 collective-permute-done.5.refs_3_
  37.4 2.4 %score.6.refs_1_ = bf16[256,1024]{1,0:T(8,128)(2,1)S(1)} custom-call(bf16[64,4096]{1,0:T(8,128)(2,1)S(1)} %collective-permute-done.1.refs_0_, bf16[64,4096]{1,0:T(8,128)(2,1)S(1)} %collective-permute-done.4.refs_1_, bf16[64,4096]{1,0:T(8,128)(2,1)S(1)} %collective-permute-done.2.refs_2_, bf16[64,4096]{1,0:T(8,128)(2,1)S(1)} %collective-permute-done.5.refs_3_, ...), custom_call_target="tpu_custom_call" | custom-call | flops 2147483648 | bytes 11010048 | tf_op jit(solution)/shard_map/score/pallas_call | solution.py:143
  39.8 3.4 %collective-permute-done.6.refs_2_ = bf16[64,4096]{1,0:T(8,128)(2,1)S(1)} collective-permute-done((bf16[64,4096]{1,0:T(8,128)(2,1)S(1)}, bf16[64,4096]{1,0:T(8,128)(2,1)S(1)}, u32[]{:S(2)}, u32[]{:S(2)}) %collective-permute-start.6) | collective-permute-done | bytes 524320 | tf_op jit(solution)/shard_map/ppermute | solution.py:17
  43.1 1.3 %collective-permute-start.9 = (bf16[64,4096]{1,0:T(8,128)(2,1)S(1)}, bf16[64,4096]{1,0:T(8,128)(2,1)S(1)}, u32[]{:S(2)}, u32[]{:S(2)}) collective-permute-start(bf16[64,4096]{1,0:T(8,128)(2,1)S(1)} %collective-permute-done.6.refs_2_), channel_id=1, source_target_pairs={{0,1},{1,0},{2,3},{3,2},{4,5},{5,4},{6,7},{7,6},{8,9},{9,8},{10,11... | collective-permute-start | bytes 1572872 | tf_op jit(solution)/shard_map/ppermute | solution.py:17
  44.5 2.1 %collective-permute-start.11 = (bf16[64,4096]{1,0:T(8,128)(2,1)S(1)}, bf16[64,4096]{1,0:T(8,128)(2,1)S(1)}, u32[]{:S(2)}, u32[]{:S(2)}) collective-permute-start(bf16[64,4096]{1,0:T(8,128)(2,1)S(1)} %collective-permute-done.6.refs_2_), channel_id=1, source_target_pairs={{0,4},{1,29},{2,6},{3,31},{4,8},{5,1},{6,10},{7,3},{8,12},{9,5},{1... | collective-permute-start | bytes 1572872 | tf_op jit(solution)/shard_map/ppermute | solution.py:17
  46.6 2.2 %collective-permute-done.7.refs_0_ = bf16[64,4096]{1,0:T(8,128)(2,1)S(1)} collective-permute-done((bf16[64,4096]{1,0:T(8,128)(2,1)S(1)}, bf16[64,4096]{1,0:T(8,128)(2,1)S(1)}, u32[]{:S(2)}, u32[]{:S(2)}) %collective-permute-start.7) | collective-permute-done | bytes 524320 | tf_op jit(solution)/shard_map/ppermute | solution.py:17
  48.8 0.0 collective-permute-done.10.refs_4_
  48.8 0.0 collective-permute-done.9.refs_3_
  48.8 3.0 %score.7.refs_2_ = bf16[320,1024]{1,0:T(8,128)(2,1)S(1)} custom-call(bf16[64,4096]{1,0:T(8,128)(2,1)S(1)} %collective-permute-done.3.refs_0_, bf16[64,4096]{1,0:T(8,128)(2,1)S(1)} %collective-permute-done.8.refs_1_, bf16[64,4096]{1,0:T(8,128)(2,1)S(1)} %collective-permute-done.6.refs_2_, bf16[64,4096]{1,0:T(8,128)(2,1)S(1)} %collective-permute-done.9.refs_3_, ...), custom_call_target="tpu_custom_call" | custom-call | flops 2684354560 | bytes 11665408 | tf_op jit(solution)/shard_map/score/pallas_call | solution.py:143
  51.8 2.6 %collective-permute-done.11.refs_2_.refs_0_ = bf16[64,4096]{1,0:T(8,128)(2,1)S(1)} collective-permute-done((bf16[64,4096]{1,0:T(8,128)(2,1)S(1)}, bf16[64,4096]{1,0:T(8,128)(2,1)S(1)}, u32[]{:S(2)}, u32[]{:S(2)}) %collective-permute-start.11) | collective-permute-done | bytes 524320 | tf_op jit(solution)/shard_map/ppermute | solution.py:17
  54.4 1.3 %collective-permute-start.13 = (bf16[64,4096]{1,0:T(8,128)(2,1)S(1)}, bf16[64,4096]{1,0:T(8,128)(2,1)S(1)}, u32[]{:S(2)}, u32[]{:S(2)}) collective-permute-start(bf16[64,4096]{1,0:T(8,128)(2,1)S(1)} %collective-permute-done.7.refs_0_), channel_id=1, source_target_pairs={{0,1},{1,0},{2,3},{3,2},{4,5},{5,4},{6,7},{7,6},{8,9},{9,8},{10,11... | collective-permute-start | bytes 1572872 | tf_op jit(solution)/shard_map/ppermute | solution.py:17
  55.7 0.0 collective-permute-start.14
  55.7 2.3 %collective-permute-start.12 = (bf16[32,4096]{1,0:T(8,128)(2,1)S(1)}, bf16[32,4096]{1,0:T(8,128)(2,1)S(1)}, u32[]{:S(2)}, u32[]{:S(2)}) collective-permute-start(bf16[32,4096]{1,0:T(8,128)(2,1)S(1)} %joined.4), channel_id=1, source_target_pairs={{0,4},{1,29},{2,6},{3,31},{4,8},{5,1},{6,10},{7,3},{8,12},{9,5},{1... | collective-permute-start | bytes 786440 | tf_op jit(solution)/shard_map/ppermute | solution.py:17
  58.0 0.1 collective-permute-start.15
  58.1 3.2 %collective-permute-done.12.refs_0_ = bf16[32,4096]{1,0:T(8,128)(2,1)S(1)} collective-permute-done((bf16[32,4096]{1,0:T(8,128)(2,1)S(1)}, bf16[32,4096]{1,0:T(8,128)(2,1)S(1)}, u32[]{:S(2)}, u32[]{:S(2)}) %collective-permute-start.12) | collective-permute-done | bytes 262176 | tf_op jit(solution)/shard_map/ppermute | solution.py:17
  61.3 2.5 %collective-permute-start.16 = (bf16[32,4096]{1,0:T(8,128)(2,1)S(1)}, bf16[32,4096]{1,0:T(8,128)(2,1)S(1)}, u32[]{:S(2)}, u32[]{:S(2)}) collective-permute-start(bf16[32,4096]{1,0:T(8,128)(2,1)S(1)} %collective-permute-done.12.refs_0_), channel_id=1, source_target_pairs={{0,1},{1,0},{2,3},{3,2},{4,5},{5,4},{6,7},{7,6},{8,9},{9,8},{10,11... | collective-permute-start | bytes 786440 | tf_op jit(solution)/shard_map/ppermute | solution.py:17
  63.8 0.0 collective-permute-done.13.refs_1_
  63.8 0.0 collective-permute-done.14.refs_3_
  63.8 2.4 %score.8.refs_3_ = bf16[256,1024]{1,0:T(8,128)(2,1)S(1)} custom-call(bf16[64,4096]{1,0:T(8,128)(2,1)S(1)} %collective-permute-done.7.refs_0_, bf16[64,4096]{1,0:T(8,128)(2,1)S(1)} %collective-permute-done.13.refs_1_, bf16[64,4096]{1,0:T(8,128)(2,1)S(1)} %collective-permute-done.11.refs_2_.refs_0_, bf16[64,4096]{1,0:T(8,128)(2,1)S(1)} %collective-permute-done.14.refs_3_, ...), custom_call_target="tpu_custom_call" | custom-call | flops 2147483648 | bytes 11010048 | tf_op jit(solution)/shard_map/score/pallas_call | solution.py:143
  66.2 0.0 collective-permute-done.15.refs_2_
  66.2 0.3 collective-permute-start.17
  66.6 1.3 %collective-permute-done.17.refs_3_ = bf16[32,4096]{1,0:T(8,128)(2,1)S(1)} collective-permute-done((bf16[32,4096]{1,0:T(8,128)(2,1)S(1)}, bf16[32,4096]{1,0:T(8,128)(2,1)S(1)}, u32[]{:S(2)}, u32[]{:S(2)}) %collective-permute-start.17) | collective-permute-done | bytes 262176 | tf_op jit(solution)/shard_map/ppermute | solution.py:17
  67.9 2.9 %score.9.refs_4_ = bf16[128,1024]{1,0:T(8,128)(2,1)S(1)} custom-call(bf16[32,4096]{1,0:T(8,128)(2,1)S(1)} %collective-permute-done.12.refs_0_, bf16[32,4096]{1,0:T(8,128)(2,1)S(1)} %collective-permute-done.16.refs_1_, bf16[32,4096]{1,0:T(8,128)(2,1)S(1)} %collective-permute-done.15.refs_2_, bf16[32,4096]{1,0:T(8,128)(2,1)S(1)} %collective-permute-done.17.refs_3_, ...), custom_call_target="tpu_custom_call" | custom-call | flops 1073741824 | bytes 9699328 | tf_op jit(solution)/shard_map/score/pallas_call | solution.py:143
  70.8 0.7 place.1
  71.4 31.0 %all_to_all.5.in_ref = bf16[8,128,1024]{2,1,0:T(8,128)(2,1)S(1)} all-to-all(bf16[8,128,1024]{2,1,0:T(8,128)(2,1)S(1)} %bitcast.42), channel_id=1, replica_groups=mesh['group'=8,'blk'=32] {'group'}, dimensions={0} | all-to-all | bytes 4194304 | tf_op jit(solution)/shard_map/all_to_all | solution.py:267
  102.5 1.9 %total.1 = f32[1024,128]{1,0:T(8,128)} custom-call(bf16[8,128,1024]{2,1,0:T(8,128)(2,1)S(1)} %all_to_all.5.in_ref), custom_call_target="tpu_custom_call" | custom-call | tf_op jit(solution)/shard_map/total/pallas_call | solution.py:188
  (12 shorter events, 0.1 us)
Async XLA Ops:
  0.0 0.9 copy-start.2
  1.0 0.8 copy-start.3
  1.7 0.8 copy-start.4
  5.1 4.5 %collective-permute-start = (bf16[32,4096]{1,0:T(8,128)(2,1)S(1)}, bf16[32,4096]{1,0:T(8,128)(2,1)S(1)}, u32[]{:S(2)}, u32[]{:S(2)}) collective-permute-start(bf16[32,4096]{1,0:T(8,128)(2,1)S(1)} %precond.1.refs_0_), channel_id=1, source_target_pairs={{0,1},{1,0},{2,3},{3,2},{4,5},{5,4},{6,7},{7,6},{8,9},{9,8},{10,11... | collective-permute-start | bytes 786440 | tf_op jit(solution)/shard_map/ppermute | solution.py:17
  9.7 10.0 %collective-permute-start.1 = (bf16[64,4096]{1,0:T(8,128)(2,1)S(1)}, bf16[64,4096]{1,0:T(8,128)(2,1)S(1)}, u32[]{:S(2)}, u32[]{:S(2)}) collective-permute-start(bf16[64,4096]{1,0:T(8,128)(2,1)S(1)} %joined.3.refs_0_), channel_id=1, source_target_pairs={{0,4},{1,29},{2,6},{3,31},{4,8},{5,1},{6,10},{7,3},{8,12},{9,5},{1... | collective-permute-start | bytes 1572872 | tf_op jit(solution)/shard_map/ppermute | solution.py:17
  13.6 15.3 %collective-permute-start.2 = (bf16[64,4096]{1,0:T(8,128)(2,1)S(1)}, bf16[64,4096]{1,0:T(8,128)(2,1)S(1)}, u32[]{:S(2)}, u32[]{:S(2)}) collective-permute-start(bf16[64,4096]{1,0:T(8,128)(2,1)S(1)} %joined.3.refs_0_), channel_id=1, source_target_pairs={{0,6},{1,31},{2,4},{3,29},{4,10},{5,3},{6,8},{7,1},{8,14},{9,7},{1... | collective-permute-start | bytes 1572872 | tf_op jit(solution)/shard_map/ppermute | solution.py:17
  19.7 17.4 %collective-permute-start.3 = (bf16[64,4096]{1,0:T(8,128)(2,1)S(1)}, bf16[64,4096]{1,0:T(8,128)(2,1)S(1)}, u32[]{:S(2)}, u32[]{:S(2)}) collective-permute-start(bf16[64,4096]{1,0:T(8,128)(2,1)S(1)} %collective-permute-done.1.refs_0_), channel_id=1, source_target_pairs={{0,4},{1,29},{2,6},{3,31},{4,8},{5,1},{6,10},{7,3},{8,12},{9,5},{1... | collective-permute-start | bytes 1572872 | tf_op jit(solution)/shard_map/ppermute | solution.py:17
  22.8 14.3 %collective-permute-start.4 = (bf16[64,4096]{1,0:T(8,128)(2,1)S(1)}, bf16[64,4096]{1,0:T(8,128)(2,1)S(1)}, u32[]{:S(2)}, u32[]{:S(2)}) collective-permute-start(bf16[64,4096]{1,0:T(8,128)(2,1)S(1)} %collective-permute-done.1.refs_0_), channel_id=1, source_target_pairs={{0,1},{1,0},{2,3},{3,2},{4,5},{5,4},{6,7},{7,6},{8,9},{9,8},{10,11... | collective-permute-start | bytes 1572872 | tf_op jit(solution)/shard_map/ppermute | solution.py:17
  22.8 3.4 %copy-start = (bf16[1024,1,4096]{2,0,1:T(8,128)(2,1)S(1)}, bf16[1024,1,4096]{2,0,1:T(8,128)(2,1)}, u32[]{:S(2)}) copy-start(bf16[1024,1,4096]{2,0,1:T(8,128)(2,1)} %param.5) | copy-start | bytes 25165828
  26.2 11.2 %copy-start.1 = (bf16[1024,1,4096]{2,0,1:T(8,128)(2,1)S(1)}, bf16[1024,1,4096]{2,0,1:T(8,128)(2,1)}, u32[]{:S(2)}) copy-start(bf16[1024,1,4096]{2,0,1:T(8,128)(2,1)} %param.5) | copy-start | bytes 25165828
  28.9 8.5 %collective-permute-start.5 = (bf16[64,4096]{1,0:T(8,128)(2,1)S(1)}, bf16[64,4096]{1,0:T(8,128)(2,1)S(1)}, u32[]{:S(2)}, u32[]{:S(2)}) collective-permute-start(bf16[64,4096]{1,0:T(8,128)(2,1)S(1)} %collective-permute-done.2.refs_2_), channel_id=1, source_target_pairs={{0,1},{1,0},{2,3},{3,2},{4,5},{5,4},{6,7},{7,6},{8,9},{9,8},{10,11... | collective-permute-start | bytes 1572872 | tf_op jit(solution)/shard_map/ppermute | solution.py:17
  30.8 12.4 %collective-permute-start.6 = (bf16[64,4096]{1,0:T(8,128)(2,1)S(1)}, bf16[64,4096]{1,0:T(8,128)(2,1)S(1)}, u32[]{:S(2)}, u32[]{:S(2)}) collective-permute-start(bf16[64,4096]{1,0:T(8,128)(2,1)S(1)} %collective-permute-done.2.refs_2_), channel_id=1, source_target_pairs={{0,4},{1,29},{2,6},{3,31},{4,8},{5,1},{6,10},{7,3},{8,12},{9,5},{1... | collective-permute-start | bytes 1572872 | tf_op jit(solution)/shard_map/ppermute | solution.py:17
  37.0 11.8 %collective-permute-start.10 = (bf16[64,4096]{1,0:T(8,128)(2,1)S(1)}, bf16[64,4096]{1,0:T(8,128)(2,1)S(1)}, u32[]{:S(2)}, u32[]{:S(2)}) collective-permute-start(bf16[64,4096]{1,0:T(8,128)(2,1)S(1)} %joined.3.refs_0_), channel_id=1, source_target_pairs={{0,2},{1,3},{2,0},{3,1},{4,6},{5,7},{6,4},{7,5},{8,10},{9,11},{10,... | collective-permute-start | bytes 1572872 | tf_op jit(solution)/shard_map/ppermute | solution.py:17
  37.1 11.7 %collective-permute-start.7 = (bf16[64,4096]{1,0:T(8,128)(2,1)S(1)}, bf16[64,4096]{1,0:T(8,128)(2,1)S(1)}, u32[]{:S(2)}, u32[]{:S(2)}) collective-permute-start(bf16[64,4096]{1,0:T(8,128)(2,1)S(1)} %collective-permute-done.3.refs_0_), channel_id=1, source_target_pairs={{0,4},{1,29},{2,6},{3,31},{4,8},{5,1},{6,10},{7,3},{8,12},{9,5},{1... | collective-permute-start | bytes 1572872 | tf_op jit(solution)/shard_map/ppermute | solution.py:17
  37.1 11.7 %collective-permute-start.8 = (bf16[64,4096]{1,0:T(8,128)(2,1)S(1)}, bf16[64,4096]{1,0:T(8,128)(2,1)S(1)}, u32[]{:S(2)}, u32[]{:S(2)}) collective-permute-start(bf16[64,4096]{1,0:T(8,128)(2,1)S(1)} %collective-permute-done.3.refs_0_), channel_id=1, source_target_pairs={{0,1},{1,0},{2,3},{3,2},{4,5},{5,4},{6,7},{7,6},{8,9},{9,8},{10,11... | collective-permute-start | bytes 1572872 | tf_op jit(solution)/shard_map/ppermute | solution.py:17
  43.1 5.7 %collective-permute-start.9 = (bf16[64,4096]{1,0:T(8,128)(2,1)S(1)}, bf16[64,4096]{1,0:T(8,128)(2,1)S(1)}, u32[]{:S(2)}, u32[]{:S(2)}) collective-permute-start(bf16[64,4096]{1,0:T(8,128)(2,1)S(1)} %collective-permute-done.6.refs_2_), channel_id=1, source_target_pairs={{0,1},{1,0},{2,3},{3,2},{4,5},{5,4},{6,7},{7,6},{8,9},{9,8},{10,11... | collective-permute-start | bytes 1572872 | tf_op jit(solution)/shard_map/ppermute | solution.py:17
  44.5 9.9 %collective-permute-start.11 = (bf16[64,4096]{1,0:T(8,128)(2,1)S(1)}, bf16[64,4096]{1,0:T(8,128)(2,1)S(1)}, u32[]{:S(2)}, u32[]{:S(2)}) collective-permute-start(bf16[64,4096]{1,0:T(8,128)(2,1)S(1)} %collective-permute-done.6.refs_2_), channel_id=1, source_target_pairs={{0,4},{1,29},{2,6},{3,31},{4,8},{5,1},{6,10},{7,3},{8,12},{9,5},{1... | collective-permute-start | bytes 1572872 | tf_op jit(solution)/shard_map/ppermute | solution.py:17
  54.4 9.4 %collective-permute-start.13 = (bf16[64,4096]{1,0:T(8,128)(2,1)S(1)}, bf16[64,4096]{1,0:T(8,128)(2,1)S(1)}, u32[]{:S(2)}, u32[]{:S(2)}) collective-permute-start(bf16[64,4096]{1,0:T(8,128)(2,1)S(1)} %collective-permute-done.7.refs_0_), channel_id=1, source_target_pairs={{0,1},{1,0},{2,3},{3,2},{4,5},{5,4},{6,7},{7,6},{8,9},{9,8},{10,11... | collective-permute-start | bytes 1572872 | tf_op jit(solution)/shard_map/ppermute | solution.py:17
  55.7 8.1 %collective-permute-start.14 = (bf16[64,4096]{1,0:T(8,128)(2,1)S(1)}, bf16[64,4096]{1,0:T(8,128)(2,1)S(1)}, u32[]{:S(2)}, u32[]{:S(2)}) collective-permute-start(bf16[64,4096]{1,0:T(8,128)(2,1)S(1)} %collective-permute-done.11.refs_2_.refs_0_), channel_id=1, source_target_pairs={{0,1},{1,0},{2,3},{3,2},{4,5},{5,4},{6,7},{7,6},{8,9},{9,8},{10,11... | collective-permute-start | bytes 1572872 | tf_op jit(solution)/shard_map/ppermute | solution.py:17
  55.7 5.6 %collective-permute-start.12 = (bf16[32,4096]{1,0:T(8,128)(2,1)S(1)}, bf16[32,4096]{1,0:T(8,128)(2,1)S(1)}, u32[]{:S(2)}, u32[]{:S(2)}) collective-permute-start(bf16[32,4096]{1,0:T(8,128)(2,1)S(1)} %joined.4), channel_id=1, source_target_pairs={{0,4},{1,29},{2,6},{3,31},{4,8},{5,1},{6,10},{7,3},{8,12},{9,5},{1... | collective-permute-start | bytes 786440 | tf_op jit(solution)/shard_map/ppermute | solution.py:17
  58.0 8.2 %collective-permute-start.15 = (bf16[32,4096]{1,0:T(8,128)(2,1)S(1)}, bf16[32,4096]{1,0:T(8,128)(2,1)S(1)}, u32[]{:S(2)}, u32[]{:S(2)}) collective-permute-start(bf16[32,4096]{1,0:T(8,128)(2,1)S(1)} %joined.5), channel_id=1, source_target_pairs={{0,4},{1,29},{2,6},{3,31},{4,8},{5,1},{6,10},{7,3},{8,12},{9,5},{1... | collective-permute-start | bytes 786440 | tf_op jit(solution)/shard_map/ppermute | solution.py:17
  61.3 5.3 %collective-permute-start.16 = (bf16[32,4096]{1,0:T(8,128)(2,1)S(1)}, bf16[32,4096]{1,0:T(8,128)(2,1)S(1)}, u32[]{:S(2)}, u32[]{:S(2)}) collective-permute-start(bf16[32,4096]{1,0:T(8,128)(2,1)S(1)} %collective-permute-done.12.refs_0_), channel_id=1, source_target_pairs={{0,1},{1,0},{2,3},{3,2},{4,5},{5,4},{6,7},{7,6},{8,9},{9,8},{10,11... | collective-permute-start | bytes 786440 | tf_op jit(solution)/shard_map/ppermute | solution.py:17
  66.2 1.6 %collective-permute-start.17 = (bf16[32,4096]{1,0:T(8,128)(2,1)S(1)}, bf16[32,4096]{1,0:T(8,128)(2,1)S(1)}, u32[]{:S(2)}, u32[]{:S(2)}) collective-permute-start(bf16[32,4096]{1,0:T(8,128)(2,1)S(1)} %collective-permute-done.15.refs_2_), channel_id=1, source_target_pairs={{0,1},{1,0},{2,3},{3,2},{4,5},{5,4},{6,7},{7,6},{8,9},{9,8},{10,11... | collective-permute-start | bytes 786440 | tf_op jit(solution)/shard_map/ppermute | solution.py:17

commit v5 on v4

--- a/solution.py
+++ b/solution.py
@@ -19,10 +19,6 @@
 
 def _along(x):
     return _route(x, lambda z, rest: ((z + (1 if rest % 2 == 0 else -1)) % NZ) * 4 + rest)
-
-
-def _across(x):
-    return _route(x, lambda z, rest: ((z + (1 if rest % 2 == 0 else -1)) % NZ) * 4 + (rest ^ 2))
 
 
 def _swap_core(x):
@@ -103,7 +99,7 @@
         ],
         compiler_params=pltpu.CompilerParams(vmem_limit_bytes=12 << 20),
         name="precond",
-    )(out_factor, in_factor, queries)
+    )(*(pltpu.with_memory_space_constraint(x, pltpu.HBM) for x in (out_factor, in_factor, queries)))
 
 
 def _joined_kernel(*refs):
@@ -221,13 +217,12 @@
         sources.append(((z + dz) % NZ) * 4 + (rest ^ (2 * dy)))
 
     note(0, 0)
+    note(0, 1)
     for s in range(1, NZ // 2):
         note(-s * up, 0)
         note_far(s * up, 0)
         note(-s * up, 1)
         note_far(s * up, 1)
-        if s == 2:
-            note(0, 1)
     for dy in (0, 1):
         sources.append(((z + NZ // 2) % NZ) * 4 + (rest ^ (2 * dy)))
         sources.append(((z + NZ // 2) % NZ) * 4 + (rest ^ (2 * dy) ^ 1))
@@ -237,32 +232,33 @@
 
     steps = []
 
+    across = _swap_y(panel)
     near = _joined(panel, _swap_core(panel))
     near, where = lax.optimization_barrier((near, where))
-    pieces = [near]
     start = near
-    near, far = _along(start), _across(start)
-    more = []
-    for s in range(1, NZ // 2 + 1):
+    near = _along(near)
+    near, across = lax.optimization_barrier((near, across))
+    home = _joined(across, _swap_core(across))
+    far = _along(home)
+    pieces = [start, home]
+    for s in range(1, NZ // 2):
         if s == NZ // 2 - 1:
             cut = _joined(near)
             near, cut, pieces[0] = lax.optimization_barrier((near, cut, pieces[0]))
-        else:
+        elif s > 1:
             near, pieces[0] = lax.optimization_barrier((near, pieces[0]))
         steps.append(_score(pieces, flat, scale))
-        if s == 1:
-            steps[0], far, start = lax.optimization_barrier((steps[0], far, start))
-            more = [_swap_y(start)]
-        else:
-            steps[-1], far = lax.optimization_barrier((steps[-1], far))
+        if s == NZ // 2 - 1:
+            steps[-1], last = lax.optimization_barrier((steps[-1], _along(cut)))
+            last, far = lax.optimization_barrier((last, far))
+        steps[-1], far = lax.optimization_barrier((steps[-1], far))
         pieces = [near, _swap_core(near), far, _swap_core(far)]
-        if s == 2:
-            pieces += more
         if s < NZ // 2 - 1:
             near, far = _along(near), _along(far)
-        elif s == NZ // 2 - 1:
-            near, far = _along(cut), _along(_joined(far))
+    beyond = _swap_y(last)
     steps.append(_score(pieces, flat, scale))
+    steps[-1], beyond = lax.optimization_barrier((steps[-1], beyond))
+    steps.append(_score([last, _swap_core(last), beyond, _swap_core(beyond)], flat, scale))
     buffer = _place(steps, where).reshape(groups, -1, cand_rows)
     parts = lax.all_to_all(buffer, "group", split_axis=0, concat_axis=0, tiled=True)
     return _total(parts)

time: 105 us -> 106 us (level)
  local copies, waits for them, and re-layouts: 5.96 us -> 3.49 us
  waiting for transfers between devices: 15.7 us -> 17.4 us
  starting transfers between devices: 32.1 us -> 33.2 us
    unnamed x10 -> x4, local copies, waits for them, and re-layouts: 5.85 us -> 3.39 us
    ppermute x18 -> x19, waiting for transfers between devices: 15.7 us -> 17.4 us  [_route(): lax.ppermute(x, 'blk', [(i, target(*divmod(i, 4))) for i in range(NZ * 4)])]
    ppermute x18 -> x19, starting transfers between devices: 32.1 us -> 33.2 us  [_route(): lax.ppermute(x, 'blk', [(i, target(*divmod(i, 4))) for i in range(NZ * 4)])]
  transfers between devices with their start and end apart: 18 -> 19, of which waited for: 7 -> 9; matrix products, arithmetic and copies ran while one was open for 1% -> 1% of each run, Pallas kernels for 10% -> 10%
where the time goes in v5:
time: 106 us; the launch traced here: 105 us
  starting transfers between devices  33.2 us (31%)
  blocking collectives  31.1 us (29%)
  Pallas kernels  19.4 us (18%)
  waiting for transfers between devices  17.4 us (16%)
  local copies, waits for them, and re-layouts  3.49 us (3%)
    ppermute x19, starting transfers between devices, _route(): lax.ppermute(x, 'blk', [(i, target(*divmod(i, 4))) for i in range(NZ * 4)])  33.2 us
    all_to_all x1, blocking collectives, body(): lax.all_to_all(buffer, 'group', split_axis=0, concat_axis=0, tiled=True)  31.1 us
    ppermute x19, waiting for transfers between devices, _route(): lax.ppermute(x, 'blk', [(i, target(*divmod(i, 4))) for i in range(NZ * 4)])  17.4 us
    pallas_call x5, Pallas kernels, _score(): pl.pallas_call(functools.partial(_score_kernel, scale, len(pieces)), in_s...  13 us
    pallas_call x1, Pallas kernels, _precond(): pl.pallas_call(_precond_kernel, in_specs=[pl.BlockSpec(memory_space=pltpu...  3.66 us
    unnamed x4, local copies, waits for them, and re-layouts  3.39 us
  transfers between devices with their start and end apart: 19, of which 9 were waited for; matrix products, arithmetic and copies ran while one was open for 1% of the time, Pallas kernels for 10%

profile of v5, /device:TPU:1, one launch (start us, length us, event | category | flops | bytes accessed | tf_op | source)
XLA Modules:
  0.0 105.5 jit_solution(6158119486461962443)
XLA Ops:
  0.0 3.7 %precond.1.refs_0_ = bf16[32,4096]{1,0:T(8,128)(2,1)S(1)} custom-call(f32[64,64]{1,0:T(8,128)} %bitcast.44, f32[64,64]{1,0:T(8,128)} %bitcast.45, bf16[32,4096]{1,0:T(8,128)(2,1)} %bitcast.43), custom_call_target="tpu_custom_call" | custom-call | tf_op jit(solution)/shard_map/precond/pallas_call | solution.py:90
  3.7 3.3 %collective-permute-start = (bf16[32,4096]{1,0:T(8,128)(2,1)S(1)}, bf16[32,4096]{1,0:T(8,128)(2,1)S(1)}, u32[]{:S(2)}, u32[]{:S(2)}) collective-permute-start(bf16[32,4096]{1,0:T(8,128)(2,1)S(1)} %precond.1.refs_0_), channel_id=1, source_target_pairs={{0,1},{1,0},{2,3},{3,2},{4,5},{5,4},{6,7},{7,6},{8,9},{9,8},{10,11... | collective-permute-start | bytes 786440 | tf_op jit(solution)/shard_map/ppermute | solution.py:17
  7.0 0.1 stack.131
  7.1 0.8 select_reduce_fusion.where_ref
  7.9 0.2 collective-permute-done.refs_1_
  8.2 3.9 %collective-permute-start.1 = (bf16[64,4096]{1,0:T(8,128)(2,1)S(1)}, bf16[64,4096]{1,0:T(8,128)(2,1)S(1)}, u32[]{:S(2)}, u32[]{:S(2)}) collective-permute-start(bf16[64,4096]{1,0:T(8,128)(2,1)S(1)} %joined.3.refs_0_), channel_id=1, source_target_pairs={{0,4},{1,29},{2,6},{3,31},{4,8},{5,1},{6,10},{7,3},{8,12},{9,5},{1... | collective-permute-start | bytes 1572872 | tf_op jit(solution)/shard_map/ppermute | solution.py:17
  12.1 2.9 %collective-permute-start.2 = (bf16[32,4096]{1,0:T(8,128)(2,1)S(1)}, bf16[32,4096]{1,0:T(8,128)(2,1)S(1)}, u32[]{:S(2)}, u32[]{:S(2)}) collective-permute-start(bf16[32,4096]{1,0:T(8,128)(2,1)S(1)} %precond.1.refs_0_), channel_id=1, source_target_pairs={{0,2},{1,3},{2,0},{3,1},{4,6},{5,7},{6,4},{7,5},{8,10},{9,11},{10,... | collective-permute-start | bytes 786440 | tf_op jit(solution)/shard_map/ppermute | solution.py:17
  15.0 3.8 %collective-permute-done.2.refs_0_ = bf16[32,4096]{1,0:T(8,128)(2,1)S(1)} collective-permute-done((bf16[32,4096]{1,0:T(8,128)(2,1)S(1)}, bf16[32,4096]{1,0:T(8,128)(2,1)S(1)}, u32[]{:S(2)}, u32[]{:S(2)}) %collective-permute-start.2) | collective-permute-done | bytes 262176 | tf_op jit(solution)/shard_map/ppermute | solution.py:17
  18.8 0.0 collective-permute-done.1.refs_0_
  18.8 1.1 %collective-permute-start.3 = (bf16[32,4096]{1,0:T(8,128)(2,1)S(1)}, bf16[32,4096]{1,0:T(8,128)(2,1)S(1)}, u32[]{:S(2)}, u32[]{:S(2)}) collective-permute-start(bf16[32,4096]{1,0:T(8,128)(2,1)S(1)} %collective-permute-done.2.refs_0_), channel_id=1, source_target_pairs={{0,1},{1,0},{2,3},{3,2},{4,5},{5,4},{6,7},{7,6},{8,9},{9,8},{10,11... | collective-permute-start | bytes 786440 | tf_op jit(solution)/shard_map/ppermute | solution.py:17
  19.9 1.2 %collective-permute-done.3.refs_1_ = bf16[32,4096]{1,0:T(8,128)(2,1)S(1)} collective-permute-done((bf16[32,4096]{1,0:T(8,128)(2,1)S(1)}, bf16[32,4096]{1,0:T(8,128)(2,1)S(1)}, u32[]{:S(2)}, u32[]{:S(2)}) %collective-permute-start.3) | collective-permute-done | bytes 262176 | tf_op jit(solution)/shard_map/ppermute | solution.py:17
  21.1 3.2 %collective-permute-start.4 = (bf16[64,4096]{1,0:T(8,128)(2,1)S(1)}, bf16[64,4096]{1,0:T(8,128)(2,1)S(1)}, u32[]{:S(2)}, u32[]{:S(2)}) collective-permute-start(bf16[64,4096]{1,0:T(8,128)(2,1)S(1)} %joined.4.refs_1_), channel_id=1, source_target_pairs={{0,4},{1,29},{2,6},{3,31},{4,8},{5,1},{6,10},{7,3},{8,12},{9,5},{1... | collective-permute-start | bytes 1572872 | tf_op jit(solution)/shard_map/ppermute | solution.py:17
  24.3 0.7 collective-permute-start.5
  25.1 0.0 collective-permute-start.6
  25.1 3.4 %copy-done = bf16[1024,1,4096]{2,0,1:T(8,128)(2,1)S(1)} copy-done((bf16[1024,1,4096]{2,0,1:T(8,128)(2,1)S(1)}, bf16[1024,1,4096]{2,0,1:T(8,128)(2,1)}, u32[]{:S(2)}) %copy-start) | copy-done | bytes 8388632
  28.5 2.9 %score.5.refs_0_ = bf16[128,1024]{1,0:T(8,128)(2,1)S(1)} custom-call(bf16[64,4096]{1,0:T(8,128)(2,1)S(1)} %joined.3.refs_0_, bf16[64,4096]{1,0:T(8,128)(2,1)S(1)} %joined.4.refs_1_, bf16[1024,4096]{1,0:T(8,128)(2,1)S(1)} %bitcast.37), custom_call_target="tpu_custom_call" | custom-call | flops 1073741824 | bytes 9699328 | tf_op jit(solution)/shard_map/score/pallas_call | solution.py:139
  31.3 0.0 collective-permute-done.4.refs_2_
  31.3 0.8 collective-permute-start.7
  32.2 1.7 %collective-permute-start.8 = (bf16[64,4096]{1,0:T(8,128)(2,1)S(1)}, bf16[64,4096]{1,0:T(8,128)(2,1)S(1)}, u32[]{:S(2)}, u32[]{:S(2)}) collective-permute-start(bf16[64,4096]{1,0:T(8,128)(2,1)S(1)} %collective-permute-done.4.refs_2_), channel_id=1, source_target_pairs={{0,4},{1,29},{2,6},{3,31},{4,8},{5,1},{6,10},{7,3},{8,12},{9,5},{1... | collective-permute-start | bytes 1572872 | tf_op jit(solution)/shard_map/ppermute | solution.py:17
  33.9 2.2 %collective-permute-done.5.refs_0_ = bf16[64,4096]{1,0:T(8,128)(2,1)S(1)} collective-permute-done((bf16[64,4096]{1,0:T(8,128)(2,1)S(1)}, bf16[64,4096]{1,0:T(8,128)(2,1)S(1)}, u32[]{:S(2)}, u32[]{:S(2)}) %collective-permute-start.5) | collective-permute-done | bytes 524320 | tf_op jit(solution)/shard_map/ppermute | solution.py:17
  36.1 3.1 %collective-permute-start.9 = (bf16[64,4096]{1,0:T(8,128)(2,1)S(1)}, bf16[64,4096]{1,0:T(8,128)(2,1)S(1)}, u32[]{:S(2)}, u32[]{:S(2)}) collective-permute-start(bf16[64,4096]{1,0:T(8,128)(2,1)S(1)} %collective-permute-done.5.refs_0_), channel_id=1, source_target_pairs={{0,4},{1,29},{2,6},{3,31},{4,8},{5,1},{6,10},{7,3},{8,12},{9,5},{1... | collective-permute-start | bytes 1572872 | tf_op jit(solution)/shard_map/ppermute | solution.py:17
  39.2 0.0 collective-permute-start.10
  39.2 0.0 collective-permute-done.6.refs_1_
  39.2 0.0 collective-permute-done.7.refs_3_
  39.2 2.4 %score.6.refs_1_ = bf16[256,1024]{1,0:T(8,128)(2,1)S(1)} custom-call(bf16[64,4096]{1,0:T(8,128)(2,1)S(1)} %collective-permute-done.1.refs_0_, bf16[64,4096]{1,0:T(8,128)(2,1)S(1)} %collective-permute-done.6.refs_1_, bf16[64,4096]{1,0:T(8,128)(2,1)S(1)} %collective-permute-done.4.refs_2_, bf16[64,4096]{1,0:T(8,128)(2,1)S(1)} %collective-permute-done.7.refs_3_, ...), custom_call_target="tpu_custom_call" | custom-call | flops 2147483648 | bytes 11010048 | tf_op jit(solution)/shard_map/score/pallas_call | solution.py:139
  41.6 0.1 collective-permute-done.8.refs_2_
  41.7 1.7 %collective-permute-start.11 = (bf16[64,4096]{1,0:T(8,128)(2,1)S(1)}, bf16[64,4096]{1,0:T(8,128)(2,1)S(1)}, u32[]{:S(2)}, u32[]{:S(2)}) collective-permute-start(bf16[64,4096]{1,0:T(8,128)(2,1)S(1)} %collective-permute-done.8.refs_2_), channel_id=1, source_target_pairs={{0,1},{1,0},{2,3},{3,2},{4,5},{5,4},{6,7},{7,6},{8,9},{9,8},{10,11... | collective-permute-start | bytes 1572872 | tf_op jit(solution)/shard_map/ppermute | solution.py:17
  43.4 1.7 %collective-permute-start.13 = (bf16[64,4096]{1,0:T(8,128)(2,1)S(1)}, bf16[64,4096]{1,0:T(8,128)(2,1)S(1)}, u32[]{:S(2)}, u32[]{:S(2)}) collective-permute-start(bf16[64,4096]{1,0:T(8,128)(2,1)S(1)} %collective-permute-done.8.refs_2_), channel_id=1, source_target_pairs={{0,4},{1,29},{2,6},{3,31},{4,8},{5,1},{6,10},{7,3},{8,12},{9,5},{1... | collective-permute-start | bytes 1572872 | tf_op jit(solution)/shard_map/ppermute | solution.py:17
  45.1 2.2 %collective-permute-done.9.refs_0_ = bf16[64,4096]{1,0:T(8,128)(2,1)S(1)} collective-permute-done((bf16[64,4096]{1,0:T(8,128)(2,1)S(1)}, bf16[64,4096]{1,0:T(8,128)(2,1)S(1)}, u32[]{:S(2)}, u32[]{:S(2)}) %collective-permute-start.9) | collective-permute-done | bytes 524320 | tf_op jit(solution)/shard_map/ppermute | solution.py:17
  47.4 3.2 %collective-permute-start.12 = (bf16[32,4096]{1,0:T(8,128)(2,1)S(1)}, bf16[32,4096]{1,0:T(8,128)(2,1)S(1)}, u32[]{:S(2)}, u32[]{:S(2)}) collective-permute-start(bf16[32,4096]{1,0:T(8,128)(2,1)S(1)} %joined.5), channel_id=1, source_target_pairs={{0,4},{1,29},{2,6},{3,31},{4,8},{5,1},{6,10},{7,3},{8,12},{9,5},{1... | collective-permute-start | bytes 786440 | tf_op jit(solution)/shard_map/ppermute | solution.py:17
  50.5 0.0 collective-permute-start.14
  50.5 0.0 collective-permute-done.10.refs_1_
  50.5 0.0 collective-permute-done.11.refs_3_
  50.6 2.4 %score.7.refs_2_ = bf16[256,1024]{1,0:T(8,128)(2,1)S(1)} custom-call(bf16[64,4096]{1,0:T(8,128)(2,1)S(1)} %collective-permute-done.5.refs_0_, bf16[64,4096]{1,0:T(8,128)(2,1)S(1)} %collective-permute-done.10.refs_1_, bf16[64,4096]{1,0:T(8,128)(2,1)S(1)} %collective-permute-done.8.refs_2_, bf16[64,4096]{1,0:T(8,128)(2,1)S(1)} %collective-permute-done.11.refs_3_, ...), custom_call_target="tpu_custom_call" | custom-call | flops 2147483648 | bytes 11010048 | tf_op jit(solution)/shard_map/score/pallas_call | solution.py:139
  53.0 2.8 %collective-permute-done.12.refs_0_ = bf16[32,4096]{1,0:T(8,128)(2,1)S(1)} collective-permute-done((bf16[32,4096]{1,0:T(8,128)(2,1)S(1)}, bf16[32,4096]{1,0:T(8,128)(2,1)S(1)}, u32[]{:S(2)}, u32[]{:S(2)}) %collective-permute-start.12) | collective-permute-done | bytes 262176 | tf_op jit(solution)/shard_map/ppermute | solution.py:17
  55.8 0.0 collective-permute-done.13.refs_2_
  55.8 1.7 %collective-permute-start.15 = (bf16[64,4096]{1,0:T(8,128)(2,1)S(1)}, bf16[64,4096]{1,0:T(8,128)(2,1)S(1)}, u32[]{:S(2)}, u32[]{:S(2)}) collective-permute-start(bf16[64,4096]{1,0:T(8,128)(2,1)S(1)} %collective-permute-done.13.refs_2_), channel_id=1, source_target_pairs={{0,1},{1,0},{2,3},{3,2},{4,5},{5,4},{6,7},{7,6},{8,9},{9,8},{10,11... | collective-permute-start | bytes 1572872 | tf_op jit(solution)/shard_map/ppermute | solution.py:17
  57.4 2.9 %collective-permute-start.16 = (bf16[32,4096]{1,0:T(8,128)(2,1)S(1)}, bf16[32,4096]{1,0:T(8,128)(2,1)S(1)}, u32[]{:S(2)}, u32[]{:S(2)}) collective-permute-start(bf16[32,4096]{1,0:T(8,128)(2,1)S(1)} %collective-permute-done.12.refs_0_), channel_id=1, source_target_pairs={{0,2},{1,3},{2,0},{3,1},{4,6},{5,7},{6,4},{7,5},{8,10},{9,11},{10,... | collective-permute-start | bytes 786440 | tf_op jit(solution)/shard_map/ppermute | solution.py:17
  60.4 0.3 collective-permute-start.17
  60.6 0.0 collective-permute-done.14.refs_1_
  60.7 2.5 %score.8.refs_3_ = bf16[256,1024]{1,0:T(8,128)(2,1)S(1)} custom-call(bf16[64,4096]{1,0:T(8,128)(2,1)S(1)} %collective-permute-done.9.refs_0_, bf16[64,4096]{1,0:T(8,128)(2,1)S(1)} %collective-permute-done.14.refs_1_, bf16[64,4096]{1,0:T(8,128)(2,1)S(1)} %collective-permute-done.13.refs_2_, bf16[64,4096]{1,0:T(8,128)(2,1)S(1)} %collective-permute-done.15.refs_3_, ...), custom_call_target="tpu_custom_call" | custom-call | flops 2147483648 | bytes 11010048 | tf_op jit(solution)/shard_map/score/pallas_call | solution.py:139
  63.1 3.8 %collective-permute-done.16.refs_2_ = bf16[32,4096]{1,0:T(8,128)(2,1)S(1)} collective-permute-done((bf16[32,4096]{1,0:T(8,128)(2,1)S(1)}, bf16[32,4096]{1,0:T(8,128)(2,1)S(1)}, u32[]{:S(2)}, u32[]{:S(2)}) %collective-permute-start.16) | collective-permute-done | bytes 262176 | tf_op jit(solution)/shard_map/ppermute | solution.py:17
  66.9 0.8 collective-permute-start.18
  67.7 1.2 %collective-permute-done.18.refs_3_ = bf16[32,4096]{1,0:T(8,128)(2,1)S(1)} collective-permute-done((bf16[32,4096]{1,0:T(8,128)(2,1)S(1)}, bf16[32,4096]{1,0:T(8,128)(2,1)S(1)}, u32[]{:S(2)}, u32[]{:S(2)}) %collective-permute-start.18) | collective-permute-done | bytes 262176 | tf_op jit(solution)/shard_map/ppermute | solution.py:17
  68.8 2.9 %score.9.refs_4_ = bf16[128,1024]{1,0:T(8,128)(2,1)S(1)} custom-call(bf16[32,4096]{1,0:T(8,128)(2,1)S(1)} %collective-permute-done.12.refs_0_, bf16[32,4096]{1,0:T(8,128)(2,1)S(1)} %collective-permute-done.17.refs_1_, bf16[32,4096]{1,0:T(8,128)(2,1)S(1)} %collective-permute-done.16.refs_2_, bf16[32,4096]{1,0:T(8,128)(2,1)S(1)} %collective-permute-done.18.refs_3_, ...), custom_call_target="tpu_custom_call" | custom-call | flops 1073741824 | bytes 9699328 | tf_op jit(solution)/shard_map/score/pallas_call | solution.py:139
  71.7 0.7 place.1
  72.4 31.1 %all_to_all.5.in_ref = bf16[8,128,1024]{2,1,0:T(8,128)(2,1)S(1)} all-to-all(bf16[8,128,1024]{2,1,0:T(8,128)(2,1)S(1)} %bitcast.42), channel_id=1, replica_groups=mesh['group'=8,'blk'=32] {'group'}, dimensions={0} | all-to-all | bytes 4194304 | tf_op jit(solution)/shard_map/all_to_all | solution.py:263
  103.5 1.9 %total.1 = f32[1024,128]{1,0:T(8,128)} custom-call(bf16[8,128,1024]{2,1,0:T(8,128)(2,1)S(1)} %all_to_all.5.in_ref), custom_call_target="tpu_custom_call" | custom-call | tf_op jit(solution)/shard_map/total/pallas_call | solution.py:184
  (8 shorter events, 0.1 us)
Async XLA Ops:
  3.7 4.5 %collective-permute-start = (bf16[32,4096]{1,0:T(8,128)(2,1)S(1)}, bf16[32,4096]{1,0:T(8,128)(2,1)S(1)}, u32[]{:S(2)}, u32[]{:S(2)}) collective-permute-start(bf16[32,4096]{1,0:T(8,128)(2,1)S(1)} %precond.1.refs_0_), channel_id=1, source_target_pairs={{0,1},{1,0},{2,3},{3,2},{4,5},{5,4},{6,7},{7,6},{8,9},{9,8},{10,11... | collective-permute-start | bytes 786440 | tf_op jit(solution)/shard_map/ppermute | solution.py:17
  8.2 10.6 %collective-permute-start.1 = (bf16[64,4096]{1,0:T(8,128)(2,1)S(1)}, bf16[64,4096]{1,0:T(8,128)(2,1)S(1)}, u32[]{:S(2)}, u32[]{:S(2)}) collective-permute-start(bf16[64,4096]{1,0:T(8,128)(2,1)S(1)} %joined.3.refs_0_), channel_id=1, source_target_pairs={{0,4},{1,29},{2,6},{3,31},{4,8},{5,1},{6,10},{7,3},{8,12},{9,5},{1... | collective-permute-start | bytes 1572872 | tf_op jit(solution)/shard_map/ppermute | solution.py:17
  12.1 6.7 %collective-permute-start.2 = (bf16[32,4096]{1,0:T(8,128)(2,1)S(1)}, bf16[32,4096]{1,0:T(8,128)(2,1)S(1)}, u32[]{:S(2)}, u32[]{:S(2)}) collective-permute-start(bf16[32,4096]{1,0:T(8,128)(2,1)S(1)} %precond.1.refs_0_), channel_id=1, source_target_pairs={{0,2},{1,3},{2,0},{3,1},{4,6},{5,7},{6,4},{7,5},{8,10},{9,11},{10,... | collective-permute-start | bytes 786440 | tf_op jit(solution)/shard_map/ppermute | solution.py:17
  18.8 2.2 %collective-permute-start.3 = (bf16[32,4096]{1,0:T(8,128)(2,1)S(1)}, bf16[32,4096]{1,0:T(8,128)(2,1)S(1)}, u32[]{:S(2)}, u32[]{:S(2)}) collective-permute-start(bf16[32,4096]{1,0:T(8,128)(2,1)S(1)} %collective-permute-done.2.refs_0_), channel_id=1, source_target_pairs={{0,1},{1,0},{2,3},{3,2},{4,5},{5,4},{6,7},{7,6},{8,9},{9,8},{10,11... | collective-permute-start | bytes 786440 | tf_op jit(solution)/shard_map/ppermute | solution.py:17
  21.1 10.2 %collective-permute-start.4 = (bf16[64,4096]{1,0:T(8,128)(2,1)S(1)}, bf16[64,4096]{1,0:T(8,128)(2,1)S(1)}, u32[]{:S(2)}, u32[]{:S(2)}) collective-permute-start(bf16[64,4096]{1,0:T(8,128)(2,1)S(1)} %joined.4.refs_1_), channel_id=1, source_target_pairs={{0,4},{1,29},{2,6},{3,31},{4,8},{5,1},{6,10},{7,3},{8,12},{9,5},{1... | collective-permute-start | bytes 1572872 | tf_op jit(solution)/shard_map/ppermute | solution.py:17
  24.3 11.7 %collective-permute-start.5 = (bf16[64,4096]{1,0:T(8,128)(2,1)S(1)}, bf16[64,4096]{1,0:T(8,128)(2,1)S(1)}, u32[]{:S(2)}, u32[]{:S(2)}) collective-permute-start(bf16[64,4096]{1,0:T(8,128)(2,1)S(1)} %collective-permute-done.1.refs_0_), channel_id=1, source_target_pairs={{0,4},{1,29},{2,6},{3,31},{4,8},{5,1},{6,10},{7,3},{8,12},{9,5},{1... | collective-permute-start | bytes 1572872 | tf_op jit(solution)/shard_map/ppermute | solution.py:17
  25.1 14.1 %collective-permute-start.6 = (bf16[64,4096]{1,0:T(8,128)(2,1)S(1)}, bf16[64,4096]{1,0:T(8,128)(2,1)S(1)}, u32[]{:S(2)}, u32[]{:S(2)}) collective-permute-start(bf16[64,4096]{1,0:T(8,128)(2,1)S(1)} %collective-permute-done.1.refs_0_), channel_id=1, source_target_pairs={{0,1},{1,0},{2,3},{3,2},{4,5},{5,4},{6,7},{7,6},{8,9},{9,8},{10,11... | collective-permute-start | bytes 1572872 | tf_op jit(solution)/shard_map/ppermute | solution.py:17
  25.1 3.4 %copy-start = (bf16[1024,1,4096]{2,0,1:T(8,128)(2,1)S(1)}, bf16[1024,1,4096]{2,0,1:T(8,128)(2,1)}, u32[]{:S(2)}) copy-start(bf16[1024,1,4096]{2,0,1:T(8,128)(2,1)} %param.5) | copy-start | bytes 25165828
  28.5 10.8 %copy-start.1 = (bf16[1024,1,4096]{2,0,1:T(8,128)(2,1)S(1)}, bf16[1024,1,4096]{2,0,1:T(8,128)(2,1)}, u32[]{:S(2)}) copy-start(bf16[1024,1,4096]{2,0,1:T(8,128)(2,1)} %param.5) | copy-start | bytes 25165828
  31.3 7.9 %collective-permute-start.7 = (bf16[64,4096]{1,0:T(8,128)(2,1)S(1)}, bf16[64,4096]{1,0:T(8,128)(2,1)S(1)}, u32[]{:S(2)}, u32[]{:S(2)}) collective-permute-start(bf16[64,4096]{1,0:T(8,128)(2,1)S(1)} %collective-permute-done.4.refs_2_), channel_id=1, source_target_pairs={{0,1},{1,0},{2,3},{3,2},{4,5},{5,4},{6,7},{7,6},{8,9},{9,8},{10,11... | collective-permute-start | bytes 1572872 | tf_op jit(solution)/shard_map/ppermute | solution.py:17
  32.2 9.5 %collective-permute-start.8 = (bf16[64,4096]{1,0:T(8,128)(2,1)S(1)}, bf16[64,4096]{1,0:T(8,128)(2,1)S(1)}, u32[]{:S(2)}, u32[]{:S(2)}) collective-permute-start(bf16[64,4096]{1,0:T(8,128)(2,1)S(1)} %collective-permute-done.4.refs_2_), channel_id=1, source_target_pairs={{0,4},{1,29},{2,6},{3,31},{4,8},{5,1},{6,10},{7,3},{8,12},{9,5},{1... | collective-permute-start | bytes 1572872 | tf_op jit(solution)/shard_map/ppermute | solution.py:17
  36.1 11.2 %collective-permute-start.9 = (bf16[64,4096]{1,0:T(8,128)(2,1)S(1)}, bf16[64,4096]{1,0:T(8,128)(2,1)S(1)}, u32[]{:S(2)}, u32[]{:S(2)}) collective-permute-start(bf16[64,4096]{1,0:T(8,128)(2,1)S(1)} %collective-permute-done.5.refs_0_), channel_id=1, source_target_pairs={{0,4},{1,29},{2,6},{3,31},{4,8},{5,1},{6,10},{7,3},{8,12},{9,5},{1... | collective-permute-start | bytes 1572872 | tf_op jit(solution)/shard_map/ppermute | solution.py:17
  39.2 11.3 %collective-permute-start.10 = (bf16[64,4096]{1,0:T(8,128)(2,1)S(1)}, bf16[64,4096]{1,0:T(8,128)(2,1)S(1)}, u32[]{:S(2)}, u32[]{:S(2)}) collective-permute-start(bf16[64,4096]{1,0:T(8,128)(2,1)S(1)} %collective-permute-done.5.refs_0_), channel_id=1, source_target_pairs={{0,1},{1,0},{2,3},{3,2},{4,5},{5,4},{6,7},{7,6},{8,9},{9,8},{10,11... | collective-permute-start | bytes 1572872 | tf_op jit(solution)/shard_map/ppermute | solution.py:17
  41.7 8.8 %collective-permute-start.11 = (bf16[64,4096]{1,0:T(8,128)(2,1)S(1)}, bf16[64,4096]{1,0:T(8,128)(2,1)S(1)}, u32[]{:S(2)}, u32[]{:S(2)}) collective-permute-start(bf16[64,4096]{1,0:T(8,128)(2,1)S(1)} %collective-permute-done.8.refs_2_), channel_id=1, source_target_pairs={{0,1},{1,0},{2,3},{3,2},{4,5},{5,4},{6,7},{7,6},{8,9},{9,8},{10,11... | collective-permute-start | bytes 1572872 | tf_op jit(solution)/shard_map/ppermute | solution.py:17
  43.4 12.4 %collective-permute-start.13 = (bf16[64,4096]{1,0:T(8,128)(2,1)S(1)}, bf16[64,4096]{1,0:T(8,128)(2,1)S(1)}, u32[]{:S(2)}, u32[]{:S(2)}) collective-permute-start(bf16[64,4096]{1,0:T(8,128)(2,1)S(1)} %collective-permute-done.8.refs_2_), channel_id=1, source_target_pairs={{0,4},{1,29},{2,6},{3,31},{4,8},{5,1},{6,10},{7,3},{8,12},{9,5},{1... | collective-permute-start | bytes 1572872 | tf_op jit(solution)/shard_map/ppermute | solution.py:17
  47.4 8.4 %collective-permute-start.12 = (bf16[32,4096]{1,0:T(8,128)(2,1)S(1)}, bf16[32,4096]{1,0:T(8,128)(2,1)S(1)}, u32[]{:S(2)}, u32[]{:S(2)}) collective-permute-start(bf16[32,4096]{1,0:T(8,128)(2,1)S(1)} %joined.5), channel_id=1, source_target_pairs={{0,4},{1,29},{2,6},{3,31},{4,8},{5,1},{6,10},{7,3},{8,12},{9,5},{1... | collective-permute-start | bytes 786440 | tf_op jit(solution)/shard_map/ppermute | solution.py:17
  50.5 10.1 %collective-permute-start.14 = (bf16[64,4096]{1,0:T(8,128)(2,1)S(1)}, bf16[64,4096]{1,0:T(8,128)(2,1)S(1)}, u32[]{:S(2)}, u32[]{:S(2)}) collective-permute-start(bf16[64,4096]{1,0:T(8,128)(2,1)S(1)} %collective-permute-done.9.refs_0_), channel_id=1, source_target_pairs={{0,1},{1,0},{2,3},{3,2},{4,5},{5,4},{6,7},{7,6},{8,9},{9,8},{10,11... | collective-permute-start | bytes 1572872 | tf_op jit(solution)/shard_map/ppermute | solution.py:17
  55.8 4.9 %collective-permute-start.15 = (bf16[64,4096]{1,0:T(8,128)(2,1)S(1)}, bf16[64,4096]{1,0:T(8,128)(2,1)S(1)}, u32[]{:S(2)}, u32[]{:S(2)}) collective-permute-start(bf16[64,4096]{1,0:T(8,128)(2,1)S(1)} %collective-permute-done.13.refs_2_), channel_id=1, source_target_pairs={{0,1},{1,0},{2,3},{3,2},{4,5},{5,4},{6,7},{7,6},{8,9},{9,8},{10,11... | collective-permute-start | bytes 1572872 | tf_op jit(solution)/shard_map/ppermute | solution.py:17
  57.4 9.4 %collective-permute-start.16 = (bf16[32,4096]{1,0:T(8,128)(2,1)S(1)}, bf16[32,4096]{1,0:T(8,128)(2,1)S(1)}, u32[]{:S(2)}, u32[]{:S(2)}) collective-permute-start(bf16[32,4096]{1,0:T(8,128)(2,1)S(1)} %collective-permute-done.12.refs_0_), channel_id=1, source_target_pairs={{0,2},{1,3},{2,0},{3,1},{4,6},{5,7},{6,4},{7,5},{8,10},{9,11},{10,... | collective-permute-start | bytes 786440 | tf_op jit(solution)/shard_map/ppermute | solution.py:17
  60.4 7.3 %collective-permute-start.17 = (bf16[32,4096]{1,0:T(8,128)(2,1)S(1)}, bf16[32,4096]{1,0:T(8,128)(2,1)S(1)}, u32[]{:S(2)}, u32[]{:S(2)}) collective-permute-start(bf16[32,4096]{1,0:T(8,128)(2,1)S(1)} %collective-permute-done.12.refs_0_), channel_id=1, source_target_pairs={{0,1},{1,0},{2,3},{3,2},{4,5},{5,4},{6,7},{7,6},{8,9},{9,8},{10,11... | collective-permute-start | bytes 786440 | tf_op jit(solution)/shard_map/ppermute | solution.py:17
  66.9 1.9 %collective-permute-start.18 = (bf16[32,4096]{1,0:T(8,128)(2,1)S(1)}, bf16[32,4096]{1,0:T(8,128)(2,1)S(1)}, u32[]{:S(2)}, u32[]{:S(2)}) collective-permute-start(bf16[32,4096]{1,0:T(8,128)(2,1)S(1)} %collective-permute-done.16.refs_2_), channel_id=1, source_target_pairs={{0,1},{1,0},{2,3},{3,2},{4,5},{5,4},{6,7},{7,6},{8,9},{9,8},{10,11... | collective-permute-start | bytes 786440 | tf_op jit(solution)/shard_map/ppermute | solution.py:17

commit v6 on v5

--- a/solution.py
+++ b/solution.py
@@ -233,32 +233,28 @@
     steps = []
 
     across = _swap_y(panel)
-    near = _joined(panel, _swap_core(panel))
-    near, where = lax.optimization_barrier((near, where))
-    start = near
-    near = _along(near)
-    near, across = lax.optimization_barrier((near, across))
-    home = _joined(across, _swap_core(across))
-    far = _along(home)
-    pieces = [start, home]
-    for s in range(1, NZ // 2):
+    other = _swap_core(panel)
+    other, where = lax.optimization_barrier((other, where))
+    own, next_to = _along(panel), _along(other)
+    own, next_to, across = lax.optimization_barrier((own, next_to, across))
+    near = _joined(own, next_to)
+    across_other = _swap_core(across)
+    far = _along(_joined(across, across_other))
+    pieces = [panel, other, across, across_other, near, _swap_core(near), far, _swap_core(far)]
+    for s in range(2, NZ // 2 + 1):
+        if s < NZ // 2:
+            near, far = _along(near), _along(far)
+        else:
+            near, far = _along(cut), _along(_joined(far))
         if s == NZ // 2 - 1:
             cut = _joined(near)
             near, cut, pieces[0] = lax.optimization_barrier((near, cut, pieces[0]))
-        elif s > 1:
+        elif s < NZ // 2:
             near, pieces[0] = lax.optimization_barrier((near, pieces[0]))
         steps.append(_score(pieces, flat, scale))
-        if s == NZ // 2 - 1:
-            steps[-1], last = lax.optimization_barrier((steps[-1], _along(cut)))
-            last, far = lax.optimization_barrier((last, far))
         steps[-1], far = lax.optimization_barrier((steps[-1], far))
         pieces = [near, _swap_core(near), far, _swap_core(far)]
-        if s < NZ // 2 - 1:
-            near, far = _along(near), _along(far)
-    beyond = _swap_y(last)
     steps.append(_score(pieces, flat, scale))
-    steps[-1], beyond = lax.optimization_barrier((steps[-1], beyond))
-    steps.append(_score([last, _swap_core(last), beyond, _swap_core(beyond)], flat, scale))
     buffer = _place(steps, where).reshape(groups, -1, cand_rows)
     parts = lax.all_to_all(buffer, "group", split_axis=0, concat_axis=0, tiled=True)
     return _total(parts)

time: 106 us -> 104 us (0.981)
  waiting for transfers between devices: 17.4 us -> 22.4 us
  starting transfers between devices: 33.2 us -> 29.3 us
  Pallas kernels: 19.4 us -> 17.4 us
    ppermute x19 -> x20, waiting for transfers between devices: 17.4 us -> 22.4 us  [_route(): lax.ppermute(x, 'blk', [(i, target(*divmod(i, 4))) for i in range(NZ * 4)])]
    ppermute x19 -> x20, starting transfers between devices: 33.2 us -> 29.3 us  [_route(): lax.ppermute(x, 'blk', [(i, target(*divmod(i, 4))) for i in range(NZ * 4)])]
    pallas_call x5 -> x4, Pallas kernels: 13 us -> 11 us  [_score(): pl.pallas_call(functools.partial(_score_kernel, scale, len(pieces)), in_s...]
  transfers between devices with their start and end apart: 19 -> 20, of which waited for: 9 -> 8; matrix products, arithmetic and copies ran while one was open for 1% -> 1% of each run, Pallas kernels for 10% -> 8%
where the time goes in v6:
time: 104 us
  blocking collectives  30.8 us (30%)
  starting transfers between devices  29.3 us (28%)
  waiting for transfers between devices  22.4 us (22%)
  Pallas kernels  17.4 us (17%)
  local copies, waits for them, and re-layouts  3.49 us (3%)
    all_to_all x1, blocking collectives, body(): lax.all_to_all(buffer, 'group', split_axis=0, concat_axis=0, tiled=True)  30.8 us
    ppermute x20, starting transfers between devices, _route(): lax.ppermute(x, 'blk', [(i, target(*divmod(i, 4))) for i in range(NZ * 4)])  29.3 us
    ppermute x20, waiting for transfers between devices, _route(): lax.ppermute(x, 'blk', [(i, target(*divmod(i, 4))) for i in range(NZ * 4)])  22.4 us
    pallas_call x4, Pallas kernels, _score(): pl.pallas_call(functools.partial(_score_kernel, scale, len(pieces)), in_s...  11 us
    pallas_call x1, Pallas kernels, _precond(): pl.pallas_call(_precond_kernel, in_specs=[pl.BlockSpec(memory_space=pltpu...  3.66 us
    unnamed x4, local copies, waits for them, and re-layouts  3.38 us
  transfers between devices with their start and end apart: 20, of which 8 were waited for; matrix products, arithmetic and copies ran while one was open for 1% of the time, Pallas kernels for 8%

profile of v6, /device:TPU:1, one launch (start us, length us, event | category | flops | bytes accessed | tf_op | source)
XLA Modules:
  0.0 104.3 jit_solution(13824230957948599536)
XLA Ops:
  0.0 3.7 %precond.1.refs_0_ = bf16[32,4096]{1,0:T(8,128)(2,1)S(1)} custom-call(f32[64,64]{1,0:T(8,128)} %bitcast.43, f32[64,64]{1,0:T(8,128)} %bitcast.44, bf16[32,4096]{1,0:T(8,128)(2,1)} %bitcast.42), custom_call_target="tpu_custom_call" | custom-call | tf_op jit(solution)/shard_map/precond/pallas_call | solution.py:90
  3.7 3.3 %collective-permute-start = (bf16[32,4096]{1,0:T(8,128)(2,1)S(1)}, bf16[32,4096]{1,0:T(8,128)(2,1)S(1)}, u32[]{:S(2)}, u32[]{:S(2)}) collective-permute-start(bf16[32,4096]{1,0:T(8,128)(2,1)S(1)} %precond.1.refs_0_), channel_id=1, source_target_pairs={{0,1},{1,0},{2,3},{3,2},{4,5},{5,4},{6,7},{7,6},{8,9},{9,8},{10,11... | collective-permute-start | bytes 786440 | tf_op jit(solution)/shard_map/ppermute | solution.py:17
  7.0 3.8 %collective-permute-start.1 = (bf16[32,4096]{1,0:T(8,128)(2,1)S(1)}, bf16[32,4096]{1,0:T(8,128)(2,1)S(1)}, u32[]{:S(2)}, u32[]{:S(2)}) collective-permute-start(bf16[32,4096]{1,0:T(8,128)(2,1)S(1)} %precond.1.refs_0_), channel_id=1, source_target_pairs={{0,4},{1,29},{2,6},{3,31},{4,8},{5,1},{6,10},{7,3},{8,12},{9,5},{1... | collective-permute-start | bytes 786440 | tf_op jit(solution)/shard_map/ppermute | solution.py:17
  10.8 2.9 %collective-permute-start.3 = (bf16[32,4096]{1,0:T(8,128)(2,1)S(1)}, bf16[32,4096]{1,0:T(8,128)(2,1)S(1)}, u32[]{:S(2)}, u32[]{:S(2)}) collective-permute-start(bf16[32,4096]{1,0:T(8,128)(2,1)S(1)} %precond.1.refs_0_), channel_id=1, source_target_pairs={{0,2},{1,3},{2,0},{3,1},{4,6},{5,7},{6,4},{7,5},{8,10},{9,11},{10,... | collective-permute-start | bytes 786440 | tf_op jit(solution)/shard_map/ppermute | solution.py:17
  13.8 0.1 stack.131
  13.9 0.8 select_reduce_fusion.where_ref
  14.7 0.0 collective-permute-done.refs_1_
  14.7 0.8 collective-permute-start.2
  15.5 0.0 collective-permute-done.1.refs_0_
  15.5 2.0 %collective-permute-done.3.refs_0_.refs_2_ = bf16[32,4096]{1,0:T(8,128)(2,1)S(1)} collective-permute-done((bf16[32,4096]{1,0:T(8,128)(2,1)S(1)}, bf16[32,4096]{1,0:T(8,128)(2,1)S(1)}, u32[]{:S(2)}, u32[]{:S(2)}) %collective-permute-start.3) | collective-permute-done | bytes 262176 | tf_op jit(solution)/shard_map/ppermute | solution.py:17
  17.6 2.4 %collective-permute-done.2.refs_1_ = bf16[32,4096]{1,0:T(8,128)(2,1)S(1)} collective-permute-done((bf16[32,4096]{1,0:T(8,128)(2,1)S(1)}, bf16[32,4096]{1,0:T(8,128)(2,1)S(1)}, u32[]{:S(2)}, u32[]{:S(2)}) %collective-permute-start.2) | collective-permute-done | bytes 262176 | tf_op jit(solution)/shard_map/ppermute | solution.py:17
  20.0 1.5 %collective-permute-done.5.refs_1_.refs_3_ = bf16[32,4096]{1,0:T(8,128)(2,1)S(1)} collective-permute-done((bf16[32,4096]{1,0:T(8,128)(2,1)S(1)}, bf16[32,4096]{1,0:T(8,128)(2,1)S(1)}, u32[]{:S(2)}, u32[]{:S(2)}) %collective-permute-start.5) | collective-permute-done | bytes 262176 | tf_op jit(solution)/shard_map/ppermute | solution.py:17
  21.6 2.0 %collective-permute-start.7 = (bf16[64,4096]{1,0:T(8,128)(2,1)S(1)}, bf16[64,4096]{1,0:T(8,128)(2,1)S(1)}, u32[]{:S(2)}, u32[]{:S(2)}) collective-permute-start(bf16[64,4096]{1,0:T(8,128)(2,1)S(1)} %joined.5), channel_id=1, source_target_pairs={{0,4},{1,29},{2,6},{3,31},{4,8},{5,1},{6,10},{7,3},{8,12},{9,5},{1... | collective-permute-start | bytes 1572872 | tf_op jit(solution)/shard_map/ppermute | solution.py:17
  23.6 1.0 collective-permute-start.4
  24.7 0.0 collective-permute-start.6
  24.7 5.3 %collective-permute-done.7.refs_6_ = bf16[64,4096]{1,0:T(8,128)(2,1)S(1)} collective-permute-done((bf16[64,4096]{1,0:T(8,128)(2,1)S(1)}, bf16[64,4096]{1,0:T(8,128)(2,1)S(1)}, u32[]{:S(2)}, u32[]{:S(2)}) %collective-permute-start.7) | collective-permute-done | bytes 524320 | tf_op jit(solution)/shard_map/ppermute | solution.py:17
  30.0 2.2 %collective-permute-start.8 = (bf16[64,4096]{1,0:T(8,128)(2,1)S(1)}, bf16[64,4096]{1,0:T(8,128)(2,1)S(1)}, u32[]{:S(2)}, u32[]{:S(2)}) collective-permute-start(bf16[64,4096]{1,0:T(8,128)(2,1)S(1)} %collective-permute-done.7.refs_6_), channel_id=1, source_target_pairs={{0,1},{1,0},{2,3},{3,2},{4,5},{5,4},{6,7},{7,6},{8,9},{9,8},{10,11... | collective-permute-start | bytes 1572872 | tf_op jit(solution)/shard_map/ppermute | solution.py:17
  32.2 0.7 collective-permute-start.9
  32.9 2.7 %collective-permute-done.4.refs_0_ = bf16[64,4096]{1,0:T(8,128)(2,1)S(1)} collective-permute-done((bf16[64,4096]{1,0:T(8,128)(2,1)S(1)}, bf16[64,4096]{1,0:T(8,128)(2,1)S(1)}, u32[]{:S(2)}, u32[]{:S(2)}) %collective-permute-start.4) | collective-permute-done | bytes 524320 | tf_op jit(solution)/shard_map/ppermute | solution.py:17
  35.6 2.9 %collective-permute-start.10 = (bf16[64,4096]{1,0:T(8,128)(2,1)S(1)}, bf16[64,4096]{1,0:T(8,128)(2,1)S(1)}, u32[]{:S(2)}, u32[]{:S(2)}) collective-permute-start(bf16[64,4096]{1,0:T(8,128)(2,1)S(1)} %collective-permute-done.4.refs_0_), channel_id=1, source_target_pairs={{0,4},{1,29},{2,6},{3,31},{4,8},{5,1},{6,10},{7,3},{8,12},{9,5},{1... | collective-permute-start | bytes 1572872 | tf_op jit(solution)/shard_map/ppermute | solution.py:17
  38.5 0.0 collective-permute-start.11
  38.5 0.0 collective-permute-done.8.refs_7_
  38.5 0.0 copy-start
  38.5 3.4 %copy-done = bf16[1024,1,4096]{2,0,1:T(8,128)(2,1)S(1)} copy-done((bf16[1024,1,4096]{2,0,1:T(8,128)(2,1)S(1)}, bf16[1024,1,4096]{2,0,1:T(8,128)(2,1)}, u32[]{:S(2)}) %copy-start) | copy-done | bytes 8388632
  41.9 3.4 %score.4.refs_0_ = bf16[384,1024]{1,0:T(8,128)(2,1)S(1)} custom-call(bf16[32,4096]{1,0:T(8,128)(2,1)S(1)} %precond.1.refs_0_, bf16[32,4096]{1,0:T(8,128)(2,1)S(1)} %collective-permute-done.refs_1_, bf16[32,4096]{1,0:T(8,128)(2,1)S(1)} %collective-permute-done.3.refs_0_.refs_2_, bf16[32,4096]{1,0:T(8,128)(2,1)S(1)} %collective-permute-done.5.refs_1_.refs_3_, ...), custom_call_target="tpu_custom_call" | custom-call | flops 3221225472 | bytes 12320768 | tf_op jit(solution)/shard_map/score/pallas_call | solution.py:139
  45.3 0.0 collective-permute-done.9.refs_2_
  45.3 0.6 collective-permute-start.12
  45.9 1.9 %collective-permute-start.13 = (bf16[64,4096]{1,0:T(8,128)(2,1)S(1)}, bf16[64,4096]{1,0:T(8,128)(2,1)S(1)}, u32[]{:S(2)}, u32[]{:S(2)}) collective-permute-start(bf16[64,4096]{1,0:T(8,128)(2,1)S(1)} %collective-permute-done.9.refs_2_), channel_id=1, source_target_pairs={{0,4},{1,29},{2,6},{3,31},{4,8},{5,1},{6,10},{7,3},{8,12},{9,5},{1... | collective-permute-start | bytes 1572872 | tf_op jit(solution)/shard_map/ppermute | solution.py:17
  47.8 0.0 collective-permute-done.10.refs_0_
  47.8 1.3 %collective-permute-start.14 = (bf16[64,4096]{1,0:T(8,128)(2,1)S(1)}, bf16[64,4096]{1,0:T(8,128)(2,1)S(1)}, u32[]{:S(2)}, u32[]{:S(2)}) collective-permute-start(bf16[64,4096]{1,0:T(8,128)(2,1)S(1)} %collective-permute-done.10.refs_0_), channel_id=1, source_target_pairs={{0,1},{1,0},{2,3},{3,2},{4,5},{5,4},{6,7},{7,6},{8,9},{9,8},{10,11... | collective-permute-start | bytes 1572872 | tf_op jit(solution)/shard_map/ppermute | solution.py:17
  49.2 0.0 collective-permute-done.11.refs_1_
  49.2 0.0 collective-permute-done.12.refs_3_
  49.2 2.4 %score.5.refs_1_ = bf16[256,1024]{1,0:T(8,128)(2,1)S(1)} custom-call(bf16[64,4096]{1,0:T(8,128)(2,1)S(1)} %collective-permute-done.4.refs_0_, bf16[64,4096]{1,0:T(8,128)(2,1)S(1)} %collective-permute-done.11.refs_1_, bf16[64,4096]{1,0:T(8,128)(2,1)S(1)} %collective-permute-done.9.refs_2_, bf16[64,4096]{1,0:T(8,128)(2,1)S(1)} %collective-permute-done.12.refs_3_, ...), custom_call_target="tpu_custom_call" | custom-call | flops 2147483648 | bytes 11010048 | tf_op jit(solution)/shard_map/score/pallas_call | solution.py:139
  51.5 2.7 %collective-permute-done.13.refs_2_.refs_0_ = bf16[64,4096]{1,0:T(8,128)(2,1)S(1)} collective-permute-done((bf16[64,4096]{1,0:T(8,128)(2,1)S(1)}, bf16[64,4096]{1,0:T(8,128)(2,1)S(1)}, u32[]{:S(2)}, u32[]{:S(2)}) %collective-permute-start.13) | collective-permute-done | bytes 524320 | tf_op jit(solution)/shard_map/ppermute | solution.py:17
  54.2 2.2 %collective-permute-start.15 = (bf16[64,4096]{1,0:T(8,128)(2,1)S(1)}, bf16[64,4096]{1,0:T(8,128)(2,1)S(1)}, u32[]{:S(2)}, u32[]{:S(2)}) collective-permute-start(bf16[64,4096]{1,0:T(8,128)(2,1)S(1)} %collective-permute-done.13.refs_2_.refs_0_), channel_id=1, source_target_pairs={{0,1},{1,0},{2,3},{3,2},{4,5},{5,4},{6,7},{7,6},{8,9},{9,8},{10,11... | collective-permute-start | bytes 1572872 | tf_op jit(solution)/shard_map/ppermute | solution.py:17
  56.4 1.0 collective-permute-start.17
  57.4 0.1 collective-permute-start.16
  57.5 4.4 %collective-permute-done.17.refs_0_ = bf16[32,4096]{1,0:T(8,128)(2,1)S(1)} collective-permute-done((bf16[32,4096]{1,0:T(8,128)(2,1)S(1)}, bf16[32,4096]{1,0:T(8,128)(2,1)S(1)}, u32[]{:S(2)}, u32[]{:S(2)}) %collective-permute-start.17) | collective-permute-done | bytes 262176 | tf_op jit(solution)/shard_map/ppermute | solution.py:17
  61.9 2.1 %collective-permute-start.18 = (bf16[32,4096]{1,0:T(8,128)(2,1)S(1)}, bf16[32,4096]{1,0:T(8,128)(2,1)S(1)}, u32[]{:S(2)}, u32[]{:S(2)}) collective-permute-start(bf16[32,4096]{1,0:T(8,128)(2,1)S(1)} %collective-permute-done.17.refs_0_), channel_id=1, source_target_pairs={{0,1},{1,0},{2,3},{3,2},{4,5},{5,4},{6,7},{7,6},{8,9},{9,8},{10,11... | collective-permute-start | bytes 786440 | tf_op jit(solution)/shard_map/ppermute | solution.py:17
  64.0 0.0 collective-permute-done.14.refs_1_
  64.0 0.0 collective-permute-done.15.refs_3_
  64.0 2.4 %score.6.refs_2_ = bf16[256,1024]{1,0:T(8,128)(2,1)S(1)} custom-call(bf16[64,4096]{1,0:T(8,128)(2,1)S(1)} %collective-permute-done.10.refs_0_, bf16[64,4096]{1,0:T(8,128)(2,1)S(1)} %collective-permute-done.14.refs_1_, bf16[64,4096]{1,0:T(8,128)(2,1)S(1)} %collective-permute-done.13.refs_2_.refs_0_, bf16[64,4096]{1,0:T(8,128)(2,1)S(1)} %collective-permute-done.15.refs_3_, ...), custom_call_target="tpu_custom_call" | custom-call | flops 2147483648 | bytes 11010048 | tf_op jit(solution)/shard_map/score/pallas_call | solution.py:139
  66.3 0.4 collective-permute-start.19
  66.8 1.2 %collective-permute-done.19.refs_3_ = bf16[32,4096]{1,0:T(8,128)(2,1)S(1)} collective-permute-done((bf16[32,4096]{1,0:T(8,128)(2,1)S(1)}, bf16[32,4096]{1,0:T(8,128)(2,1)S(1)}, u32[]{:S(2)}, u32[]{:S(2)}) %collective-permute-start.19) | collective-permute-done | bytes 262176 | tf_op jit(solution)/shard_map/ppermute | solution.py:17
  68.0 2.9 %score.7.refs_3_ = bf16[128,1024]{1,0:T(8,128)(2,1)S(1)} custom-call(bf16[32,4096]{1,0:T(8,128)(2,1)S(1)} %collective-permute-done.17.refs_0_, bf16[32,4096]{1,0:T(8,128)(2,1)S(1)} %collective-permute-done.18.refs_1_, bf16[32,4096]{1,0:T(8,128)(2,1)S(1)} %collective-permute-done.16.refs_2_, bf16[32,4096]{1,0:T(8,128)(2,1)S(1)} %collective-permute-done.19.refs_3_, ...), custom_call_target="tpu_custom_call" | custom-call | flops 1073741824 | bytes 9699328 | tf_op jit(solution)/shard_map/score/pallas_call | solution.py:139
  70.8 0.7 place.1
  71.5 30.8 %all_to_all.5.in_ref = bf16[8,128,1024]{2,1,0:T(8,128)(2,1)S(1)} all-to-all(bf16[8,128,1024]{2,1,0:T(8,128)(2,1)S(1)} %bitcast.41), channel_id=1, replica_groups=mesh['group'=8,'blk'=32] {'group'}, dimensions={0} | all-to-all | bytes 4194304 | tf_op jit(solution)/shard_map/all_to_all | solution.py:259
  102.4 1.9 %total.1 = f32[1024,128]{1,0:T(8,128)} custom-call(bf16[8,128,1024]{2,1,0:T(8,128)(2,1)S(1)} %all_to_all.5.in_ref), custom_call_target="tpu_custom_call" | custom-call | tf_op jit(solution)/shard_map/total/pallas_call | solution.py:184
  (10 shorter events, 0.1 us)
Async XLA Ops:
  3.7 11.0 %collective-permute-start = (bf16[32,4096]{1,0:T(8,128)(2,1)S(1)}, bf16[32,4096]{1,0:T(8,128)(2,1)S(1)}, u32[]{:S(2)}, u32[]{:S(2)}) collective-permute-start(bf16[32,4096]{1,0:T(8,128)(2,1)S(1)} %precond.1.refs_0_), channel_id=1, source_target_pairs={{0,1},{1,0},{2,3},{3,2},{4,5},{5,4},{6,7},{7,6},{8,9},{9,8},{10,11... | collective-permute-start | bytes 786440 | tf_op jit(solution)/shard_map/ppermute | solution.py:17
  7.0 8.5 %collective-permute-start.1 = (bf16[32,4096]{1,0:T(8,128)(2,1)S(1)}, bf16[32,4096]{1,0:T(8,128)(2,1)S(1)}, u32[]{:S(2)}, u32[]{:S(2)}) collective-permute-start(bf16[32,4096]{1,0:T(8,128)(2,1)S(1)} %precond.1.refs_0_), channel_id=1, source_target_pairs={{0,4},{1,29},{2,6},{3,31},{4,8},{5,1},{6,10},{7,3},{8,12},{9,5},{1... | collective-permute-start | bytes 786440 | tf_op jit(solution)/shard_map/ppermute | solution.py:17
  10.8 6.7 %collective-permute-start.3 = (bf16[32,4096]{1,0:T(8,128)(2,1)S(1)}, bf16[32,4096]{1,0:T(8,128)(2,1)S(1)}, u32[]{:S(2)}, u32[]{:S(2)}) collective-permute-start(bf16[32,4096]{1,0:T(8,128)(2,1)S(1)} %precond.1.refs_0_), channel_id=1, source_target_pairs={{0,2},{1,3},{2,0},{3,1},{4,6},{5,7},{6,4},{7,5},{8,10},{9,11},{10,... | collective-permute-start | bytes 786440 | tf_op jit(solution)/shard_map/ppermute | solution.py:17
  14.7 5.3 %collective-permute-start.2 = (bf16[32,4096]{1,0:T(8,128)(2,1)S(1)}, bf16[32,4096]{1,0:T(8,128)(2,1)S(1)}, u32[]{:S(2)}, u32[]{:S(2)}) collective-permute-start(bf16[32,4096]{1,0:T(8,128)(2,1)S(1)} %collective-permute-done.refs_1_), channel_id=1, source_target_pairs={{0,4},{1,29},{2,6},{3,31},{4,8},{5,1},{6,10},{7,3},{8,12},{9,5},{1... | collective-permute-start | bytes 786440 | tf_op jit(solution)/shard_map/ppermute | solution.py:17
  20.0 1.5 %collective-permute-start.5 = (bf16[32,4096]{1,0:T(8,128)(2,1)S(1)}, bf16[32,4096]{1,0:T(8,128)(2,1)S(1)}, u32[]{:S(2)}, u32[]{:S(2)}) collective-permute-start(bf16[32,4096]{1,0:T(8,128)(2,1)S(1)} %collective-permute-done.3.refs_0_.refs_2_), channel_id=1, source_target_pairs={{0,1},{1,0},{2,3},{3,2},{4,5},{5,4},{6,7},{7,6},{8,9},{9,8},{10,11... | collective-permute-start | bytes 786440 | tf_op jit(solution)/shard_map/ppermute | solution.py:17
  21.6 8.4 %collective-permute-start.7 = (bf16[64,4096]{1,0:T(8,128)(2,1)S(1)}, bf16[64,4096]{1,0:T(8,128)(2,1)S(1)}, u32[]{:S(2)}, u32[]{:S(2)}) collective-permute-start(bf16[64,4096]{1,0:T(8,128)(2,1)S(1)} %joined.5), channel_id=1, source_target_pairs={{0,4},{1,29},{2,6},{3,31},{4,8},{5,1},{6,10},{7,3},{8,12},{9,5},{1... | collective-permute-start | bytes 1572872 | tf_op jit(solution)/shard_map/ppermute | solution.py:17
  23.6 12.0 %collective-permute-start.4 = (bf16[64,4096]{1,0:T(8,128)(2,1)S(1)}, bf16[64,4096]{1,0:T(8,128)(2,1)S(1)}, u32[]{:S(2)}, u32[]{:S(2)}) collective-permute-start(bf16[64,4096]{1,0:T(8,128)(2,1)S(1)} %joined.4.refs_4_), channel_id=1, source_target_pairs={{0,4},{1,29},{2,6},{3,31},{4,8},{5,1},{6,10},{7,3},{8,12},{9,5},{1... | collective-permute-start | bytes 1572872 | tf_op jit(solution)/shard_map/ppermute | solution.py:17
  24.7 13.8 %collective-permute-start.6 = (bf16[64,4096]{1,0:T(8,128)(2,1)S(1)}, bf16[64,4096]{1,0:T(8,128)(2,1)S(1)}, u32[]{:S(2)}, u32[]{:S(2)}) collective-permute-start(bf16[64,4096]{1,0:T(8,128)(2,1)S(1)} %joined.4.refs_4_), channel_id=1, source_target_pairs={{0,1},{1,0},{2,3},{3,2},{4,5},{5,4},{6,7},{7,6},{8,9},{9,8},{10,11... | collective-permute-start | bytes 1572872 | tf_op jit(solution)/shard_map/ppermute | solution.py:17
  30.0 8.5 %collective-permute-start.8 = (bf16[64,4096]{1,0:T(8,128)(2,1)S(1)}, bf16[64,4096]{1,0:T(8,128)(2,1)S(1)}, u32[]{:S(2)}, u32[]{:S(2)}) collective-permute-start(bf16[64,4096]{1,0:T(8,128)(2,1)S(1)} %collective-permute-done.7.refs_6_), channel_id=1, source_target_pairs={{0,1},{1,0},{2,3},{3,2},{4,5},{5,4},{6,7},{7,6},{8,9},{9,8},{10,11... | collective-permute-start | bytes 1572872 | tf_op jit(solution)/shard_map/ppermute | solution.py:17
  32.2 13.1 %collective-permute-start.9 = (bf16[64,4096]{1,0:T(8,128)(2,1)S(1)}, bf16[64,4096]{1,0:T(8,128)(2,1)S(1)}, u32[]{:S(2)}, u32[]{:S(2)}) collective-permute-start(bf16[64,4096]{1,0:T(8,128)(2,1)S(1)} %collective-permute-done.7.refs_6_), channel_id=1, source_target_pairs={{0,4},{1,29},{2,6},{3,31},{4,8},{5,1},{6,10},{7,3},{8,12},{9,5},{1... | collective-permute-start | bytes 1572872 | tf_op jit(solution)/shard_map/ppermute | solution.py:17
  35.6 12.2 %collective-permute-start.10 = (bf16[64,4096]{1,0:T(8,128)(2,1)S(1)}, bf16[64,4096]{1,0:T(8,128)(2,1)S(1)}, u32[]{:S(2)}, u32[]{:S(2)}) collective-permute-start(bf16[64,4096]{1,0:T(8,128)(2,1)S(1)} %collective-permute-done.4.refs_0_), channel_id=1, source_target_pairs={{0,4},{1,29},{2,6},{3,31},{4,8},{5,1},{6,10},{7,3},{8,12},{9,5},{1... | collective-permute-start | bytes 1572872 | tf_op jit(solution)/shard_map/ppermute | solution.py:17
  38.5 10.7 %collective-permute-start.11 = (bf16[64,4096]{1,0:T(8,128)(2,1)S(1)}, bf16[64,4096]{1,0:T(8,128)(2,1)S(1)}, u32[]{:S(2)}, u32[]{:S(2)}) collective-permute-start(bf16[64,4096]{1,0:T(8,128)(2,1)S(1)} %collective-permute-done.4.refs_0_), channel_id=1, source_target_pairs={{0,1},{1,0},{2,3},{3,2},{4,5},{5,4},{6,7},{7,6},{8,9},{9,8},{10,11... | collective-permute-start | bytes 1572872 | tf_op jit(solution)/shard_map/ppermute | solution.py:17
  38.5 3.4 %copy-start = (bf16[1024,1,4096]{2,0,1:T(8,128)(2,1)S(1)}, bf16[1024,1,4096]{2,0,1:T(8,128)(2,1)}, u32[]{:S(2)}) copy-start(bf16[1024,1,4096]{2,0,1:T(8,128)(2,1)} %param.5) | copy-start | bytes 25165828
  41.9 7.3 %copy-start.1 = (bf16[1024,1,4096]{2,0,1:T(8,128)(2,1)S(1)}, bf16[1024,1,4096]{2,0,1:T(8,128)(2,1)}, u32[]{:S(2)}) copy-start(bf16[1024,1,4096]{2,0,1:T(8,128)(2,1)} %param.5) | copy-start | bytes 25165828
  45.3 3.9 %collective-permute-start.12 = (bf16[64,4096]{1,0:T(8,128)(2,1)S(1)}, bf16[64,4096]{1,0:T(8,128)(2,1)S(1)}, u32[]{:S(2)}, u32[]{:S(2)}) collective-permute-start(bf16[64,4096]{1,0:T(8,128)(2,1)S(1)} %collective-permute-done.9.refs_2_), channel_id=1, source_target_pairs={{0,1},{1,0},{2,3},{3,2},{4,5},{5,4},{6,7},{7,6},{8,9},{9,8},{10,11... | collective-permute-start | bytes 1572872 | tf_op jit(solution)/shard_map/ppermute | solution.py:17
  45.9 8.3 %collective-permute-start.13 = (bf16[64,4096]{1,0:T(8,128)(2,1)S(1)}, bf16[64,4096]{1,0:T(8,128)(2,1)S(1)}, u32[]{:S(2)}, u32[]{:S(2)}) collective-permute-start(bf16[64,4096]{1,0:T(8,128)(2,1)S(1)} %collective-permute-done.9.refs_2_), channel_id=1, source_target_pairs={{0,4},{1,29},{2,6},{3,31},{4,8},{5,1},{6,10},{7,3},{8,12},{9,5},{1... | collective-permute-start | bytes 1572872 | tf_op jit(solution)/shard_map/ppermute | solution.py:17
  47.8 16.2 %collective-permute-start.14 = (bf16[64,4096]{1,0:T(8,128)(2,1)S(1)}, bf16[64,4096]{1,0:T(8,128)(2,1)S(1)}, u32[]{:S(2)}, u32[]{:S(2)}) collective-permute-start(bf16[64,4096]{1,0:T(8,128)(2,1)S(1)} %collective-permute-done.10.refs_0_), channel_id=1, source_target_pairs={{0,1},{1,0},{2,3},{3,2},{4,5},{5,4},{6,7},{7,6},{8,9},{9,8},{10,11... | collective-permute-start | bytes 1572872 | tf_op jit(solution)/shard_map/ppermute | solution.py:17
  54.2 9.7 %collective-permute-start.15 = (bf16[64,4096]{1,0:T(8,128)(2,1)S(1)}, bf16[64,4096]{1,0:T(8,128)(2,1)S(1)}, u32[]{:S(2)}, u32[]{:S(2)}) collective-permute-start(bf16[64,4096]{1,0:T(8,128)(2,1)S(1)} %collective-permute-done.13.refs_2_.refs_0_), channel_id=1, source_target_pairs={{0,1},{1,0},{2,3},{3,2},{4,5},{5,4},{6,7},{7,6},{8,9},{9,8},{10,11... | collective-permute-start | bytes 1572872 | tf_op jit(solution)/shard_map/ppermute | solution.py:17
  56.4 5.5 %collective-permute-start.17 = (bf16[32,4096]{1,0:T(8,128)(2,1)S(1)}, bf16[32,4096]{1,0:T(8,128)(2,1)S(1)}, u32[]{:S(2)}, u32[]{:S(2)}) collective-permute-start(bf16[32,4096]{1,0:T(8,128)(2,1)S(1)} %joined.6), channel_id=1, source_target_pairs={{0,4},{1,29},{2,6},{3,31},{4,8},{5,1},{6,10},{7,3},{8,12},{9,5},{1... | collective-permute-start | bytes 786440 | tf_op jit(solution)/shard_map/ppermute | solution.py:17
  57.4 8.9 %collective-permute-start.16 = (bf16[32,4096]{1,0:T(8,128)(2,1)S(1)}, bf16[32,4096]{1,0:T(8,128)(2,1)S(1)}, u32[]{:S(2)}, u32[]{:S(2)}) collective-permute-start(bf16[32,4096]{1,0:T(8,128)(2,1)S(1)} %joined.7), channel_id=1, source_target_pairs={{0,4},{1,29},{2,6},{3,31},{4,8},{5,1},{6,10},{7,3},{8,12},{9,5},{1... | collective-permute-start | bytes 786440 | tf_op jit(solution)/shard_map/ppermute | solution.py:17
  61.9 4.9 %collective-permute-start.18 = (bf16[32,4096]{1,0:T(8,128)(2,1)S(1)}, bf16[32,4096]{1,0:T(8,128)(2,1)S(1)}, u32[]{:S(2)}, u32[]{:S(2)}) collective-permute-start(bf16[32,4096]{1,0:T(8,128)(2,1)S(1)} %collective-permute-done.17.refs_0_), channel_id=1, source_target_pairs={{0,1},{1,0},{2,3},{3,2},{4,5},{5,4},{6,7},{7,6},{8,9},{9,8},{10,11... | collective-permute-start | bytes 786440 | tf_op jit(solution)/shard_map/ppermute | solution.py:17
  66.3 1.6 %collective-permute-start.19 = (bf16[32,4096]{1,0:T(8,128)(2,1)S(1)}, bf16[32,4096]{1,0:T(8,128)(2,1)S(1)}, u32[]{:S(2)}, u32[]{:S(2)}) collective-permute-start(bf16[32,4096]{1,0:T(8,128)(2,1)S(1)} %collective-permute-done.16.refs_2_), channel_id=1, source_target_pairs={{0,1},{1,0},{2,3},{3,2},{4,5},{5,4},{6,7},{7,6},{8,9},{9,8},{10,11... | collective-permute-start | bytes 786440 | tf_op jit(solution)/shard_map/ppermute | solution.py:17

commit v7 on v6

--- a/solution.py
+++ b/solution.py
@@ -122,6 +122,18 @@
     )(*parts)
 
 
+def _held(x):
+    return pl.pallas_call(
+        pltpu.sync_copy,
+        in_specs=[pl.BlockSpec(memory_space=pl.ANY)],
+        out_specs=pl.BlockSpec(memory_space=pltpu.VMEM),
+        out_shape=pltpu.VMEM(x.shape, x.dtype),
+        compiler_params=pltpu.CompilerParams(vmem_limit_bytes=1 << 20),
+        cost_estimate=pl.CostEstimate(flops=0, bytes_accessed=2 * x.size * 2, transcendentals=0),
+        name="held",
+    )(x)
+
+
 def _score_kernel(scale, count, *refs):
     c_ref, o_ref = refs[count], refs[count + 1]
     panels = jnp.concatenate([r[...] for r in refs[:count]], axis=0)
@@ -166,26 +178,60 @@
         in_specs=[pl.BlockSpec(memory_space=pltpu.SMEM)]
         + [pl.BlockSpec(memory_space=pltpu.VMEM) for _ in parts],
         out_specs=pl.BlockSpec(memory_space=pltpu.VMEM),
-        out_shape=jax.ShapeDtypeStruct((sum(counts), PANEL, rows), jnp.bfloat16),
+        out_shape=jax.ShapeDtypeStruct((where.shape[0], PANEL, rows), jnp.bfloat16),
         compiler_params=pltpu.CompilerParams(vmem_limit_bytes=12 << 20),
         name="place",
     )(where, *parts)
 
 
+def _finish_kernel(scale, count, where_ref, *refs):
+    c_ref, o_ref = refs[count], refs[count + 2]
+    first = where_ref.shape[0] - count
+    panels = jnp.concatenate([r[...] for r in refs[:count]], axis=0)
+    for i in range(c_ref.shape[0] // CBLK):
+        block = slice(i * CBLK, (i + 1) * CBLK)
+        part = lax.dot_general(
+            panels, c_ref[block, :], (((1,), (1,)), ((), ())), preferred_element_type=jnp.float32
+        )
+        part = (part * scale).astype(o_ref.dtype)
+        for j in range(count):
+            o_ref[where_ref[first + j], :, block] = part[j * PANEL : (j + 1) * PANEL, :]
+
+
+def _finish(pieces, flat, scale, where, early):
+    rows, feats = flat.shape
+    n = len(pieces) * PANEL
+    return pl.pallas_call(
+        functools.partial(_finish_kernel, scale, len(pieces)),
+        in_specs=[pl.BlockSpec(memory_space=pltpu.SMEM)]
+        + [pl.BlockSpec(memory_space=pltpu.VMEM) for _ in range(len(pieces) + 2)],
+        out_specs=pl.BlockSpec(memory_space=pltpu.VMEM),
+        out_shape=jax.ShapeDtypeStruct(early.shape, early.dtype),
+        input_output_aliases={len(pieces) + 2: 0},
+        compiler_params=pltpu.CompilerParams(vmem_limit_bytes=16 << 20),
+        cost_estimate=pl.CostEstimate(
+            flops=2 * n * rows * feats, bytes_accessed=2 * (rows * feats + n * feats + n * rows), transcendentals=0
+        ),
+        name="finish",
+    )(where, *pieces, flat, early)
+
+
 def _total_kernel(in_ref, o_ref):
-    total = in_ref[0].astype(jnp.float32)
-    for g in range(1, in_ref.shape[0]):
-        total += in_ref[g].astype(jnp.float32)
-    o_ref[...] = total.T
+    width = in_ref.shape[1]
+    for i in range(in_ref.shape[2] // width):
+        block = slice(i * width, (i + 1) * width)
+        total = in_ref[0, :, block].astype(jnp.float32)
+        for g in range(1, in_ref.shape[0]):
+            total += in_ref[g, :, block].astype(jnp.float32)
+        o_ref[block, :] = total.T
 
 
 def _total(parts):
     groups, width, rows = parts.shape
     return pl.pallas_call(
         _total_kernel,
-        grid=(rows // CBLK,),
-        in_specs=[pl.BlockSpec((groups, width, CBLK), lambda i: (0, 0, i))],
-        out_specs=pl.BlockSpec((CBLK, width), lambda i: (i, 0)),
+        in_specs=[pl.BlockSpec(memory_space=pltpu.VMEM)],
+        out_specs=pl.BlockSpec(memory_space=pltpu.VMEM),
         out_shape=jax.ShapeDtypeStruct((rows, width), jnp.float32),
         compiler_params=pltpu.CompilerParams(vmem_limit_bytes=12 << 20),
         name="total",
@@ -200,7 +246,6 @@
     panel = _precond(out_factor[0], in_factor[0], queries.reshape(width, layer_count * features))
     flat = candidates.reshape(cand_rows, layer_count * features)
 
-    flat = pltpu.with_memory_space_constraint(flat, pltpu.VMEM)
     me = lax.axis_index("blk")
     z, rest = me // 4, me % 4
     core = me % 2
@@ -236,26 +281,28 @@
     other = _swap_core(panel)
     other, where = lax.optimization_barrier((other, where))
     own, next_to = _along(panel), _along(other)
-    own, next_to, across = lax.optimization_barrier((own, next_to, across))
+    flat = _held(pltpu.with_memory_space_constraint(flat, pltpu.HBM))
+    own, next_to, across, flat = lax.optimization_barrier((own, next_to, across, flat))
     near = _joined(own, next_to)
     across_other = _swap_core(across)
     far = _along(_joined(across, across_other))
     pieces = [panel, other, across, across_other, near, _swap_core(near), far, _swap_core(far)]
-    for s in range(2, NZ // 2 + 1):
-        if s < NZ // 2:
-            near, far = _along(near), _along(far)
-        else:
-            near, far = _along(cut), _along(_joined(far))
+    for s in range(2, NZ // 2):
+        near, far = _along(near), _along(far)
+        cut = _joined(near)
+        near, cut, pieces[0] = lax.optimization_barrier((near, cut, pieces[0]))
+        steps.append(_score(pieces, flat, scale))
         if s == NZ // 2 - 1:
-            cut = _joined(near)
-            near, cut, pieces[0] = lax.optimization_barrier((near, cut, pieces[0]))
-        elif s < NZ // 2:
-            near, pieces[0] = lax.optimization_barrier((near, pieces[0]))
-        steps.append(_score(pieces, flat, scale))
+            steps[-1], last = lax.optimization_barrier((steps[-1], _along(cut)))
+            last, far = lax.optimization_barrier((last, far))
         steps[-1], far = lax.optimization_barrier((steps[-1], far))
         pieces = [near, _swap_core(near), far, _swap_core(far)]
+    beyond = _along(_joined(far))
     steps.append(_score(pieces, flat, scale))
-    buffer = _place(steps, where).reshape(groups, -1, cand_rows)
+    early = _place(steps, where)
+    early, beyond = lax.optimization_barrier((early, beyond))
+    buffer = _finish([last, _swap_core(last), beyond, _swap_core(beyond)], flat, scale, where, early)
+    buffer = buffer.reshape(groups, -1, cand_rows)
     parts = lax.all_to_all(buffer, "group", split_axis=0, concat_axis=0, tiled=True)
     return _total(parts)
 

time: 104 us -> 103 us (level)
  local copies, waits for them, and re-layouts: 3.49 us -> 0.11 us
  Pallas kernels: 17.4 us -> 20.5 us
  waiting for transfers between devices: 22.4 us -> 19.6 us
  starting transfers between devices: 29.3 us -> 31.2 us
    pallas_call x1 -> x3, Pallas kernels: 1.95 us -> 7.91 us  [the longest x1 3.41 us: _finish(): pl.pallas_call(functools.partial(_finish_kernel, scale, len(pieces)), in_...]
    unnamed x4 -> x0, local copies, waits for them, and re-layouts: 3.38 us -> none
    pallas_call x4 -> x3, Pallas kernels: 11 us -> 8.15 us  [_score(): pl.pallas_call(functools.partial(_score_kernel, scale, len(pieces)), in_s...]
    ppermute x20, waiting for transfers between devices: 22.4 us -> 19.6 us  [_route(): lax.ppermute(x, 'blk', [(i, target(*divmod(i, 4))) for i in range(NZ * 4)])]
    ppermute x20, starting transfers between devices: 29.3 us -> 31.2 us  [_route(): lax.ppermute(x, 'blk', [(i, target(*divmod(i, 4))) for i in range(NZ * 4)])]
  transfers between devices with their start and end apart: 20 -> 20, of which waited for: 8 -> 9; matrix products, arithmetic and copies ran while one was open for 1% -> 1% of each run, Pallas kernels for 8% -> 12%
where the time goes in v7:
time: 103 us
  starting transfers between devices  31.2 us (30%)
  blocking collectives  30.3 us (29%)
  Pallas kernels  20.5 us (20%)
  waiting for transfers between devices  19.6 us (19%)
    ppermute x20, starting transfers between devices, _route(): lax.ppermute(x, 'blk', [(i, target(*divmod(i, 4))) for i in range(NZ * 4)])  31.2 us
    all_to_all x1, blocking collectives, body(): lax.all_to_all(buffer, 'group', split_axis=0, concat_axis=0, tiled=True)  30.3 us
    ppermute x20, waiting for transfers between devices, _route(): lax.ppermute(x, 'blk', [(i, target(*divmod(i, 4))) for i in range(NZ * 4)])  19.6 us
    pallas_call x3, Pallas kernels, _score(): pl.pallas_call(functools.partial(_score_kernel, scale, len(pieces)), in_s...  8.15 us
    pallas_call x1, Pallas kernels, _precond(): pl.pallas_call(_precond_kernel, in_specs=[pl.BlockSpec(memory_space=pltpu...  3.66 us
    pallas_call x1, Pallas kernels, _finish(): pl.pallas_call(functools.partial(_finish_kernel, scale, len(pieces)), in_...  3.41 us
    pallas_call x1, Pallas kernels, _held(): pl.pallas_call(pltpu.sync_copy, in_specs=[pl.BlockSpec(memory_space=pl.AN...  3.38 us
  transfers between devices with their start and end apart: 20, of which 9 were waited for; matrix products, arithmetic and copies ran while one was open for 1% of the time, Pallas kernels for 12%

profile of v7, /device:TPU:1, one launch (start us, length us, event | category | flops | bytes accessed | tf_op | source)
XLA Modules:
  0.0 102.6 jit_solution(5754104847914110943)
XLA Ops:
  0.0 3.7 %precond.1.refs_0_ = bf16[32,4096]{1,0:T(8,128)(2,1)S(1)} custom-call(f32[64,64]{1,0:T(8,128)} %bitcast.40, f32[64,64]{1,0:T(8,128)} %bitcast.41, bf16[32,4096]{1,0:T(8,128)(2,1)} %bitcast.39), custom_call_target="tpu_custom_call" | custom-call | tf_op jit(solution)/shard_map/precond/pallas_call | solution.py:90
  3.7 3.3 %collective-permute-start = (bf16[32,4096]{1,0:T(8,128)(2,1)S(1)}, bf16[32,4096]{1,0:T(8,128)(2,1)S(1)}, u32[]{:S(2)}, u32[]{:S(2)}) collective-permute-start(bf16[32,4096]{1,0:T(8,128)(2,1)S(1)} %precond.1.refs_0_), channel_id=1, source_target_pairs={{0,1},{1,0},{2,3},{3,2},{4,5},{5,4},{6,7},{7,6},{8,9},{9,8},{10,11... | collective-permute-start | bytes 786440 | tf_op jit(solution)/shard_map/ppermute | solution.py:17
  7.0 1.2 %collective-permute-start.3 = (bf16[32,4096]{1,0:T(8,128)(2,1)S(1)}, bf16[32,4096]{1,0:T(8,128)(2,1)S(1)}, u32[]{:S(2)}, u32[]{:S(2)}) collective-permute-start(bf16[32,4096]{1,0:T(8,128)(2,1)S(1)} %precond.1.refs_0_), channel_id=1, source_target_pairs={{0,2},{1,3},{2,0},{3,1},{4,6},{5,7},{6,4},{7,5},{8,10},{9,11},{10,... | collective-permute-start | bytes 786440 | tf_op jit(solution)/shard_map/ppermute | solution.py:17
  8.2 5.6 %collective-permute-start.1 = (bf16[32,4096]{1,0:T(8,128)(2,1)S(1)}, bf16[32,4096]{1,0:T(8,128)(2,1)S(1)}, u32[]{:S(2)}, u32[]{:S(2)}) collective-permute-start(bf16[32,4096]{1,0:T(8,128)(2,1)S(1)} %precond.1.refs_0_), channel_id=1, source_target_pairs={{0,4},{1,29},{2,6},{3,31},{4,8},{5,1},{6,10},{7,3},{8,12},{9,5},{1... | collective-permute-start | bytes 786440 | tf_op jit(solution)/shard_map/ppermute | solution.py:17
  13.8 0.1 stack.131
  13.9 0.8 select_reduce_fusion.where_ref
  14.7 0.0 collective-permute-done.refs_1_
  14.7 0.8 collective-permute-start.2
  15.5 3.4 %held.1.refs_8_.refs_4_ = bf16[1024,4096]{1,0:T(8,128)(2,1)S(1)} custom-call(bf16[1024,4096]{1,0:T(8,128)(2,1)} %bitcast.38), custom_call_target="tpu_custom_call" | custom-call | bytes 16777216 | tf_op jit(solution)/shard_map/held/pallas_call | solution.py:126
  18.9 0.0 collective-permute-done.3.refs_0_.refs_2_
  18.9 0.0 collective-permute-done.1.refs_0_
  18.9 1.4 %collective-permute-done.2.refs_1_ = bf16[32,4096]{1,0:T(8,128)(2,1)S(1)} collective-permute-done((bf16[32,4096]{1,0:T(8,128)(2,1)S(1)}, bf16[32,4096]{1,0:T(8,128)(2,1)S(1)}, u32[]{:S(2)}, u32[]{:S(2)}) %collective-permute-start.2) | collective-permute-done | bytes 262176 | tf_op jit(solution)/shard_map/ppermute | solution.py:17
  20.3 1.2 %collective-permute-start.7 = (bf16[32,4096]{1,0:T(8,128)(2,1)S(1)}, bf16[32,4096]{1,0:T(8,128)(2,1)S(1)}, u32[]{:S(2)}, u32[]{:S(2)}) collective-permute-start(bf16[32,4096]{1,0:T(8,128)(2,1)S(1)} %collective-permute-done.3.refs_0_.refs_2_), channel_id=1, source_target_pairs={{0,1},{1,0},{2,3},{3,2},{4,5},{5,4},{6,7},{7,6},{8,9},{9,8},{10,11... | collective-permute-start | bytes 786440 | tf_op jit(solution)/shard_map/ppermute | solution.py:17
  21.6 1.2 %collective-permute-done.7.refs_1_.refs_3_ = bf16[32,4096]{1,0:T(8,128)(2,1)S(1)} collective-permute-done((bf16[32,4096]{1,0:T(8,128)(2,1)S(1)}, bf16[32,4096]{1,0:T(8,128)(2,1)S(1)}, u32[]{:S(2)}, u32[]{:S(2)}) %collective-permute-start.7) | collective-permute-done | bytes 262176 | tf_op jit(solution)/shard_map/ppermute | solution.py:17
  22.8 1.9 %collective-permute-start.9 = (bf16[64,4096]{1,0:T(8,128)(2,1)S(1)}, bf16[64,4096]{1,0:T(8,128)(2,1)S(1)}, u32[]{:S(2)}, u32[]{:S(2)}) collective-permute-start(bf16[64,4096]{1,0:T(8,128)(2,1)S(1)} %joined.7), channel_id=1, source_target_pairs={{0,4},{1,29},{2,6},{3,31},{4,8},{5,1},{6,10},{7,3},{8,12},{9,5},{1... | collective-permute-start | bytes 1572872 | tf_op jit(solution)/shard_map/ppermute | solution.py:17
  24.7 0.7 collective-permute-start.4
  25.4 0.0 collective-permute-start.8
  25.4 5.7 %collective-permute-done.9.refs_6_ = bf16[64,4096]{1,0:T(8,128)(2,1)S(1)} collective-permute-done((bf16[64,4096]{1,0:T(8,128)(2,1)S(1)}, bf16[64,4096]{1,0:T(8,128)(2,1)S(1)}, u32[]{:S(2)}, u32[]{:S(2)}) %collective-permute-start.9) | collective-permute-done | bytes 524320 | tf_op jit(solution)/shard_map/ppermute | solution.py:17
  31.2 2.4 %collective-permute-start.10 = (bf16[64,4096]{1,0:T(8,128)(2,1)S(1)}, bf16[64,4096]{1,0:T(8,128)(2,1)S(1)}, u32[]{:S(2)}, u32[]{:S(2)}) collective-permute-start(bf16[64,4096]{1,0:T(8,128)(2,1)S(1)} %collective-permute-done.9.refs_6_), channel_id=1, source_target_pairs={{0,1},{1,0},{2,3},{3,2},{4,5},{5,4},{6,7},{7,6},{8,9},{9,8},{10,11... | collective-permute-start | bytes 1572872 | tf_op jit(solution)/shard_map/ppermute | solution.py:17
  33.6 0.5 collective-permute-start.11
  34.1 2.6 %collective-permute-done.4.refs_0_ = bf16[64,4096]{1,0:T(8,128)(2,1)S(1)} collective-permute-done((bf16[64,4096]{1,0:T(8,128)(2,1)S(1)}, bf16[64,4096]{1,0:T(8,128)(2,1)S(1)}, u32[]{:S(2)}, u32[]{:S(2)}) %collective-permute-start.4) | collective-permute-done | bytes 524320 | tf_op jit(solution)/shard_map/ppermute | solution.py:17
  36.8 2.4 %collective-permute-start.6 = (bf16[64,4096]{1,0:T(8,128)(2,1)S(1)}, bf16[64,4096]{1,0:T(8,128)(2,1)S(1)}, u32[]{:S(2)}, u32[]{:S(2)}) collective-permute-start(bf16[64,4096]{1,0:T(8,128)(2,1)S(1)} %collective-permute-done.4.refs_0_), channel_id=1, source_target_pairs={{0,1},{1,0},{2,3},{3,2},{4,5},{5,4},{6,7},{7,6},{8,9},{9,8},{10,11... | collective-permute-start | bytes 1572872 | tf_op jit(solution)/shard_map/ppermute | solution.py:17
  39.2 0.5 collective-permute-start.5
  39.8 0.0 collective-permute-done.8.refs_5_
  39.8 0.0 collective-permute-done.10.refs_7_
  39.8 3.4 %score.3.refs_0_ = bf16[384,1024]{1,0:T(8,128)(2,1)S(1)} custom-call(bf16[32,4096]{1,0:T(8,128)(2,1)S(1)} %precond.1.refs_0_, bf16[32,4096]{1,0:T(8,128)(2,1)S(1)} %collective-permute-done.refs_1_, bf16[32,4096]{1,0:T(8,128)(2,1)S(1)} %collective-permute-done.3.refs_0_.refs_2_, bf16[32,4096]{1,0:T(8,128)(2,1)S(1)} %collective-permute-done.7.refs_1_.refs_3_, ...), custom_call_target="tpu_custom_call" | custom-call | flops 3221225472 | bytes 12320768 | tf_op jit(solution)/shard_map/score/pallas_call | solution.py:151
  43.2 0.0 collective-permute-done.11.refs_2_
  43.2 1.6 %collective-permute-start.12 = (bf16[64,4096]{1,0:T(8,128)(2,1)S(1)}, bf16[64,4096]{1,0:T(8,128)(2,1)S(1)}, u32[]{:S(2)}, u32[]{:S(2)}) collective-permute-start(bf16[64,4096]{1,0:T(8,128)(2,1)S(1)} %collective-permute-done.11.refs_2_), channel_id=1, source_target_pairs={{0,1},{1,0},{2,3},{3,2},{4,5},{5,4},{6,7},{7,6},{8,9},{9,8},{10,11... | collective-permute-start | bytes 1572872 | tf_op jit(solution)/shard_map/ppermute | solution.py:17
  44.8 0.9 collective-permute-start.14
  45.7 2.3 %collective-permute-done.5.refs_0_ = bf16[64,4096]{1,0:T(8,128)(2,1)S(1)} collective-permute-done((bf16[64,4096]{1,0:T(8,128)(2,1)S(1)}, bf16[64,4096]{1,0:T(8,128)(2,1)S(1)}, u32[]{:S(2)}, u32[]{:S(2)}) %collective-permute-start.5) | collective-permute-done | bytes 524320 | tf_op jit(solution)/shard_map/ppermute | solution.py:17
  48.0 2.8 %collective-permute-start.13 = (bf16[32,4096]{1,0:T(8,128)(2,1)S(1)}, bf16[32,4096]{1,0:T(8,128)(2,1)S(1)}, u32[]{:S(2)}, u32[]{:S(2)}) collective-permute-start(bf16[32,4096]{1,0:T(8,128)(2,1)S(1)} %joined.6), channel_id=1, source_target_pairs={{0,4},{1,29},{2,6},{3,31},{4,8},{5,1},{6,10},{7,3},{8,12},{9,5},{1... | collective-permute-start | bytes 786440 | tf_op jit(solution)/shard_map/ppermute | solution.py:17
  50.9 0.0 collective-permute-start.16
  50.9 0.0 collective-permute-done.12.refs_3_
  50.9 2.4 %score.4.refs_1_ = bf16[256,1024]{1,0:T(8,128)(2,1)S(1)} custom-call(bf16[64,4096]{1,0:T(8,128)(2,1)S(1)} %collective-permute-done.4.refs_0_, bf16[64,4096]{1,0:T(8,128)(2,1)S(1)} %collective-permute-done.6.refs_1_, bf16[64,4096]{1,0:T(8,128)(2,1)S(1)} %collective-permute-done.11.refs_2_, bf16[64,4096]{1,0:T(8,128)(2,1)S(1)} %collective-permute-done.12.refs_3_, ...), custom_call_target="tpu_custom_call" | custom-call | flops 2147483648 | bytes 11010048 | tf_op jit(solution)/shard_map/score/pallas_call | solution.py:151
  53.2 3.2 %collective-permute-done.13.refs_0_ = bf16[32,4096]{1,0:T(8,128)(2,1)S(1)} collective-permute-done((bf16[32,4096]{1,0:T(8,128)(2,1)S(1)}, bf16[32,4096]{1,0:T(8,128)(2,1)S(1)}, u32[]{:S(2)}, u32[]{:S(2)}) %collective-permute-start.13) | collective-permute-done | bytes 262176 | tf_op jit(solution)/shard_map/ppermute | solution.py:17
  56.5 2.4 %collective-permute-start.17 = (bf16[64,4096]{1,0:T(8,128)(2,1)S(1)}, bf16[64,4096]{1,0:T(8,128)(2,1)S(1)}, u32[]{:S(2)}, u32[]{:S(2)}) collective-permute-start(bf16[64,4096]{1,0:T(8,128)(2,1)S(1)} %collective-permute-done.14.refs_2_.refs_0_), channel_id=1, source_target_pairs={{0,1},{1,0},{2,3},{3,2},{4,5},{5,4},{6,7},{7,6},{8,9},{9,8},{10,11... | collective-permute-start | bytes 1572872 | tf_op jit(solution)/shard_map/ppermute | solution.py:17
  58.9 0.6 collective-permute-start.18
  59.5 0.0 collective-permute-start.15
  59.5 0.0 collective-permute-done.16.refs_1_
  59.5 0.9 collective-permute-done.17.refs_3_
  60.4 2.4 %score.5.refs_2_ = bf16[256,1024]{1,0:T(8,128)(2,1)S(1)} custom-call(bf16[64,4096]{1,0:T(8,128)(2,1)S(1)} %collective-permute-done.5.refs_0_, bf16[64,4096]{1,0:T(8,128)(2,1)S(1)} %collective-permute-done.16.refs_1_, bf16[64,4096]{1,0:T(8,128)(2,1)S(1)} %collective-permute-done.14.refs_2_.refs_0_, bf16[64,4096]{1,0:T(8,128)(2,1)S(1)} %collective-permute-done.17.refs_3_, ...), custom_call_target="tpu_custom_call" | custom-call | flops 2147483648 | bytes 11010048 | tf_op jit(solution)/shard_map/score/pallas_call | solution.py:151
  62.8 0.7 place.1.refs_5_
  63.5 1.0 %collective-permute-done.18.refs_2_ = bf16[32,4096]{1,0:T(8,128)(2,1)S(1)} collective-permute-done((bf16[32,4096]{1,0:T(8,128)(2,1)S(1)}, bf16[32,4096]{1,0:T(8,128)(2,1)S(1)}, u32[]{:S(2)}, u32[]{:S(2)}) %collective-permute-start.18) | collective-permute-done | bytes 262176 | tf_op jit(solution)/shard_map/ppermute | solution.py:17
  64.5 2.1 %collective-permute-start.19 = (bf16[32,4096]{1,0:T(8,128)(2,1)S(1)}, bf16[32,4096]{1,0:T(8,128)(2,1)S(1)}, u32[]{:S(2)}, u32[]{:S(2)}) collective-permute-start(bf16[32,4096]{1,0:T(8,128)(2,1)S(1)} %collective-permute-done.18.refs_2_), channel_id=1, source_target_pairs={{0,1},{1,0},{2,3},{3,2},{4,5},{5,4},{6,7},{7,6},{8,9},{9,8},{10,11... | collective-permute-start | bytes 786440 | tf_op jit(solution)/shard_map/ppermute | solution.py:17
  66.6 1.2 %collective-permute-done.19.refs_3_ = bf16[32,4096]{1,0:T(8,128)(2,1)S(1)} collective-permute-done((bf16[32,4096]{1,0:T(8,128)(2,1)S(1)}, bf16[32,4096]{1,0:T(8,128)(2,1)S(1)}, u32[]{:S(2)}, u32[]{:S(2)}) %collective-permute-start.19) | collective-permute-done | bytes 262176 | tf_op jit(solution)/shard_map/ppermute | solution.py:17
  67.7 3.4 %finish.1 = bf16[32,32,1024]{2,1,0:T(8,128)(2,1)S(1)} custom-call(s32[32]{0:T(128)S(1)} %select_reduce_fusion.where_ref, bf16[32,4096]{1,0:T(8,128)(2,1)S(1)} %collective-permute-done.13.refs_0_, bf16[32,4096]{1,0:T(8,128)(2,1)S(1)} %collective-permute-done.15.refs_1_, ...), custom_call_target="tpu_custom_call", output_to_operand_aliasing={{}: (6, {})} | custom-call | flops 1073741824 | bytes 9699328 | tf_op jit(solution)/shard_map/finish/pallas_call | solution.py:204
  71.2 30.3 %all_to_all.5.in_ref = bf16[8,128,1024]{2,1,0:T(8,128)(2,1)S(1)} all-to-all(bf16[8,128,1024]{2,1,0:T(8,128)(2,1)S(1)} %bitcast.37), channel_id=1, replica_groups=mesh['group'=8,'blk'=32] {'group'}, dimensions={0} | all-to-all | bytes 4194304 | tf_op jit(solution)/shard_map/all_to_all | solution.py:306
  101.4 1.1 %total.1 = f32[1024,128]{1,0:T(8,128)} custom-call(bf16[8,128,1024]{2,1,0:T(8,128)(2,1)S(1)} %all_to_all.5.in_ref), custom_call_target="tpu_custom_call" | custom-call | tf_op jit(solution)/shard_map/total/pallas_call | solution.py:231
  (7 shorter events, 0.1 us)
Async XLA Ops:
  3.7 11.1 %collective-permute-start = (bf16[32,4096]{1,0:T(8,128)(2,1)S(1)}, bf16[32,4096]{1,0:T(8,128)(2,1)S(1)}, u32[]{:S(2)}, u32[]{:S(2)}) collective-permute-start(bf16[32,4096]{1,0:T(8,128)(2,1)S(1)} %precond.1.refs_0_), channel_id=1, source_target_pairs={{0,1},{1,0},{2,3},{3,2},{4,5},{5,4},{6,7},{7,6},{8,9},{9,8},{10,11... | collective-permute-start | bytes 786440 | tf_op jit(solution)/shard_map/ppermute | solution.py:17
  7.0 11.9 %collective-permute-start.3 = (bf16[32,4096]{1,0:T(8,128)(2,1)S(1)}, bf16[32,4096]{1,0:T(8,128)(2,1)S(1)}, u32[]{:S(2)}, u32[]{:S(2)}) collective-permute-start(bf16[32,4096]{1,0:T(8,128)(2,1)S(1)} %precond.1.refs_0_), channel_id=1, source_target_pairs={{0,2},{1,3},{2,0},{3,1},{4,6},{5,7},{6,4},{7,5},{8,10},{9,11},{10,... | collective-permute-start | bytes 786440 | tf_op jit(solution)/shard_map/ppermute | solution.py:17
  8.2 10.7 %collective-permute-start.1 = (bf16[32,4096]{1,0:T(8,128)(2,1)S(1)}, bf16[32,4096]{1,0:T(8,128)(2,1)S(1)}, u32[]{:S(2)}, u32[]{:S(2)}) collective-permute-start(bf16[32,4096]{1,0:T(8,128)(2,1)S(1)} %precond.1.refs_0_), channel_id=1, source_target_pairs={{0,4},{1,29},{2,6},{3,31},{4,8},{5,1},{6,10},{7,3},{8,12},{9,5},{1... | collective-permute-start | bytes 786440 | tf_op jit(solution)/shard_map/ppermute | solution.py:17
  14.7 5.6 %collective-permute-start.2 = (bf16[32,4096]{1,0:T(8,128)(2,1)S(1)}, bf16[32,4096]{1,0:T(8,128)(2,1)S(1)}, u32[]{:S(2)}, u32[]{:S(2)}) collective-permute-start(bf16[32,4096]{1,0:T(8,128)(2,1)S(1)} %collective-permute-done.refs_1_), channel_id=1, source_target_pairs={{0,4},{1,29},{2,6},{3,31},{4,8},{5,1},{6,10},{7,3},{8,12},{9,5},{1... | collective-permute-start | bytes 786440 | tf_op jit(solution)/shard_map/ppermute | solution.py:17
  20.3 2.4 %collective-permute-start.7 = (bf16[32,4096]{1,0:T(8,128)(2,1)S(1)}, bf16[32,4096]{1,0:T(8,128)(2,1)S(1)}, u32[]{:S(2)}, u32[]{:S(2)}) collective-permute-start(bf16[32,4096]{1,0:T(8,128)(2,1)S(1)} %collective-permute-done.3.refs_0_.refs_2_), channel_id=1, source_target_pairs={{0,1},{1,0},{2,3},{3,2},{4,5},{5,4},{6,7},{7,6},{8,9},{9,8},{10,11... | collective-permute-start | bytes 786440 | tf_op jit(solution)/shard_map/ppermute | solution.py:17
  22.8 8.4 %collective-permute-start.9 = (bf16[64,4096]{1,0:T(8,128)(2,1)S(1)}, bf16[64,4096]{1,0:T(8,128)(2,1)S(1)}, u32[]{:S(2)}, u32[]{:S(2)}) collective-permute-start(bf16[64,4096]{1,0:T(8,128)(2,1)S(1)} %joined.7), channel_id=1, source_target_pairs={{0,4},{1,29},{2,6},{3,31},{4,8},{5,1},{6,10},{7,3},{8,12},{9,5},{1... | collective-permute-start | bytes 1572872 | tf_op jit(solution)/shard_map/ppermute | solution.py:17
  24.7 12.1 %collective-permute-start.4 = (bf16[64,4096]{1,0:T(8,128)(2,1)S(1)}, bf16[64,4096]{1,0:T(8,128)(2,1)S(1)}, u32[]{:S(2)}, u32[]{:S(2)}) collective-permute-start(bf16[64,4096]{1,0:T(8,128)(2,1)S(1)} %joined.5.refs_4_), channel_id=1, source_target_pairs={{0,4},{1,29},{2,6},{3,31},{4,8},{5,1},{6,10},{7,3},{8,12},{9,5},{1... | collective-permute-start | bytes 1572872 | tf_op jit(solution)/shard_map/ppermute | solution.py:17
  25.4 14.3 %collective-permute-start.8 = (bf16[64,4096]{1,0:T(8,128)(2,1)S(1)}, bf16[64,4096]{1,0:T(8,128)(2,1)S(1)}, u32[]{:S(2)}, u32[]{:S(2)}) collective-permute-start(bf16[64,4096]{1,0:T(8,128)(2,1)S(1)} %joined.5.refs_4_), channel_id=1, source_target_pairs={{0,1},{1,0},{2,3},{3,2},{4,5},{5,4},{6,7},{7,6},{8,9},{9,8},{10,11... | collective-permute-start | bytes 1572872 | tf_op jit(solution)/shard_map/ppermute | solution.py:17
  31.2 8.6 %collective-permute-start.10 = (bf16[64,4096]{1,0:T(8,128)(2,1)S(1)}, bf16[64,4096]{1,0:T(8,128)(2,1)S(1)}, u32[]{:S(2)}, u32[]{:S(2)}) collective-permute-start(bf16[64,4096]{1,0:T(8,128)(2,1)S(1)} %collective-permute-done.9.refs_6_), channel_id=1, source_target_pairs={{0,1},{1,0},{2,3},{3,2},{4,5},{5,4},{6,7},{7,6},{8,9},{9,8},{10,11... | collective-permute-start | bytes 1572872 | tf_op jit(solution)/shard_map/ppermute | solution.py:17
  33.6 9.6 %collective-permute-start.11 = (bf16[64,4096]{1,0:T(8,128)(2,1)S(1)}, bf16[64,4096]{1,0:T(8,128)(2,1)S(1)}, u32[]{:S(2)}, u32[]{:S(2)}) collective-permute-start(bf16[64,4096]{1,0:T(8,128)(2,1)S(1)} %collective-permute-done.9.refs_6_), channel_id=1, source_target_pairs={{0,4},{1,29},{2,6},{3,31},{4,8},{5,1},{6,10},{7,3},{8,12},{9,5},{1... | collective-permute-start | bytes 1572872 | tf_op jit(solution)/shard_map/ppermute | solution.py:17
  36.8 14.1 %collective-permute-start.6 = (bf16[64,4096]{1,0:T(8,128)(2,1)S(1)}, bf16[64,4096]{1,0:T(8,128)(2,1)S(1)}, u32[]{:S(2)}, u32[]{:S(2)}) collective-permute-start(bf16[64,4096]{1,0:T(8,128)(2,1)S(1)} %collective-permute-done.4.refs_0_), channel_id=1, source_target_pairs={{0,1},{1,0},{2,3},{3,2},{4,5},{5,4},{6,7},{7,6},{8,9},{9,8},{10,11... | collective-permute-start | bytes 1572872 | tf_op jit(solution)/shard_map/ppermute | solution.py:17
  39.2 8.8 %collective-permute-start.5 = (bf16[64,4096]{1,0:T(8,128)(2,1)S(1)}, bf16[64,4096]{1,0:T(8,128)(2,1)S(1)}, u32[]{:S(2)}, u32[]{:S(2)}) collective-permute-start(bf16[64,4096]{1,0:T(8,128)(2,1)S(1)} %collective-permute-done.4.refs_0_), channel_id=1, source_target_pairs={{0,4},{1,29},{2,6},{3,31},{4,8},{5,1},{6,10},{7,3},{8,12},{9,5},{1... | collective-permute-start | bytes 1572872 | tf_op jit(solution)/shard_map/ppermute | solution.py:17
  43.2 7.6 %collective-permute-start.12 = (bf16[64,4096]{1,0:T(8,128)(2,1)S(1)}, bf16[64,4096]{1,0:T(8,128)(2,1)S(1)}, u32[]{:S(2)}, u32[]{:S(2)}) collective-permute-start(bf16[64,4096]{1,0:T(8,128)(2,1)S(1)} %collective-permute-done.11.refs_2_), channel_id=1, source_target_pairs={{0,1},{1,0},{2,3},{3,2},{4,5},{5,4},{6,7},{7,6},{8,9},{9,8},{10,11... | collective-permute-start | bytes 1572872 | tf_op jit(solution)/shard_map/ppermute | solution.py:17
  44.8 11.6 %collective-permute-start.14 = (bf16[64,4096]{1,0:T(8,128)(2,1)S(1)}, bf16[64,4096]{1,0:T(8,128)(2,1)S(1)}, u32[]{:S(2)}, u32[]{:S(2)}) collective-permute-start(bf16[64,4096]{1,0:T(8,128)(2,1)S(1)} %collective-permute-done.11.refs_2_), channel_id=1, source_target_pairs={{0,4},{1,29},{2,6},{3,31},{4,8},{5,1},{6,10},{7,3},{8,12},{9,5},{1... | collective-permute-start | bytes 1572872 | tf_op jit(solution)/shard_map/ppermute | solution.py:17
  48.0 8.4 %collective-permute-start.13 = (bf16[32,4096]{1,0:T(8,128)(2,1)S(1)}, bf16[32,4096]{1,0:T(8,128)(2,1)S(1)}, u32[]{:S(2)}, u32[]{:S(2)}) collective-permute-start(bf16[32,4096]{1,0:T(8,128)(2,1)S(1)} %joined.6), channel_id=1, source_target_pairs={{0,4},{1,29},{2,6},{3,31},{4,8},{5,1},{6,10},{7,3},{8,12},{9,5},{1... | collective-permute-start | bytes 786440 | tf_op jit(solution)/shard_map/ppermute | solution.py:17
  50.9 8.7 %collective-permute-start.16 = (bf16[64,4096]{1,0:T(8,128)(2,1)S(1)}, bf16[64,4096]{1,0:T(8,128)(2,1)S(1)}, u32[]{:S(2)}, u32[]{:S(2)}) collective-permute-start(bf16[64,4096]{1,0:T(8,128)(2,1)S(1)} %collective-permute-done.5.refs_0_), channel_id=1, source_target_pairs={{0,1},{1,0},{2,3},{3,2},{4,5},{5,4},{6,7},{7,6},{8,9},{9,8},{10,11... | collective-permute-start | bytes 1572872 | tf_op jit(solution)/shard_map/ppermute | solution.py:17
  56.5 4.0 %collective-permute-start.17 = (bf16[64,4096]{1,0:T(8,128)(2,1)S(1)}, bf16[64,4096]{1,0:T(8,128)(2,1)S(1)}, u32[]{:S(2)}, u32[]{:S(2)}) collective-permute-start(bf16[64,4096]{1,0:T(8,128)(2,1)S(1)} %collective-permute-done.14.refs_2_.refs_0_), channel_id=1, source_target_pairs={{0,1},{1,0},{2,3},{3,2},{4,5},{5,4},{6,7},{7,6},{8,9},{9,8},{10,11... | collective-permute-start | bytes 1572872 | tf_op jit(solution)/shard_map/ppermute | solution.py:17
  58.9 5.6 %collective-permute-start.18 = (bf16[32,4096]{1,0:T(8,128)(2,1)S(1)}, bf16[32,4096]{1,0:T(8,128)(2,1)S(1)}, u32[]{:S(2)}, u32[]{:S(2)}) collective-permute-start(bf16[32,4096]{1,0:T(8,128)(2,1)S(1)} %joined.8), channel_id=1, source_target_pairs={{0,4},{1,29},{2,6},{3,31},{4,8},{5,1},{6,10},{7,3},{8,12},{9,5},{1... | collective-permute-start | bytes 786440 | tf_op jit(solution)/shard_map/ppermute | solution.py:17
  59.5 7.1 %collective-permute-start.15 = (bf16[32,4096]{1,0:T(8,128)(2,1)S(1)}, bf16[32,4096]{1,0:T(8,128)(2,1)S(1)}, u32[]{:S(2)}, u32[]{:S(2)}) collective-permute-start(bf16[32,4096]{1,0:T(8,128)(2,1)S(1)} %collective-permute-done.13.refs_0_), channel_id=1, source_target_pairs={{0,1},{1,0},{2,3},{3,2},{4,5},{5,4},{6,7},{7,6},{8,9},{9,8},{10,11... | collective-permute-start | bytes 786440 | tf_op jit(solution)/shard_map/ppermute | solution.py:17
  64.5 3.2 %collective-permute-start.19 = (bf16[32,4096]{1,0:T(8,128)(2,1)S(1)}, bf16[32,4096]{1,0:T(8,128)(2,1)S(1)}, u32[]{:S(2)}, u32[]{:S(2)}) collective-permute-start(bf16[32,4096]{1,0:T(8,128)(2,1)S(1)} %collective-permute-done.18.refs_2_), channel_id=1, source_target_pairs={{0,1},{1,0},{2,3},{3,2},{4,5},{5,4},{6,7},{7,6},{8,9},{9,8},{10,11... | collective-permute-start | bytes 786440 | tf_op jit(solution)/shard_map/ppermute | solution.py:17

commit v8 on v7

--- a/solution.py
+++ b/solution.py
@@ -277,13 +277,14 @@
 
     steps = []
 
-    across = _swap_y(panel)
     other = _swap_core(panel)
-    other, where = lax.optimization_barrier((other, where))
+    other, sent = lax.optimization_barrier((other, panel))
+    across = _swap_y(sent)
     own, next_to = _along(panel), _along(other)
+    flat, where = lax.optimization_barrier((flat, where))
     flat = _held(pltpu.with_memory_space_constraint(flat, pltpu.HBM))
-    own, next_to, across, flat = lax.optimization_barrier((own, next_to, across, flat))
     near = _joined(own, next_to)
+    near, across, flat = lax.optimization_barrier((near, across, flat))
     across_other = _swap_core(across)
     far = _along(_joined(across, across_other))
     pieces = [panel, other, across, across_other, near, _swap_core(near), far, _swap_core(far)]

time: 103 us -> 102 us (level)
  waiting for transfers between devices: 19.6 us -> 16.1 us
  starting transfers between devices: 31.2 us -> 33.1 us
    ppermute x20, waiting for transfers between devices: 19.6 us -> 16.1 us  [_route(): lax.ppermute(x, 'blk', [(i, target(*divmod(i, 4))) for i in range(NZ * 4)])]
    ppermute x20, starting transfers between devices: 31.2 us -> 33.1 us  [_route(): lax.ppermute(x, 'blk', [(i, target(*divmod(i, 4))) for i in range(NZ * 4)])]
  transfers between devices with their start and end apart: 20 -> 20, of which waited for: 9 -> 7; matrix products, arithmetic and copies ran while one was open for 1% -> 1% of each run, Pallas kernels for 12% -> 12%
where the time goes in v8:
time: 102 us
  starting transfers between devices  33.1 us (32%)
  blocking collectives  31.2 us (31%)
  Pallas kernels  20.5 us (20%)
  waiting for transfers between devices  16.1 us (16%)
    ppermute x20, starting transfers between devices, _route(): lax.ppermute(x, 'blk', [(i, target(*divmod(i, 4))) for i in range(NZ * 4)])  33.1 us
    all_to_all x1, blocking collectives, body(): lax.all_to_all(buffer, 'group', split_axis=0, concat_axis=0, tiled=True)  31.2 us
    ppermute x20, waiting for transfers between devices, _route(): lax.ppermute(x, 'blk', [(i, target(*divmod(i, 4))) for i in range(NZ * 4)])  16.1 us
    pallas_call x3, Pallas kernels, _score(): pl.pallas_call(functools.partial(_score_kernel, scale, len(pieces)), in_s...  8.15 us
    pallas_call x1, Pallas kernels, _precond(): pl.pallas_call(_precond_kernel, in_specs=[pl.BlockSpec(memory_space=pltpu...  3.66 us
    pallas_call x1, Pallas kernels, _finish(): pl.pallas_call(functools.partial(_finish_kernel, scale, len(pieces)), in_...  3.41 us
    pallas_call x1, Pallas kernels, _held(): pl.pallas_call(pltpu.sync_copy, in_specs=[pl.BlockSpec(memory_space=pl.AN...  3.39 us
  transfers between devices with their start and end apart: 20, of which 7 were waited for; matrix products, arithmetic and copies ran while one was open for 1% of the time, Pallas kernels for 12%

profile of v8, /device:TPU:1, one launch (start us, length us, event | category | flops | bytes accessed | tf_op | source)
XLA Modules:
  0.0 101.9 jit_solution(433848466260468505)
XLA Ops:
  0.0 3.7 %precond.1.refs_0_ = bf16[32,4096]{1,0:T(8,128)(2,1)S(1)} custom-call(f32[64,64]{1,0:T(8,128)} %bitcast.40, f32[64,64]{1,0:T(8,128)} %bitcast.41, bf16[32,4096]{1,0:T(8,128)(2,1)} %bitcast.39), custom_call_target="tpu_custom_call" | custom-call | tf_op jit(solution)/shard_map/precond/pallas_call | solution.py:90
  3.7 3.3 %collective-permute-start.1 = (bf16[32,4096]{1,0:T(8,128)(2,1)S(1)}, bf16[32,4096]{1,0:T(8,128)(2,1)S(1)}, u32[]{:S(2)}, u32[]{:S(2)}) collective-permute-start(bf16[32,4096]{1,0:T(8,128)(2,1)S(1)} %precond.1.refs_0_), channel_id=1, source_target_pairs={{0,1},{1,0},{2,3},{3,2},{4,5},{5,4},{6,7},{7,6},{8,9},{9,8},{10,11... | collective-permute-start | bytes 786440 | tf_op jit(solution)/shard_map/ppermute | solution.py:17
  7.0 3.8 %collective-permute-start = (bf16[32,4096]{1,0:T(8,128)(2,1)S(1)}, bf16[32,4096]{1,0:T(8,128)(2,1)S(1)}, u32[]{:S(2)}, u32[]{:S(2)}) collective-permute-start(bf16[32,4096]{1,0:T(8,128)(2,1)S(1)} %precond.1.refs_0_), channel_id=1, source_target_pairs={{0,4},{1,29},{2,6},{3,31},{4,8},{5,1},{6,10},{7,3},{8,12},{9,5},{1... | collective-permute-start | bytes 786440 | tf_op jit(solution)/shard_map/ppermute | solution.py:17
  10.8 0.0 collective-permute-done.1.refs_1_
  10.8 1.2 %collective-permute-start.2 = (bf16[32,4096]{1,0:T(8,128)(2,1)S(1)}, bf16[32,4096]{1,0:T(8,128)(2,1)S(1)}, u32[]{:S(2)}, u32[]{:S(2)}) collective-permute-start(bf16[32,4096]{1,0:T(8,128)(2,1)S(1)} %collective-permute-done.1.refs_1_), channel_id=1, source_target_pairs={{0,4},{1,29},{2,6},{3,31},{4,8},{5,1},{6,10},{7,3},{8,12},{9,5},{1... | collective-permute-start | bytes 786440 | tf_op jit(solution)/shard_map/ppermute | solution.py:17
  12.0 2.9 %collective-permute-start.3 = (bf16[32,4096]{1,0:T(8,128)(2,1)S(1)}, bf16[32,4096]{1,0:T(8,128)(2,1)S(1)}, u32[]{:S(2)}, u32[]{:S(2)}) collective-permute-start(bf16[32,4096]{1,0:T(8,128)(2,1)S(1)} %precond.1.refs_0_), channel_id=1, source_target_pairs={{0,2},{1,3},{2,0},{3,1},{4,6},{5,7},{6,4},{7,5},{8,10},{9,11},{10,... | collective-permute-start | bytes 786440 | tf_op jit(solution)/shard_map/ppermute | solution.py:17
  14.9 0.1 stack.131
  15.0 0.8 select_reduce_fusion.where_ref
  15.9 3.4 %held.1.refs_8_.refs_4_ = bf16[1024,4096]{1,0:T(8,128)(2,1)S(1)} custom-call(bf16[1024,4096]{1,0:T(8,128)(2,1)} %bitcast.38), custom_call_target="tpu_custom_call" | custom-call | bytes 16777216 | tf_op jit(solution)/shard_map/held/pallas_call | solution.py:126
  19.2 0.0 collective-permute-done.refs_0_
  19.3 0.0 collective-permute-done.2.refs_1_
  19.3 0.0 collective-permute-done.3.refs_0_.refs_2_
  19.3 0.1 collective-permute-start.7
  19.4 1.5 %collective-permute-done.7.refs_1_.refs_3_ = bf16[32,4096]{1,0:T(8,128)(2,1)S(1)} collective-permute-done((bf16[32,4096]{1,0:T(8,128)(2,1)S(1)}, bf16[32,4096]{1,0:T(8,128)(2,1)S(1)}, u32[]{:S(2)}, u32[]{:S(2)}) %collective-permute-start.7) | collective-permute-done | bytes 262176 | tf_op jit(solution)/shard_map/ppermute | solution.py:17
  21.0 3.3 %collective-permute-start.9 = (bf16[64,4096]{1,0:T(8,128)(2,1)S(1)}, bf16[64,4096]{1,0:T(8,128)(2,1)S(1)}, u32[]{:S(2)}, u32[]{:S(2)}) collective-permute-start(bf16[64,4096]{1,0:T(8,128)(2,1)S(1)} %joined.7), channel_id=1, source_target_pairs={{0,4},{1,29},{2,6},{3,31},{4,8},{5,1},{6,10},{7,3},{8,12},{9,5},{1... | collective-permute-start | bytes 1572872 | tf_op jit(solution)/shard_map/ppermute | solution.py:17
  24.2 0.7 collective-permute-start.4
  25.0 0.0 collective-permute-start.8
  25.0 5.4 %collective-permute-done.9.refs_6_ = bf16[64,4096]{1,0:T(8,128)(2,1)S(1)} collective-permute-done((bf16[64,4096]{1,0:T(8,128)(2,1)S(1)}, bf16[64,4096]{1,0:T(8,128)(2,1)S(1)}, u32[]{:S(2)}, u32[]{:S(2)}) %collective-permute-start.9) | collective-permute-done | bytes 524320 | tf_op jit(solution)/shard_map/ppermute | solution.py:17
  30.4 1.7 %collective-permute-start.10 = (bf16[64,4096]{1,0:T(8,128)(2,1)S(1)}, bf16[64,4096]{1,0:T(8,128)(2,1)S(1)}, u32[]{:S(2)}, u32[]{:S(2)}) collective-permute-start(bf16[64,4096]{1,0:T(8,128)(2,1)S(1)} %collective-permute-done.9.refs_6_), channel_id=1, source_target_pairs={{0,1},{1,0},{2,3},{3,2},{4,5},{5,4},{6,7},{7,6},{8,9},{9,8},{10,11... | collective-permute-start | bytes 1572872 | tf_op jit(solution)/shard_map/ppermute | solution.py:17
  32.0 1.7 %collective-permute-start.11 = (bf16[64,4096]{1,0:T(8,128)(2,1)S(1)}, bf16[64,4096]{1,0:T(8,128)(2,1)S(1)}, u32[]{:S(2)}, u32[]{:S(2)}) collective-permute-start(bf16[64,4096]{1,0:T(8,128)(2,1)S(1)} %collective-permute-done.9.refs_6_), channel_id=1, source_target_pairs={{0,4},{1,29},{2,6},{3,31},{4,8},{5,1},{6,10},{7,3},{8,12},{9,5},{1... | collective-permute-start | bytes 1572872 | tf_op jit(solution)/shard_map/ppermute | solution.py:17
  33.8 2.2 %collective-permute-done.4.refs_0_ = bf16[64,4096]{1,0:T(8,128)(2,1)S(1)} collective-permute-done((bf16[64,4096]{1,0:T(8,128)(2,1)S(1)}, bf16[64,4096]{1,0:T(8,128)(2,1)S(1)}, u32[]{:S(2)}, u32[]{:S(2)}) %collective-permute-start.4) | collective-permute-done | bytes 524320 | tf_op jit(solution)/shard_map/ppermute | solution.py:17
  36.0 1.7 %collective-permute-start.6 = (bf16[64,4096]{1,0:T(8,128)(2,1)S(1)}, bf16[64,4096]{1,0:T(8,128)(2,1)S(1)}, u32[]{:S(2)}, u32[]{:S(2)}) collective-permute-start(bf16[64,4096]{1,0:T(8,128)(2,1)S(1)} %collective-permute-done.4.refs_0_), channel_id=1, source_target_pairs={{0,1},{1,0},{2,3},{3,2},{4,5},{5,4},{6,7},{7,6},{8,9},{9,8},{10,11... | collective-permute-start | bytes 1572872 | tf_op jit(solution)/shard_map/ppermute | solution.py:17
  37.7 1.7 %collective-permute-start.5 = (bf16[64,4096]{1,0:T(8,128)(2,1)S(1)}, bf16[64,4096]{1,0:T(8,128)(2,1)S(1)}, u32[]{:S(2)}, u32[]{:S(2)}) collective-permute-start(bf16[64,4096]{1,0:T(8,128)(2,1)S(1)} %collective-permute-done.4.refs_0_), channel_id=1, source_target_pairs={{0,4},{1,29},{2,6},{3,31},{4,8},{5,1},{6,10},{7,3},{8,12},{9,5},{1... | collective-permute-start | bytes 1572872 | tf_op jit(solution)/shard_map/ppermute | solution.py:17
  39.4 0.0 collective-permute-done.8.refs_5_
  39.4 0.0 collective-permute-done.10.refs_7_
  39.4 3.4 %score.3.refs_0_ = bf16[384,1024]{1,0:T(8,128)(2,1)S(1)} custom-call(bf16[32,4096]{1,0:T(8,128)(2,1)S(1)} %precond.1.refs_0_, bf16[32,4096]{1,0:T(8,128)(2,1)S(1)} %collective-permute-done.1.refs_1_, bf16[32,4096]{1,0:T(8,128)(2,1)S(1)} %collective-permute-done.3.refs_0_.refs_2_, bf16[32,4096]{1,0:T(8,128)(2,1)S(1)} %collective-permute-done.7.refs_1_.refs_3_, ...), custom_call_target="tpu_custom_call" | custom-call | flops 3221225472 | bytes 12320768 | tf_op jit(solution)/shard_map/score/pallas_call | solution.py:151
  42.9 0.0 collective-permute-done.11.refs_2_
  42.9 0.4 collective-permute-start.12
  43.3 1.7 %collective-permute-start.14 = (bf16[64,4096]{1,0:T(8,128)(2,1)S(1)}, bf16[64,4096]{1,0:T(8,128)(2,1)S(1)}, u32[]{:S(2)}, u32[]{:S(2)}) collective-permute-start(bf16[64,4096]{1,0:T(8,128)(2,1)S(1)} %collective-permute-done.11.refs_2_), channel_id=1, source_target_pairs={{0,4},{1,29},{2,6},{3,31},{4,8},{5,1},{6,10},{7,3},{8,12},{9,5},{1... | collective-permute-start | bytes 1572872 | tf_op jit(solution)/shard_map/ppermute | solution.py:17
  45.0 2.2 %collective-permute-done.5.refs_0_ = bf16[64,4096]{1,0:T(8,128)(2,1)S(1)} collective-permute-done((bf16[64,4096]{1,0:T(8,128)(2,1)S(1)}, bf16[64,4096]{1,0:T(8,128)(2,1)S(1)}, u32[]{:S(2)}, u32[]{:S(2)}) %collective-permute-start.5) | collective-permute-done | bytes 524320 | tf_op jit(solution)/shard_map/ppermute | solution.py:17
  47.2 3.2 %collective-permute-start.13 = (bf16[32,4096]{1,0:T(8,128)(2,1)S(1)}, bf16[32,4096]{1,0:T(8,128)(2,1)S(1)}, u32[]{:S(2)}, u32[]{:S(2)}) collective-permute-start(bf16[32,4096]{1,0:T(8,128)(2,1)S(1)} %joined.6), channel_id=1, source_target_pairs={{0,4},{1,29},{2,6},{3,31},{4,8},{5,1},{6,10},{7,3},{8,12},{9,5},{1... | collective-permute-start | bytes 786440 | tf_op jit(solution)/shard_map/ppermute | solution.py:17
  50.4 0.0 collective-permute-start.16
  50.4 0.0 collective-permute-done.6.refs_1_
  50.4 0.0 collective-permute-done.12.refs_3_
  50.4 2.4 %score.4.refs_1_ = bf16[256,1024]{1,0:T(8,128)(2,1)S(1)} custom-call(bf16[64,4096]{1,0:T(8,128)(2,1)S(1)} %collective-permute-done.4.refs_0_, bf16[64,4096]{1,0:T(8,128)(2,1)S(1)} %collective-permute-done.6.refs_1_, bf16[64,4096]{1,0:T(8,128)(2,1)S(1)} %collective-permute-done.11.refs_2_, bf16[64,4096]{1,0:T(8,128)(2,1)S(1)} %collective-permute-done.12.refs_3_, ...), custom_call_target="tpu_custom_call" | custom-call | flops 2147483648 | bytes 11010048 | tf_op jit(solution)/shard_map/score/pallas_call | solution.py:151
  52.8 2.8 %collective-permute-done.13.refs_0_ = bf16[32,4096]{1,0:T(8,128)(2,1)S(1)} collective-permute-done((bf16[32,4096]{1,0:T(8,128)(2,1)S(1)}, bf16[32,4096]{1,0:T(8,128)(2,1)S(1)}, u32[]{:S(2)}, u32[]{:S(2)}) %collective-permute-start.13) | collective-permute-done | bytes 262176 | tf_op jit(solution)/shard_map/ppermute | solution.py:17
  55.6 0.0 collective-permute-done.14.refs_2_.refs_0_
  55.6 1.7 %collective-permute-start.17 = (bf16[64,4096]{1,0:T(8,128)(2,1)S(1)}, bf16[64,4096]{1,0:T(8,128)(2,1)S(1)}, u32[]{:S(2)}, u32[]{:S(2)}) collective-permute-start(bf16[64,4096]{1,0:T(8,128)(2,1)S(1)} %collective-permute-done.14.refs_2_.refs_0_), channel_id=1, source_target_pairs={{0,1},{1,0},{2,3},{3,2},{4,5},{5,4},{6,7},{7,6},{8,9},{9,8},{10,11... | collective-permute-start | bytes 1572872 | tf_op jit(solution)/shard_map/ppermute | solution.py:17
  57.4 1.8 %collective-permute-start.18 = (bf16[32,4096]{1,0:T(8,128)(2,1)S(1)}, bf16[32,4096]{1,0:T(8,128)(2,1)S(1)}, u32[]{:S(2)}, u32[]{:S(2)}) collective-permute-start(bf16[32,4096]{1,0:T(8,128)(2,1)S(1)} %joined.8), channel_id=1, source_target_pairs={{0,4},{1,29},{2,6},{3,31},{4,8},{5,1},{6,10},{7,3},{8,12},{9,5},{1... | collective-permute-start | bytes 786440 | tf_op jit(solution)/shard_map/ppermute | solution.py:17
  59.2 2.4 %score.5.refs_2_ = bf16[256,1024]{1,0:T(8,128)(2,1)S(1)} custom-call(bf16[64,4096]{1,0:T(8,128)(2,1)S(1)} %collective-permute-done.5.refs_0_, bf16[64,4096]{1,0:T(8,128)(2,1)S(1)} %collective-permute-done.16.refs_1_, bf16[64,4096]{1,0:T(8,128)(2,1)S(1)} %collective-permute-done.14.refs_2_.refs_0_, bf16[64,4096]{1,0:T(8,128)(2,1)S(1)} %collective-permute-done.17.refs_3_, ...), custom_call_target="tpu_custom_call" | custom-call | flops 2147483648 | bytes 11010048 | tf_op jit(solution)/shard_map/score/pallas_call | solution.py:151
  61.5 0.7 place.1.refs_5_
  62.2 0.7 collective-permute-done.18.refs_2_
  62.9 2.1 %collective-permute-start.19 = (bf16[32,4096]{1,0:T(8,128)(2,1)S(1)}, bf16[32,4096]{1,0:T(8,128)(2,1)S(1)}, u32[]{:S(2)}, u32[]{:S(2)}) collective-permute-start(bf16[32,4096]{1,0:T(8,128)(2,1)S(1)} %collective-permute-done.18.refs_2_), channel_id=1, source_target_pairs={{0,1},{1,0},{2,3},{3,2},{4,5},{5,4},{6,7},{7,6},{8,9},{9,8},{10,11... | collective-permute-start | bytes 786440 | tf_op jit(solution)/shard_map/ppermute | solution.py:17
  65.0 0.0 collective-permute-done.15.refs_1_
  65.0 1.2 %collective-permute-done.19.refs_3_ = bf16[32,4096]{1,0:T(8,128)(2,1)S(1)} collective-permute-done((bf16[32,4096]{1,0:T(8,128)(2,1)S(1)}, bf16[32,4096]{1,0:T(8,128)(2,1)S(1)}, u32[]{:S(2)}, u32[]{:S(2)}) %collective-permute-start.19) | collective-permute-done | bytes 262176 | tf_op jit(solution)/shard_map/ppermute | solution.py:17
  66.2 3.4 %finish.1 = bf16[32,32,1024]{2,1,0:T(8,128)(2,1)S(1)} custom-call(s32[32]{0:T(128)S(1)} %select_reduce_fusion.where_ref, bf16[32,4096]{1,0:T(8,128)(2,1)S(1)} %collective-permute-done.13.refs_0_, bf16[32,4096]{1,0:T(8,128)(2,1)S(1)} %collective-permute-done.15.refs_1_, ...), custom_call_target="tpu_custom_call", output_to_operand_aliasing={{}: (6, {})} | custom-call | flops 1073741824 | bytes 9699328 | tf_op jit(solution)/shard_map/finish/pallas_call | solution.py:204
  69.6 31.2 %all_to_all.5.in_ref = bf16[8,128,1024]{2,1,0:T(8,128)(2,1)S(1)} all-to-all(bf16[8,128,1024]{2,1,0:T(8,128)(2,1)S(1)} %bitcast.37), channel_id=1, replica_groups=mesh['group'=8,'blk'=32] {'group'}, dimensions={0} | all-to-all | bytes 4194304 | tf_op jit(solution)/shard_map/all_to_all | solution.py:307
  100.8 1.1 %total.1 = f32[1024,128]{1,0:T(8,128)} custom-call(bf16[8,128,1024]{2,1,0:T(8,128)(2,1)S(1)} %all_to_all.5.in_ref), custom_call_target="tpu_custom_call" | custom-call | tf_op jit(solution)/shard_map/total/pallas_call | solution.py:231
  (7 shorter events, 0.1 us)
Async XLA Ops:
  3.7 7.2 %collective-permute-start.1 = (bf16[32,4096]{1,0:T(8,128)(2,1)S(1)}, bf16[32,4096]{1,0:T(8,128)(2,1)S(1)}, u32[]{:S(2)}, u32[]{:S(2)}) collective-permute-start(bf16[32,4096]{1,0:T(8,128)(2,1)S(1)} %precond.1.refs_0_), channel_id=1, source_target_pairs={{0,1},{1,0},{2,3},{3,2},{4,5},{5,4},{6,7},{7,6},{8,9},{9,8},{10,11... | collective-permute-start | bytes 786440 | tf_op jit(solution)/shard_map/ppermute | solution.py:17
  7.0 12.3 %collective-permute-start = (bf16[32,4096]{1,0:T(8,128)(2,1)S(1)}, bf16[32,4096]{1,0:T(8,128)(2,1)S(1)}, u32[]{:S(2)}, u32[]{:S(2)}) collective-permute-start(bf16[32,4096]{1,0:T(8,128)(2,1)S(1)} %precond.1.refs_0_), channel_id=1, source_target_pairs={{0,4},{1,29},{2,6},{3,31},{4,8},{5,1},{6,10},{7,3},{8,12},{9,5},{1... | collective-permute-start | bytes 786440 | tf_op jit(solution)/shard_map/ppermute | solution.py:17
  10.8 8.4 %collective-permute-start.2 = (bf16[32,4096]{1,0:T(8,128)(2,1)S(1)}, bf16[32,4096]{1,0:T(8,128)(2,1)S(1)}, u32[]{:S(2)}, u32[]{:S(2)}) collective-permute-start(bf16[32,4096]{1,0:T(8,128)(2,1)S(1)} %collective-permute-done.1.refs_1_), channel_id=1, source_target_pairs={{0,4},{1,29},{2,6},{3,31},{4,8},{5,1},{6,10},{7,3},{8,12},{9,5},{1... | collective-permute-start | bytes 786440 | tf_op jit(solution)/shard_map/ppermute | solution.py:17
  12.0 7.3 %collective-permute-start.3 = (bf16[32,4096]{1,0:T(8,128)(2,1)S(1)}, bf16[32,4096]{1,0:T(8,128)(2,1)S(1)}, u32[]{:S(2)}, u32[]{:S(2)}) collective-permute-start(bf16[32,4096]{1,0:T(8,128)(2,1)S(1)} %precond.1.refs_0_), channel_id=1, source_target_pairs={{0,2},{1,3},{2,0},{3,1},{4,6},{5,7},{6,4},{7,5},{8,10},{9,11},{10,... | collective-permute-start | bytes 786440 | tf_op jit(solution)/shard_map/ppermute | solution.py:17
  19.3 1.6 %collective-permute-start.7 = (bf16[32,4096]{1,0:T(8,128)(2,1)S(1)}, bf16[32,4096]{1,0:T(8,128)(2,1)S(1)}, u32[]{:S(2)}, u32[]{:S(2)}) collective-permute-start(bf16[32,4096]{1,0:T(8,128)(2,1)S(1)} %collective-permute-done.3.refs_0_.refs_2_), channel_id=1, source_target_pairs={{0,1},{1,0},{2,3},{3,2},{4,5},{5,4},{6,7},{7,6},{8,9},{9,8},{10,11... | collective-permute-start | bytes 786440 | tf_op jit(solution)/shard_map/ppermute | solution.py:17
  21.0 9.4 %collective-permute-start.9 = (bf16[64,4096]{1,0:T(8,128)(2,1)S(1)}, bf16[64,4096]{1,0:T(8,128)(2,1)S(1)}, u32[]{:S(2)}, u32[]{:S(2)}) collective-permute-start(bf16[64,4096]{1,0:T(8,128)(2,1)S(1)} %joined.7), channel_id=1, source_target_pairs={{0,4},{1,29},{2,6},{3,31},{4,8},{5,1},{6,10},{7,3},{8,12},{9,5},{1... | collective-permute-start | bytes 1572872 | tf_op jit(solution)/shard_map/ppermute | solution.py:17
  24.2 11.7 %collective-permute-start.4 = (bf16[64,4096]{1,0:T(8,128)(2,1)S(1)}, bf16[64,4096]{1,0:T(8,128)(2,1)S(1)}, u32[]{:S(2)}, u32[]{:S(2)}) collective-permute-start(bf16[64,4096]{1,0:T(8,128)(2,1)S(1)} %joined.5.refs_4_), channel_id=1, source_target_pairs={{0,4},{1,29},{2,6},{3,31},{4,8},{5,1},{6,10},{7,3},{8,12},{9,5},{1... | collective-permute-start | bytes 1572872 | tf_op jit(solution)/shard_map/ppermute | solution.py:17
  25.0 14.4 %collective-permute-start.8 = (bf16[64,4096]{1,0:T(8,128)(2,1)S(1)}, bf16[64,4096]{1,0:T(8,128)(2,1)S(1)}, u32[]{:S(2)}, u32[]{:S(2)}) collective-permute-start(bf16[64,4096]{1,0:T(8,128)(2,1)S(1)} %joined.5.refs_4_), channel_id=1, source_target_pairs={{0,1},{1,0},{2,3},{3,2},{4,5},{5,4},{6,7},{7,6},{8,9},{9,8},{10,11... | collective-permute-start | bytes 1572872 | tf_op jit(solution)/shard_map/ppermute | solution.py:17
  30.4 9.1 %collective-permute-start.10 = (bf16[64,4096]{1,0:T(8,128)(2,1)S(1)}, bf16[64,4096]{1,0:T(8,128)(2,1)S(1)}, u32[]{:S(2)}, u32[]{:S(2)}) collective-permute-start(bf16[64,4096]{1,0:T(8,128)(2,1)S(1)} %collective-permute-done.9.refs_6_), channel_id=1, source_target_pairs={{0,1},{1,0},{2,3},{3,2},{4,5},{5,4},{6,7},{7,6},{8,9},{9,8},{10,11... | collective-permute-start | bytes 1572872 | tf_op jit(solution)/shard_map/ppermute | solution.py:17
  32.0 10.8 %collective-permute-start.11 = (bf16[64,4096]{1,0:T(8,128)(2,1)S(1)}, bf16[64,4096]{1,0:T(8,128)(2,1)S(1)}, u32[]{:S(2)}, u32[]{:S(2)}) collective-permute-start(bf16[64,4096]{1,0:T(8,128)(2,1)S(1)} %collective-permute-done.9.refs_6_), channel_id=1, source_target_pairs={{0,4},{1,29},{2,6},{3,31},{4,8},{5,1},{6,10},{7,3},{8,12},{9,5},{1... | collective-permute-start | bytes 1572872 | tf_op jit(solution)/shard_map/ppermute | solution.py:17
  36.0 14.5 %collective-permute-start.6 = (bf16[64,4096]{1,0:T(8,128)(2,1)S(1)}, bf16[64,4096]{1,0:T(8,128)(2,1)S(1)}, u32[]{:S(2)}, u32[]{:S(2)}) collective-permute-start(bf16[64,4096]{1,0:T(8,128)(2,1)S(1)} %collective-permute-done.4.refs_0_), channel_id=1, source_target_pairs={{0,1},{1,0},{2,3},{3,2},{4,5},{5,4},{6,7},{7,6},{8,9},{9,8},{10,11... | collective-permute-start | bytes 1572872 | tf_op jit(solution)/shard_map/ppermute | solution.py:17
  37.7 9.5 %collective-permute-start.5 = (bf16[64,4096]{1,0:T(8,128)(2,1)S(1)}, bf16[64,4096]{1,0:T(8,128)(2,1)S(1)}, u32[]{:S(2)}, u32[]{:S(2)}) collective-permute-start(bf16[64,4096]{1,0:T(8,128)(2,1)S(1)} %collective-permute-done.4.refs_0_), channel_id=1, source_target_pairs={{0,4},{1,29},{2,6},{3,31},{4,8},{5,1},{6,10},{7,3},{8,12},{9,5},{1... | collective-permute-start | bytes 1572872 | tf_op jit(solution)/shard_map/ppermute | solution.py:17
  42.9 7.6 %collective-permute-start.12 = (bf16[64,4096]{1,0:T(8,128)(2,1)S(1)}, bf16[64,4096]{1,0:T(8,128)(2,1)S(1)}, u32[]{:S(2)}, u32[]{:S(2)}) collective-permute-start(bf16[64,4096]{1,0:T(8,128)(2,1)S(1)} %collective-permute-done.11.refs_2_), channel_id=1, source_target_pairs={{0,1},{1,0},{2,3},{3,2},{4,5},{5,4},{6,7},{7,6},{8,9},{9,8},{10,11... | collective-permute-start | bytes 1572872 | tf_op jit(solution)/shard_map/ppermute | solution.py:17
  43.3 12.4 %collective-permute-start.14 = (bf16[64,4096]{1,0:T(8,128)(2,1)S(1)}, bf16[64,4096]{1,0:T(8,128)(2,1)S(1)}, u32[]{:S(2)}, u32[]{:S(2)}) collective-permute-start(bf16[64,4096]{1,0:T(8,128)(2,1)S(1)} %collective-permute-done.11.refs_2_), channel_id=1, source_target_pairs={{0,4},{1,29},{2,6},{3,31},{4,8},{5,1},{6,10},{7,3},{8,12},{9,5},{1... | collective-permute-start | bytes 1572872 | tf_op jit(solution)/shard_map/ppermute | solution.py:17
  47.2 8.4 %collective-permute-start.13 = (bf16[32,4096]{1,0:T(8,128)(2,1)S(1)}, bf16[32,4096]{1,0:T(8,128)(2,1)S(1)}, u32[]{:S(2)}, u32[]{:S(2)}) collective-permute-start(bf16[32,4096]{1,0:T(8,128)(2,1)S(1)} %joined.6), channel_id=1, source_target_pairs={{0,4},{1,29},{2,6},{3,31},{4,8},{5,1},{6,10},{7,3},{8,12},{9,5},{1... | collective-permute-start | bytes 786440 | tf_op jit(solution)/shard_map/ppermute | solution.py:17
  50.4 8.7 %collective-permute-start.16 = (bf16[64,4096]{1,0:T(8,128)(2,1)S(1)}, bf16[64,4096]{1,0:T(8,128)(2,1)S(1)}, u32[]{:S(2)}, u32[]{:S(2)}) collective-permute-start(bf16[64,4096]{1,0:T(8,128)(2,1)S(1)} %collective-permute-done.5.refs_0_), channel_id=1, source_target_pairs={{0,1},{1,0},{2,3},{3,2},{4,5},{5,4},{6,7},{7,6},{8,9},{9,8},{10,11... | collective-permute-start | bytes 1572872 | tf_op jit(solution)/shard_map/ppermute | solution.py:17
  55.6 3.5 %collective-permute-start.17 = (bf16[64,4096]{1,0:T(8,128)(2,1)S(1)}, bf16[64,4096]{1,0:T(8,128)(2,1)S(1)}, u32[]{:S(2)}, u32[]{:S(2)}) collective-permute-start(bf16[64,4096]{1,0:T(8,128)(2,1)S(1)} %collective-permute-done.14.refs_2_.refs_0_), channel_id=1, source_target_pairs={{0,1},{1,0},{2,3},{3,2},{4,5},{5,4},{6,7},{7,6},{8,9},{9,8},{10,11... | collective-permute-start | bytes 1572872 | tf_op jit(solution)/shard_map/ppermute | solution.py:17
  57.4 5.6 %collective-permute-start.18 = (bf16[32,4096]{1,0:T(8,128)(2,1)S(1)}, bf16[32,4096]{1,0:T(8,128)(2,1)S(1)}, u32[]{:S(2)}, u32[]{:S(2)}) collective-permute-start(bf16[32,4096]{1,0:T(8,128)(2,1)S(1)} %joined.8), channel_id=1, source_target_pairs={{0,4},{1,29},{2,6},{3,31},{4,8},{5,1},{6,10},{7,3},{8,12},{9,5},{1... | collective-permute-start | bytes 786440 | tf_op jit(solution)/shard_map/ppermute | solution.py:17
  59.2 5.9 %collective-permute-start.15 = (bf16[32,4096]{1,0:T(8,128)(2,1)S(1)}, bf16[32,4096]{1,0:T(8,128)(2,1)S(1)}, u32[]{:S(2)}, u32[]{:S(2)}) collective-permute-start(bf16[32,4096]{1,0:T(8,128)(2,1)S(1)} %collective-permute-done.13.refs_0_), channel_id=1, source_target_pairs={{0,1},{1,0},{2,3},{3,2},{4,5},{5,4},{6,7},{7,6},{8,9},{9,8},{10,11... | collective-permute-start | bytes 786440 | tf_op jit(solution)/shard_map/ppermute | solution.py:17
  62.9 3.2 %collective-permute-start.19 = (bf16[32,4096]{1,0:T(8,128)(2,1)S(1)}, bf16[32,4096]{1,0:T(8,128)(2,1)S(1)}, u32[]{:S(2)}, u32[]{:S(2)}) collective-permute-start(bf16[32,4096]{1,0:T(8,128)(2,1)S(1)} %collective-permute-done.18.refs_2_), channel_id=1, source_target_pairs={{0,1},{1,0},{2,3},{3,2},{4,5},{5,4},{6,7},{7,6},{8,9},{9,8},{10,11... | collective-permute-start | bytes 786440 | tf_op jit(solution)/shard_map/ppermute | solution.py:17

commit v9 on v8

--- a/solution.py
+++ b/solution.py
@@ -191,9 +191,9 @@
     for i in range(c_ref.shape[0] // CBLK):
         block = slice(i * CBLK, (i + 1) * CBLK)
         part = lax.dot_general(
-            panels, c_ref[block, :], (((1,), (1,)), ((), ())), preferred_element_type=jnp.float32
+            c_ref[block, :], panels, (((1,), (1,)), ((), ())), preferred_element_type=jnp.float32
         )
-        part = (part * scale).astype(o_ref.dtype)
+        part = (part * scale).T.astype(o_ref.dtype)
         for j in range(count):
             o_ref[where_ref[first + j], :, block] = part[j * PANEL : (j + 1) * PANEL, :]
 

time: 102 us -> 102 us (level)
  no operation moved by 1% of the time
where the time goes in v9:
time: 102 us
  starting transfers between devices  33.1 us (32%)
  blocking collectives  31.5 us (31%)
  Pallas kernels  20 us (20%)
  waiting for transfers between devices  16.1 us (16%)
    ppermute x20, starting transfers between devices, _route(): lax.ppermute(x, 'blk', [(i, target(*divmod(i, 4))) for i in range(NZ * 4)])  33.1 us
    all_to_all x1, blocking collectives, body(): lax.all_to_all(buffer, 'group', split_axis=0, concat_axis=0, tiled=True)  31.5 us
    ppermute x20, waiting for transfers between devices, _route(): lax.ppermute(x, 'blk', [(i, target(*divmod(i, 4))) for i in range(NZ * 4)])  16.1 us
    pallas_call x3, Pallas kernels, _score(): pl.pallas_call(functools.partial(_score_kernel, scale, len(pieces)), in_s...  8.15 us
    pallas_call x1, Pallas kernels, _precond(): pl.pallas_call(_precond_kernel, in_specs=[pl.BlockSpec(memory_space=pltpu...  3.66 us
    pallas_call x1, Pallas kernels, _held(): pl.pallas_call(pltpu.sync_copy, in_specs=[pl.BlockSpec(memory_space=pl.AN...  3.39 us
    pallas_call x1, Pallas kernels, _finish(): pl.pallas_call(functools.partial(_finish_kernel, scale, len(pieces)), in_...  2.93 us
  transfers between devices with their start and end apart: 20, of which 7 were waited for; matrix products, arithmetic and copies ran while one was open for 1% of the time, Pallas kernels for 12%

profile of v9, /device:TPU:1, one launch (start us, length us, event | category | flops | bytes accessed | tf_op | source)
XLA Modules:
  0.0 101.7 jit_solution(7511847851029949024)
XLA Ops:
  0.0 3.7 %precond.1.refs_0_ = bf16[32,4096]{1,0:T(8,128)(2,1)S(1)} custom-call(f32[64,64]{1,0:T(8,128)} %bitcast.40, f32[64,64]{1,0:T(8,128)} %bitcast.41, bf16[32,4096]{1,0:T(8,128)(2,1)} %bitcast.39), custom_call_target="tpu_custom_call" | custom-call | tf_op jit(solution)/shard_map/precond/pallas_call | solution.py:90
  3.7 3.3 %collective-permute-start.1 = (bf16[32,4096]{1,0:T(8,128)(2,1)S(1)}, bf16[32,4096]{1,0:T(8,128)(2,1)S(1)}, u32[]{:S(2)}, u32[]{:S(2)}) collective-permute-start(bf16[32,4096]{1,0:T(8,128)(2,1)S(1)} %precond.1.refs_0_), channel_id=1, source_target_pairs={{0,1},{1,0},{2,3},{3,2},{4,5},{5,4},{6,7},{7,6},{8,9},{9,8},{10,11... | collective-permute-start | bytes 786440 | tf_op jit(solution)/shard_map/ppermute | solution.py:17
  7.0 3.8 %collective-permute-start = (bf16[32,4096]{1,0:T(8,128)(2,1)S(1)}, bf16[32,4096]{1,0:T(8,128)(2,1)S(1)}, u32[]{:S(2)}, u32[]{:S(2)}) collective-permute-start(bf16[32,4096]{1,0:T(8,128)(2,1)S(1)} %precond.1.refs_0_), channel_id=1, source_target_pairs={{0,4},{1,29},{2,6},{3,31},{4,8},{5,1},{6,10},{7,3},{8,12},{9,5},{1... | collective-permute-start | bytes 786440 | tf_op jit(solution)/shard_map/ppermute | solution.py:17
  10.8 0.0 collective-permute-done.1.refs_1_
  10.8 1.2 %collective-permute-start.2 = (bf16[32,4096]{1,0:T(8,128)(2,1)S(1)}, bf16[32,4096]{1,0:T(8,128)(2,1)S(1)}, u32[]{:S(2)}, u32[]{:S(2)}) collective-permute-start(bf16[32,4096]{1,0:T(8,128)(2,1)S(1)} %collective-permute-done.1.refs_1_), channel_id=1, source_target_pairs={{0,4},{1,29},{2,6},{3,31},{4,8},{5,1},{6,10},{7,3},{8,12},{9,5},{1... | collective-permute-start | bytes 786440 | tf_op jit(solution)/shard_map/ppermute | solution.py:17
  12.0 2.9 %collective-permute-start.3 = (bf16[32,4096]{1,0:T(8,128)(2,1)S(1)}, bf16[32,4096]{1,0:T(8,128)(2,1)S(1)}, u32[]{:S(2)}, u32[]{:S(2)}) collective-permute-start(bf16[32,4096]{1,0:T(8,128)(2,1)S(1)} %precond.1.refs_0_), channel_id=1, source_target_pairs={{0,2},{1,3},{2,0},{3,1},{4,6},{5,7},{6,4},{7,5},{8,10},{9,11},{10,... | collective-permute-start | bytes 786440 | tf_op jit(solution)/shard_map/ppermute | solution.py:17
  14.9 0.1 stack.131
  15.0 0.8 select_reduce_fusion.where_ref
  15.9 3.4 %held.1.refs_8_.refs_4_ = bf16[1024,4096]{1,0:T(8,128)(2,1)S(1)} custom-call(bf16[1024,4096]{1,0:T(8,128)(2,1)} %bitcast.38), custom_call_target="tpu_custom_call" | custom-call | bytes 16777216 | tf_op jit(solution)/shard_map/held/pallas_call | solution.py:126
  19.2 0.0 collective-permute-done.refs_0_
  19.3 0.0 collective-permute-done.2.refs_1_
  19.3 0.0 collective-permute-done.3.refs_0_.refs_2_
  19.3 0.1 collective-permute-start.7
  19.4 1.5 %collective-permute-done.7.refs_1_.refs_3_ = bf16[32,4096]{1,0:T(8,128)(2,1)S(1)} collective-permute-done((bf16[32,4096]{1,0:T(8,128)(2,1)S(1)}, bf16[32,4096]{1,0:T(8,128)(2,1)S(1)}, u32[]{:S(2)}, u32[]{:S(2)}) %collective-permute-start.7) | collective-permute-done | bytes 262176 | tf_op jit(solution)/shard_map/ppermute | solution.py:17
  21.0 3.3 %collective-permute-start.9 = (bf16[64,4096]{1,0:T(8,128)(2,1)S(1)}, bf16[64,4096]{1,0:T(8,128)(2,1)S(1)}, u32[]{:S(2)}, u32[]{:S(2)}) collective-permute-start(bf16[64,4096]{1,0:T(8,128)(2,1)S(1)} %joined.7), channel_id=1, source_target_pairs={{0,4},{1,29},{2,6},{3,31},{4,8},{5,1},{6,10},{7,3},{8,12},{9,5},{1... | collective-permute-start | bytes 1572872 | tf_op jit(solution)/shard_map/ppermute | solution.py:17
  24.2 0.7 collective-permute-start.4
  25.0 0.0 collective-permute-start.8
  25.0 5.4 %collective-permute-done.9.refs_6_ = bf16[64,4096]{1,0:T(8,128)(2,1)S(1)} collective-permute-done((bf16[64,4096]{1,0:T(8,128)(2,1)S(1)}, bf16[64,4096]{1,0:T(8,128)(2,1)S(1)}, u32[]{:S(2)}, u32[]{:S(2)}) %collective-permute-start.9) | collective-permute-done | bytes 524320 | tf_op jit(solution)/shard_map/ppermute | solution.py:17
  30.4 1.7 %collective-permute-start.10 = (bf16[64,4096]{1,0:T(8,128)(2,1)S(1)}, bf16[64,4096]{1,0:T(8,128)(2,1)S(1)}, u32[]{:S(2)}, u32[]{:S(2)}) collective-permute-start(bf16[64,4096]{1,0:T(8,128)(2,1)S(1)} %collective-permute-done.9.refs_6_), channel_id=1, source_target_pairs={{0,1},{1,0},{2,3},{3,2},{4,5},{5,4},{6,7},{7,6},{8,9},{9,8},{10,11... | collective-permute-start | bytes 1572872 | tf_op jit(solution)/shard_map/ppermute | solution.py:17
  32.0 1.7 %collective-permute-start.11 = (bf16[64,4096]{1,0:T(8,128)(2,1)S(1)}, bf16[64,4096]{1,0:T(8,128)(2,1)S(1)}, u32[]{:S(2)}, u32[]{:S(2)}) collective-permute-start(bf16[64,4096]{1,0:T(8,128)(2,1)S(1)} %collective-permute-done.9.refs_6_), channel_id=1, source_target_pairs={{0,4},{1,29},{2,6},{3,31},{4,8},{5,1},{6,10},{7,3},{8,12},{9,5},{1... | collective-permute-start | bytes 1572872 | tf_op jit(solution)/shard_map/ppermute | solution.py:17
  33.8 2.2 %collective-permute-done.4.refs_0_ = bf16[64,4096]{1,0:T(8,128)(2,1)S(1)} collective-permute-done((bf16[64,4096]{1,0:T(8,128)(2,1)S(1)}, bf16[64,4096]{1,0:T(8,128)(2,1)S(1)}, u32[]{:S(2)}, u32[]{:S(2)}) %collective-permute-start.4) | collective-permute-done | bytes 524320 | tf_op jit(solution)/shard_map/ppermute | solution.py:17
  36.0 1.7 %collective-permute-start.6 = (bf16[64,4096]{1,0:T(8,128)(2,1)S(1)}, bf16[64,4096]{1,0:T(8,128)(2,1)S(1)}, u32[]{:S(2)}, u32[]{:S(2)}) collective-permute-start(bf16[64,4096]{1,0:T(8,128)(2,1)S(1)} %collective-permute-done.4.refs_0_), channel_id=1, source_target_pairs={{0,1},{1,0},{2,3},{3,2},{4,5},{5,4},{6,7},{7,6},{8,9},{9,8},{10,11... | collective-permute-start | bytes 1572872 | tf_op jit(solution)/shard_map/ppermute | solution.py:17
  37.7 1.7 %collective-permute-start.5 = (bf16[64,4096]{1,0:T(8,128)(2,1)S(1)}, bf16[64,4096]{1,0:T(8,128)(2,1)S(1)}, u32[]{:S(2)}, u32[]{:S(2)}) collective-permute-start(bf16[64,4096]{1,0:T(8,128)(2,1)S(1)} %collective-permute-done.4.refs_0_), channel_id=1, source_target_pairs={{0,4},{1,29},{2,6},{3,31},{4,8},{5,1},{6,10},{7,3},{8,12},{9,5},{1... | collective-permute-start | bytes 1572872 | tf_op jit(solution)/shard_map/ppermute | solution.py:17
  39.4 0.0 collective-permute-done.8.refs_5_
  39.4 0.0 collective-permute-done.10.refs_7_
  39.4 3.4 %score.3.refs_0_ = bf16[384,1024]{1,0:T(8,128)(2,1)S(1)} custom-call(bf16[32,4096]{1,0:T(8,128)(2,1)S(1)} %precond.1.refs_0_, bf16[32,4096]{1,0:T(8,128)(2,1)S(1)} %collective-permute-done.1.refs_1_, bf16[32,4096]{1,0:T(8,128)(2,1)S(1)} %collective-permute-done.3.refs_0_.refs_2_, bf16[32,4096]{1,0:T(8,128)(2,1)S(1)} %collective-permute-done.7.refs_1_.refs_3_, ...), custom_call_target="tpu_custom_call" | custom-call | flops 3221225472 | bytes 12320768 | tf_op jit(solution)/shard_map/score/pallas_call | solution.py:151
  42.9 0.4 collective-permute-start.12
  43.3 1.7 %collective-permute-start.14 = (bf16[64,4096]{1,0:T(8,128)(2,1)S(1)}, bf16[64,4096]{1,0:T(8,128)(2,1)S(1)}, u32[]{:S(2)}, u32[]{:S(2)}) collective-permute-start(bf16[64,4096]{1,0:T(8,128)(2,1)S(1)} %collective-permute-done.11.refs_2_), channel_id=1, source_target_pairs={{0,4},{1,29},{2,6},{3,31},{4,8},{5,1},{6,10},{7,3},{8,12},{9,5},{1... | collective-permute-start | bytes 1572872 | tf_op jit(solution)/shard_map/ppermute | solution.py:17
  45.0 2.2 %collective-permute-done.5.refs_0_ = bf16[64,4096]{1,0:T(8,128)(2,1)S(1)} collective-permute-done((bf16[64,4096]{1,0:T(8,128)(2,1)S(1)}, bf16[64,4096]{1,0:T(8,128)(2,1)S(1)}, u32[]{:S(2)}, u32[]{:S(2)}) %collective-permute-start.5) | collective-permute-done | bytes 524320 | tf_op jit(solution)/shard_map/ppermute | solution.py:17
  47.2 3.2 %collective-permute-start.13 = (bf16[32,4096]{1,0:T(8,128)(2,1)S(1)}, bf16[32,4096]{1,0:T(8,128)(2,1)S(1)}, u32[]{:S(2)}, u32[]{:S(2)}) collective-permute-start(bf16[32,4096]{1,0:T(8,128)(2,1)S(1)} %joined.6), channel_id=1, source_target_pairs={{0,4},{1,29},{2,6},{3,31},{4,8},{5,1},{6,10},{7,3},{8,12},{9,5},{1... | collective-permute-start | bytes 786440 | tf_op jit(solution)/shard_map/ppermute | solution.py:17
  50.4 0.0 collective-permute-done.6.refs_1_
  50.4 0.0 collective-permute-done.12.refs_3_
  50.4 2.4 %score.4.refs_1_ = bf16[256,1024]{1,0:T(8,128)(2,1)S(1)} custom-call(bf16[64,4096]{1,0:T(8,128)(2,1)S(1)} %collective-permute-done.4.refs_0_, bf16[64,4096]{1,0:T(8,128)(2,1)S(1)} %collective-permute-done.6.refs_1_, bf16[64,4096]{1,0:T(8,128)(2,1)S(1)} %collective-permute-done.11.refs_2_, bf16[64,4096]{1,0:T(8,128)(2,1)S(1)} %collective-permute-done.12.refs_3_, ...), custom_call_target="tpu_custom_call" | custom-call | flops 2147483648 | bytes 11010048 | tf_op jit(solution)/shard_map/score/pallas_call | solution.py:151
  52.8 2.8 %collective-permute-done.13.refs_0_ = bf16[32,4096]{1,0:T(8,128)(2,1)S(1)} collective-permute-done((bf16[32,4096]{1,0:T(8,128)(2,1)S(1)}, bf16[32,4096]{1,0:T(8,128)(2,1)S(1)}, u32[]{:S(2)}, u32[]{:S(2)}) %collective-permute-start.13) | collective-permute-done | bytes 262176 | tf_op jit(solution)/shard_map/ppermute | solution.py:17
  55.6 1.7 %collective-permute-start.17 = (bf16[64,4096]{1,0:T(8,128)(2,1)S(1)}, bf16[64,4096]{1,0:T(8,128)(2,1)S(1)}, u32[]{:S(2)}, u32[]{:S(2)}) collective-permute-start(bf16[64,4096]{1,0:T(8,128)(2,1)S(1)} %collective-permute-done.14.refs_2_.refs_0_), channel_id=1, source_target_pairs={{0,1},{1,0},{2,3},{3,2},{4,5},{5,4},{6,7},{7,6},{8,9},{9,8},{10,11... | collective-permute-start | bytes 1572872 | tf_op jit(solution)/shard_map/ppermute | solution.py:17
  57.4 1.8 %collective-permute-start.18 = (bf16[32,4096]{1,0:T(8,128)(2,1)S(1)}, bf16[32,4096]{1,0:T(8,128)(2,1)S(1)}, u32[]{:S(2)}, u32[]{:S(2)}) collective-permute-start(bf16[32,4096]{1,0:T(8,128)(2,1)S(1)} %joined.8), channel_id=1, source_target_pairs={{0,4},{1,29},{2,6},{3,31},{4,8},{5,1},{6,10},{7,3},{8,12},{9,5},{1... | collective-permute-start | bytes 786440 | tf_op jit(solution)/shard_map/ppermute | solution.py:17
  59.2 0.0 collective-permute-start.15
  59.2 0.0 collective-permute-done.16.refs_1_
  59.2 0.0 collective-permute-done.17.refs_3_
  59.2 2.4 %score.5.refs_2_ = bf16[256,1024]{1,0:T(8,128)(2,1)S(1)} custom-call(bf16[64,4096]{1,0:T(8,128)(2,1)S(1)} %collective-permute-done.5.refs_0_, bf16[64,4096]{1,0:T(8,128)(2,1)S(1)} %collective-permute-done.16.refs_1_, bf16[64,4096]{1,0:T(8,128)(2,1)S(1)} %collective-permute-done.14.refs_2_.refs_0_, bf16[64,4096]{1,0:T(8,128)(2,1)S(1)} %collective-permute-done.17.refs_3_, ...), custom_call_target="tpu_custom_call" | custom-call | flops 2147483648 | bytes 11010048 | tf_op jit(solution)/shard_map/score/pallas_call | solution.py:151
  61.5 0.7 place.1.refs_5_
  62.2 0.7 collective-permute-done.18.refs_2_
  62.9 2.1 %collective-permute-start.19 = (bf16[32,4096]{1,0:T(8,128)(2,1)S(1)}, bf16[32,4096]{1,0:T(8,128)(2,1)S(1)}, u32[]{:S(2)}, u32[]{:S(2)}) collective-permute-start(bf16[32,4096]{1,0:T(8,128)(2,1)S(1)} %collective-permute-done.18.refs_2_), channel_id=1, source_target_pairs={{0,1},{1,0},{2,3},{3,2},{4,5},{5,4},{6,7},{7,6},{8,9},{9,8},{10,11... | collective-permute-start | bytes 786440 | tf_op jit(solution)/shard_map/ppermute | solution.py:17
  65.0 0.0 collective-permute-done.15.refs_1_
  65.0 1.2 %collective-permute-done.19.refs_3_ = bf16[32,4096]{1,0:T(8,128)(2,1)S(1)} collective-permute-done((bf16[32,4096]{1,0:T(8,128)(2,1)S(1)}, bf16[32,4096]{1,0:T(8,128)(2,1)S(1)}, u32[]{:S(2)}, u32[]{:S(2)}) %collective-permute-start.19) | collective-permute-done | bytes 262176 | tf_op jit(solution)/shard_map/ppermute | solution.py:17
  66.2 2.9 %finish.1 = bf16[32,32,1024]{2,1,0:T(8,128)(2,1)S(1)} custom-call(s32[32]{0:T(128)S(1)} %select_reduce_fusion.where_ref, bf16[32,4096]{1,0:T(8,128)(2,1)S(1)} %collective-permute-done.13.refs_0_, bf16[32,4096]{1,0:T(8,128)(2,1)S(1)} %collective-permute-done.15.refs_1_, ...), custom_call_target="tpu_custom_call", output_to_operand_aliasing={{}: (6, {})} | custom-call | flops 1073741824 | bytes 9699328 | tf_op jit(solution)/shard_map/finish/pallas_call | solution.py:204
  69.1 31.5 %all_to_all.5.in_ref = bf16[8,128,1024]{2,1,0:T(8,128)(2,1)S(1)} all-to-all(bf16[8,128,1024]{2,1,0:T(8,128)(2,1)S(1)} %bitcast.37), channel_id=1, replica_groups=mesh['group'=8,'blk'=32] {'group'}, dimensions={0} | all-to-all | bytes 4194304 | tf_op jit(solution)/shard_map/all_to_all | solution.py:307
  100.6 1.1 %total.1 = f32[1024,128]{1,0:T(8,128)} custom-call(bf16[8,128,1024]{2,1,0:T(8,128)(2,1)S(1)} %all_to_all.5.in_ref), custom_call_target="tpu_custom_call" | custom-call | tf_op jit(solution)/shard_map/total/pallas_call | solution.py:231
  (7 shorter events, 0.1 us)
Async XLA Ops:
  3.7 7.2 %collective-permute-start.1 = (bf16[32,4096]{1,0:T(8,128)(2,1)S(1)}, bf16[32,4096]{1,0:T(8,128)(2,1)S(1)}, u32[]{:S(2)}, u32[]{:S(2)}) collective-permute-start(bf16[32,4096]{1,0:T(8,128)(2,1)S(1)} %precond.1.refs_0_), channel_id=1, source_target_pairs={{0,1},{1,0},{2,3},{3,2},{4,5},{5,4},{6,7},{7,6},{8,9},{9,8},{10,11... | collective-permute-start | bytes 786440 | tf_op jit(solution)/shard_map/ppermute | solution.py:17
  7.0 12.3 %collective-permute-start = (bf16[32,4096]{1,0:T(8,128)(2,1)S(1)}, bf16[32,4096]{1,0:T(8,128)(2,1)S(1)}, u32[]{:S(2)}, u32[]{:S(2)}) collective-permute-start(bf16[32,4096]{1,0:T(8,128)(2,1)S(1)} %precond.1.refs_0_), channel_id=1, source_target_pairs={{0,4},{1,29},{2,6},{3,31},{4,8},{5,1},{6,10},{7,3},{8,12},{9,5},{1... | collective-permute-start | bytes 786440 | tf_op jit(solution)/shard_map/ppermute | solution.py:17
  10.8 8.4 %collective-permute-start.2 = (bf16[32,4096]{1,0:T(8,128)(2,1)S(1)}, bf16[32,4096]{1,0:T(8,128)(2,1)S(1)}, u32[]{:S(2)}, u32[]{:S(2)}) collective-permute-start(bf16[32,4096]{1,0:T(8,128)(2,1)S(1)} %collective-permute-done.1.refs_1_), channel_id=1, source_target_pairs={{0,4},{1,29},{2,6},{3,31},{4,8},{5,1},{6,10},{7,3},{8,12},{9,5},{1... | collective-permute-start | bytes 786440 | tf_op jit(solution)/shard_map/ppermute | solution.py:17
  12.0 7.3 %collective-permute-start.3 = (bf16[32,4096]{1,0:T(8,128)(2,1)S(1)}, bf16[32,4096]{1,0:T(8,128)(2,1)S(1)}, u32[]{:S(2)}, u32[]{:S(2)}) collective-permute-start(bf16[32,4096]{1,0:T(8,128)(2,1)S(1)} %precond.1.refs_0_), channel_id=1, source_target_pairs={{0,2},{1,3},{2,0},{3,1},{4,6},{5,7},{6,4},{7,5},{8,10},{9,11},{10,... | collective-permute-start | bytes 786440 | tf_op jit(solution)/shard_map/ppermute | solution.py:17
  19.3 1.6 %collective-permute-start.7 = (bf16[32,4096]{1,0:T(8,128)(2,1)S(1)}, bf16[32,4096]{1,0:T(8,128)(2,1)S(1)}, u32[]{:S(2)}, u32[]{:S(2)}) collective-permute-start(bf16[32,4096]{1,0:T(8,128)(2,1)S(1)} %collective-permute-done.3.refs_0_.refs_2_), channel_id=1, source_target_pairs={{0,1},{1,0},{2,3},{3,2},{4,5},{5,4},{6,7},{7,6},{8,9},{9,8},{10,11... | collective-permute-start | bytes 786440 | tf_op jit(solution)/shard_map/ppermute | solution.py:17
  21.0 9.4 %collective-permute-start.9 = (bf16[64,4096]{1,0:T(8,128)(2,1)S(1)}, bf16[64,4096]{1,0:T(8,128)(2,1)S(1)}, u32[]{:S(2)}, u32[]{:S(2)}) collective-permute-start(bf16[64,4096]{1,0:T(8,128)(2,1)S(1)} %joined.7), channel_id=1, source_target_pairs={{0,4},{1,29},{2,6},{3,31},{4,8},{5,1},{6,10},{7,3},{8,12},{9,5},{1... | collective-permute-start | bytes 1572872 | tf_op jit(solution)/shard_map/ppermute | solution.py:17
  24.2 11.7 %collective-permute-start.4 = (bf16[64,4096]{1,0:T(8,128)(2,1)S(1)}, bf16[64,4096]{1,0:T(8,128)(2,1)S(1)}, u32[]{:S(2)}, u32[]{:S(2)}) collective-permute-start(bf16[64,4096]{1,0:T(8,128)(2,1)S(1)} %joined.5.refs_4_), channel_id=1, source_target_pairs={{0,4},{1,29},{2,6},{3,31},{4,8},{5,1},{6,10},{7,3},{8,12},{9,5},{1... | collective-permute-start | bytes 1572872 | tf_op jit(solution)/shard_map/ppermute | solution.py:17
  25.0 14.4 %collective-permute-start.8 = (bf16[64,4096]{1,0:T(8,128)(2,1)S(1)}, bf16[64,4096]{1,0:T(8,128)(2,1)S(1)}, u32[]{:S(2)}, u32[]{:S(2)}) collective-permute-start(bf16[64,4096]{1,0:T(8,128)(2,1)S(1)} %joined.5.refs_4_), channel_id=1, source_target_pairs={{0,1},{1,0},{2,3},{3,2},{4,5},{5,4},{6,7},{7,6},{8,9},{9,8},{10,11... | collective-permute-start | bytes 1572872 | tf_op jit(solution)/shard_map/ppermute | solution.py:17
  30.4 9.1 %collective-permute-start.10 = (bf16[64,4096]{1,0:T(8,128)(2,1)S(1)}, bf16[64,4096]{1,0:T(8,128)(2,1)S(1)}, u32[]{:S(2)}, u32[]{:S(2)}) collective-permute-start(bf16[64,4096]{1,0:T(8,128)(2,1)S(1)} %collective-permute-done.9.refs_6_), channel_id=1, source_target_pairs={{0,1},{1,0},{2,3},{3,2},{4,5},{5,4},{6,7},{7,6},{8,9},{9,8},{10,11... | collective-permute-start | bytes 1572872 | tf_op jit(solution)/shard_map/ppermute | solution.py:17
  32.0 10.8 %collective-permute-start.11 = (bf16[64,4096]{1,0:T(8,128)(2,1)S(1)}, bf16[64,4096]{1,0:T(8,128)(2,1)S(1)}, u32[]{:S(2)}, u32[]{:S(2)}) collective-permute-start(bf16[64,4096]{1,0:T(8,128)(2,1)S(1)} %collective-permute-done.9.refs_6_), channel_id=1, source_target_pairs={{0,4},{1,29},{2,6},{3,31},{4,8},{5,1},{6,10},{7,3},{8,12},{9,5},{1... | collective-permute-start | bytes 1572872 | tf_op jit(solution)/shard_map/ppermute | solution.py:17
  36.0 14.5 %collective-permute-start.6 = (bf16[64,4096]{1,0:T(8,128)(2,1)S(1)}, bf16[64,4096]{1,0:T(8,128)(2,1)S(1)}, u32[]{:S(2)}, u32[]{:S(2)}) collective-permute-start(bf16[64,4096]{1,0:T(8,128)(2,1)S(1)} %collective-permute-done.4.refs_0_), channel_id=1, source_target_pairs={{0,1},{1,0},{2,3},{3,2},{4,5},{5,4},{6,7},{7,6},{8,9},{9,8},{10,11... | collective-permute-start | bytes 1572872 | tf_op jit(solution)/shard_map/ppermute | solution.py:17
  37.7 9.5 %collective-permute-start.5 = (bf16[64,4096]{1,0:T(8,128)(2,1)S(1)}, bf16[64,4096]{1,0:T(8,128)(2,1)S(1)}, u32[]{:S(2)}, u32[]{:S(2)}) collective-permute-start(bf16[64,4096]{1,0:T(8,128)(2,1)S(1)} %collective-permute-done.4.refs_0_), channel_id=1, source_target_pairs={{0,4},{1,29},{2,6},{3,31},{4,8},{5,1},{6,10},{7,3},{8,12},{9,5},{1... | collective-permute-start | bytes 1572872 | tf_op jit(solution)/shard_map/ppermute | solution.py:17
  42.9 7.6 %collective-permute-start.12 = (bf16[64,4096]{1,0:T(8,128)(2,1)S(1)}, bf16[64,4096]{1,0:T(8,128)(2,1)S(1)}, u32[]{:S(2)}, u32[]{:S(2)}) collective-permute-start(bf16[64,4096]{1,0:T(8,128)(2,1)S(1)} %collective-permute-done.11.refs_2_), channel_id=1, source_target_pairs={{0,1},{1,0},{2,3},{3,2},{4,5},{5,4},{6,7},{7,6},{8,9},{9,8},{10,11... | collective-permute-start | bytes 1572872 | tf_op jit(solution)/shard_map/ppermute | solution.py:17
  43.3 12.4 %collective-permute-start.14 = (bf16[64,4096]{1,0:T(8,128)(2,1)S(1)}, bf16[64,4096]{1,0:T(8,128)(2,1)S(1)}, u32[]{:S(2)}, u32[]{:S(2)}) collective-permute-start(bf16[64,4096]{1,0:T(8,128)(2,1)S(1)} %collective-permute-done.11.refs_2_), channel_id=1, source_target_pairs={{0,4},{1,29},{2,6},{3,31},{4,8},{5,1},{6,10},{7,3},{8,12},{9,5},{1... | collective-permute-start | bytes 1572872 | tf_op jit(solution)/shard_map/ppermute | solution.py:17
  47.2 8.4 %collective-permute-start.13 = (bf16[32,4096]{1,0:T(8,128)(2,1)S(1)}, bf16[32,4096]{1,0:T(8,128)(2,1)S(1)}, u32[]{:S(2)}, u32[]{:S(2)}) collective-permute-start(bf16[32,4096]{1,0:T(8,128)(2,1)S(1)} %joined.6), channel_id=1, source_target_pairs={{0,4},{1,29},{2,6},{3,31},{4,8},{5,1},{6,10},{7,3},{8,12},{9,5},{1... | collective-permute-start | bytes 786440 | tf_op jit(solution)/shard_map/ppermute | solution.py:17
  50.4 8.7 %collective-permute-start.16 = (bf16[64,4096]{1,0:T(8,128)(2,1)S(1)}, bf16[64,4096]{1,0:T(8,128)(2,1)S(1)}, u32[]{:S(2)}, u32[]{:S(2)}) collective-permute-start(bf16[64,4096]{1,0:T(8,128)(2,1)S(1)} %collective-permute-done.5.refs_0_), channel_id=1, source_target_pairs={{0,1},{1,0},{2,3},{3,2},{4,5},{5,4},{6,7},{7,6},{8,9},{9,8},{10,11... | collective-permute-start | bytes 1572872 | tf_op jit(solution)/shard_map/ppermute | solution.py:17
  55.6 3.5 %collective-permute-start.17 = (bf16[64,4096]{1,0:T(8,128)(2,1)S(1)}, bf16[64,4096]{1,0:T(8,128)(2,1)S(1)}, u32[]{:S(2)}, u32[]{:S(2)}) collective-permute-start(bf16[64,4096]{1,0:T(8,128)(2,1)S(1)} %collective-permute-done.14.refs_2_.refs_0_), channel_id=1, source_target_pairs={{0,1},{1,0},{2,3},{3,2},{4,5},{5,4},{6,7},{7,6},{8,9},{9,8},{10,11... | collective-permute-start | bytes 1572872 | tf_op jit(solution)/shard_map/ppermute | solution.py:17
  57.4 5.6 %collective-permute-start.18 = (bf16[32,4096]{1,0:T(8,128)(2,1)S(1)}, bf16[32,4096]{1,0:T(8,128)(2,1)S(1)}, u32[]{:S(2)}, u32[]{:S(2)}) collective-permute-start(bf16[32,4096]{1,0:T(8,128)(2,1)S(1)} %joined.8), channel_id=1, source_target_pairs={{0,4},{1,29},{2,6},{3,31},{4,8},{5,1},{6,10},{7,3},{8,12},{9,5},{1... | collective-permute-start | bytes 786440 | tf_op jit(solution)/shard_map/ppermute | solution.py:17
  59.2 5.9 %collective-permute-start.15 = (bf16[32,4096]{1,0:T(8,128)(2,1)S(1)}, bf16[32,4096]{1,0:T(8,128)(2,1)S(1)}, u32[]{:S(2)}, u32[]{:S(2)}) collective-permute-start(bf16[32,4096]{1,0:T(8,128)(2,1)S(1)} %collective-permute-done.13.refs_0_), channel_id=1, source_target_pairs={{0,1},{1,0},{2,3},{3,2},{4,5},{5,4},{6,7},{7,6},{8,9},{9,8},{10,11... | collective-permute-start | bytes 786440 | tf_op jit(solution)/shard_map/ppermute | solution.py:17
  62.9 3.2 %collective-permute-start.19 = (bf16[32,4096]{1,0:T(8,128)(2,1)S(1)}, bf16[32,4096]{1,0:T(8,128)(2,1)S(1)}, u32[]{:S(2)}, u32[]{:S(2)}) collective-permute-start(bf16[32,4096]{1,0:T(8,128)(2,1)S(1)} %collective-permute-done.18.refs_2_), channel_id=1, source_target_pairs={{0,1},{1,0},{2,3},{3,2},{4,5},{5,4},{6,7},{7,6},{8,9},{9,8},{10,11... | collective-permute-start | bytes 786440 | tf_op jit(solution)/shard_map/ppermute | solution.py:17

commit v10 on v9

--- a/solution.py
+++ b/solution.py
@@ -299,10 +299,10 @@
         steps[-1], far = lax.optimization_barrier((steps[-1], far))
         pieces = [near, _swap_core(near), far, _swap_core(far)]
     beyond = _along(_joined(far))
-    steps.append(_score(pieces, flat, scale))
+    steps.append(_score(pieces + [last, _swap_core(last)], flat, scale))
     early = _place(steps, where)
     early, beyond = lax.optimization_barrier((early, beyond))
-    buffer = _finish([last, _swap_core(last), beyond, _swap_core(beyond)], flat, scale, where, early)
+    buffer = _finish([beyond, _swap_core(beyond)], flat, scale, where, early)
     buffer = buffer.reshape(groups, -1, cand_rows)
     parts = lax.all_to_all(buffer, "group", split_axis=0, concat_axis=0, tiled=True)
     return _total(parts)

time: 102 us -> 102 us (level)
  transfers between devices with their start and end apart: 20 -> 20, of which waited for: 7 -> 6; matrix products, arithmetic and copies ran while one was open for 1% -> 1% of each run, Pallas kernels for 12% -> 13%
where the time goes in v10:
time: 102 us
  starting transfers between devices  33.8 us (33%)
  blocking collectives  31.5 us (31%)
  Pallas kernels  20.5 us (20%)
  waiting for transfers between devices  15.3 us (15%)
    ppermute x20, starting transfers between devices, _route(): lax.ppermute(x, 'blk', [(i, target(*divmod(i, 4))) for i in range(NZ * 4)])  33.8 us
    all_to_all x1, blocking collectives, body(): lax.all_to_all(buffer, 'group', split_axis=0, concat_axis=0, tiled=True)  31.5 us
    ppermute x20, waiting for transfers between devices, _route(): lax.ppermute(x, 'blk', [(i, target(*divmod(i, 4))) for i in range(NZ * 4)])  15.3 us
    pallas_call x3, Pallas kernels, _score(): pl.pallas_call(functools.partial(_score_kernel, scale, len(pieces)), in_s...  8.69 us
    pallas_call x1, Pallas kernels, _precond(): pl.pallas_call(_precond_kernel, in_specs=[pl.BlockSpec(memory_space=pltpu...  3.66 us
    pallas_call x1, Pallas kernels, _held(): pl.pallas_call(pltpu.sync_copy, in_specs=[pl.BlockSpec(memory_space=pl.AN...  3.39 us
    pallas_call x1, Pallas kernels, _finish(): pl.pallas_call(functools.partial(_finish_kernel, scale, len(pieces)), in_...  2.89 us
  transfers between devices with their start and end apart: 20, of which 6 were waited for; matrix products, arithmetic and copies ran while one was open for 1% of the time, Pallas kernels for 13%

profile of v10, /device:TPU:1, one launch (start us, length us, event | category | flops | bytes accessed | tf_op | source)
XLA Modules:
  0.0 102.2 jit_solution(16543137023193831676)
XLA Ops:
  0.0 3.7 %precond.1.refs_0_ = bf16[32,4096]{1,0:T(8,128)(2,1)S(1)} custom-call(f32[64,64]{1,0:T(8,128)} %bitcast.40, f32[64,64]{1,0:T(8,128)} %bitcast.41, bf16[32,4096]{1,0:T(8,128)(2,1)} %bitcast.39), custom_call_target="tpu_custom_call" | custom-call | tf_op jit(solution)/shard_map/precond/pallas_call | solution.py:90
  3.7 3.3 %collective-permute-start.1 = (bf16[32,4096]{1,0:T(8,128)(2,1)S(1)}, bf16[32,4096]{1,0:T(8,128)(2,1)S(1)}, u32[]{:S(2)}, u32[]{:S(2)}) collective-permute-start(bf16[32,4096]{1,0:T(8,128)(2,1)S(1)} %precond.1.refs_0_), channel_id=1, source_target_pairs={{0,1},{1,0},{2,3},{3,2},{4,5},{5,4},{6,7},{7,6},{8,9},{9,8},{10,11... | collective-permute-start | bytes 786440 | tf_op jit(solution)/shard_map/ppermute | solution.py:17
  7.0 3.8 %collective-permute-start = (bf16[32,4096]{1,0:T(8,128)(2,1)S(1)}, bf16[32,4096]{1,0:T(8,128)(2,1)S(1)}, u32[]{:S(2)}, u32[]{:S(2)}) collective-permute-start(bf16[32,4096]{1,0:T(8,128)(2,1)S(1)} %precond.1.refs_0_), channel_id=1, source_target_pairs={{0,4},{1,29},{2,6},{3,31},{4,8},{5,1},{6,10},{7,3},{8,12},{9,5},{1... | collective-permute-start | bytes 786440 | tf_op jit(solution)/shard_map/ppermute | solution.py:17
  10.8 0.0 collective-permute-done.1.refs_1_
  10.8 1.2 %collective-permute-start.2 = (bf16[32,4096]{1,0:T(8,128)(2,1)S(1)}, bf16[32,4096]{1,0:T(8,128)(2,1)S(1)}, u32[]{:S(2)}, u32[]{:S(2)}) collective-permute-start(bf16[32,4096]{1,0:T(8,128)(2,1)S(1)} %collective-permute-done.1.refs_1_), channel_id=1, source_target_pairs={{0,4},{1,29},{2,6},{3,31},{4,8},{5,1},{6,10},{7,3},{8,12},{9,5},{1... | collective-permute-start | bytes 786440 | tf_op jit(solution)/shard_map/ppermute | solution.py:17
  12.0 2.9 %collective-permute-start.3 = (bf16[32,4096]{1,0:T(8,128)(2,1)S(1)}, bf16[32,4096]{1,0:T(8,128)(2,1)S(1)}, u32[]{:S(2)}, u32[]{:S(2)}) collective-permute-start(bf16[32,4096]{1,0:T(8,128)(2,1)S(1)} %precond.1.refs_0_), channel_id=1, source_target_pairs={{0,2},{1,3},{2,0},{3,1},{4,6},{5,7},{6,4},{7,5},{8,10},{9,11},{10,... | collective-permute-start | bytes 786440 | tf_op jit(solution)/shard_map/ppermute | solution.py:17
  14.9 0.1 stack.131
  15.0 0.8 select_reduce_fusion.where_ref
  15.9 3.4 %held.1.refs_8_.refs_4_.refs_6_.refs_2_ = bf16[1024,4096]{1,0:T(8,128)(2,1)S(1)} custom-call(bf16[1024,4096]{1,0:T(8,128)(2,1)} %bitcast.38), custom_call_target="tpu_custom_call" | custom-call | bytes 16777216 | tf_op jit(solution)/shard_map/held/pallas_call | solution.py:126
  19.2 0.0 collective-permute-done.refs_0_
  19.3 0.0 collective-permute-done.2.refs_1_
  19.3 0.0 collective-permute-done.3.refs_0_.refs_2_
  19.3 0.1 collective-permute-start.5
  19.4 1.5 %collective-permute-done.5.refs_1_.refs_3_ = bf16[32,4096]{1,0:T(8,128)(2,1)S(1)} collective-permute-done((bf16[32,4096]{1,0:T(8,128)(2,1)S(1)}, bf16[32,4096]{1,0:T(8,128)(2,1)S(1)}, u32[]{:S(2)}, u32[]{:S(2)}) %collective-permute-start.5) | collective-permute-done | bytes 262176 | tf_op jit(solution)/shard_map/ppermute | solution.py:17
  21.0 3.3 %collective-permute-start.7 = (bf16[64,4096]{1,0:T(8,128)(2,1)S(1)}, bf16[64,4096]{1,0:T(8,128)(2,1)S(1)}, u32[]{:S(2)}, u32[]{:S(2)}) collective-permute-start(bf16[64,4096]{1,0:T(8,128)(2,1)S(1)} %joined.6), channel_id=1, source_target_pairs={{0,4},{1,29},{2,6},{3,31},{4,8},{5,1},{6,10},{7,3},{8,12},{9,5},{1... | collective-permute-start | bytes 1572872 | tf_op jit(solution)/shard_map/ppermute | solution.py:17
  24.2 0.7 collective-permute-start.4
  25.0 0.0 collective-permute-start.6
  25.0 5.4 %collective-permute-done.7.refs_6_ = bf16[64,4096]{1,0:T(8,128)(2,1)S(1)} collective-permute-done((bf16[64,4096]{1,0:T(8,128)(2,1)S(1)}, bf16[64,4096]{1,0:T(8,128)(2,1)S(1)}, u32[]{:S(2)}, u32[]{:S(2)}) %collective-permute-start.7) | collective-permute-done | bytes 524320 | tf_op jit(solution)/shard_map/ppermute | solution.py:17
  30.4 1.7 %collective-permute-start.8 = (bf16[64,4096]{1,0:T(8,128)(2,1)S(1)}, bf16[64,4096]{1,0:T(8,128)(2,1)S(1)}, u32[]{:S(2)}, u32[]{:S(2)}) collective-permute-start(bf16[64,4096]{1,0:T(8,128)(2,1)S(1)} %collective-permute-done.7.refs_6_), channel_id=1, source_target_pairs={{0,1},{1,0},{2,3},{3,2},{4,5},{5,4},{6,7},{7,6},{8,9},{9,8},{10,11... | collective-permute-start | bytes 1572872 | tf_op jit(solution)/shard_map/ppermute | solution.py:17
  32.0 1.7 %collective-permute-start.9 = (bf16[64,4096]{1,0:T(8,128)(2,1)S(1)}, bf16[64,4096]{1,0:T(8,128)(2,1)S(1)}, u32[]{:S(2)}, u32[]{:S(2)}) collective-permute-start(bf16[64,4096]{1,0:T(8,128)(2,1)S(1)} %collective-permute-done.7.refs_6_), channel_id=1, source_target_pairs={{0,4},{1,29},{2,6},{3,31},{4,8},{5,1},{6,10},{7,3},{8,12},{9,5},{1... | collective-permute-start | bytes 1572872 | tf_op jit(solution)/shard_map/ppermute | solution.py:17
  33.8 2.2 %collective-permute-done.4.refs_0_ = bf16[64,4096]{1,0:T(8,128)(2,1)S(1)} collective-permute-done((bf16[64,4096]{1,0:T(8,128)(2,1)S(1)}, bf16[64,4096]{1,0:T(8,128)(2,1)S(1)}, u32[]{:S(2)}, u32[]{:S(2)}) %collective-permute-start.4) | collective-permute-done | bytes 524320 | tf_op jit(solution)/shard_map/ppermute | solution.py:17
  36.0 3.1 %collective-permute-start.10 = (bf16[64,4096]{1,0:T(8,128)(2,1)S(1)}, bf16[64,4096]{1,0:T(8,128)(2,1)S(1)}, u32[]{:S(2)}, u32[]{:S(2)}) collective-permute-start(bf16[64,4096]{1,0:T(8,128)(2,1)S(1)} %collective-permute-done.4.refs_0_), channel_id=1, source_target_pairs={{0,4},{1,29},{2,6},{3,31},{4,8},{5,1},{6,10},{7,3},{8,12},{9,5},{1... | collective-permute-start | bytes 1572872 | tf_op jit(solution)/shard_map/ppermute | solution.py:17
  39.1 0.0 collective-permute-start.11
  39.1 0.0 collective-permute-done.6.refs_5_
  39.1 0.0 collective-permute-done.8.refs_7_
  39.1 3.4 %score.3.refs_0_ = bf16[384,1024]{1,0:T(8,128)(2,1)S(1)} custom-call(bf16[32,4096]{1,0:T(8,128)(2,1)S(1)} %precond.1.refs_0_, bf16[32,4096]{1,0:T(8,128)(2,1)S(1)} %collective-permute-done.1.refs_1_, bf16[32,4096]{1,0:T(8,128)(2,1)S(1)} %collective-permute-done.3.refs_0_.refs_2_, bf16[32,4096]{1,0:T(8,128)(2,1)S(1)} %collective-permute-done.5.refs_1_.refs_3_, ...), custom_call_target="tpu_custom_call" | custom-call | flops 3221225472 | bytes 12320768 | tf_op jit(solution)/shard_map/score/pallas_call | solution.py:151
  42.5 0.0 collective-permute-done.9.refs_2_
  42.6 0.7 collective-permute-start.12
  43.3 1.7 %collective-permute-start.14 = (bf16[64,4096]{1,0:T(8,128)(2,1)S(1)}, bf16[64,4096]{1,0:T(8,128)(2,1)S(1)}, u32[]{:S(2)}, u32[]{:S(2)}) collective-permute-start(bf16[64,4096]{1,0:T(8,128)(2,1)S(1)} %collective-permute-done.9.refs_2_), channel_id=1, source_target_pairs={{0,4},{1,29},{2,6},{3,31},{4,8},{5,1},{6,10},{7,3},{8,12},{9,5},{1... | collective-permute-start | bytes 1572872 | tf_op jit(solution)/shard_map/ppermute | solution.py:17
  45.0 2.2 %collective-permute-done.10.refs_0_ = bf16[64,4096]{1,0:T(8,128)(2,1)S(1)} collective-permute-done((bf16[64,4096]{1,0:T(8,128)(2,1)S(1)}, bf16[64,4096]{1,0:T(8,128)(2,1)S(1)}, u32[]{:S(2)}, u32[]{:S(2)}) %collective-permute-start.10) | collective-permute-done | bytes 524320 | tf_op jit(solution)/shard_map/ppermute | solution.py:17
  47.2 3.2 %collective-permute-start.13 = (bf16[32,4096]{1,0:T(8,128)(2,1)S(1)}, bf16[32,4096]{1,0:T(8,128)(2,1)S(1)}, u32[]{:S(2)}, u32[]{:S(2)}) collective-permute-start(bf16[32,4096]{1,0:T(8,128)(2,1)S(1)} %joined.7), channel_id=1, source_target_pairs={{0,4},{1,29},{2,6},{3,31},{4,8},{5,1},{6,10},{7,3},{8,12},{9,5},{1... | collective-permute-start | bytes 786440 | tf_op jit(solution)/shard_map/ppermute | solution.py:17
  50.4 0.0 collective-permute-start.15
  50.4 0.0 collective-permute-done.11.refs_1_
  50.4 0.0 collective-permute-done.12.refs_3_
  50.4 2.4 %score.4.refs_1_ = bf16[256,1024]{1,0:T(8,128)(2,1)S(1)} custom-call(bf16[64,4096]{1,0:T(8,128)(2,1)S(1)} %collective-permute-done.4.refs_0_, bf16[64,4096]{1,0:T(8,128)(2,1)S(1)} %collective-permute-done.11.refs_1_, bf16[64,4096]{1,0:T(8,128)(2,1)S(1)} %collective-permute-done.9.refs_2_, bf16[64,4096]{1,0:T(8,128)(2,1)S(1)} %collective-permute-done.12.refs_3_, ...), custom_call_target="tpu_custom_call" | custom-call | flops 2147483648 | bytes 11010048 | tf_op jit(solution)/shard_map/score/pallas_call | solution.py:151
  52.8 2.8 %collective-permute-done.13.refs_4_ = bf16[32,4096]{1,0:T(8,128)(2,1)S(1)} collective-permute-done((bf16[32,4096]{1,0:T(8,128)(2,1)S(1)}, bf16[32,4096]{1,0:T(8,128)(2,1)S(1)}, u32[]{:S(2)}, u32[]{:S(2)}) %collective-permute-start.13) | collective-permute-done | bytes 262176 | tf_op jit(solution)/shard_map/ppermute | solution.py:17
  55.6 1.7 %collective-permute-start.16 = (bf16[64,4096]{1,0:T(8,128)(2,1)S(1)}, bf16[64,4096]{1,0:T(8,128)(2,1)S(1)}, u32[]{:S(2)}, u32[]{:S(2)}) collective-permute-start(bf16[64,4096]{1,0:T(8,128)(2,1)S(1)} %collective-permute-done.14.refs_2_.refs_0_), channel_id=1, source_target_pairs={{0,1},{1,0},{2,3},{3,2},{4,5},{5,4},{6,7},{7,6},{8,9},{9,8},{10,11... | collective-permute-start | bytes 1572872 | tf_op jit(solution)/shard_map/ppermute | solution.py:17
  57.3 0.0 collective-permute-start.17
  57.4 2.0 %collective-permute-start.18 = (bf16[32,4096]{1,0:T(8,128)(2,1)S(1)}, bf16[32,4096]{1,0:T(8,128)(2,1)S(1)}, u32[]{:S(2)}, u32[]{:S(2)}) collective-permute-start(bf16[32,4096]{1,0:T(8,128)(2,1)S(1)} %joined.8), channel_id=1, source_target_pairs={{0,4},{1,29},{2,6},{3,31},{4,8},{5,1},{6,10},{7,3},{8,12},{9,5},{1... | collective-permute-start | bytes 786440 | tf_op jit(solution)/shard_map/ppermute | solution.py:17
  59.4 0.0 collective-permute-done.15.refs_1_
  59.4 0.0 collective-permute-done.17.refs_5_
  59.4 2.9 %score.5.refs_2_ = bf16[320,1024]{1,0:T(8,128)(2,1)S(1)} custom-call(bf16[64,4096]{1,0:T(8,128)(2,1)S(1)} %collective-permute-done.10.refs_0_, bf16[64,4096]{1,0:T(8,128)(2,1)S(1)} %collective-permute-done.15.refs_1_, bf16[64,4096]{1,0:T(8,128)(2,1)S(1)} %collective-permute-done.14.refs_2_.refs_0_, bf16[64,4096]{1,0:T(8,128)(2,1)S(1)} %collective-permute-done.16.refs_3_, ...), custom_call_target="tpu_custom_call" | custom-call | flops 2684354560 | bytes 11665408 | tf_op jit(solution)/shard_map/score/pallas_call | solution.py:151
  62.3 0.7 place.1.refs_3_
  63.0 2.5 %collective-permute-start.19 = (bf16[32,4096]{1,0:T(8,128)(2,1)S(1)}, bf16[32,4096]{1,0:T(8,128)(2,1)S(1)}, u32[]{:S(2)}, u32[]{:S(2)}) collective-permute-start(bf16[32,4096]{1,0:T(8,128)(2,1)S(1)} %collective-permute-done.18.refs_0_), channel_id=1, source_target_pairs={{0,1},{1,0},{2,3},{3,2},{4,5},{5,4},{6,7},{7,6},{8,9},{9,8},{10,11... | collective-permute-start | bytes 786440 | tf_op jit(solution)/shard_map/ppermute | solution.py:17
  65.5 1.2 %collective-permute-done.19.refs_1_ = bf16[32,4096]{1,0:T(8,128)(2,1)S(1)} collective-permute-done((bf16[32,4096]{1,0:T(8,128)(2,1)S(1)}, bf16[32,4096]{1,0:T(8,128)(2,1)S(1)}, u32[]{:S(2)}, u32[]{:S(2)}) %collective-permute-start.19) | collective-permute-done | bytes 262176 | tf_op jit(solution)/shard_map/ppermute | solution.py:17
  66.7 2.9 %finish.1 = bf16[32,32,1024]{2,1,0:T(8,128)(2,1)S(1)} custom-call(s32[32]{0:T(128)S(1)} %select_reduce_fusion.where_ref, bf16[32,4096]{1,0:T(8,128)(2,1)S(1)} %collective-permute-done.18.refs_0_, bf16[32,4096]{1,0:T(8,128)(2,1)S(1)} %collective-permute-done.19.refs_1_, ...), custom_call_target="tpu_custom_call", output_to_operand_aliasing={{}: (4, {})} | custom-call | flops 536870912 | bytes 9043968 | tf_op jit(solution)/shard_map/finish/pallas_call | solution.py:204
  69.6 31.5 %all_to_all.5.in_ref = bf16[8,128,1024]{2,1,0:T(8,128)(2,1)S(1)} all-to-all(bf16[8,128,1024]{2,1,0:T(8,128)(2,1)S(1)} %bitcast.37), channel_id=1, replica_groups=mesh['group'=8,'blk'=32] {'group'}, dimensions={0} | all-to-all | bytes 4194304 | tf_op jit(solution)/shard_map/all_to_all | solution.py:307
  101.1 1.1 %total.1 = f32[1024,128]{1,0:T(8,128)} custom-call(bf16[8,128,1024]{2,1,0:T(8,128)(2,1)S(1)} %all_to_all.5.in_ref), custom_call_target="tpu_custom_call" | custom-call | tf_op jit(solution)/shard_map/total/pallas_call | solution.py:231
  (7 shorter events, 0.1 us)
Async XLA Ops:
  3.7 7.2 %collective-permute-start.1 = (bf16[32,4096]{1,0:T(8,128)(2,1)S(1)}, bf16[32,4096]{1,0:T(8,128)(2,1)S(1)}, u32[]{:S(2)}, u32[]{:S(2)}) collective-permute-start(bf16[32,4096]{1,0:T(8,128)(2,1)S(1)} %precond.1.refs_0_), channel_id=1, source_target_pairs={{0,1},{1,0},{2,3},{3,2},{4,5},{5,4},{6,7},{7,6},{8,9},{9,8},{10,11... | collective-permute-start | bytes 786440 | tf_op jit(solution)/shard_map/ppermute | solution.py:17
  7.0 12.3 %collective-permute-start = (bf16[32,4096]{1,0:T(8,128)(2,1)S(1)}, bf16[32,4096]{1,0:T(8,128)(2,1)S(1)}, u32[]{:S(2)}, u32[]{:S(2)}) collective-permute-start(bf16[32,4096]{1,0:T(8,128)(2,1)S(1)} %precond.1.refs_0_), channel_id=1, source_target_pairs={{0,4},{1,29},{2,6},{3,31},{4,8},{5,1},{6,10},{7,3},{8,12},{9,5},{1... | collective-permute-start | bytes 786440 | tf_op jit(solution)/shard_map/ppermute | solution.py:17
  10.8 8.4 %collective-permute-start.2 = (bf16[32,4096]{1,0:T(8,128)(2,1)S(1)}, bf16[32,4096]{1,0:T(8,128)(2,1)S(1)}, u32[]{:S(2)}, u32[]{:S(2)}) collective-permute-start(bf16[32,4096]{1,0:T(8,128)(2,1)S(1)} %collective-permute-done.1.refs_1_), channel_id=1, source_target_pairs={{0,4},{1,29},{2,6},{3,31},{4,8},{5,1},{6,10},{7,3},{8,12},{9,5},{1... | collective-permute-start | bytes 786440 | tf_op jit(solution)/shard_map/ppermute | solution.py:17
  12.0 7.3 %collective-permute-start.3 = (bf16[32,4096]{1,0:T(8,128)(2,1)S(1)}, bf16[32,4096]{1,0:T(8,128)(2,1)S(1)}, u32[]{:S(2)}, u32[]{:S(2)}) collective-permute-start(bf16[32,4096]{1,0:T(8,128)(2,1)S(1)} %precond.1.refs_0_), channel_id=1, source_target_pairs={{0,2},{1,3},{2,0},{3,1},{4,6},{5,7},{6,4},{7,5},{8,10},{9,11},{10,... | collective-permute-start | bytes 786440 | tf_op jit(solution)/shard_map/ppermute | solution.py:17
  19.3 1.6 %collective-permute-start.5 = (bf16[32,4096]{1,0:T(8,128)(2,1)S(1)}, bf16[32,4096]{1,0:T(8,128)(2,1)S(1)}, u32[]{:S(2)}, u32[]{:S(2)}) collective-permute-start(bf16[32,4096]{1,0:T(8,128)(2,1)S(1)} %collective-permute-done.3.refs_0_.refs_2_), channel_id=1, source_target_pairs={{0,1},{1,0},{2,3},{3,2},{4,5},{5,4},{6,7},{7,6},{8,9},{9,8},{10,11... | collective-permute-start | bytes 786440 | tf_op jit(solution)/shard_map/ppermute | solution.py:17
  21.0 9.4 %collective-permute-start.7 = (bf16[64,4096]{1,0:T(8,128)(2,1)S(1)}, bf16[64,4096]{1,0:T(8,128)(2,1)S(1)}, u32[]{:S(2)}, u32[]{:S(2)}) collective-permute-start(bf16[64,4096]{1,0:T(8,128)(2,1)S(1)} %joined.6), channel_id=1, source_target_pairs={{0,4},{1,29},{2,6},{3,31},{4,8},{5,1},{6,10},{7,3},{8,12},{9,5},{1... | collective-permute-start | bytes 1572872 | tf_op jit(solution)/shard_map/ppermute | solution.py:17
  24.2 11.7 %collective-permute-start.4 = (bf16[64,4096]{1,0:T(8,128)(2,1)S(1)}, bf16[64,4096]{1,0:T(8,128)(2,1)S(1)}, u32[]{:S(2)}, u32[]{:S(2)}) collective-permute-start(bf16[64,4096]{1,0:T(8,128)(2,1)S(1)} %joined.5.refs_4_), channel_id=1, source_target_pairs={{0,4},{1,29},{2,6},{3,31},{4,8},{5,1},{6,10},{7,3},{8,12},{9,5},{1... | collective-permute-start | bytes 1572872 | tf_op jit(solution)/shard_map/ppermute | solution.py:17
  25.0 14.1 %collective-permute-start.6 = (bf16[64,4096]{1,0:T(8,128)(2,1)S(1)}, bf16[64,4096]{1,0:T(8,128)(2,1)S(1)}, u32[]{:S(2)}, u32[]{:S(2)}) collective-permute-start(bf16[64,4096]{1,0:T(8,128)(2,1)S(1)} %joined.5.refs_4_), channel_id=1, source_target_pairs={{0,1},{1,0},{2,3},{3,2},{4,5},{5,4},{6,7},{7,6},{8,9},{9,8},{10,11... | collective-permute-start | bytes 1572872 | tf_op jit(solution)/shard_map/ppermute | solution.py:17
  30.4 8.7 %collective-permute-start.8 = (bf16[64,4096]{1,0:T(8,128)(2,1)S(1)}, bf16[64,4096]{1,0:T(8,128)(2,1)S(1)}, u32[]{:S(2)}, u32[]{:S(2)}) collective-permute-start(bf16[64,4096]{1,0:T(8,128)(2,1)S(1)} %collective-permute-done.7.refs_6_), channel_id=1, source_target_pairs={{0,1},{1,0},{2,3},{3,2},{4,5},{5,4},{6,7},{7,6},{8,9},{9,8},{10,11... | collective-permute-start | bytes 1572872 | tf_op jit(solution)/shard_map/ppermute | solution.py:17
  32.0 10.5 %collective-permute-start.9 = (bf16[64,4096]{1,0:T(8,128)(2,1)S(1)}, bf16[64,4096]{1,0:T(8,128)(2,1)S(1)}, u32[]{:S(2)}, u32[]{:S(2)}) collective-permute-start(bf16[64,4096]{1,0:T(8,128)(2,1)S(1)} %collective-permute-done.7.refs_6_), channel_id=1, source_target_pairs={{0,4},{1,29},{2,6},{3,31},{4,8},{5,1},{6,10},{7,3},{8,12},{9,5},{1... | collective-permute-start | bytes 1572872 | tf_op jit(solution)/shard_map/ppermute | solution.py:17
  36.0 11.2 %collective-permute-start.10 = (bf16[64,4096]{1,0:T(8,128)(2,1)S(1)}, bf16[64,4096]{1,0:T(8,128)(2,1)S(1)}, u32[]{:S(2)}, u32[]{:S(2)}) collective-permute-start(bf16[64,4096]{1,0:T(8,128)(2,1)S(1)} %collective-permute-done.4.refs_0_), channel_id=1, source_target_pairs={{0,4},{1,29},{2,6},{3,31},{4,8},{5,1},{6,10},{7,3},{8,12},{9,5},{1... | collective-permute-start | bytes 1572872 | tf_op jit(solution)/shard_map/ppermute | solution.py:17
  39.1 11.3 %collective-permute-start.11 = (bf16[64,4096]{1,0:T(8,128)(2,1)S(1)}, bf16[64,4096]{1,0:T(8,128)(2,1)S(1)}, u32[]{:S(2)}, u32[]{:S(2)}) collective-permute-start(bf16[64,4096]{1,0:T(8,128)(2,1)S(1)} %collective-permute-done.4.refs_0_), channel_id=1, source_target_pairs={{0,1},{1,0},{2,3},{3,2},{4,5},{5,4},{6,7},{7,6},{8,9},{9,8},{10,11... | collective-permute-start | bytes 1572872 | tf_op jit(solution)/shard_map/ppermute | solution.py:17
  42.6 7.9 %collective-permute-start.12 = (bf16[64,4096]{1,0:T(8,128)(2,1)S(1)}, bf16[64,4096]{1,0:T(8,128)(2,1)S(1)}, u32[]{:S(2)}, u32[]{:S(2)}) collective-permute-start(bf16[64,4096]{1,0:T(8,128)(2,1)S(1)} %collective-permute-done.9.refs_2_), channel_id=1, source_target_pairs={{0,1},{1,0},{2,3},{3,2},{4,5},{5,4},{6,7},{7,6},{8,9},{9,8},{10,11... | collective-permute-start | bytes 1572872 | tf_op jit(solution)/shard_map/ppermute | solution.py:17
  43.3 12.4 %collective-permute-start.14 = (bf16[64,4096]{1,0:T(8,128)(2,1)S(1)}, bf16[64,4096]{1,0:T(8,128)(2,1)S(1)}, u32[]{:S(2)}, u32[]{:S(2)}) collective-permute-start(bf16[64,4096]{1,0:T(8,128)(2,1)S(1)} %collective-permute-done.9.refs_2_), channel_id=1, source_target_pairs={{0,4},{1,29},{2,6},{3,31},{4,8},{5,1},{6,10},{7,3},{8,12},{9,5},{1... | collective-permute-start | bytes 1572872 | tf_op jit(solution)/shard_map/ppermute | solution.py:17
  47.2 8.4 %collective-permute-start.13 = (bf16[32,4096]{1,0:T(8,128)(2,1)S(1)}, bf16[32,4096]{1,0:T(8,128)(2,1)S(1)}, u32[]{:S(2)}, u32[]{:S(2)}) collective-permute-start(bf16[32,4096]{1,0:T(8,128)(2,1)S(1)} %joined.7), channel_id=1, source_target_pairs={{0,4},{1,29},{2,6},{3,31},{4,8},{5,1},{6,10},{7,3},{8,12},{9,5},{1... | collective-permute-start | bytes 786440 | tf_op jit(solution)/shard_map/ppermute | solution.py:17
  50.4 8.9 %collective-permute-start.15 = (bf16[64,4096]{1,0:T(8,128)(2,1)S(1)}, bf16[64,4096]{1,0:T(8,128)(2,1)S(1)}, u32[]{:S(2)}, u32[]{:S(2)}) collective-permute-start(bf16[64,4096]{1,0:T(8,128)(2,1)S(1)} %collective-permute-done.10.refs_0_), channel_id=1, source_target_pairs={{0,1},{1,0},{2,3},{3,2},{4,5},{5,4},{6,7},{7,6},{8,9},{9,8},{10,11... | collective-permute-start | bytes 1572872 | tf_op jit(solution)/shard_map/ppermute | solution.py:17
  55.6 3.7 %collective-permute-start.16 = (bf16[64,4096]{1,0:T(8,128)(2,1)S(1)}, bf16[64,4096]{1,0:T(8,128)(2,1)S(1)}, u32[]{:S(2)}, u32[]{:S(2)}) collective-permute-start(bf16[64,4096]{1,0:T(8,128)(2,1)S(1)} %collective-permute-done.14.refs_2_.refs_0_), channel_id=1, source_target_pairs={{0,1},{1,0},{2,3},{3,2},{4,5},{5,4},{6,7},{7,6},{8,9},{9,8},{10,11... | collective-permute-start | bytes 1572872 | tf_op jit(solution)/shard_map/ppermute | solution.py:17
  57.3 2.0 %collective-permute-start.17 = (bf16[32,4096]{1,0:T(8,128)(2,1)S(1)}, bf16[32,4096]{1,0:T(8,128)(2,1)S(1)}, u32[]{:S(2)}, u32[]{:S(2)}) collective-permute-start(bf16[32,4096]{1,0:T(8,128)(2,1)S(1)} %collective-permute-done.13.refs_4_), channel_id=1, source_target_pairs={{0,1},{1,0},{2,3},{3,2},{4,5},{5,4},{6,7},{7,6},{8,9},{9,8},{10,11... | collective-permute-start | bytes 786440 | tf_op jit(solution)/shard_map/ppermute | solution.py:17
  57.4 5.6 %collective-permute-start.18 = (bf16[32,4096]{1,0:T(8,128)(2,1)S(1)}, bf16[32,4096]{1,0:T(8,128)(2,1)S(1)}, u32[]{:S(2)}, u32[]{:S(2)}) collective-permute-start(bf16[32,4096]{1,0:T(8,128)(2,1)S(1)} %joined.8), channel_id=1, source_target_pairs={{0,4},{1,29},{2,6},{3,31},{4,8},{5,1},{6,10},{7,3},{8,12},{9,5},{1... | collective-permute-start | bytes 786440 | tf_op jit(solution)/shard_map/ppermute | solution.py:17
  63.0 3.7 %collective-permute-start.19 = (bf16[32,4096]{1,0:T(8,128)(2,1)S(1)}, bf16[32,4096]{1,0:T(8,128)(2,1)S(1)}, u32[]{:S(2)}, u32[]{:S(2)}) collective-permute-start(bf16[32,4096]{1,0:T(8,128)(2,1)S(1)} %collective-permute-done.18.refs_0_), channel_id=1, source_target_pairs={{0,1},{1,0},{2,3},{3,2},{4,5},{5,4},{6,7},{7,6},{8,9},{9,8},{10,11... | collective-permute-start | bytes 786440 | tf_op jit(solution)/shard_map/ppermute | solution.py:17

commit v11 on v10

--- a/solution.py
+++ b/solution.py
@@ -286,7 +286,7 @@
     near = _joined(own, next_to)
     near, across, flat = lax.optimization_barrier((near, across, flat))
     across_other = _swap_core(across)
-    far = _along(_joined(across, across_other))
+    far = _joined(_along(across), _along(across_other))
     pieces = [panel, other, across, across_other, near, _swap_core(near), far, _swap_core(far)]
     for s in range(2, NZ // 2):
         near, far = _along(near), _along(far)

time: 102 us -> 100 us (0.980)
  waiting for transfers between devices: 15.3 us -> 13 us
    ppermute x20 -> x21, waiting for transfers between devices: 15.3 us -> 13 us  [_route(): lax.ppermute(x, 'blk', [(i, target(*divmod(i, 4))) for i in range(NZ * 4)])]
    ppermute x20 -> x21, starting transfers between devices: 33.8 us -> 34.4 us  [_route(): lax.ppermute(x, 'blk', [(i, target(*divmod(i, 4))) for i in range(NZ * 4)])]
  transfers between devices with their start and end apart: 20 -> 21, of which waited for: 6 -> 6; matrix products, arithmetic and copies ran while one was open for 1% -> 1% of each run, Pallas kernels for 13% -> 13%
where the time goes in v11:
time: 100 us
  starting transfers between devices  34.4 us (34%)
  blocking collectives  31.2 us (31%)
  Pallas kernels  20.5 us (20%)
  waiting for transfers between devices  13 us (13%)
    ppermute x21, starting transfers between devices, _route(): lax.ppermute(x, 'blk', [(i, target(*divmod(i, 4))) for i in range(NZ * 4)])  34.4 us
    all_to_all x1, blocking collectives, body(): lax.all_to_all(buffer, 'group', split_axis=0, concat_axis=0, tiled=True)  31.2 us
    ppermute x21, waiting for transfers between devices, _route(): lax.ppermute(x, 'blk', [(i, target(*divmod(i, 4))) for i in range(NZ * 4)])  13 us
    pallas_call x3, Pallas kernels, _score(): pl.pallas_call(functools.partial(_score_kernel, scale, len(pieces)), in_s...  8.69 us
    pallas_call x1, Pallas kernels, _precond(): pl.pallas_call(_precond_kernel, in_specs=[pl.BlockSpec(memory_space=pltpu...  3.66 us
    pallas_call x1, Pallas kernels, _held(): pl.pallas_call(pltpu.sync_copy, in_specs=[pl.BlockSpec(memory_space=pl.AN...  3.39 us
    pallas_call x1, Pallas kernels, _finish(): pl.pallas_call(functools.partial(_finish_kernel, scale, len(pieces)), in_...  2.9 us
  transfers between devices with their start and end apart: 21, of which 6 were waited for; matrix products, arithmetic and copies ran while one was open for 1% of the time, Pallas kernels for 13%

profile of v11, /device:TPU:1, one launch (start us, length us, event | category | flops | bytes accessed | tf_op | source)
XLA Modules:
  0.0 100.2 jit_solution(13536401703696143124)
XLA Ops:
  0.0 3.7 %precond.1.refs_0_ = bf16[32,4096]{1,0:T(8,128)(2,1)S(1)} custom-call(f32[64,64]{1,0:T(8,128)} %bitcast.40, f32[64,64]{1,0:T(8,128)} %bitcast.41, bf16[32,4096]{1,0:T(8,128)(2,1)} %bitcast.39), custom_call_target="tpu_custom_call" | custom-call | tf_op jit(solution)/shard_map/precond/pallas_call | solution.py:90
  3.7 3.3 %collective-permute-start.1 = (bf16[32,4096]{1,0:T(8,128)(2,1)S(1)}, bf16[32,4096]{1,0:T(8,128)(2,1)S(1)}, u32[]{:S(2)}, u32[]{:S(2)}) collective-permute-start(bf16[32,4096]{1,0:T(8,128)(2,1)S(1)} %precond.1.refs_0_), channel_id=1, source_target_pairs={{0,1},{1,0},{2,3},{3,2},{4,5},{5,4},{6,7},{7,6},{8,9},{9,8},{10,11... | collective-permute-start | bytes 786440 | tf_op jit(solution)/shard_map/ppermute | solution.py:17
  7.0 3.8 %collective-permute-start = (bf16[32,4096]{1,0:T(8,128)(2,1)S(1)}, bf16[32,4096]{1,0:T(8,128)(2,1)S(1)}, u32[]{:S(2)}, u32[]{:S(2)}) collective-permute-start(bf16[32,4096]{1,0:T(8,128)(2,1)S(1)} %precond.1.refs_0_), channel_id=1, source_target_pairs={{0,4},{1,29},{2,6},{3,31},{4,8},{5,1},{6,10},{7,3},{8,12},{9,5},{1... | collective-permute-start | bytes 786440 | tf_op jit(solution)/shard_map/ppermute | solution.py:17
  10.8 0.0 collective-permute-done.1.refs_1_
  10.8 1.2 %collective-permute-start.2 = (bf16[32,4096]{1,0:T(8,128)(2,1)S(1)}, bf16[32,4096]{1,0:T(8,128)(2,1)S(1)}, u32[]{:S(2)}, u32[]{:S(2)}) collective-permute-start(bf16[32,4096]{1,0:T(8,128)(2,1)S(1)} %collective-permute-done.1.refs_1_), channel_id=1, source_target_pairs={{0,4},{1,29},{2,6},{3,31},{4,8},{5,1},{6,10},{7,3},{8,12},{9,5},{1... | collective-permute-start | bytes 786440 | tf_op jit(solution)/shard_map/ppermute | solution.py:17
  12.0 2.9 %collective-permute-start.3 = (bf16[32,4096]{1,0:T(8,128)(2,1)S(1)}, bf16[32,4096]{1,0:T(8,128)(2,1)S(1)}, u32[]{:S(2)}, u32[]{:S(2)}) collective-permute-start(bf16[32,4096]{1,0:T(8,128)(2,1)S(1)} %precond.1.refs_0_), channel_id=1, source_target_pairs={{0,2},{1,3},{2,0},{3,1},{4,6},{5,7},{6,4},{7,5},{8,10},{9,11},{10,... | collective-permute-start | bytes 786440 | tf_op jit(solution)/shard_map/ppermute | solution.py:17
  14.9 0.1 stack.131
  15.0 0.8 select_reduce_fusion.where_ref
  15.9 3.4 %held.1.refs_8_.refs_4_.refs_6_.refs_2_ = bf16[1024,4096]{1,0:T(8,128)(2,1)S(1)} custom-call(bf16[1024,4096]{1,0:T(8,128)(2,1)} %bitcast.38), custom_call_target="tpu_custom_call" | custom-call | bytes 16777216 | tf_op jit(solution)/shard_map/held/pallas_call | solution.py:126
  19.2 0.0 collective-permute-done.refs_0_
  19.3 0.0 collective-permute-done.2.refs_1_
  19.3 0.0 collective-permute-done.3.refs_2_
  19.3 0.1 collective-permute-start.5
  19.4 3.5 %collective-permute-start.7 = (bf16[32,4096]{1,0:T(8,128)(2,1)S(1)}, bf16[32,4096]{1,0:T(8,128)(2,1)S(1)}, u32[]{:S(2)}, u32[]{:S(2)}) collective-permute-start(bf16[32,4096]{1,0:T(8,128)(2,1)S(1)} %collective-permute-done.3.refs_2_), channel_id=1, source_target_pairs={{0,4},{1,29},{2,6},{3,31},{4,8},{5,1},{6,10},{7,3},{8,12},{9,5},{1... | collective-permute-start | bytes 786440 | tf_op jit(solution)/shard_map/ppermute | solution.py:17
  23.0 0.0 collective-permute-done.5.refs_3_
  23.0 1.2 %collective-permute-start.8 = (bf16[32,4096]{1,0:T(8,128)(2,1)S(1)}, bf16[32,4096]{1,0:T(8,128)(2,1)S(1)}, u32[]{:S(2)}, u32[]{:S(2)}) collective-permute-start(bf16[32,4096]{1,0:T(8,128)(2,1)S(1)} %collective-permute-done.5.refs_3_), channel_id=1, source_target_pairs={{0,4},{1,29},{2,6},{3,31},{4,8},{5,1},{6,10},{7,3},{8,12},{9,5},{1... | collective-permute-start | bytes 786440 | tf_op jit(solution)/shard_map/ppermute | solution.py:17
  24.1 0.7 collective-permute-start.4
  24.8 1.4 %collective-permute-done.7.refs_0_ = bf16[32,4096]{1,0:T(8,128)(2,1)S(1)} collective-permute-done((bf16[32,4096]{1,0:T(8,128)(2,1)S(1)}, bf16[32,4096]{1,0:T(8,128)(2,1)S(1)}, u32[]{:S(2)}, u32[]{:S(2)}) %collective-permute-start.7) | collective-permute-done | bytes 262176 | tf_op jit(solution)/shard_map/ppermute | solution.py:17
  26.3 2.8 %collective-permute-done.8.refs_1_ = bf16[32,4096]{1,0:T(8,128)(2,1)S(1)} collective-permute-done((bf16[32,4096]{1,0:T(8,128)(2,1)S(1)}, bf16[32,4096]{1,0:T(8,128)(2,1)S(1)}, u32[]{:S(2)}, u32[]{:S(2)}) %collective-permute-start.8) | collective-permute-done | bytes 262176 | tf_op jit(solution)/shard_map/ppermute | solution.py:17
  29.1 1.4 %collective-permute-start.9 = (bf16[64,4096]{1,0:T(8,128)(2,1)S(1)}, bf16[64,4096]{1,0:T(8,128)(2,1)S(1)}, u32[]{:S(2)}, u32[]{:S(2)}) collective-permute-start(bf16[64,4096]{1,0:T(8,128)(2,1)S(1)} %joined.6.refs_6_), channel_id=1, source_target_pairs={{0,1},{1,0},{2,3},{3,2},{4,5},{5,4},{6,7},{7,6},{8,9},{9,8},{10,11... | collective-permute-start | bytes 1572872 | tf_op jit(solution)/shard_map/ppermute | solution.py:17
  30.5 1.9 %collective-permute-start.10 = (bf16[64,4096]{1,0:T(8,128)(2,1)S(1)}, bf16[64,4096]{1,0:T(8,128)(2,1)S(1)}, u32[]{:S(2)}, u32[]{:S(2)}) collective-permute-start(bf16[64,4096]{1,0:T(8,128)(2,1)S(1)} %joined.6.refs_6_), channel_id=1, source_target_pairs={{0,4},{1,29},{2,6},{3,31},{4,8},{5,1},{6,10},{7,3},{8,12},{9,5},{1... | collective-permute-start | bytes 1572872 | tf_op jit(solution)/shard_map/ppermute | solution.py:17
  32.4 2.3 %collective-permute-done.4.refs_0_ = bf16[64,4096]{1,0:T(8,128)(2,1)S(1)} collective-permute-done((bf16[64,4096]{1,0:T(8,128)(2,1)S(1)}, bf16[64,4096]{1,0:T(8,128)(2,1)S(1)}, u32[]{:S(2)}, u32[]{:S(2)}) %collective-permute-start.4) | collective-permute-done | bytes 524320 | tf_op jit(solution)/shard_map/ppermute | solution.py:17
  34.7 3.1 %collective-permute-start.11 = (bf16[64,4096]{1,0:T(8,128)(2,1)S(1)}, bf16[64,4096]{1,0:T(8,128)(2,1)S(1)}, u32[]{:S(2)}, u32[]{:S(2)}) collective-permute-start(bf16[64,4096]{1,0:T(8,128)(2,1)S(1)} %collective-permute-done.4.refs_0_), channel_id=1, source_target_pairs={{0,4},{1,29},{2,6},{3,31},{4,8},{5,1},{6,10},{7,3},{8,12},{9,5},{1... | collective-permute-start | bytes 1572872 | tf_op jit(solution)/shard_map/ppermute | solution.py:17
  37.8 0.0 collective-permute-start.12
  37.8 3.4 %score.3.refs_0_ = bf16[384,1024]{1,0:T(8,128)(2,1)S(1)} custom-call(bf16[32,4096]{1,0:T(8,128)(2,1)S(1)} %precond.1.refs_0_, bf16[32,4096]{1,0:T(8,128)(2,1)S(1)} %collective-permute-done.1.refs_1_, bf16[32,4096]{1,0:T(8,128)(2,1)S(1)} %collective-permute-done.3.refs_2_, bf16[32,4096]{1,0:T(8,128)(2,1)S(1)} %collective-permute-done.5.refs_3_, ...), custom_call_target="tpu_custom_call" | custom-call | flops 3221225472 | bytes 12320768 | tf_op jit(solution)/shard_map/score/pallas_call | solution.py:151
  41.3 0.0 collective-permute-done.10.refs_2_
  41.3 0.6 collective-permute-start.13
  41.9 1.6 %collective-permute-start.15 = (bf16[64,4096]{1,0:T(8,128)(2,1)S(1)}, bf16[64,4096]{1,0:T(8,128)(2,1)S(1)}, u32[]{:S(2)}, u32[]{:S(2)}) collective-permute-start(bf16[64,4096]{1,0:T(8,128)(2,1)S(1)} %collective-permute-done.10.refs_2_), channel_id=1, source_target_pairs={{0,4},{1,29},{2,6},{3,31},{4,8},{5,1},{6,10},{7,3},{8,12},{9,5},{1... | collective-permute-start | bytes 1572872 | tf_op jit(solution)/shard_map/ppermute | solution.py:17
  43.4 2.5 %collective-permute-done.11.refs_0_ = bf16[64,4096]{1,0:T(8,128)(2,1)S(1)} collective-permute-done((bf16[64,4096]{1,0:T(8,128)(2,1)S(1)}, bf16[64,4096]{1,0:T(8,128)(2,1)S(1)}, u32[]{:S(2)}, u32[]{:S(2)}) %collective-permute-start.11) | collective-permute-done | bytes 524320 | tf_op jit(solution)/shard_map/ppermute | solution.py:17
  46.0 3.2 %collective-permute-start.14 = (bf16[32,4096]{1,0:T(8,128)(2,1)S(1)}, bf16[32,4096]{1,0:T(8,128)(2,1)S(1)}, u32[]{:S(2)}, u32[]{:S(2)}) collective-permute-start(bf16[32,4096]{1,0:T(8,128)(2,1)S(1)} %joined.7), channel_id=1, source_target_pairs={{0,4},{1,29},{2,6},{3,31},{4,8},{5,1},{6,10},{7,3},{8,12},{9,5},{1... | collective-permute-start | bytes 786440 | tf_op jit(solution)/shard_map/ppermute | solution.py:17
  49.1 0.0 collective-permute-done.12.refs_1_
  49.2 0.0 collective-permute-done.13.refs_3_
  49.2 2.4 %score.4.refs_1_ = bf16[256,1024]{1,0:T(8,128)(2,1)S(1)} custom-call(bf16[64,4096]{1,0:T(8,128)(2,1)S(1)} %collective-permute-done.4.refs_0_, bf16[64,4096]{1,0:T(8,128)(2,1)S(1)} %collective-permute-done.12.refs_1_, bf16[64,4096]{1,0:T(8,128)(2,1)S(1)} %collective-permute-done.10.refs_2_, bf16[64,4096]{1,0:T(8,128)(2,1)S(1)} %collective-permute-done.13.refs_3_, ...), custom_call_target="tpu_custom_call" | custom-call | flops 2147483648 | bytes 11010048 | tf_op jit(solution)/shard_map/score/pallas_call | solution.py:151
  51.5 2.8 %collective-permute-done.14.refs_4_ = bf16[32,4096]{1,0:T(8,128)(2,1)S(1)} collective-permute-done((bf16[32,4096]{1,0:T(8,128)(2,1)S(1)}, bf16[32,4096]{1,0:T(8,128)(2,1)S(1)}, u32[]{:S(2)}, u32[]{:S(2)}) %collective-permute-start.14) | collective-permute-done | bytes 262176 | tf_op jit(solution)/shard_map/ppermute | solution.py:17
  54.4 1.3 %collective-permute-start.17 = (bf16[64,4096]{1,0:T(8,128)(2,1)S(1)}, bf16[64,4096]{1,0:T(8,128)(2,1)S(1)}, u32[]{:S(2)}, u32[]{:S(2)}) collective-permute-start(bf16[64,4096]{1,0:T(8,128)(2,1)S(1)} %collective-permute-done.15.refs_2_.refs_0_), channel_id=1, source_target_pairs={{0,1},{1,0},{2,3},{3,2},{4,5},{5,4},{6,7},{7,6},{8,9},{9,8},{10,11... | collective-permute-start | bytes 1572872 | tf_op jit(solution)/shard_map/ppermute | solution.py:17
  55.7 0.0 collective-permute-start.18
  55.7 2.4 %collective-permute-start.19 = (bf16[32,4096]{1,0:T(8,128)(2,1)S(1)}, bf16[32,4096]{1,0:T(8,128)(2,1)S(1)}, u32[]{:S(2)}, u32[]{:S(2)}) collective-permute-start(bf16[32,4096]{1,0:T(8,128)(2,1)S(1)} %joined.8), channel_id=1, source_target_pairs={{0,4},{1,29},{2,6},{3,31},{4,8},{5,1},{6,10},{7,3},{8,12},{9,5},{1... | collective-permute-start | bytes 786440 | tf_op jit(solution)/shard_map/ppermute | solution.py:17
  58.1 0.0 collective-permute-done.16.refs_1_
  58.1 0.0 collective-permute-done.18.refs_5_
  58.1 0.0 collective-permute-done.17.refs_3_
  58.1 2.9 %score.5.refs_2_ = bf16[320,1024]{1,0:T(8,128)(2,1)S(1)} custom-call(bf16[64,4096]{1,0:T(8,128)(2,1)S(1)} %collective-permute-done.11.refs_0_, bf16[64,4096]{1,0:T(8,128)(2,1)S(1)} %collective-permute-done.16.refs_1_, bf16[64,4096]{1,0:T(8,128)(2,1)S(1)} %collective-permute-done.15.refs_2_.refs_0_, bf16[64,4096]{1,0:T(8,128)(2,1)S(1)} %collective-permute-done.17.refs_3_, ...), custom_call_target="tpu_custom_call" | custom-call | flops 2684354560 | bytes 11665408 | tf_op jit(solution)/shard_map/score/pallas_call | solution.py:151
  61.0 0.7 place.1.refs_3_
  61.7 0.0 collective-permute-done.19.refs_0_
  61.7 2.2 %collective-permute-start.20 = (bf16[32,4096]{1,0:T(8,128)(2,1)S(1)}, bf16[32,4096]{1,0:T(8,128)(2,1)S(1)}, u32[]{:S(2)}, u32[]{:S(2)}) collective-permute-start(bf16[32,4096]{1,0:T(8,128)(2,1)S(1)} %collective-permute-done.19.refs_0_), channel_id=1, source_target_pairs={{0,1},{1,0},{2,3},{3,2},{4,5},{5,4},{6,7},{7,6},{8,9},{9,8},{10,11... | collective-permute-start | bytes 786440 | tf_op jit(solution)/shard_map/ppermute | solution.py:17
  63.9 1.2 %collective-permute-done.20.refs_1_ = bf16[32,4096]{1,0:T(8,128)(2,1)S(1)} collective-permute-done((bf16[32,4096]{1,0:T(8,128)(2,1)S(1)}, bf16[32,4096]{1,0:T(8,128)(2,1)S(1)}, u32[]{:S(2)}, u32[]{:S(2)}) %collective-permute-start.20) | collective-permute-done | bytes 262176 | tf_op jit(solution)/shard_map/ppermute | solution.py:17
  65.0 2.9 %finish.1 = bf16[32,32,1024]{2,1,0:T(8,128)(2,1)S(1)} custom-call(s32[32]{0:T(128)S(1)} %select_reduce_fusion.where_ref, bf16[32,4096]{1,0:T(8,128)(2,1)S(1)} %collective-permute-done.19.refs_0_, bf16[32,4096]{1,0:T(8,128)(2,1)S(1)} %collective-permute-done.20.refs_1_, ...), custom_call_target="tpu_custom_call", output_to_operand_aliasing={{}: (4, {})} | custom-call | flops 536870912 | bytes 9043968 | tf_op jit(solution)/shard_map/finish/pallas_call | solution.py:204
  67.9 31.2 %all_to_all.5.in_ref = bf16[8,128,1024]{2,1,0:T(8,128)(2,1)S(1)} all-to-all(bf16[8,128,1024]{2,1,0:T(8,128)(2,1)S(1)} %bitcast.37), channel_id=1, replica_groups=mesh['group'=8,'blk'=32] {'group'}, dimensions={0} | all-to-all | bytes 4194304 | tf_op jit(solution)/shard_map/all_to_all | solution.py:307
  99.1 1.1 %total.1 = f32[1024,128]{1,0:T(8,128)} custom-call(bf16[8,128,1024]{2,1,0:T(8,128)(2,1)S(1)} %all_to_all.5.in_ref), custom_call_target="tpu_custom_call" | custom-call | tf_op jit(solution)/shard_map/total/pallas_call | solution.py:231
  (9 shorter events, 0.1 us)
Async XLA Ops:
  3.7 7.2 %collective-permute-start.1 = (bf16[32,4096]{1,0:T(8,128)(2,1)S(1)}, bf16[32,4096]{1,0:T(8,128)(2,1)S(1)}, u32[]{:S(2)}, u32[]{:S(2)}) collective-permute-start(bf16[32,4096]{1,0:T(8,128)(2,1)S(1)} %precond.1.refs_0_), channel_id=1, source_target_pairs={{0,1},{1,0},{2,3},{3,2},{4,5},{5,4},{6,7},{7,6},{8,9},{9,8},{10,11... | collective-permute-start | bytes 786440 | tf_op jit(solution)/shard_map/ppermute | solution.py:17
  7.0 12.3 %collective-permute-start = (bf16[32,4096]{1,0:T(8,128)(2,1)S(1)}, bf16[32,4096]{1,0:T(8,128)(2,1)S(1)}, u32[]{:S(2)}, u32[]{:S(2)}) collective-permute-start(bf16[32,4096]{1,0:T(8,128)(2,1)S(1)} %precond.1.refs_0_), channel_id=1, source_target_pairs={{0,4},{1,29},{2,6},{3,31},{4,8},{5,1},{6,10},{7,3},{8,12},{9,5},{1... | collective-permute-start | bytes 786440 | tf_op jit(solution)/shard_map/ppermute | solution.py:17
  10.8 8.4 %collective-permute-start.2 = (bf16[32,4096]{1,0:T(8,128)(2,1)S(1)}, bf16[32,4096]{1,0:T(8,128)(2,1)S(1)}, u32[]{:S(2)}, u32[]{:S(2)}) collective-permute-start(bf16[32,4096]{1,0:T(8,128)(2,1)S(1)} %collective-permute-done.1.refs_1_), channel_id=1, source_target_pairs={{0,4},{1,29},{2,6},{3,31},{4,8},{5,1},{6,10},{7,3},{8,12},{9,5},{1... | collective-permute-start | bytes 786440 | tf_op jit(solution)/shard_map/ppermute | solution.py:17
  12.0 7.3 %collective-permute-start.3 = (bf16[32,4096]{1,0:T(8,128)(2,1)S(1)}, bf16[32,4096]{1,0:T(8,128)(2,1)S(1)}, u32[]{:S(2)}, u32[]{:S(2)}) collective-permute-start(bf16[32,4096]{1,0:T(8,128)(2,1)S(1)} %precond.1.refs_0_), channel_id=1, source_target_pairs={{0,2},{1,3},{2,0},{3,1},{4,6},{5,7},{6,4},{7,5},{8,10},{9,11},{10,... | collective-permute-start | bytes 786440 | tf_op jit(solution)/shard_map/ppermute | solution.py:17
  19.3 3.6 %collective-permute-start.5 = (bf16[32,4096]{1,0:T(8,128)(2,1)S(1)}, bf16[32,4096]{1,0:T(8,128)(2,1)S(1)}, u32[]{:S(2)}, u32[]{:S(2)}) collective-permute-start(bf16[32,4096]{1,0:T(8,128)(2,1)S(1)} %collective-permute-done.3.refs_2_), channel_id=1, source_target_pairs={{0,1},{1,0},{2,3},{3,2},{4,5},{5,4},{6,7},{7,6},{8,9},{9,8},{10,11... | collective-permute-start | bytes 786440 | tf_op jit(solution)/shard_map/ppermute | solution.py:17
  19.4 6.9 %collective-permute-start.7 = (bf16[32,4096]{1,0:T(8,128)(2,1)S(1)}, bf16[32,4096]{1,0:T(8,128)(2,1)S(1)}, u32[]{:S(2)}, u32[]{:S(2)}) collective-permute-start(bf16[32,4096]{1,0:T(8,128)(2,1)S(1)} %collective-permute-done.3.refs_2_), channel_id=1, source_target_pairs={{0,4},{1,29},{2,6},{3,31},{4,8},{5,1},{6,10},{7,3},{8,12},{9,5},{1... | collective-permute-start | bytes 786440 | tf_op jit(solution)/shard_map/ppermute | solution.py:17
  23.0 6.1 %collective-permute-start.8 = (bf16[32,4096]{1,0:T(8,128)(2,1)S(1)}, bf16[32,4096]{1,0:T(8,128)(2,1)S(1)}, u32[]{:S(2)}, u32[]{:S(2)}) collective-permute-start(bf16[32,4096]{1,0:T(8,128)(2,1)S(1)} %collective-permute-done.5.refs_3_), channel_id=1, source_target_pairs={{0,4},{1,29},{2,6},{3,31},{4,8},{5,1},{6,10},{7,3},{8,12},{9,5},{1... | collective-permute-start | bytes 786440 | tf_op jit(solution)/shard_map/ppermute | solution.py:17
  24.1 10.6 %collective-permute-start.4 = (bf16[64,4096]{1,0:T(8,128)(2,1)S(1)}, bf16[64,4096]{1,0:T(8,128)(2,1)S(1)}, u32[]{:S(2)}, u32[]{:S(2)}) collective-permute-start(bf16[64,4096]{1,0:T(8,128)(2,1)S(1)} %joined.5.refs_4_), channel_id=1, source_target_pairs={{0,4},{1,29},{2,6},{3,31},{4,8},{5,1},{6,10},{7,3},{8,12},{9,5},{1... | collective-permute-start | bytes 1572872 | tf_op jit(solution)/shard_map/ppermute | solution.py:17
  24.8 13.0 %collective-permute-start.6 = (bf16[64,4096]{1,0:T(8,128)(2,1)S(1)}, bf16[64,4096]{1,0:T(8,128)(2,1)S(1)}, u32[]{:S(2)}, u32[]{:S(2)}) collective-permute-start(bf16[64,4096]{1,0:T(8,128)(2,1)S(1)} %joined.5.refs_4_), channel_id=1, source_target_pairs={{0,1},{1,0},{2,3},{3,2},{4,5},{5,4},{6,7},{7,6},{8,9},{9,8},{10,11... | collective-permute-start | bytes 1572872 | tf_op jit(solution)/shard_map/ppermute | solution.py:17
  29.1 8.7 %collective-permute-start.9 = (bf16[64,4096]{1,0:T(8,128)(2,1)S(1)}, bf16[64,4096]{1,0:T(8,128)(2,1)S(1)}, u32[]{:S(2)}, u32[]{:S(2)}) collective-permute-start(bf16[64,4096]{1,0:T(8,128)(2,1)S(1)} %joined.6.refs_6_), channel_id=1, source_target_pairs={{0,1},{1,0},{2,3},{3,2},{4,5},{5,4},{6,7},{7,6},{8,9},{9,8},{10,11... | collective-permute-start | bytes 1572872 | tf_op jit(solution)/shard_map/ppermute | solution.py:17
  30.5 10.7 %collective-permute-start.10 = (bf16[64,4096]{1,0:T(8,128)(2,1)S(1)}, bf16[64,4096]{1,0:T(8,128)(2,1)S(1)}, u32[]{:S(2)}, u32[]{:S(2)}) collective-permute-start(bf16[64,4096]{1,0:T(8,128)(2,1)S(1)} %joined.6.refs_6_), channel_id=1, source_target_pairs={{0,4},{1,29},{2,6},{3,31},{4,8},{5,1},{6,10},{7,3},{8,12},{9,5},{1... | collective-permute-start | bytes 1572872 | tf_op jit(solution)/shard_map/ppermute | solution.py:17
  34.7 11.2 %collective-permute-start.11 = (bf16[64,4096]{1,0:T(8,128)(2,1)S(1)}, bf16[64,4096]{1,0:T(8,128)(2,1)S(1)}, u32[]{:S(2)}, u32[]{:S(2)}) collective-permute-start(bf16[64,4096]{1,0:T(8,128)(2,1)S(1)} %collective-permute-done.4.refs_0_), channel_id=1, source_target_pairs={{0,4},{1,29},{2,6},{3,31},{4,8},{5,1},{6,10},{7,3},{8,12},{9,5},{1... | collective-permute-start | bytes 1572872 | tf_op jit(solution)/shard_map/ppermute | solution.py:17
  37.8 11.3 %collective-permute-start.12 = (bf16[64,4096]{1,0:T(8,128)(2,1)S(1)}, bf16[64,4096]{1,0:T(8,128)(2,1)S(1)}, u32[]{:S(2)}, u32[]{:S(2)}) collective-permute-start(bf16[64,4096]{1,0:T(8,128)(2,1)S(1)} %collective-permute-done.4.refs_0_), channel_id=1, source_target_pairs={{0,1},{1,0},{2,3},{3,2},{4,5},{5,4},{6,7},{7,6},{8,9},{9,8},{10,11... | collective-permute-start | bytes 1572872 | tf_op jit(solution)/shard_map/ppermute | solution.py:17
  41.3 7.9 %collective-permute-start.13 = (bf16[64,4096]{1,0:T(8,128)(2,1)S(1)}, bf16[64,4096]{1,0:T(8,128)(2,1)S(1)}, u32[]{:S(2)}, u32[]{:S(2)}) collective-permute-start(bf16[64,4096]{1,0:T(8,128)(2,1)S(1)} %collective-permute-done.10.refs_2_), channel_id=1, source_target_pairs={{0,1},{1,0},{2,3},{3,2},{4,5},{5,4},{6,7},{7,6},{8,9},{9,8},{10,11... | collective-permute-start | bytes 1572872 | tf_op jit(solution)/shard_map/ppermute | solution.py:17
  41.9 12.5 %collective-permute-start.15 = (bf16[64,4096]{1,0:T(8,128)(2,1)S(1)}, bf16[64,4096]{1,0:T(8,128)(2,1)S(1)}, u32[]{:S(2)}, u32[]{:S(2)}) collective-permute-start(bf16[64,4096]{1,0:T(8,128)(2,1)S(1)} %collective-permute-done.10.refs_2_), channel_id=1, source_target_pairs={{0,4},{1,29},{2,6},{3,31},{4,8},{5,1},{6,10},{7,3},{8,12},{9,5},{1... | collective-permute-start | bytes 1572872 | tf_op jit(solution)/shard_map/ppermute | solution.py:17
  46.0 8.4 %collective-permute-start.14 = (bf16[32,4096]{1,0:T(8,128)(2,1)S(1)}, bf16[32,4096]{1,0:T(8,128)(2,1)S(1)}, u32[]{:S(2)}, u32[]{:S(2)}) collective-permute-start(bf16[32,4096]{1,0:T(8,128)(2,1)S(1)} %joined.7), channel_id=1, source_target_pairs={{0,4},{1,29},{2,6},{3,31},{4,8},{5,1},{6,10},{7,3},{8,12},{9,5},{1... | collective-permute-start | bytes 786440 | tf_op jit(solution)/shard_map/ppermute | solution.py:17
  49.1 8.9 %collective-permute-start.16 = (bf16[64,4096]{1,0:T(8,128)(2,1)S(1)}, bf16[64,4096]{1,0:T(8,128)(2,1)S(1)}, u32[]{:S(2)}, u32[]{:S(2)}) collective-permute-start(bf16[64,4096]{1,0:T(8,128)(2,1)S(1)} %collective-permute-done.11.refs_0_), channel_id=1, source_target_pairs={{0,1},{1,0},{2,3},{3,2},{4,5},{5,4},{6,7},{7,6},{8,9},{9,8},{10,11... | collective-permute-start | bytes 1572872 | tf_op jit(solution)/shard_map/ppermute | solution.py:17
  54.4 3.7 %collective-permute-start.17 = (bf16[64,4096]{1,0:T(8,128)(2,1)S(1)}, bf16[64,4096]{1,0:T(8,128)(2,1)S(1)}, u32[]{:S(2)}, u32[]{:S(2)}) collective-permute-start(bf16[64,4096]{1,0:T(8,128)(2,1)S(1)} %collective-permute-done.15.refs_2_.refs_0_), channel_id=1, source_target_pairs={{0,1},{1,0},{2,3},{3,2},{4,5},{5,4},{6,7},{7,6},{8,9},{9,8},{10,11... | collective-permute-start | bytes 1572872 | tf_op jit(solution)/shard_map/ppermute | solution.py:17
  55.7 2.4 %collective-permute-start.18 = (bf16[32,4096]{1,0:T(8,128)(2,1)S(1)}, bf16[32,4096]{1,0:T(8,128)(2,1)S(1)}, u32[]{:S(2)}, u32[]{:S(2)}) collective-permute-start(bf16[32,4096]{1,0:T(8,128)(2,1)S(1)} %collective-permute-done.14.refs_4_), channel_id=1, source_target_pairs={{0,1},{1,0},{2,3},{3,2},{4,5},{5,4},{6,7},{7,6},{8,9},{9,8},{10,11... | collective-permute-start | bytes 786440 | tf_op jit(solution)/shard_map/ppermute | solution.py:17
  55.7 6.0 %collective-permute-start.19 = (bf16[32,4096]{1,0:T(8,128)(2,1)S(1)}, bf16[32,4096]{1,0:T(8,128)(2,1)S(1)}, u32[]{:S(2)}, u32[]{:S(2)}) collective-permute-start(bf16[32,4096]{1,0:T(8,128)(2,1)S(1)} %joined.8), channel_id=1, source_target_pairs={{0,4},{1,29},{2,6},{3,31},{4,8},{5,1},{6,10},{7,3},{8,12},{9,5},{1... | collective-permute-start | bytes 786440 | tf_op jit(solution)/shard_map/ppermute | solution.py:17
  61.7 3.3 %collective-permute-start.20 = (bf16[32,4096]{1,0:T(8,128)(2,1)S(1)}, bf16[32,4096]{1,0:T(8,128)(2,1)S(1)}, u32[]{:S(2)}, u32[]{:S(2)}) collective-permute-start(bf16[32,4096]{1,0:T(8,128)(2,1)S(1)} %collective-permute-done.19.refs_0_), channel_id=1, source_target_pairs={{0,1},{1,0},{2,3},{3,2},{4,5},{5,4},{6,7},{7,6},{8,9},{9,8},{10,11... | collective-permute-start | bytes 786440 | tf_op jit(solution)/shard_map/ppermute | solution.py:17

commit v12 on v11

--- a/solution.py
+++ b/solution.py
@@ -286,10 +286,11 @@
     near = _joined(own, next_to)
     near, across, flat = lax.optimization_barrier((near, across, flat))
     across_other = _swap_core(across)
-    far = _joined(_along(across), _along(across_other))
+    halves = _along(across), _along(across_other)
+    far = _joined(*halves)
     pieces = [panel, other, across, across_other, near, _swap_core(near), far, _swap_core(far)]
     for s in range(2, NZ // 2):
-        near, far = _along(near), _along(far)
+        near, far = _along(near), _joined(*map(_along, halves)) if s == 2 else _along(far)
         cut = _joined(near)
         near, cut, pieces[0] = lax.optimization_barrier((near, cut, pieces[0]))
         steps.append(_score(pieces, flat, scale))

time: 100 us -> 103 us (1.030)
  starting transfers between devices: 34.4 us -> 36.8 us
    ppermute x21 -> x22, starting transfers between devices: 34.4 us -> 36.8 us  [_route(): lax.ppermute(x, 'blk', [(i, target(*divmod(i, 4))) for i in range(NZ * 4)])]
    ppermute x21 -> x22, waiting for transfers between devices: 13 us -> 13.4 us  [_route(): lax.ppermute(x, 'blk', [(i, target(*divmod(i, 4))) for i in range(NZ * 4)])]
  transfers between devices with their start and end apart: 21 -> 22, of which waited for: 6 -> 8; matrix products, arithmetic and copies ran while one was open for 1% -> 1% of each run, Pallas kernels for 13% -> 13%
where the time goes in v12:
time: 103 us
  starting transfers between devices  36.8 us (36%)
  blocking collectives  31.2 us (30%)
  Pallas kernels  20.6 us (20%)
  waiting for transfers between devices  13.4 us (13%)
    ppermute x22, starting transfers between devices, _route(): lax.ppermute(x, 'blk', [(i, target(*divmod(i, 4))) for i in range(NZ * 4)])  36.8 us
    all_to_all x1, blocking collectives, body(): lax.all_to_all(buffer, 'group', split_axis=0, concat_axis=0, tiled=True)  31.2 us
    ppermute x22, waiting for transfers between devices, _route(): lax.ppermute(x, 'blk', [(i, target(*divmod(i, 4))) for i in range(NZ * 4)])  13.4 us
    pallas_call x3, Pallas kernels, _score(): pl.pallas_call(functools.partial(_score_kernel, scale, len(pieces)), in_s...  8.69 us
    pallas_call x1, Pallas kernels, _precond(): pl.pallas_call(_precond_kernel, in_specs=[pl.BlockSpec(memory_space=pltpu...  3.66 us
    pallas_call x1, Pallas kernels, _held(): pl.pallas_call(pltpu.sync_copy, in_specs=[pl.BlockSpec(memory_space=pl.AN...  3.39 us
    pallas_call x1, Pallas kernels, _finish(): pl.pallas_call(functools.partial(_finish_kernel, scale, len(pieces)), in_...  2.9 us
  transfers between devices with their start and end apart: 22, of which 8 were waited for; matrix products, arithmetic and copies ran while one was open for 1% of the time, Pallas kernels for 13%

profile of v12, /device:TPU:1, one launch (start us, length us, event | category | flops | bytes accessed | tf_op | source)
XLA Modules:
  0.0 103.1 jit_solution(7513201728553883414)
XLA Ops:
  0.0 3.7 %precond.1.refs_0_ = bf16[32,4096]{1,0:T(8,128)(2,1)S(1)} custom-call(f32[64,64]{1,0:T(8,128)} %bitcast.40, f32[64,64]{1,0:T(8,128)} %bitcast.41, bf16[32,4096]{1,0:T(8,128)(2,1)} %bitcast.39), custom_call_target="tpu_custom_call" | custom-call | tf_op jit(solution)/shard_map/precond/pallas_call | solution.py:90
  3.7 3.3 %collective-permute-start.1 = (bf16[32,4096]{1,0:T(8,128)(2,1)S(1)}, bf16[32,4096]{1,0:T(8,128)(2,1)S(1)}, u32[]{:S(2)}, u32[]{:S(2)}) collective-permute-start(bf16[32,4096]{1,0:T(8,128)(2,1)S(1)} %precond.1.refs_0_), channel_id=1, source_target_pairs={{0,1},{1,0},{2,3},{3,2},{4,5},{5,4},{6,7},{7,6},{8,9},{9,8},{10,11... | collective-permute-start | bytes 786440 | tf_op jit(solution)/shard_map/ppermute | solution.py:17
  7.0 3.8 %collective-permute-start = (bf16[32,4096]{1,0:T(8,128)(2,1)S(1)}, bf16[32,4096]{1,0:T(8,128)(2,1)S(1)}, u32[]{:S(2)}, u32[]{:S(2)}) collective-permute-start(bf16[32,4096]{1,0:T(8,128)(2,1)S(1)} %precond.1.refs_0_), channel_id=1, source_target_pairs={{0,4},{1,29},{2,6},{3,31},{4,8},{5,1},{6,10},{7,3},{8,12},{9,5},{1... | collective-permute-start | bytes 786440 | tf_op jit(solution)/shard_map/ppermute | solution.py:17
  10.8 0.0 collective-permute-done.1.refs_1_
  10.8 1.2 %collective-permute-start.2 = (bf16[32,4096]{1,0:T(8,128)(2,1)S(1)}, bf16[32,4096]{1,0:T(8,128)(2,1)S(1)}, u32[]{:S(2)}, u32[]{:S(2)}) collective-permute-start(bf16[32,4096]{1,0:T(8,128)(2,1)S(1)} %collective-permute-done.1.refs_1_), channel_id=1, source_target_pairs={{0,4},{1,29},{2,6},{3,31},{4,8},{5,1},{6,10},{7,3},{8,12},{9,5},{1... | collective-permute-start | bytes 786440 | tf_op jit(solution)/shard_map/ppermute | solution.py:17
  12.0 2.9 %collective-permute-start.3 = (bf16[32,4096]{1,0:T(8,128)(2,1)S(1)}, bf16[32,4096]{1,0:T(8,128)(2,1)S(1)}, u32[]{:S(2)}, u32[]{:S(2)}) collective-permute-start(bf16[32,4096]{1,0:T(8,128)(2,1)S(1)} %precond.1.refs_0_), channel_id=1, source_target_pairs={{0,2},{1,3},{2,0},{3,1},{4,6},{5,7},{6,4},{7,5},{8,10},{9,11},{10,... | collective-permute-start | bytes 786440 | tf_op jit(solution)/shard_map/ppermute | solution.py:17
  14.9 0.1 stack.131
  15.0 0.8 select_reduce_fusion.where_ref
  15.9 3.4 %held.1.refs_8_.refs_4_.refs_6_.refs_2_ = bf16[1024,4096]{1,0:T(8,128)(2,1)S(1)} custom-call(bf16[1024,4096]{1,0:T(8,128)(2,1)} %bitcast.38), custom_call_target="tpu_custom_call" | custom-call | bytes 16777216 | tf_op jit(solution)/shard_map/held/pallas_call | solution.py:126
  19.2 0.0 collective-permute-done.refs_0_
  19.3 0.0 collective-permute-done.2.refs_1_
  19.3 0.0 collective-permute-done.3.refs_2_
  19.3 0.1 collective-permute-start.5
  19.4 3.5 %collective-permute-start.7 = (bf16[32,4096]{1,0:T(8,128)(2,1)S(1)}, bf16[32,4096]{1,0:T(8,128)(2,1)S(1)}, u32[]{:S(2)}, u32[]{:S(2)}) collective-permute-start(bf16[32,4096]{1,0:T(8,128)(2,1)S(1)} %collective-permute-done.3.refs_2_), channel_id=1, source_target_pairs={{0,4},{1,29},{2,6},{3,31},{4,8},{5,1},{6,10},{7,3},{8,12},{9,5},{1... | collective-permute-start | bytes 786440 | tf_op jit(solution)/shard_map/ppermute | solution.py:17
  23.0 0.0 collective-permute-done.5.refs_3_
  23.0 1.2 %collective-permute-start.8 = (bf16[32,4096]{1,0:T(8,128)(2,1)S(1)}, bf16[32,4096]{1,0:T(8,128)(2,1)S(1)}, u32[]{:S(2)}, u32[]{:S(2)}) collective-permute-start(bf16[32,4096]{1,0:T(8,128)(2,1)S(1)} %collective-permute-done.5.refs_3_), channel_id=1, source_target_pairs={{0,4},{1,29},{2,6},{3,31},{4,8},{5,1},{6,10},{7,3},{8,12},{9,5},{1... | collective-permute-start | bytes 786440 | tf_op jit(solution)/shard_map/ppermute | solution.py:17
  24.1 0.7 collective-permute-start.4
  24.8 1.4 %collective-permute-done.7.refs_0_ = bf16[32,4096]{1,0:T(8,128)(2,1)S(1)} collective-permute-done((bf16[32,4096]{1,0:T(8,128)(2,1)S(1)}, bf16[32,4096]{1,0:T(8,128)(2,1)S(1)}, u32[]{:S(2)}, u32[]{:S(2)}) %collective-permute-start.7) | collective-permute-done | bytes 262176 | tf_op jit(solution)/shard_map/ppermute | solution.py:17
  26.3 2.8 %collective-permute-done.8.refs_1_ = bf16[32,4096]{1,0:T(8,128)(2,1)S(1)} collective-permute-done((bf16[32,4096]{1,0:T(8,128)(2,1)S(1)}, bf16[32,4096]{1,0:T(8,128)(2,1)S(1)}, u32[]{:S(2)}, u32[]{:S(2)}) %collective-permute-start.8) | collective-permute-done | bytes 262176 | tf_op jit(solution)/shard_map/ppermute | solution.py:17
  29.1 1.4 %collective-permute-start.9 = (bf16[64,4096]{1,0:T(8,128)(2,1)S(1)}, bf16[64,4096]{1,0:T(8,128)(2,1)S(1)}, u32[]{:S(2)}, u32[]{:S(2)}) collective-permute-start(bf16[64,4096]{1,0:T(8,128)(2,1)S(1)} %joined.7.refs_6_), channel_id=1, source_target_pairs={{0,1},{1,0},{2,3},{3,2},{4,5},{5,4},{6,7},{7,6},{8,9},{9,8},{10,11... | collective-permute-start | bytes 1572872 | tf_op jit(solution)/shard_map/ppermute | solution.py:17
  30.5 1.9 %collective-permute-start.10 = (bf16[32,4096]{1,0:T(8,128)(2,1)S(1)}, bf16[32,4096]{1,0:T(8,128)(2,1)S(1)}, u32[]{:S(2)}, u32[]{:S(2)}) collective-permute-start(bf16[32,4096]{1,0:T(8,128)(2,1)S(1)} %collective-permute-done.7.refs_0_), channel_id=1, source_target_pairs={{0,4},{1,29},{2,6},{3,31},{4,8},{5,1},{6,10},{7,3},{8,12},{9,5},{1... | collective-permute-start | bytes 786440 | tf_op jit(solution)/shard_map/ppermute | solution.py:17
  32.4 0.6 collective-permute-start.11
  33.0 1.7 %collective-permute-done.4.refs_0_ = bf16[64,4096]{1,0:T(8,128)(2,1)S(1)} collective-permute-done((bf16[64,4096]{1,0:T(8,128)(2,1)S(1)}, bf16[64,4096]{1,0:T(8,128)(2,1)S(1)}, u32[]{:S(2)}, u32[]{:S(2)}) %collective-permute-start.4) | collective-permute-done | bytes 524320 | tf_op jit(solution)/shard_map/ppermute | solution.py:17
  34.7 1.3 %collective-permute-start.13 = (bf16[64,4096]{1,0:T(8,128)(2,1)S(1)}, bf16[64,4096]{1,0:T(8,128)(2,1)S(1)}, u32[]{:S(2)}, u32[]{:S(2)}) collective-permute-start(bf16[64,4096]{1,0:T(8,128)(2,1)S(1)} %collective-permute-done.4.refs_0_), channel_id=1, source_target_pairs={{0,1},{1,0},{2,3},{3,2},{4,5},{5,4},{6,7},{7,6},{8,9},{9,8},{10,11... | collective-permute-start | bytes 1572872 | tf_op jit(solution)/shard_map/ppermute | solution.py:17
  36.0 1.5 %collective-permute-done.10.refs_0_ = bf16[32,4096]{1,0:T(8,128)(2,1)S(1)} collective-permute-done((bf16[32,4096]{1,0:T(8,128)(2,1)S(1)}, bf16[32,4096]{1,0:T(8,128)(2,1)S(1)}, u32[]{:S(2)}, u32[]{:S(2)}) %collective-permute-start.10) | collective-permute-done | bytes 262176 | tf_op jit(solution)/shard_map/ppermute | solution.py:17
  37.5 3.1 %collective-permute-start.12 = (bf16[64,4096]{1,0:T(8,128)(2,1)S(1)}, bf16[64,4096]{1,0:T(8,128)(2,1)S(1)}, u32[]{:S(2)}, u32[]{:S(2)}) collective-permute-start(bf16[64,4096]{1,0:T(8,128)(2,1)S(1)} %collective-permute-done.4.refs_0_), channel_id=1, source_target_pairs={{0,4},{1,29},{2,6},{3,31},{4,8},{5,1},{6,10},{7,3},{8,12},{9,5},{1... | collective-permute-start | bytes 1572872 | tf_op jit(solution)/shard_map/ppermute | solution.py:17
  40.6 0.0 collective-permute-done.11.refs_1_
  40.7 0.0 collective-permute-done.9.refs_7_
  40.7 3.4 %score.3.refs_0_ = bf16[384,1024]{1,0:T(8,128)(2,1)S(1)} custom-call(bf16[32,4096]{1,0:T(8,128)(2,1)S(1)} %precond.1.refs_0_, bf16[32,4096]{1,0:T(8,128)(2,1)S(1)} %collective-permute-done.1.refs_1_, bf16[32,4096]{1,0:T(8,128)(2,1)S(1)} %collective-permute-done.3.refs_2_, bf16[32,4096]{1,0:T(8,128)(2,1)S(1)} %collective-permute-done.5.refs_3_, ...), custom_call_target="tpu_custom_call" | custom-call | flops 3221225472 | bytes 12320768 | tf_op jit(solution)/shard_map/score/pallas_call | solution.py:151
  44.1 1.1 %collective-permute-start.14 = (bf16[64,4096]{1,0:T(8,128)(2,1)S(1)}, bf16[64,4096]{1,0:T(8,128)(2,1)S(1)}, u32[]{:S(2)}, u32[]{:S(2)}) collective-permute-start(bf16[64,4096]{1,0:T(8,128)(2,1)S(1)} %joined.8.refs_2_), channel_id=1, source_target_pairs={{0,1},{1,0},{2,3},{3,2},{4,5},{5,4},{6,7},{7,6},{8,9},{9,8},{10,11... | collective-permute-start | bytes 1572872 | tf_op jit(solution)/shard_map/ppermute | solution.py:17
  45.2 1.9 %collective-permute-start.16 = (bf16[64,4096]{1,0:T(8,128)(2,1)S(1)}, bf16[64,4096]{1,0:T(8,128)(2,1)S(1)}, u32[]{:S(2)}, u32[]{:S(2)}) collective-permute-start(bf16[64,4096]{1,0:T(8,128)(2,1)S(1)} %joined.8.refs_2_), channel_id=1, source_target_pairs={{0,4},{1,29},{2,6},{3,31},{4,8},{5,1},{6,10},{7,3},{8,12},{9,5},{1... | collective-permute-start | bytes 1572872 | tf_op jit(solution)/shard_map/ppermute | solution.py:17
  47.1 0.0 collective-permute-done.12.refs_0_
  47.1 2.8 %collective-permute-start.15 = (bf16[32,4096]{1,0:T(8,128)(2,1)S(1)}, bf16[32,4096]{1,0:T(8,128)(2,1)S(1)}, u32[]{:S(2)}, u32[]{:S(2)}) collective-permute-start(bf16[32,4096]{1,0:T(8,128)(2,1)S(1)} %joined.9), channel_id=1, source_target_pairs={{0,4},{1,29},{2,6},{3,31},{4,8},{5,1},{6,10},{7,3},{8,12},{9,5},{1... | collective-permute-start | bytes 786440 | tf_op jit(solution)/shard_map/ppermute | solution.py:17
  50.0 0.0 collective-permute-done.14.refs_3_
  50.0 2.4 %score.4.refs_1_ = bf16[256,1024]{1,0:T(8,128)(2,1)S(1)} custom-call(bf16[64,4096]{1,0:T(8,128)(2,1)S(1)} %collective-permute-done.4.refs_0_, bf16[64,4096]{1,0:T(8,128)(2,1)S(1)} %collective-permute-done.13.refs_1_, bf16[64,4096]{1,0:T(8,128)(2,1)S(1)} %joined.8.refs_2_, bf16[64,4096]{1,0:T(8,128)(2,1)S(1)} %collective-permute-done.14.refs_3_, ...), custom_call_target="tpu_custom_call" | custom-call | flops 2147483648 | bytes 11010048 | tf_op jit(solution)/shard_map/score/pallas_call | solution.py:151
  52.3 4.0 %collective-permute-done.15.refs_4_ = bf16[32,4096]{1,0:T(8,128)(2,1)S(1)} collective-permute-done((bf16[32,4096]{1,0:T(8,128)(2,1)S(1)}, bf16[32,4096]{1,0:T(8,128)(2,1)S(1)}, u32[]{:S(2)}, u32[]{:S(2)}) %collective-permute-start.15) | collective-permute-done | bytes 262176 | tf_op jit(solution)/shard_map/ppermute | solution.py:17
  56.4 2.2 %collective-permute-start.18 = (bf16[64,4096]{1,0:T(8,128)(2,1)S(1)}, bf16[64,4096]{1,0:T(8,128)(2,1)S(1)}, u32[]{:S(2)}, u32[]{:S(2)}) collective-permute-start(bf16[64,4096]{1,0:T(8,128)(2,1)S(1)} %collective-permute-done.16.refs_2_.refs_0_), channel_id=1, source_target_pairs={{0,1},{1,0},{2,3},{3,2},{4,5},{5,4},{6,7},{7,6},{8,9},{9,8},{10,11... | collective-permute-start | bytes 1572872 | tf_op jit(solution)/shard_map/ppermute | solution.py:17
  58.5 0.0 collective-permute-start.19
  58.5 1.2 %collective-permute-start.20 = (bf16[32,4096]{1,0:T(8,128)(2,1)S(1)}, bf16[32,4096]{1,0:T(8,128)(2,1)S(1)}, u32[]{:S(2)}, u32[]{:S(2)}) collective-permute-start(bf16[32,4096]{1,0:T(8,128)(2,1)S(1)} %joined.10), channel_id=1, source_target_pairs={{0,4},{1,29},{2,6},{3,31},{4,8},{5,1},{6,10},{7,3},{8,12},{9,5},{1... | collective-permute-start | bytes 786440 | tf_op jit(solution)/shard_map/ppermute | solution.py:17
  59.8 0.7 collective-permute-done.19.refs_5_
  60.4 2.9 %score.5.refs_2_ = bf16[320,1024]{1,0:T(8,128)(2,1)S(1)} custom-call(bf16[64,4096]{1,0:T(8,128)(2,1)S(1)} %collective-permute-done.12.refs_0_, bf16[64,4096]{1,0:T(8,128)(2,1)S(1)} %collective-permute-done.17.refs_1_, bf16[64,4096]{1,0:T(8,128)(2,1)S(1)} %collective-permute-done.16.refs_2_.refs_0_, bf16[64,4096]{1,0:T(8,128)(2,1)S(1)} %collective-permute-done.18.refs_3_, ...), custom_call_target="tpu_custom_call" | custom-call | flops 2684354560 | bytes 11665408 | tf_op jit(solution)/shard_map/score/pallas_call | solution.py:151
  63.3 0.7 place.1.refs_3_
  64.0 0.1 collective-permute-done.20.refs_0_
  64.1 2.6 %collective-permute-start.21 = (bf16[32,4096]{1,0:T(8,128)(2,1)S(1)}, bf16[32,4096]{1,0:T(8,128)(2,1)S(1)}, u32[]{:S(2)}, u32[]{:S(2)}) collective-permute-start(bf16[32,4096]{1,0:T(8,128)(2,1)S(1)} %collective-permute-done.20.refs_0_), channel_id=1, source_target_pairs={{0,1},{1,0},{2,3},{3,2},{4,5},{5,4},{6,7},{7,6},{8,9},{9,8},{10,11... | collective-permute-start | bytes 786440 | tf_op jit(solution)/shard_map/ppermute | solution.py:17
  66.7 1.2 %collective-permute-done.21.refs_1_ = bf16[32,4096]{1,0:T(8,128)(2,1)S(1)} collective-permute-done((bf16[32,4096]{1,0:T(8,128)(2,1)S(1)}, bf16[32,4096]{1,0:T(8,128)(2,1)S(1)}, u32[]{:S(2)}, u32[]{:S(2)}) %collective-permute-start.21) | collective-permute-done | bytes 262176 | tf_op jit(solution)/shard_map/ppermute | solution.py:17
  67.9 2.9 %finish.1 = bf16[32,32,1024]{2,1,0:T(8,128)(2,1)S(1)} custom-call(s32[32]{0:T(128)S(1)} %select_reduce_fusion.where_ref, bf16[32,4096]{1,0:T(8,128)(2,1)S(1)} %collective-permute-done.20.refs_0_, bf16[32,4096]{1,0:T(8,128)(2,1)S(1)} %collective-permute-done.21.refs_1_, ...), custom_call_target="tpu_custom_call", output_to_operand_aliasing={{}: (4, {})} | custom-call | flops 536870912 | bytes 9043968 | tf_op jit(solution)/shard_map/finish/pallas_call | solution.py:204
  70.8 31.2 %all_to_all.5.in_ref = bf16[8,128,1024]{2,1,0:T(8,128)(2,1)S(1)} all-to-all(bf16[8,128,1024]{2,1,0:T(8,128)(2,1)S(1)} %bitcast.37), channel_id=1, replica_groups=mesh['group'=8,'blk'=32] {'group'}, dimensions={0} | all-to-all | bytes 4194304 | tf_op jit(solution)/shard_map/all_to_all | solution.py:308
  101.9 1.1 %total.1 = f32[1024,128]{1,0:T(8,128)} custom-call(bf16[8,128,1024]{2,1,0:T(8,128)(2,1)S(1)} %all_to_all.5.in_ref), custom_call_target="tpu_custom_call" | custom-call | tf_op jit(solution)/shard_map/total/pallas_call | solution.py:231
  (12 shorter events, 0.2 us)
Async XLA Ops:
  3.7 7.2 %collective-permute-start.1 = (bf16[32,4096]{1,0:T(8,128)(2,1)S(1)}, bf16[32,4096]{1,0:T(8,128)(2,1)S(1)}, u32[]{:S(2)}, u32[]{:S(2)}) collective-permute-start(bf16[32,4096]{1,0:T(8,128)(2,1)S(1)} %precond.1.refs_0_), channel_id=1, source_target_pairs={{0,1},{1,0},{2,3},{3,2},{4,5},{5,4},{6,7},{7,6},{8,9},{9,8},{10,11... | collective-permute-start | bytes 786440 | tf_op jit(solution)/shard_map/ppermute | solution.py:17
  7.0 12.3 %collective-permute-start = (bf16[32,4096]{1,0:T(8,128)(2,1)S(1)}, bf16[32,4096]{1,0:T(8,128)(2,1)S(1)}, u32[]{:S(2)}, u32[]{:S(2)}) collective-permute-start(bf16[32,4096]{1,0:T(8,128)(2,1)S(1)} %precond.1.refs_0_), channel_id=1, source_target_pairs={{0,4},{1,29},{2,6},{3,31},{4,8},{5,1},{6,10},{7,3},{8,12},{9,5},{1... | collective-permute-start | bytes 786440 | tf_op jit(solution)/shard_map/ppermute | solution.py:17
  10.8 8.4 %collective-permute-start.2 = (bf16[32,4096]{1,0:T(8,128)(2,1)S(1)}, bf16[32,4096]{1,0:T(8,128)(2,1)S(1)}, u32[]{:S(2)}, u32[]{:S(2)}) collective-permute-start(bf16[32,4096]{1,0:T(8,128)(2,1)S(1)} %collective-permute-done.1.refs_1_), channel_id=1, source_target_pairs={{0,4},{1,29},{2,6},{3,31},{4,8},{5,1},{6,10},{7,3},{8,12},{9,5},{1... | collective-permute-start | bytes 786440 | tf_op jit(solution)/shard_map/ppermute | solution.py:17
  12.0 7.3 %collective-permute-start.3 = (bf16[32,4096]{1,0:T(8,128)(2,1)S(1)}, bf16[32,4096]{1,0:T(8,128)(2,1)S(1)}, u32[]{:S(2)}, u32[]{:S(2)}) collective-permute-start(bf16[32,4096]{1,0:T(8,128)(2,1)S(1)} %precond.1.refs_0_), channel_id=1, source_target_pairs={{0,2},{1,3},{2,0},{3,1},{4,6},{5,7},{6,4},{7,5},{8,10},{9,11},{10,... | collective-permute-start | bytes 786440 | tf_op jit(solution)/shard_map/ppermute | solution.py:17
  19.3 3.6 %collective-permute-start.5 = (bf16[32,4096]{1,0:T(8,128)(2,1)S(1)}, bf16[32,4096]{1,0:T(8,128)(2,1)S(1)}, u32[]{:S(2)}, u32[]{:S(2)}) collective-permute-start(bf16[32,4096]{1,0:T(8,128)(2,1)S(1)} %collective-permute-done.3.refs_2_), channel_id=1, source_target_pairs={{0,1},{1,0},{2,3},{3,2},{4,5},{5,4},{6,7},{7,6},{8,9},{9,8},{10,11... | collective-permute-start | bytes 786440 | tf_op jit(solution)/shard_map/ppermute | solution.py:17
  19.4 6.9 %collective-permute-start.7 = (bf16[32,4096]{1,0:T(8,128)(2,1)S(1)}, bf16[32,4096]{1,0:T(8,128)(2,1)S(1)}, u32[]{:S(2)}, u32[]{:S(2)}) collective-permute-start(bf16[32,4096]{1,0:T(8,128)(2,1)S(1)} %collective-permute-done.3.refs_2_), channel_id=1, source_target_pairs={{0,4},{1,29},{2,6},{3,31},{4,8},{5,1},{6,10},{7,3},{8,12},{9,5},{1... | collective-permute-start | bytes 786440 | tf_op jit(solution)/shard_map/ppermute | solution.py:17
  23.0 6.1 %collective-permute-start.8 = (bf16[32,4096]{1,0:T(8,128)(2,1)S(1)}, bf16[32,4096]{1,0:T(8,128)(2,1)S(1)}, u32[]{:S(2)}, u32[]{:S(2)}) collective-permute-start(bf16[32,4096]{1,0:T(8,128)(2,1)S(1)} %collective-permute-done.5.refs_3_), channel_id=1, source_target_pairs={{0,4},{1,29},{2,6},{3,31},{4,8},{5,1},{6,10},{7,3},{8,12},{9,5},{1... | collective-permute-start | bytes 786440 | tf_op jit(solution)/shard_map/ppermute | solution.py:17
  24.1 10.6 %collective-permute-start.4 = (bf16[64,4096]{1,0:T(8,128)(2,1)S(1)}, bf16[64,4096]{1,0:T(8,128)(2,1)S(1)}, u32[]{:S(2)}, u32[]{:S(2)}) collective-permute-start(bf16[64,4096]{1,0:T(8,128)(2,1)S(1)} %joined.6.refs_4_), channel_id=1, source_target_pairs={{0,4},{1,29},{2,6},{3,31},{4,8},{5,1},{6,10},{7,3},{8,12},{9,5},{1... | collective-permute-start | bytes 1572872 | tf_op jit(solution)/shard_map/ppermute | solution.py:17
  24.8 15.8 %collective-permute-start.6 = (bf16[64,4096]{1,0:T(8,128)(2,1)S(1)}, bf16[64,4096]{1,0:T(8,128)(2,1)S(1)}, u32[]{:S(2)}, u32[]{:S(2)}) collective-permute-start(bf16[64,4096]{1,0:T(8,128)(2,1)S(1)} %joined.6.refs_4_), channel_id=1, source_target_pairs={{0,1},{1,0},{2,3},{3,2},{4,5},{5,4},{6,7},{7,6},{8,9},{9,8},{10,11... | collective-permute-start | bytes 1572872 | tf_op jit(solution)/shard_map/ppermute | solution.py:17
  29.1 11.6 %collective-permute-start.9 = (bf16[64,4096]{1,0:T(8,128)(2,1)S(1)}, bf16[64,4096]{1,0:T(8,128)(2,1)S(1)}, u32[]{:S(2)}, u32[]{:S(2)}) collective-permute-start(bf16[64,4096]{1,0:T(8,128)(2,1)S(1)} %joined.7.refs_6_), channel_id=1, source_target_pairs={{0,1},{1,0},{2,3},{3,2},{4,5},{5,4},{6,7},{7,6},{8,9},{9,8},{10,11... | collective-permute-start | bytes 1572872 | tf_op jit(solution)/shard_map/ppermute | solution.py:17
  30.5 7.0 %collective-permute-start.10 = (bf16[32,4096]{1,0:T(8,128)(2,1)S(1)}, bf16[32,4096]{1,0:T(8,128)(2,1)S(1)}, u32[]{:S(2)}, u32[]{:S(2)}) collective-permute-start(bf16[32,4096]{1,0:T(8,128)(2,1)S(1)} %collective-permute-done.7.refs_0_), channel_id=1, source_target_pairs={{0,4},{1,29},{2,6},{3,31},{4,8},{5,1},{6,10},{7,3},{8,12},{9,5},{1... | collective-permute-start | bytes 786440 | tf_op jit(solution)/shard_map/ppermute | solution.py:17
  32.4 8.2 %collective-permute-start.11 = (bf16[32,4096]{1,0:T(8,128)(2,1)S(1)}, bf16[32,4096]{1,0:T(8,128)(2,1)S(1)}, u32[]{:S(2)}, u32[]{:S(2)}) collective-permute-start(bf16[32,4096]{1,0:T(8,128)(2,1)S(1)} %collective-permute-done.8.refs_1_), channel_id=1, source_target_pairs={{0,4},{1,29},{2,6},{3,31},{4,8},{5,1},{6,10},{7,3},{8,12},{9,5},{1... | collective-permute-start | bytes 786440 | tf_op jit(solution)/shard_map/ppermute | solution.py:17
  34.7 15.3 %collective-permute-start.13 = (bf16[64,4096]{1,0:T(8,128)(2,1)S(1)}, bf16[64,4096]{1,0:T(8,128)(2,1)S(1)}, u32[]{:S(2)}, u32[]{:S(2)}) collective-permute-start(bf16[64,4096]{1,0:T(8,128)(2,1)S(1)} %collective-permute-done.4.refs_0_), channel_id=1, source_target_pairs={{0,1},{1,0},{2,3},{3,2},{4,5},{5,4},{6,7},{7,6},{8,9},{9,8},{10,11... | collective-permute-start | bytes 1572872 | tf_op jit(solution)/shard_map/ppermute | solution.py:17
  37.5 9.6 %collective-permute-start.12 = (bf16[64,4096]{1,0:T(8,128)(2,1)S(1)}, bf16[64,4096]{1,0:T(8,128)(2,1)S(1)}, u32[]{:S(2)}, u32[]{:S(2)}) collective-permute-start(bf16[64,4096]{1,0:T(8,128)(2,1)S(1)} %collective-permute-done.4.refs_0_), channel_id=1, source_target_pairs={{0,4},{1,29},{2,6},{3,31},{4,8},{5,1},{6,10},{7,3},{8,12},{9,5},{1... | collective-permute-start | bytes 1572872 | tf_op jit(solution)/shard_map/ppermute | solution.py:17
  44.1 5.8 %collective-permute-start.14 = (bf16[64,4096]{1,0:T(8,128)(2,1)S(1)}, bf16[64,4096]{1,0:T(8,128)(2,1)S(1)}, u32[]{:S(2)}, u32[]{:S(2)}) collective-permute-start(bf16[64,4096]{1,0:T(8,128)(2,1)S(1)} %joined.8.refs_2_), channel_id=1, source_target_pairs={{0,1},{1,0},{2,3},{3,2},{4,5},{5,4},{6,7},{7,6},{8,9},{9,8},{10,11... | collective-permute-start | bytes 1572872 | tf_op jit(solution)/shard_map/ppermute | solution.py:17
  45.2 11.1 %collective-permute-start.16 = (bf16[64,4096]{1,0:T(8,128)(2,1)S(1)}, bf16[64,4096]{1,0:T(8,128)(2,1)S(1)}, u32[]{:S(2)}, u32[]{:S(2)}) collective-permute-start(bf16[64,4096]{1,0:T(8,128)(2,1)S(1)} %joined.8.refs_2_), channel_id=1, source_target_pairs={{0,4},{1,29},{2,6},{3,31},{4,8},{5,1},{6,10},{7,3},{8,12},{9,5},{1... | collective-permute-start | bytes 1572872 | tf_op jit(solution)/shard_map/ppermute | solution.py:17
  47.1 9.2 %collective-permute-start.15 = (bf16[32,4096]{1,0:T(8,128)(2,1)S(1)}, bf16[32,4096]{1,0:T(8,128)(2,1)S(1)}, u32[]{:S(2)}, u32[]{:S(2)}) collective-permute-start(bf16[32,4096]{1,0:T(8,128)(2,1)S(1)} %joined.9), channel_id=1, source_target_pairs={{0,4},{1,29},{2,6},{3,31},{4,8},{5,1},{6,10},{7,3},{8,12},{9,5},{1... | collective-permute-start | bytes 786440 | tf_op jit(solution)/shard_map/ppermute | solution.py:17
  50.0 9.8 %collective-permute-start.17 = (bf16[64,4096]{1,0:T(8,128)(2,1)S(1)}, bf16[64,4096]{1,0:T(8,128)(2,1)S(1)}, u32[]{:S(2)}, u32[]{:S(2)}) collective-permute-start(bf16[64,4096]{1,0:T(8,128)(2,1)S(1)} %collective-permute-done.12.refs_0_), channel_id=1, source_target_pairs={{0,1},{1,0},{2,3},{3,2},{4,5},{5,4},{6,7},{7,6},{8,9},{9,8},{10,11... | collective-permute-start | bytes 1572872 | tf_op jit(solution)/shard_map/ppermute | solution.py:17
  56.4 4.1 %collective-permute-start.18 = (bf16[64,4096]{1,0:T(8,128)(2,1)S(1)}, bf16[64,4096]{1,0:T(8,128)(2,1)S(1)}, u32[]{:S(2)}, u32[]{:S(2)}) collective-permute-start(bf16[64,4096]{1,0:T(8,128)(2,1)S(1)} %collective-permute-done.16.refs_2_.refs_0_), channel_id=1, source_target_pairs={{0,1},{1,0},{2,3},{3,2},{4,5},{5,4},{6,7},{7,6},{8,9},{9,8},{10,11... | collective-permute-start | bytes 1572872 | tf_op jit(solution)/shard_map/ppermute | solution.py:17
  58.5 1.9 %collective-permute-start.19 = (bf16[32,4096]{1,0:T(8,128)(2,1)S(1)}, bf16[32,4096]{1,0:T(8,128)(2,1)S(1)}, u32[]{:S(2)}, u32[]{:S(2)}) collective-permute-start(bf16[32,4096]{1,0:T(8,128)(2,1)S(1)} %collective-permute-done.15.refs_4_), channel_id=1, source_target_pairs={{0,1},{1,0},{2,3},{3,2},{4,5},{5,4},{6,7},{7,6},{8,9},{9,8},{10,11... | collective-permute-start | bytes 786440 | tf_op jit(solution)/shard_map/ppermute | solution.py:17
  58.5 5.6 %collective-permute-start.20 = (bf16[32,4096]{1,0:T(8,128)(2,1)S(1)}, bf16[32,4096]{1,0:T(8,128)(2,1)S(1)}, u32[]{:S(2)}, u32[]{:S(2)}) collective-permute-start(bf16[32,4096]{1,0:T(8,128)(2,1)S(1)} %joined.10), channel_id=1, source_target_pairs={{0,4},{1,29},{2,6},{3,31},{4,8},{5,1},{6,10},{7,3},{8,12},{9,5},{1... | collective-permute-start | bytes 786440 | tf_op jit(solution)/shard_map/ppermute | solution.py:17
  64.1 3.7 %collective-permute-start.21 = (bf16[32,4096]{1,0:T(8,128)(2,1)S(1)}, bf16[32,4096]{1,0:T(8,128)(2,1)S(1)}, u32[]{:S(2)}, u32[]{:S(2)}) collective-permute-start(bf16[32,4096]{1,0:T(8,128)(2,1)S(1)} %collective-permute-done.20.refs_0_), channel_id=1, source_target_pairs={{0,1},{1,0},{2,3},{3,2},{4,5},{5,4},{6,7},{7,6},{8,9},{9,8},{10,11... | collective-permute-start | bytes 786440 | tf_op jit(solution)/shard_map/ppermute | solution.py:17
